TPU v7x, 32 devices: a whole 2x2x4 slice. The times are simulated.
32 devices in a mesh: dp: 4 (over y, core), ctx: 2 (over x), tensor: 4 (over z).
Axes of the slice: x: 2, y: 2, z: 4, core: 2. Of those that a mesh axis runs over, the one named last changes fastest.
Arguments:
- tokens: bfloat16 [16384, 2048], P(('dp', 'ctx')), may hold values from -6 to 6
- cotangent: bfloat16 [16384, 2048], P(('dp', 'ctx')), may hold values from -6 to 6
- span_order: int32 [4, 4], P('dp'), may hold values from 0 to 3, each once within a row
- norm_attn: float32 [2048], replicated, may hold values from 0.5 to 1.5
- w_query: bfloat16 [2048, 2048], P(None, 'tensor'), may hold values from -0.125 to 0.125
- w_key: bfloat16 [2048, 256], replicated, may hold values from -0.125 to 0.125
- w_value: bfloat16 [2048, 256], replicated, may hold values from -0.125 to 0.125
- w_output: bfloat16 [2048, 2048], P(None, 'tensor'), may hold values from -2 to 2
- norm_mlp: float32 [2048], replicated, may hold values from 0.5 to 1.5
- w_gate: bfloat16 [2048, 5632], P(None, 'tensor'), may hold values from -0.125 to 0.125
- w_up: bfloat16 [2048, 5632], P(None, 'tensor'), may hold values from -0.125 to 0.125
- w_down: bfloat16 [2048, 5632], P(None, 'tensor'), may hold values from -0.078125 to 0.078125
Outputs:
- mixed: bfloat16 [16384, 2048], P(('dp', 'ctx'))
- tokens_grad: bfloat16 [16384, 2048], P(('dp', 'ctx'))
- norm_attn_grad: float32 [2048], P(('dp', 'ctx'))
- w_query_grad: float32 [2048, 2048], P(('dp', 'ctx'), 'tensor')
- w_key_grad: float32 [2048, 256], P(('dp', 'ctx', 'tensor'))
- w_value_grad: float32 [2048, 256], P(('dp', 'ctx', 'tensor'))
- w_output_grad: float32 [2048, 2048], P(('dp', 'ctx'), 'tensor')
- norm_mlp_grad: float32 [2048], P(('dp', 'ctx'))
- w_gate_grad: float32 [2048, 5632], P(('dp', 'ctx'), 'tensor')
- w_up_grad: float32 [2048, 5632], P(('dp', 'ctx'), 'tensor')
- w_down_grad: float32 [2048, 5632], P(('dp', 'ctx'), 'tensor')
Inputs may be any that keep to these rules, and one draw needn't show every extreme that they name: Each row is a permutation of the 4 blocks of one sequence, a permuted block order; slot j holds positions span_order[s, j] * 1024 onward, and index c of ctx holds slots 2c and 2c + 1.
All inputs are finite; a program needn't handle non-finite values.
Results may differ from a plain program's by a relative error of at most 0.023.
Values may be sent and summed in bfloat16 or wider, within the bound.
No kernel may reach another device: no remote copies, remote signals or barrier semaphores. Data moves between devices by JAX's collectives and lax.ppermute only.
A program may use at most 448 MiB of HBM per device.

v0:
```python
import jax
import jax.numpy as jnp
from jax import lax
from jax.sharding import PartitionSpec as P

HD = 64


epsilon = 1e-05


def rotate(values, positions, inverse):
    half_dim = values.shape[-1] // 2
    frequency = 10000.0 ** (-jnp.arange(half_dim, dtype=jnp.float32) / half_dim)
    angles = positions.astype(jnp.float32)[:, None] * frequency[None, :]
    cosine = jnp.cos(angles)[:, None, :]
    sine_part = jnp.sin(angles)[:, None, :]
    if inverse:
        sine_part = -sine_part
    first_half = values[..., :half_dim]
    second_half = values[..., half_dim:]
    return jnp.concatenate(
        [
            first_half * cosine - second_half * sine_part,
            second_half * cosine + first_half * sine_part,
        ],
        axis=-1,
    )


def attend_block(query_block, block_positions, keys_all, values_all, key_positions, score_scale):
    scores = (
        jnp.einsum("bhd,kd->hbk", query_block, keys_all, preferred_element_type=jnp.float32)
        * score_scale
    )
    visible = key_positions[None, :] <= block_positions[:, None]
    scores = jnp.where(visible[None], scores, -1e30)
    row_max = jnp.max(scores, axis=-1, keepdims=True)
    weights = jnp.exp(scores - row_max)
    row_total = jnp.sum(weights, axis=-1, keepdims=True)
    softmax_low = (weights / row_total).astype(jnp.bfloat16)
    result = jnp.einsum("hbk,kd->bhd", softmax_low, values_all, preferred_element_type=jnp.float32)
    return (result, (row_max + jnp.log(row_total))[..., 0])


def attend_back(
    query_block,
    block_positions,
    log_total,
    grad_block,
    keys_all,
    values_all,
    key_positions,
    score_scale,
):
    scores = (
        jnp.einsum("bhd,kd->hbk", query_block, keys_all, preferred_element_type=jnp.float32)
        * score_scale
    )
    visible = key_positions[None, :] <= block_positions[:, None]
    softmax_f32 = jnp.exp(jnp.where(visible[None], scores, -1e30) - log_total[..., None])
    grad_probs = jnp.einsum(
        "bhd,kd->hbk", grad_block, values_all, preferred_element_type=jnp.float32
    )
    row_delta = jnp.sum(softmax_f32 * grad_probs, axis=-1, keepdims=True)
    grad_scores = (softmax_f32 * (grad_probs - row_delta)).astype(jnp.bfloat16)
    grad_query = (
        jnp.einsum("hbk,kd->bhd", grad_scores, keys_all, preferred_element_type=jnp.float32)
        * score_scale
    )
    grad_key = (
        jnp.einsum("hbk,bhd->kd", grad_scores, query_block, preferred_element_type=jnp.float32)
        * score_scale
    )
    grad_value = jnp.einsum(
        "hbk,bhd->kd",
        softmax_f32.astype(jnp.bfloat16),
        grad_block,
        preferred_element_type=jnp.float32,
    )
    return (grad_query, grad_key, grad_value)


def body(
    tokens,
    cotangent,
    span_order,
    norm_attn,
    w_query,
    w_key,
    w_value,
    w_output,
    norm_mlp,
    w_gate,
    w_up,
    w_down,
):
    tok_rows = tokens.shape[0]
    groups = lax.axis_size("tensor")
    member = lax.axis_index("tensor")
    ctx_index = lax.axis_index("ctx")
    head_count = w_query.shape[1] // HD
    kv_count = w_key.shape[1] // HD
    kv_start = member * kv_count // groups * HD
    key_weight = lax.dynamic_slice_in_dim(w_key, kv_start, HD, 1)
    value_weight = lax.dynamic_slice_in_dim(w_value, kv_start, HD, 1)
    span_len = tok_rows // 2
    slot_order = span_order[0]
    key_positions = (
        slot_order[:, None] * span_len + jnp.arange(span_len, dtype=jnp.int32)[None, :]
    ).reshape(-1)
    row_positions = lax.dynamic_slice_in_dim(key_positions, ctx_index * tok_rows, tok_rows)
    score_scale = HD ** (-0.5)
    block_rows = min(512, tok_rows)
    block_count = tok_rows // block_rows
    inputs = tokens.astype(jnp.float32)
    inverse_one = lax.rsqrt(jnp.mean(inputs * inputs, axis=-1, keepdims=True) + epsilon)
    normed = (inputs * inverse_one * norm_attn).astype(jnp.bfloat16)
    query_raw = jnp.dot(normed, w_query, preferred_element_type=jnp.float32)
    key_raw = jnp.dot(normed, key_weight, preferred_element_type=jnp.float32)
    value_raw = jnp.dot(normed, value_weight, preferred_element_type=jnp.float32)
    query_rot = rotate(query_raw.reshape(tok_rows, head_count, HD), row_positions, False).astype(
        jnp.bfloat16
    )
    key_rot = rotate(key_raw.reshape(tok_rows, 1, HD), row_positions, False).reshape(tok_rows, HD)
    kv_pairs = jnp.concatenate([key_rot, value_raw], axis=1).astype(jnp.bfloat16)
    kv_all = lax.all_gather(kv_pairs, "ctx", axis=0, tiled=True)
    keys_all = kv_all[:, :HD]
    values_all = kv_all[:, HD:]
    query_blocks = query_rot.reshape(block_count, block_rows, head_count, HD)
    position_blocks = row_positions.reshape(block_count, block_rows)

    def forward_block(block_items):
        return attend_block(
            block_items[0], block_items[1], keys_all, values_all, key_positions, score_scale
        )

    attended, log_totals = lax.map(forward_block, (query_blocks, position_blocks))
    attention = attended.reshape(tok_rows, head_count * HD).astype(jnp.bfloat16)
    attn_part = jnp.einsum("rq,dq->rd", attention, w_output, preferred_element_type=jnp.float32)
    attn_out = lax.psum(attn_part, "tensor")
    middle = inputs + attn_out
    inverse_two = lax.rsqrt(jnp.mean(middle * middle, axis=-1, keepdims=True) + epsilon)
    normed_mlp = (middle * inverse_two * norm_mlp).astype(jnp.bfloat16)
    gate_proj = jnp.dot(normed_mlp, w_gate, preferred_element_type=jnp.float32)
    up_proj = jnp.dot(normed_mlp, w_up, preferred_element_type=jnp.float32)
    sigmoid_gate = jax.nn.sigmoid(gate_proj)
    hidden = (gate_proj * sigmoid_gate * up_proj).astype(jnp.bfloat16)
    mlp_part = jnp.einsum("rf,df->rd", hidden, w_down, preferred_element_type=jnp.float32)
    mlp_out = lax.psum(mlp_part.astype(jnp.bfloat16), "tensor").astype(jnp.float32)
    mixed = (middle + mlp_out).astype(jnp.bfloat16)
    grad_hidden = jnp.einsum("rd,df->rf", cotangent, w_down, preferred_element_type=jnp.float32)
    grad_gate = (
        grad_hidden * up_proj * sigmoid_gate * (1.0 + gate_proj * (1.0 - sigmoid_gate))
    ).astype(jnp.bfloat16)
    grad_up = (grad_hidden * gate_proj * sigmoid_gate).astype(jnp.bfloat16)
    down_grad = jnp.einsum("rd,rf->df", cotangent, hidden, preferred_element_type=jnp.float32)
    gate_grad = jnp.einsum("rd,rf->df", normed_mlp, grad_gate, preferred_element_type=jnp.float32)
    up_grad = jnp.einsum("rd,rf->df", normed_mlp, grad_up, preferred_element_type=jnp.float32)
    grad_normed_part = jnp.einsum(
        "rf,df->rd", grad_gate, w_gate, preferred_element_type=jnp.float32
    )
    grad_normed_part = grad_normed_part + jnp.einsum(
        "rf,df->rd", grad_up, w_up, preferred_element_type=jnp.float32
    )
    grad_normed_mlp = lax.psum(grad_normed_part.astype(jnp.bfloat16), "tensor").astype(jnp.float32)
    grad_out = cotangent.astype(jnp.float32)
    mlp_gain_grad = jnp.sum(grad_normed_mlp * middle * inverse_two, axis=0)
    scaled_two = grad_normed_mlp * norm_mlp
    grad_middle = (
        grad_out
        + inverse_two * scaled_two
        - middle * inverse_two**3 * jnp.mean(scaled_two * middle, axis=-1, keepdims=True)
    )
    grad_mid_low = grad_middle.astype(jnp.bfloat16)
    output_grad = jnp.einsum(
        "rd,rq->dq", grad_mid_low, attention, preferred_element_type=jnp.float32
    )
    grad_attention = jnp.einsum(
        "rd,dq->rq", grad_mid_low, w_output, preferred_element_type=jnp.float32
    ).astype(jnp.bfloat16)
    grad_blocks = grad_attention.reshape(block_count, block_rows, head_count, HD)

    def backward_block(carry, block_items):
        grad_query, grad_key, grad_value = attend_back(
            block_items[0],
            block_items[1],
            block_items[2],
            block_items[3],
            keys_all,
            values_all,
            key_positions,
            score_scale,
        )
        return ((carry[0] + grad_key, carry[1] + grad_value), grad_query)

    start = (
        jnp.zeros((key_positions.shape[0], HD), jnp.float32),
        jnp.zeros((key_positions.shape[0], HD), jnp.float32),
    )
    kv_sums, grad_query_blocks = lax.scan(
        backward_block, start, (query_blocks, position_blocks, log_totals, grad_blocks)
    )
    kv_grad_share = lax.psum_scatter(
        jnp.concatenate([kv_sums[0], kv_sums[1]], axis=1).astype(jnp.bfloat16),
        "ctx",
        scatter_dimension=0,
        tiled=True,
    ).astype(jnp.float32)
    grad_query_raw = (
        rotate(grad_query_blocks.reshape(tok_rows, head_count, HD), row_positions, True)
        .reshape(tok_rows, head_count * HD)
        .astype(jnp.bfloat16)
    )
    grad_key_raw = (
        rotate(kv_grad_share[:, None, :HD], row_positions, True)
        .reshape(tok_rows, HD)
        .astype(jnp.bfloat16)
    )
    grad_value_raw = kv_grad_share[:, HD:].astype(jnp.bfloat16)
    query_grad = jnp.einsum("rd,rq->dq", normed, grad_query_raw, preferred_element_type=jnp.float32)
    key_part = jnp.einsum("rd,re->de", normed, grad_key_raw, preferred_element_type=jnp.float32)
    value_part = jnp.einsum("rd,re->de", normed, grad_value_raw, preferred_element_type=jnp.float32)
    zeros_full = jnp.zeros(w_key.shape, jnp.float32)
    key_grad_full = lax.dynamic_update_slice_in_dim(zeros_full, key_part, kv_start, 1)
    value_grad_full = lax.dynamic_update_slice_in_dim(zeros_full, value_part, kv_start, 1)
    grad_normed_attn = jnp.einsum(
        "rq,dq->rd", grad_query_raw, w_query, preferred_element_type=jnp.float32
    )
    grad_normed_attn = grad_normed_attn + jnp.einsum(
        "re,de->rd", grad_key_raw, key_weight, preferred_element_type=jnp.float32
    )
    grad_normed_attn = grad_normed_attn + jnp.einsum(
        "re,de->rd", grad_value_raw, value_weight, preferred_element_type=jnp.float32
    )
    grad_normed = lax.psum(grad_normed_attn.astype(jnp.bfloat16), "tensor").astype(jnp.float32)
    attn_gain_grad = jnp.sum(grad_normed * inputs * inverse_one, axis=0)
    scaled_one = grad_normed * norm_attn
    grad_inputs = (
        grad_middle
        + inverse_one * scaled_one
        - inputs * inverse_one**3 * jnp.mean(scaled_one * inputs, axis=-1, keepdims=True)
    )
    tokens_grad = grad_inputs.astype(jnp.bfloat16)
    kv_results = (
        lax.psum_scatter(key_grad_full, ("dp", "ctx", "tensor"), scatter_dimension=0, tiled=True),
        lax.psum_scatter(value_grad_full, ("dp", "ctx", "tensor"), scatter_dimension=0, tiled=True),
    )
    all_results = (
        lax.psum_scatter(
            attn_gain_grad.astype(jnp.bfloat16), ("dp", "ctx"), scatter_dimension=0, tiled=True
        ).astype(jnp.float32),
        lax.psum_scatter(
            query_grad.astype(jnp.bfloat16), ("dp", "ctx"), scatter_dimension=0, tiled=True
        ).astype(jnp.float32),
        lax.psum_scatter(
            output_grad.astype(jnp.bfloat16), ("dp", "ctx"), scatter_dimension=0, tiled=True
        ).astype(jnp.float32),
        lax.psum_scatter(
            mlp_gain_grad.astype(jnp.bfloat16), ("dp", "ctx"), scatter_dimension=0, tiled=True
        ).astype(jnp.float32),
        lax.psum_scatter(
            gate_grad.astype(jnp.bfloat16), ("dp", "ctx"), scatter_dimension=0, tiled=True
        ).astype(jnp.float32),
        lax.psum_scatter(
            up_grad.astype(jnp.bfloat16), ("dp", "ctx"), scatter_dimension=0, tiled=True
        ).astype(jnp.float32),
        lax.psum_scatter(
            down_grad.astype(jnp.bfloat16), ("dp", "ctx"), scatter_dimension=0, tiled=True
        ).astype(jnp.float32),
    )
    attn_results = (all_results[0], all_results[1], all_results[2])
    mlp_results = (all_results[3], all_results[4], all_results[5], all_results[6])
    attn_gain_out = attn_results[0]
    mlp_gain_out = mlp_results[0]
    return (
        mixed,
        tokens_grad,
        attn_gain_out,
        attn_results[1],
        kv_results[0],
        kv_results[1],
        attn_results[2],
        mlp_gain_out,
        mlp_results[1],
        mlp_results[2],
        mlp_results[3],
    )


def solution(mesh):
    placed = (
        P(("dp", "ctx"), None),
        P(("dp", "ctx"), None),
        P("dp", None),
        P(),
        P(None, "tensor"),
        P(),
        P(),
        P(None, "tensor"),
        P(),
        P(None, "tensor"),
        P(None, "tensor"),
        P(None, "tensor"),
    )
    return jax.shard_map(
        body,
        mesh=mesh,
        in_specs=placed,
        out_specs=(
            P(("dp", "ctx"), None),
            P(("dp", "ctx"), None),
            P(("dp", "ctx")),
            P(("dp", "ctx"), "tensor"),
            P(("dp", "ctx", "tensor"), None),
            P(("dp", "ctx", "tensor"), None),
            P(("dp", "ctx"), "tensor"),
            P(("dp", "ctx")),
            P(("dp", "ctx"), "tensor"),
            P(("dp", "ctx"), "tensor"),
            P(("dp", "ctx"), "tensor"),
        ),
        check_vma=False,
    )
```

profile of v0, /device:TPU:0, one launch (start us, length us, event | category | flops | bytes accessed | tf_op | source)
XLA Modules:
  0.0 3389.9 jit_solution(1318152137540785160)
XLA Ops:
  60.5 317.6 %while.28 = (s32[]{:T(128)}, bf16[4,512,8,64]{1,3,2,0:T(8,128)(2,1)}, f32[4,8,512]{2,1,0:T(8,128)}, s32[4,512]{1,0:T(4,128)}, bf16[4,512,8,64]{1,3,2,0:T(8,128)(...) while((s32[]{:T(128)}, ...), condition=%wide.region_4.5_spmd.clone, body=%wide.region_1.4_spmd.clone.sunk | while | flops 4498391040 | bytes 212539504 | solution.py:138
  65.0 25.0 bitcast_reduce_fusion.2
  90.0 22.8 fusion.171
  112.8 26.8 fusion.172
  144.3 25.0 bitcast_reduce_fusion.2
  169.3 22.8 fusion.171
  192.1 26.8 fusion.172
  223.6 25.0 bitcast_reduce_fusion.2
  248.6 22.8 fusion.171
  271.4 26.8 fusion.172
  302.9 25.0 bitcast_reduce_fusion.2
  327.9 22.8 fusion.171
  350.6 26.8 fusion.172
  392.1 562.3 %all-reduce.8.cloned.1.call-done = f32[2048,2048]{1,0:T(8,128)} async-done(((f32[2048,2048]{1,0:T(8,128)}), f32[2048,2048]{1,0:T(8,128)}) %all-reduce.8.cloned.1.call-update) | async-done | bytes 16777232 | tf_op jit(solution)/shard_map/psum | solution.py:141
  970.6 19.0 fusion.116
  989.7 15.8 fusion.115
  1005.5 29.5 multiply_convert_fusion.1
  1035.0 19.3 fusion.117
  1054.3 21.9 add_convert_fusion.1
  1076.3 289.9 %all-reduce.10.cloned.1.call-done = bf16[2048,2048]{1,0:T(8,128)(2,1)} async-done(((bf16[2048,2048]{1,0:T(8,128)(2,1)}), bf16[2048,2048]{1,0:T(8,128)(2,1)}) %all-reduce.10.cloned.1.call-update) | async-done | bytes 8388624 | tf_op jit(solution)/shard_map/psum | solution.py:166
  1412.5 822.4 %while.29 = (s32[]{:T(128)}, f32[4096,64]{0,1:T(8,128)}, f32[4096,64]{0,1:T(8,128)}, f32[4,512,8,64]{1,0,3,2:T(4,128)}, s32[4,512]{1,0:T(4,128)}, /*index=5*/bf1...) while((s32[]{:T(128)}, f32[4096,64]{0,1:T(8,128)}, ...), condition=%wide.region_12.13_spmd.clone, body=%wide.region_10.12_spmd.clone.sunk | while | flops 10892083200 | bytes 537549120 | solution.py:201
  1416.2 24.3 fusion.181
  1440.5 47.9 %fusion.182 = (f32[8,512]{1,0:T(8,128)S(1)}, f32[8,512,4096]{2,1,0:T(8,128)}) fusion(f32[512,8,4096]{2,0,1:T(8,128)} %fusion.181, f32[8,512]{1,0:T(8,128)S(1)} %dynamic-slice_bitcast_fusion.2, bf16[4096,64]{0,1:T(8,128)(2,1)S(1)} %get-tuple-element.519, bf16[4,512,8,64]{1,3,2,0:T(8,128)(2,1)} %get-tuple-element.518, s32[]{:T(128)S(6)} %copy.91, ...), kind=kOutput, calls=%fused_computation.26.clone.2 | convolution fusion | flops 2231365632 | bytes 137396224 | tf_op jit(solution)/shard_map/while/body/eval_jaxpr/bhd,kd->hbk/dot_general | solution.py:57
  1488.3 53.0 %fusion.183 = bf16[8,512,4096]{2,1,0:T(8,128)(2,1)} fusion(f32[8,512,4096]{2,1,0:T(8,128)} %get-tuple-element.458, f32[512,8,4096]{2,0,1:T(8,128)} %fusion.181, f32[8,512]{1,0:T(8,128)S(1)} %get-tuple-element.459), kind=kLoop, calls=%fused_computation.28.clone.1 | loop fusion | flops 50331648 | bytes 167788544 | tf_op jit(solution)/shard_map/while/body/eval_jaxpr/convert_element_type | solution.py:66
  1541.4 22.7 fusion.185
  1565.1 13.8 fusion.184
  1579.8 16.2 fusion.186
  1597.1 21.1 dynamic_update_slice.29
  1621.7 24.3 fusion.181
  1645.9 47.9 %fusion.182 = (f32[8,512]{1,0:T(8,128)S(1)}, f32[8,512,4096]{2,1,0:T(8,128)}) fusion(f32[512,8,4096]{2,0,1:T(8,128)} %fusion.181, f32[8,512]{1,0:T(8,128)S(1)} %dynamic-slice_bitcast_fusion.2, bf16[4096,64]{0,1:T(8,128)(2,1)S(1)} %get-tuple-element.519, bf16[4,512,8,64]{1,3,2,0:T(8,128)(2,1)} %get-tuple-element.518, s32[]{:T(128)S(6)} %copy.91, ...), kind=kOutput, calls=%fused_computation.26.clone.2 | convolution fusion | flops 2231365632 | bytes 137396224 | tf_op jit(solution)/shard_map/while/body/eval_jaxpr/bhd,kd->hbk/dot_general | solution.py:57
  1693.8 53.0 %fusion.183 = bf16[8,512,4096]{2,1,0:T(8,128)(2,1)} fusion(f32[8,512,4096]{2,1,0:T(8,128)} %get-tuple-element.458, f32[512,8,4096]{2,0,1:T(8,128)} %fusion.181, f32[8,512]{1,0:T(8,128)S(1)} %get-tuple-element.459), kind=kLoop, calls=%fused_computation.28.clone.1 | loop fusion | flops 50331648 | bytes 167788544 | tf_op jit(solution)/shard_map/while/body/eval_jaxpr/convert_element_type | solution.py:66
  1746.8 22.7 fusion.185
  1770.6 13.8 fusion.184
  1785.3 16.2 fusion.186
  1802.6 21.1 dynamic_update_slice.29
  1827.1 24.3 fusion.181
  1851.4 47.9 %fusion.182 = (f32[8,512]{1,0:T(8,128)S(1)}, f32[8,512,4096]{2,1,0:T(8,128)}) fusion(f32[512,8,4096]{2,0,1:T(8,128)} %fusion.181, f32[8,512]{1,0:T(8,128)S(1)} %dynamic-slice_bitcast_fusion.2, bf16[4096,64]{0,1:T(8,128)(2,1)S(1)} %get-tuple-element.519, bf16[4,512,8,64]{1,3,2,0:T(8,128)(2,1)} %get-tuple-element.518, s32[]{:T(128)S(6)} %copy.91, ...), kind=kOutput, calls=%fused_computation.26.clone.2 | convolution fusion | flops 2231365632 | bytes 137396224 | tf_op jit(solution)/shard_map/while/body/eval_jaxpr/bhd,kd->hbk/dot_general | solution.py:57
  1899.3 53.0 %fusion.183 = bf16[8,512,4096]{2,1,0:T(8,128)(2,1)} fusion(f32[8,512,4096]{2,1,0:T(8,128)} %get-tuple-element.458, f32[512,8,4096]{2,0,1:T(8,128)} %fusion.181, f32[8,512]{1,0:T(8,128)S(1)} %get-tuple-element.459), kind=kLoop, calls=%fused_computation.28.clone.1 | loop fusion | flops 50331648 | bytes 167788544 | tf_op jit(solution)/shard_map/while/body/eval_jaxpr/convert_element_type | solution.py:66
  1952.3 22.7 fusion.185
  1976.0 13.8 fusion.184
  1990.8 16.2 fusion.186
  2008.0 21.1 dynamic_update_slice.29
  2032.6 24.3 fusion.181
  2056.9 47.9 %fusion.182 = (f32[8,512]{1,0:T(8,128)S(1)}, f32[8,512,4096]{2,1,0:T(8,128)}) fusion(f32[512,8,4096]{2,0,1:T(8,128)} %fusion.181, f32[8,512]{1,0:T(8,128)S(1)} %dynamic-slice_bitcast_fusion.2, bf16[4096,64]{0,1:T(8,128)(2,1)S(1)} %get-tuple-element.519, bf16[4,512,8,64]{1,3,2,0:T(8,128)(2,1)} %get-tuple-element.518, s32[]{:T(128)S(6)} %copy.91, ...), kind=kOutput, calls=%fused_computation.26.clone.2 | convolution fusion | flops 2231365632 | bytes 137396224 | tf_op jit(solution)/shard_map/while/body/eval_jaxpr/bhd,kd->hbk/dot_general | solution.py:57
  2104.7 53.0 %fusion.183 = bf16[8,512,4096]{2,1,0:T(8,128)(2,1)} fusion(f32[8,512,4096]{2,1,0:T(8,128)} %get-tuple-element.458, f32[512,8,4096]{2,0,1:T(8,128)} %fusion.181, f32[8,512]{1,0:T(8,128)S(1)} %get-tuple-element.459), kind=kLoop, calls=%fused_computation.28.clone.1 | loop fusion | flops 50331648 | bytes 167788544 | tf_op jit(solution)/shard_map/while/body/eval_jaxpr/convert_element_type | solution.py:66
  2157.8 22.7 fusion.185
  2181.5 13.8 fusion.184
  2196.2 16.2 fusion.186
  2213.5 21.1 dynamic_update_slice.29
  2238.7 19.1 convolution_convert_fusion.2
  2257.9 19.1 convolution_convert_fusion.3
  2277.0 18.1 fusion.66
  2295.3 12.2 fusion.74
  2307.6 19.0 convolution_convert_fusion
  2347.9 12.9 fusion.118
  2371.2 16.1 add_convert_fusion
  2408.8 37.3 %reduce-scatter.23.cloned.1.call-done = bf16[256,1408]{0,1:T(8,128)(2,1)} async-done(((bf16[2048,1408]{0,1:T(8,128)(2,1)}), bf16[256,1408]{0,1:T(8,128)(2,1)}) %reduce-scatter.23.cloned.1.call-update) | async-done | bytes 720912 | tf_op jit(solution)/shard_map/reduce_scatter | solution.py:268
  2464.0 26.7 reduce-scatter.17.cloned.1.call-done
  2492.5 43.1 %reduce-scatter.11.cloned.1.call-done = bf16[256,512]{1,0:T(8,128)(2,1)} async-done(((bf16[2048,512]{1,0:T(8,128)(2,1)}), bf16[256,512]{1,0:T(8,128)(2,1)}) %reduce-scatter.11.cloned.1.call-update) | async-done | bytes 262160 | tf_op jit(solution)/shard_map/reduce_scatter | solution.py:253
  2537.4 564.6 %all-reduce.12.cloned.1.call-done = (bf16[2048,2048]{1,0:T(8,128)(2,1)}, bf16[2048,2048]{1,0:T(8,128)(2,1)}) async-done(((bf16[2048,2048]{1,0:T(8,128)(2,1)}, bf16[2048,2048]{1,0:T(8,128)(2,1)}), (bf16[2048,2048]{1,0:T(8,128)(2,1)}, bf16[2048,2048]{1,0:T(8,128)(2,1)})) %all-reduce.12.cloned.1.call-update) | async-done | bytes 16777232 | tf_op jit(solution)/shard_map/psum | solution.py:150
  3111.7 15.1 all-reduce.2
  3127.5 25.9 fusion.53
  3153.4 89.7 %reduce-scatter.13.cloned.1.call-done = f32[64,256]{1,0:T(8,128)} async-done(((f32[2048,256]{1,0:T(8,128)}), f32[64,256]{1,0:T(8,128)}) %reduce-scatter.13.cloned.1.call-update) | async-done | bytes 65552 | tf_op jit(solution)/shard_map/reduce_scatter | solution.py:246
  3243.1 139.5 %reduce-scatter.15.cloned.1.call-done = f32[64,256]{1,0:T(8,128)} async-done(((f32[2048,256]{1,0:T(8,128)}), f32[64,256]{1,0:T(8,128)}) %reduce-scatter.15.cloned.1.call-update) | async-done | bytes 65552 | tf_op jit(solution)/shard_map/reduce_scatter | solution.py:247
  (251 shorter events, 262.8 us)
Async XLA Ops:
  7.2 376.4 %copy-start = (bf16[2048,512]{1,0:T(8,128)(2,1)S(1)}, bf16[2048,512]{1,0:T(8,128)(2,1)}, u32[]{:S(2)}) copy-start(bf16[2048,512]{1,0:T(8,128)(2,1)} %param.23) | copy-start | bytes 6291460
  7.2 7.8 copy-start.33
  7.2 52.0 %all-gather.2.cloned.1.call-start = ((), (), s32[]{:S(2)}) async-start(), calls=%async_computation.8 | async-start | bytes 1572864 | tf_op jit(solution)/shard_map/all_gather | solution.py:127
  7.3 36.3 %copy-start.40 = (f32[32]{0:T(128)}, f32[32]{0:T(128)S(1)}, u32[]{:S(2)}) copy-start(f32[32]{0:T(128)S(1)} %multiply_power_fusion) | copy-start | bytes 388
  14.3 9.6 copy-start.27
  15.0 8.9 copy-start.21
  23.9 6.3 copy-start.3
  23.9 6.3 copy-start.23
  32.9 10.6 copy-start.29
  35.0 919.4 %all-reduce.8.cloned.1.call-start = ((), (), s32[]{:S(2)}) async-start(), calls=%async_computation.9 | async-start | bytes 33554432 | tf_op jit(solution)/shard_map/psum | solution.py:141
  45.3 1.6 copy-start.16
  378.0 14.0 copy-start.5
  378.0 14.0 copy-start.11
  382.3 1.3 copy-start.18
  392.0 573.3 %copy-start.35 = (f32[2048]{0:T(1024)S(1)}, f32[2048]{0:T(1024)}, u32[]{:S(2)}) copy-start(f32[2048]{0:T(1024)} %param.24) | copy-start | bytes 24580
  392.1 974.1 %all-reduce.10.cloned.1.call-start = ((), (), s32[]{:S(2)}) async-start(), calls=%async_computation.10 | async-start | bytes 16777216 | tf_op jit(solution)/shard_map/psum | solution.py:166
  963.5 7.1 copy-start.2
  964.2 1.2 copy-start.31
  965.4 24.3 slice-start
  970.6 19.0 copy-start.15
  970.6 19.0 slice-start.1
  1076.1 290.0 %copy-start.32 = (f32[2048]{0:T(1024)S(1)}, f32[2048]{0:T(1024)}, u32[]{:S(2)}) copy-start(f32[2048]{0:T(1024)} %copy-done.31) | copy-start | bytes 24580
  1076.1 290.0 %copy-start.36 = (f32[2048]{0:T(1024)S(1)}, f32[2048]{0:T(1024)}, u32[]{:S(2)}) copy-start(f32[2048]{0:T(1024)} %param.24) | copy-start | bytes 24580
  1076.2 1284.6 %reduce-scatter.9.cloned.1.call-start = ((), (), s32[]{:S(2)}) async-start(), calls=%async_computation.11 | async-start | bytes 1572864 | tf_op jit(solution)/shard_map/reduce_scatter | solution.py:204
  1076.2 301.0 %copy-start.38 = (f32[2048]{0:T(1024)S(1)}, f32[2048]{0:T(1024)}, u32[]{:S(2)}) copy-start(f32[2048]{0:T(1024)} %get-tuple-element.330) | copy-start | bytes 24580
  1389.4 5.7 copy-start.4
  1400.9 11.7 copy-start.6
  1400.9 11.7 copy-start.12
  1488.3 53.0 %copy-start.7 = (f32[4096,64]{0,1:T(8,128)S(1)}, f32[4096,64]{0,1:T(8,128)}, u32[]{:S(2)}) copy-start(f32[4096,64]{0,1:T(8,128)} %get-tuple-element.502) | copy-start | bytes 3145732 | tf_op jit(solution)/shard_map/while
  1541.4 23.7 copy-start.9
  1693.8 53.0 %copy-start.7 = (f32[4096,64]{0,1:T(8,128)S(1)}, f32[4096,64]{0,1:T(8,128)}, u32[]{:S(2)}) copy-start(f32[4096,64]{0,1:T(8,128)} %get-tuple-element.502) | copy-start | bytes 3145732 | tf_op jit(solution)/shard_map/while
  1746.8 23.7 copy-start.9
  1899.3 53.0 %copy-start.7 = (f32[4096,64]{0,1:T(8,128)S(1)}, f32[4096,64]{0,1:T(8,128)}, u32[]{:S(2)}) copy-start(f32[4096,64]{0,1:T(8,128)} %get-tuple-element.502) | copy-start | bytes 3145732 | tf_op jit(solution)/shard_map/while
  1952.3 23.7 copy-start.9
  1975.0 1.0 copy-start.8
  1989.8 1.0 copy-start.10
  2104.7 53.0 %copy-start.7 = (f32[4096,64]{0,1:T(8,128)S(1)}, f32[4096,64]{0,1:T(8,128)}, u32[]{:S(2)}) copy-start(f32[4096,64]{0,1:T(8,128)} %get-tuple-element.502) | copy-start | bytes 3145732 | tf_op jit(solution)/shard_map/while
  2157.8 23.7 copy-start.9
  2180.5 1.0 copy-start.8
  2238.6 165.6 %reduce-scatter.21.cloned.1.call-start = ((), (), s32[]{:S(2)}) async-start(), calls=%async_computation.17 | async-start | bytes 6488064 | tf_op jit(solution)/shard_map/reduce_scatter | solution.py:265
  2257.8 148.7 %reduce-scatter.19.cloned.1.call-start = ((), (), s32[]{:S(2)}) async-start(), calls=%async_computation.16 | async-start | bytes 6488064 | tf_op jit(solution)/shard_map/reduce_scatter | solution.py:262
  2277.0 169.2 %reduce-scatter.23.cloned.1.call-start = ((), (), s32[]{:S(2)}) async-start(), calls=%async_computation.18 | async-start | bytes 6488064 | tf_op jit(solution)/shard_map/reduce_scatter | solution.py:268
  2277.0 18.2 copy-start.19
  2295.2 195.5 %reduce-scatter.17.cloned.1.call-start = ((), (), s32[]{:S(2)}) async-start(), calls=%async_computation.15 | async-start | bytes 2359296 | tf_op jit(solution)/shard_map/reduce_scatter | solution.py:256
  2307.5 228.0 %reduce-scatter.11.cloned.1.call-start = ((), (), s32[]{:S(2)}) async-start(), calls=%async_computation.12 | async-start | bytes 2359296 | tf_op jit(solution)/shard_map/reduce_scatter | solution.py:253
  2326.6 6.4 copy-start.17
  2326.6 6.4 copy-start.25
  2336.5 1.3 copy-start.20
  2347.6 14.1 copy-start.30
  2347.6 14.1 copy-start.41
  2347.6 15.3 copy-start.24
  2347.6 754.3 %all-reduce.12.cloned.1.call-start = ((), (), s32[]{:S(2)}) async-start(), calls=%async_computation.19 | async-start | bytes 33554432 | tf_op jit(solution)/shard_map/psum | solution.py:150
  2362.9 8.3 copy-start.22
  2363.0 8.3 copy-start.26
  2387.3 15.6 copy-start.42
  2387.3 855.8 %reduce-scatter.13.cloned.1.call-start = ((), (), s32[]{:S(2)}) async-start(), calls=%async_computation.13 | async-start | bytes 2162688 | tf_op jit(solution)/shard_map/reduce_scatter | solution.py:246
  2401.5 1.3 copy-start.14
  2402.9 979.7 %reduce-scatter.15.cloned.1.call-start = ((), (), s32[]{:S(2)}) async-start(), calls=%async_computation.14 | async-start | bytes 2162688 | tf_op jit(solution)/shard_map/reduce_scatter | solution.py:247
  2448.6 653.3 %copy-start.28 = (f32[2048]{0:T(1024)S(1)}, f32[2048]{0:T(1024)}, u32[]{:S(2)}) copy-start(f32[2048]{0:T(1024)} %copy-done.27) | copy-start | bytes 24580
  2448.6 653.3 %copy-start.34 = (f32[2048]{0:T(1024)S(1)}, f32[2048]{0:T(1024)}, u32[]{:S(2)}) copy-start(f32[2048]{0:T(1024)} %param.19) | copy-start | bytes 24580
  2462.6 1.4 copy-start.13
  3101.9 9.7 copy-start.39
  3101.9 25.5 copy-start.37
  3127.5 255.2 %copy-start.1 = (bf16[2048,512]{1,0:T(8,128)(2,1)S(1)}, bf16[2048,512]{1,0:T(8,128)(2,1)}, u32[]{:S(2)}) copy-start(bf16[2048,512]{1,0:T(8,128)(2,1)} %param.23) | copy-start | bytes 6291460
  (5 other events, 4.9 us)
Sparse Core Ops, SparseCore 0:
  35.1 24.0 all-gather.1
  392.2 562.1 all-reduce.7
  1076.3 289.7 all-reduce.9
  2238.7 19.3 reduce-scatter.8
  2261.8 59.0 reduce-scatter.20
  2324.2 59.0 reduce-scatter.18
  2387.1 59.0 reduce-scatter.22
  2449.4 41.1 reduce-scatter.16
  2494.3 41.2 reduce-scatter.10
  2538.6 563.2 all-reduce.11
  3104.8 138.2 reduce-scatter.12
  3245.9 136.7 reduce-scatter.14
where the time goes:
time: 3400 us; the launch traced here: 3390 us
  waiting for transfers between devices  1760 us (52%)
  matrix products  989 us (29%)
  other arithmetic  441 us (13%)
  local copies, waits for them, and re-layouts  170 us (5%)
    psum x1, waiting for transfers between devices, body(): lax.psum(mlp_part.astype(jnp.bfloat16), 'tensor').astype(jnp.float32)  565 us
    psum x1, waiting for transfers between devices, body(): attn_out = lax.psum(attn_part, 'tensor')  562 us
    psum x1, waiting for transfers between devices, body(): lax.psum(grad_normed_part.astype(jnp.bfloat16), 'tensor')  290 us
    convert_element_type x4, other arithmetic, attend_back(): grad_scores = (softmax_f32 * (grad_probs - row_delta)).astype(jnp.bfloat16)  212 us
    dot_general x4, matrix products, attend_back(): jnp.einsum('bhd,kd->hbk', query_block, keys_all, preferred_element_type=j...  192 us
    reduce_scatter x1, waiting for transfers between devices, body(): lax.psum_scatter(value_grad_full, ('dp', 'ctx', 'tensor'), scatter_dimens...  140 us
    dot_general x4, matrix products, attend_block(): jnp.einsum('hbk,kd->bhd', softmax_low, values_all, preferred_element_type...  107 us
    dot_general x4, matrix products, attend_block(): jnp.einsum('bhd,kd->hbk', query_block, keys_all, preferred_element_type=j...  100 us
  transfers between devices with their start and end apart: 12, of which 9 were waited for; matrix products, arithmetic and copies ran while one was open for 7% of the time, Pallas kernels for 0%

commit v1 on v0

v1 whole, which is shorter than its diff:
```python
import jax
import jax.numpy as jnp
import numpy as np
from jax import lax
from jax.experimental import pallas as pl
from jax.experimental.pallas import tpu as pltpu
from jax.sharding import PartitionSpec as P

NT = (((1,), (1,)), ((), ()))
F32 = jnp.float32
BF16 = jnp.bfloat16
HD = 64
GROUP = 256


def fwd_kernel(meta, q_ref, ka_ref, kb_ref, vt_ref, o_ref, lse_ref):
    span = q_ref.shape[0]
    group = min(GROUP, span)
    queries = q_ref[...]
    own = pl.multiple_of(meta[1 + meta[0]] * span, span)
    heads = []
    for keys_ref in (ka_ref, kb_ref):
        tops, sums = [], []
        for first in range(0, span, group):
            count = first + group
            rows = pl.ds(own, count)
            scores = lax.dot_general(
                keys_ref[rows, :], queries[first:count], NT, preferred_element_type=F32
            )
            key_at = lax.broadcasted_iota(jnp.int32, scores.shape, 0)
            row_at = lax.broadcasted_iota(jnp.int32, scores.shape, 1) + first
            scores = jnp.where(key_at <= row_at, scores, -1e30)
            top = jnp.max(scores, axis=0, keepdims=True)
            weights = jnp.exp(scores - top).astype(BF16)
            tops.append(top)
            sums.append(jnp.dot(vt_ref[:, rows], weights, preferred_element_type=F32))
        heads += [jnp.concatenate(tops, axis=1), jnp.concatenate(sums, axis=1)]

    def step(index, carry):
        rows = pl.ds(pl.multiple_of(meta[1 + index] * span, span), span)
        out = []
        for side, keys_ref in enumerate((ka_ref, kb_ref)):
            top, total = carry[2 * side : 2 * side + 2]
            scores = lax.dot_general(
                keys_ref[rows, :], queries, NT, preferred_element_type=F32
            )
            new_top = jnp.maximum(top, jnp.max(scores, axis=0, keepdims=True))
            weights = jnp.exp(scores - new_top).astype(BF16)
            total = total * jnp.exp(top - new_top) + jnp.dot(
                vt_ref[:, rows], weights, preferred_element_type=F32
            )
            out += [new_top, total]
        return tuple(out)

    top0, total0, top1, total1 = lax.fori_loop(0, meta[0], step, tuple(heads))
    norm0, norm1 = total0[HD : HD + 1], total1[HD : HD + 1]
    o_ref[...] = jnp.concatenate([total0[:HD] / norm0, total1[:HD] / norm1], axis=0).T.astype(BF16)
    lse_ref[0] = jnp.concatenate(
        [top0 + jnp.log(norm0), top1 + jnp.log(norm1), jnp.zeros((6, span), F32)], axis=0
    )


def attend(meta, queries, keys_a, keys_b, values_t, fraction=0.6):
    span, width = queries.shape
    pairs = width // 128
    length = keys_a.shape[0]
    whole = pl.BlockSpec((length, 128), lambda p, m: (0, 0))
    flops = int(4 * span * length * width * fraction)
    return pl.pallas_call(
        fwd_kernel,
        grid_spec=pltpu.PrefetchScalarGridSpec(
            num_scalar_prefetch=1,
            grid=(pairs,),
            in_specs=[
                pl.BlockSpec((span, 128), lambda p, m: (0, p)),
                whole,
                whole,
                pl.BlockSpec(values_t.shape, lambda p, m: (0, 0)),
            ],
            out_specs=[
                pl.BlockSpec((span, 128), lambda p, m: (0, p)),
                pl.BlockSpec((1, 8, span), lambda p, m: (p, 0, 0)),
            ],
        ),
        out_shape=[
            jax.ShapeDtypeStruct((span, width), BF16),
            jax.ShapeDtypeStruct((pairs, 8, span), F32),
        ],
        compiler_params=pltpu.CompilerParams(vmem_limit_bytes=56 * 2**20),
        cost_estimate=pl.CostEstimate(
            flops=4 * flops, bytes_accessed=2**23, transcendentals=0
        ),
        name="attend",
    )(meta, queries, keys_a, keys_b, values_t)


def bwd_kernel(
    meta,
    q_ref,
    o_ref,
    g_ref,
    lse_ref,
    ka_ref,
    kb_ref,
    va_ref,
    vb_ref,
    kt_ref,
    cos_ref,
    sin_ref,
    dk_in,
    dv_in,
    dq_ref,
    dk_ref,
    dv_ref,
):
    span = q_ref.shape[0]
    group = min(GROUP, span)

    @pl.when(pl.program_id(0) == 0)
    def _():
        dk_ref[...] = dk_in[...]
        dv_ref[...] = dv_in[...]

    queries, grads = q_ref[...], g_ref[...]
    left = lax.broadcasted_iota(jnp.int32, (span, 128), 1) < HD
    products = (grads.astype(F32) * o_ref[...].astype(F32)).T
    zero = jnp.zeros_like(queries)
    sides = []
    for side, (keys_ref, values_ref) in enumerate(((ka_ref, va_ref), (kb_ref, vb_ref))):
        mine = left if side == 0 else jnp.logical_not(left)
        delta = jnp.sum(products[side * HD : side * HD + HD], axis=0, keepdims=True)
        sides.append(
            (
                keys_ref,
                values_ref,
                jnp.where(mine, queries, zero),
                jnp.where(mine, grads, zero),
                lse_ref[0, side : side + 1, :],
                delta,
            )
        )

    def block(rows, columns, masked):
        first, count = columns
        cut = slice(first, first + count)
        dqs = []
        dk_add = dv_add = None
        for keys_ref, values_ref, q_mine, g_mine, lse, delta in sides:
            scores = lax.dot_general(
                keys_ref[rows, :], queries[cut], NT, preferred_element_type=F32
            )
            probs = jnp.exp(scores - lse[:, cut])
            if masked:
                key_at = lax.broadcasted_iota(jnp.int32, scores.shape, 0)
                row_at = lax.broadcasted_iota(jnp.int32, scores.shape, 1) + first
                probs = jnp.where(key_at <= row_at, probs, 0.0)
            grad_probs = lax.dot_general(
                values_ref[rows, :], grads[cut], NT, preferred_element_type=F32
            )
            grad_scores = (probs * (grad_probs - delta[:, cut])).astype(BF16)
            dv_new = jnp.dot(probs.astype(BF16), g_mine[cut], preferred_element_type=F32)
            dk_new = jnp.dot(grad_scores, q_mine[cut], preferred_element_type=F32)
            dv_add = dv_new if dv_add is None else dv_add + dv_new
            dk_add = dk_new if dk_add is None else dk_add + dk_new
            dqs.append(jnp.dot(kt_ref[:, rows], grad_scores, preferred_element_type=F32))
        dv_ref[rows, :] += dv_add
        dk_ref[rows, :] += dk_add
        return jnp.concatenate(dqs, axis=0)

    own = pl.multiple_of(meta[1 + meta[0]] * span, span)
    start = jnp.concatenate(
        [block(pl.ds(own, first + group), (first, group), True) for first in range(0, span, group)],
        axis=1,
    )
    half = min(512, span)

    def step(index, total):
        base = pl.multiple_of(meta[1 + index // (span // half)] * span, span)
        rows = pl.ds(pl.multiple_of(base + (index % (span // half)) * half, half), half)
        return total + block(rows, (0, span), False)

    dq = lax.fori_loop(0, meta[0] * (span // half), step, start).T * (HD**-0.5)
    low = (lax.broadcasted_iota(jnp.int32, (span, 128), 1) % HD) < HD // 2
    swapped = jnp.where(low, pltpu.roll(dq, 128 - HD // 2, 1), pltpu.roll(dq, HD // 2, 1))
    dq_ref[...] = (dq * cos_ref[...] - swapped * sin_ref[...]).astype(BF16)


def attend_back(
    meta, queries, outputs, grads, lse, ka, kb, va, vb, kt, cos, sin, dk, dv, fraction=0.6
):
    span, width = queries.shape
    pairs = width // 128
    length = ka.shape[0]
    whole = pl.BlockSpec((length, 128), lambda p, m: (0, 0))
    pair = pl.BlockSpec((span, 128), lambda p, m: (0, p))
    table = pl.BlockSpec((span, 128), lambda p, m: (0, 0))
    flops = int(10 * span * length * width * fraction)
    return pl.pallas_call(
        bwd_kernel,
        grid_spec=pltpu.PrefetchScalarGridSpec(
            num_scalar_prefetch=1,
            grid=(pairs,),
            in_specs=[
                pair,
                pair,
                pair,
                pl.BlockSpec((1, 8, span), lambda p, m: (p, 0, 0)),
                whole,
                whole,
                whole,
                whole,
                pl.BlockSpec(kt.shape, lambda p, m: (0, 0)),
                table,
                table,
                whole,
                whole,
            ],
            out_specs=[pair, whole, whole],
        ),
        out_shape=[
            jax.ShapeDtypeStruct((span, width), BF16),
            jax.ShapeDtypeStruct((length, 128), F32),
            jax.ShapeDtypeStruct((length, 128), F32),
        ],
        compiler_params=pltpu.CompilerParams(vmem_limit_bytes=58 * 2**20),
        cost_estimate=pl.CostEstimate(
            flops=4 * flops, bytes_accessed=2**24, transcendentals=0
        ),
        name="attend_back",
    )(meta, queries, outputs, grads, lse, ka, kb, va, vb, kt, cos, sin, dk, dv)

EPSILON = 1e-05


def line_gather(piece, place, target):
    size = lax.axis_size("tensor")
    me = lax.axis_index("tensor")
    target = place(target, piece, me)
    rights, lefts = [piece], [piece]
    for step in range(1, size):
        rights.append(
            lax.ppermute(rights[-1], "tensor", [(i, i + 1) for i in range(step - 1, size - 1)])
        )
        lefts.append(
            lax.ppermute(lefts[-1], "tensor", [(i, i - 1) for i in range(1, size - step + 1)])
        )
    for step in range(1, size):
        arrived = rights[step] + lefts[size - step]
        target = place(target, arrived, lax.rem(me - step + size, size))
    return target


def line_scatter(partial):
    size = lax.axis_size("tensor")
    me = lax.axis_index("tensor")
    rows = partial.shape[0] // size

    def part(index):
        index = jnp.clip(index, 0, size - 1)
        return lax.dynamic_slice_in_dim(partial, index * rows, rows, 0)

    right = left = None
    for step in range(1, size):
        send = part(size - step + me)
        if right is not None:
            send = send + right
        right = lax.ppermute(send, "tensor", [(i, i + 1) for i in range(step)])
        send = part(me + step - size)
        if left is not None:
            send = send + left
        left = lax.ppermute(send, "tensor", [(i, i - 1) for i in range(size - step, size)])
    total = part(me).astype(F32)
    if right is not None:
        total = total + right.astype(F32) + left.astype(F32)
    return total


def exchange(pick):
    size = lax.axis_size("tensor")
    me = lax.axis_index("tensor")
    own = pick(me)
    out = jnp.zeros((size, *own.shape), own.dtype)
    out = lax.dynamic_update_index_in_dim(out, own, me, 0)
    for shift in range(1, size):
        got = lax.ppermute(
            pick(lax.rem(me + shift, size)), "tensor", [(i, (i + shift) % size) for i in range(size)]
        )
        out = lax.dynamic_update_index_in_dim(out, got, lax.rem(me - shift + size, size), 0)
    return out


def gather_weight(weight):
    plane = lax.axis_size("dp") * lax.axis_size("ctx")
    index = lax.axis_index("dp") * lax.axis_size("ctx") + lax.axis_index("ctx")
    rows = weight.shape[0] // plane
    piece = lax.dynamic_slice_in_dim(weight, index * rows, rows, 0)
    column = lax.all_gather(piece, "tensor", axis=0, tiled=False)
    whole = lax.all_gather(column, ("dp", "ctx"), axis=0, tiled=False)
    return jnp.swapaxes(whole, 0, 1).reshape(lax.axis_size("tensor"), *weight.shape)


def swap_halves(weight):
    rows, columns = weight.shape
    return weight.reshape(rows, columns // HD, 2, HD // 2)[:, :, ::-1, :].reshape(rows, columns)


def dot(a, b):
    return jnp.dot(a, b, preferred_element_type=F32)


def dot_t(a, b):
    return jnp.einsum("rf,df->rd", a, b, preferred_element_type=F32)


def t_dot(a, b):
    return jnp.einsum("rd,rf->df", a, b, preferred_element_type=F32)


def body(
    tokens,
    cotangent,
    span_order,
    norm_attn,
    w_query,
    w_key,
    w_value,
    w_output,
    norm_mlp,
    w_gate,
    w_up,
    w_down,
):
    tok_rows, width = tokens.shape
    groups = lax.axis_size("tensor")
    member = lax.axis_index("tensor")
    n_ctx = lax.axis_size("ctx")
    ctx_index = lax.axis_index("ctx")
    features = w_query.shape[1]
    kv_count = w_key.shape[1] // HD
    kv_pick = np.arange(groups) * kv_count // groups
    kv_start = member * kv_count // groups * HD
    key_weight = lax.dynamic_slice_in_dim(w_key, kv_start, HD, 1)
    value_weight = lax.dynamic_slice_in_dim(w_value, kv_start, HD, 1)
    span = tok_rows // 2
    share = span // groups
    slots = range(2)

    swap = n_ctx == 2
    order = span_order[0]
    if swap:
        order = jnp.roll(order, -2 * ctx_index)
    n_spans = order.shape[0]
    places = jnp.arange(n_spans, dtype=jnp.int32)
    slot_of = jnp.sum(
        jnp.where(order[None, :] == places[:, None], places[None, :], 0), axis=1, dtype=jnp.int32
    )
    own_first = 0 if swap else 2 * ctx_index
    own_spans = lax.dynamic_slice_in_dim(order, own_first, 2)
    metas = [jnp.concatenate([own_spans[s : s + 1], slot_of]) for s in slots]

    positions = (own_spans[:, None] * span + jnp.arange(span, dtype=jnp.int32)[None, :]).reshape(-1)
    half = HD // 2
    frequency = 10000.0 ** (-jnp.arange(half, dtype=F32) / half)
    angles = positions.astype(F32)[:, None] * frequency[None, :]
    cos_part, sin_part = jnp.cos(angles), jnp.sin(angles)
    cos_head = jnp.concatenate([cos_part, cos_part], axis=1)
    sin_head = jnp.concatenate([-sin_part, sin_part], axis=1)
    cos_pair = jnp.concatenate([cos_head, cos_head], axis=1)
    sin_pair = jnp.concatenate([sin_head, sin_head], axis=1)

    output_whole = gather_weight(w_output)
    query_whole = gather_weight(w_query)

    inputs = tokens.astype(F32)
    inverse_one = lax.rsqrt(jnp.mean(inputs * inputs, axis=-1, keepdims=True) + EPSILON)
    normed = (inputs * inverse_one * norm_attn).astype(BF16)
    kv_raw = dot(normed, jnp.concatenate([key_weight, value_weight, swap_halves(key_weight)], axis=1))
    key_rot = kv_raw[:, :HD] * cos_head + kv_raw[:, 2 * HD :] * sin_head
    kv_own = jnp.concatenate([key_rot, kv_raw[:, HD : 2 * HD]], axis=1).astype(BF16)
    if swap:
        kv_other = lax.ppermute(kv_own, "ctx", [(0, 1), (1, 0)])
        kv_all = jnp.concatenate([kv_own, kv_other], axis=0)
    else:
        kv_all = lax.all_gather(kv_own, "ctx", axis=0, tiled=True)
    length = kv_all.shape[0]
    keys, values = kv_all[:, :HD], kv_all[:, HD:]
    blank = jnp.zeros_like(keys)
    keys_a = jnp.concatenate([keys, blank], axis=1)
    keys_b = jnp.concatenate([blank, keys], axis=1)
    values_a = jnp.concatenate([values, blank], axis=1)
    values_b = jnp.concatenate([blank, values], axis=1)
    keys_t = keys.T
    values_t = jnp.concatenate(
        [values.T, jnp.ones((1, length), BF16), jnp.zeros((15, length), BF16)], axis=0
    )

    query_raw = dot(normed, jnp.concatenate([w_query, swap_halves(w_query)], axis=1))
    tiles = features // 128
    queries = (
        (
            query_raw[:, :features] * jnp.tile(cos_pair, (1, tiles))
            + query_raw[:, features:] * jnp.tile(sin_pair, (1, tiles))
        )
        * HD**-0.5
    ).astype(BF16)

    def cut(array, slot):
        return array[slot * span : (slot + 1) * span]

    def own_rows(array):
        return lax.dynamic_slice_in_dim(array, member * share, share, 0)

    def by_row(target, piece, source):
        return lax.dynamic_update_slice_in_dim(target, piece, source * share, 0)

    attention, log_totals, whole_attention = [], [], []
    for s in slots:
        out, lse = attend(metas[s], cut(queries, s), keys_a, keys_b, values_t)
        attention.append(out)
        log_totals.append(lse)
        whole_attention.append(
            line_gather(
                out,
                lambda target, piece, source: lax.dynamic_update_index_in_dim(target, piece, source, 0),
                jnp.zeros((groups, span, features), BF16),
            )
        )

    parts = []
    for s in slots:
        middle = cut(inputs, s) + jnp.einsum(
            "trq,tdq->rd", whole_attention[s], output_whole, preferred_element_type=F32
        )
        inverse_two = lax.rsqrt(jnp.mean(middle * middle, axis=-1, keepdims=True) + EPSILON)
        normed_mlp = (middle * inverse_two * norm_mlp).astype(BF16)
        gate_proj = dot(normed_mlp, w_gate)
        up_proj = dot(normed_mlp, w_up)
        sigmoid_gate = jax.nn.sigmoid(gate_proj)
        hidden = (gate_proj * sigmoid_gate * up_proj).astype(BF16)
        grad_hidden = dot(cut(cotangent, s), w_down)
        grad_gate = (
            grad_hidden * up_proj * sigmoid_gate * (1.0 + gate_proj * (1.0 - sigmoid_gate))
        ).astype(BF16)
        grad_up = (grad_hidden * gate_proj * sigmoid_gate).astype(BF16)
        grad_part = (dot_t(grad_gate, w_gate) + dot_t(grad_up, w_up)).astype(BF16)
        mlp_part = dot_t(hidden, w_down).astype(BF16)
        parts.append(
            (own_rows(middle), own_rows(inverse_two), normed_mlp, hidden, grad_gate, grad_up)
            + (grad_part, mlp_part)
        )

    mlp_gain = jnp.zeros((width,), F32)
    grad_middles, grad_lows, grad_attention = [], [], []
    for s in slots:
        middle, inverse_two = parts[s][:2]
        grad_normed_mlp = line_scatter(parts[s][6])
        mlp_gain = mlp_gain + jnp.sum(grad_normed_mlp * middle * inverse_two, axis=0)
        scaled_two = grad_normed_mlp * norm_mlp
        grad_middle = (
            own_rows(cut(cotangent, s)).astype(F32)
            + inverse_two * scaled_two
            - middle * inverse_two**3 * jnp.mean(scaled_two * middle, axis=-1, keepdims=True)
        )
        grad_middles.append(grad_middle)
        grad_low = grad_middle.astype(BF16)
        grad_lows.append(grad_low)
        blocks = jnp.einsum(
            "rd,tdq->trq", grad_low, output_whole, preferred_element_type=F32
        ).astype(BF16)
        grad_attention.append(
            exchange(lambda j: lax.dynamic_index_in_dim(blocks, j, 0, keepdims=False)).reshape(
                span, features
            )
        )

    normed_mlp, hidden, grad_gate, grad_up = (
        jnp.concatenate([parts[s][i] for s in slots], axis=0) for i in range(2, 6)
    )

    def plane_sum(gradient):
        return lax.psum_scatter(
            gradient.astype(BF16), ("dp", "ctx"), scatter_dimension=0, tiled=True
        ).astype(F32)

    gate_grad = plane_sum(t_dot(normed_mlp, grad_gate))
    up_grad = plane_sum(t_dot(normed_mlp, grad_up))
    down_grad = plane_sum(t_dot(cotangent, hidden))

    mixed = jnp.zeros((tok_rows, width), BF16)
    for s in slots:
        mixed_share = (parts[s][0] + line_scatter(parts[s][7])).astype(BF16)
        mixed = line_gather(
            mixed_share,
            lambda target, piece, source: lax.dynamic_update_slice_in_dim(
                target, piece, s * span + source * share, 0
            ),
            mixed,
        )

    dk = jnp.zeros((length, 128), F32)
    dv = jnp.zeros((length, 128), F32)
    grad_queries, exchanged = [], []
    for s in slots:
        grad_query, dk, dv = attend_back(
            metas[s],
            cut(queries, s),
            attention[s],
            grad_attention[s],
            log_totals[s],
            keys_a,
            keys_b,
            values_a,
            values_b,
            keys_t,
            cut(cos_pair, s),
            cut(sin_pair, s),
            dk,
            dv,
        )
        grad_queries.append(grad_query)
        exchanged.append(
            exchange(lambda j: lax.dynamic_slice_in_dim(grad_query, j * share, share, 0))
        )
    kv_sums = jnp.concatenate([dk[:, :HD] + dk[:, HD:], dv[:, :HD] + dv[:, HD:]], axis=1)
    if swap:
        sent = lax.ppermute(kv_sums[tok_rows:].astype(BF16), "ctx", [(0, 1), (1, 0)])
        kv_grad = kv_sums[:tok_rows] + sent.astype(F32)
    else:
        kv_grad = lax.psum_scatter(
            kv_sums.astype(BF16), "ctx", scatter_dimension=0, tiled=True
        ).astype(F32)
    grad_key = kv_grad[:, :HD]
    swapped = jnp.concatenate([grad_key[:, half:], grad_key[:, :half]], axis=1)
    grad_kv_raw = jnp.concatenate(
        [grad_key * cos_head - swapped * sin_head, kv_grad[:, HD:]], axis=1
    ).astype(BF16)
    kv_exchanged = [
        exchange(
            lambda j: lax.dynamic_slice_in_dim(grad_kv_raw, s * span + j * share, share, 0)
        )
        for s in slots
    ]
    kv_whole = jnp.stack(
        [
            jnp.concatenate(
                [w_key[:, h * HD : (h + 1) * HD], w_value[:, h * HD : (h + 1) * HD]], axis=1
            )
            for h in kv_pick
        ]
    )

    attn_gain = jnp.zeros((width,), F32)
    tokens_grad = jnp.zeros((tok_rows, width), BF16)
    for s in slots:
        grad_normed = jnp.einsum(
            "trq,tdq->rd", exchanged[s], query_whole, preferred_element_type=F32
        ) + jnp.einsum("trq,tdq->rd", kv_exchanged[s], kv_whole, preferred_element_type=F32)
        inputs_own = own_rows(cut(inputs, s))
        inverse_own = own_rows(cut(inverse_one, s))
        attn_gain = attn_gain + jnp.sum(grad_normed * inputs_own * inverse_own, axis=0)
        scaled_one = grad_normed * norm_attn
        grad_inputs = (
            grad_middles[s]
            + inverse_own * scaled_one
            - inputs_own
            * inverse_own**3
            * jnp.mean(scaled_one * inputs_own, axis=-1, keepdims=True)
        ).astype(BF16)
        tokens_grad = line_gather(
            grad_inputs,
            lambda target, piece, source: lax.dynamic_update_slice_in_dim(
                target, piece, s * span + source * share, 0
            ),
            tokens_grad,
        )

    low_rows = jnp.concatenate(grad_lows, axis=0)
    attention_rows = jnp.concatenate(
        [lax.dynamic_slice_in_dim(whole, member * share, share, 1) for whole in whole_attention],
        axis=1,
    )
    output_part = jnp.einsum("rd,trq->dtq", low_rows, attention_rows, preferred_element_type=F32)
    output_plane = lax.psum_scatter(
        output_part.astype(BF16).reshape(width, groups * features),
        ("dp", "ctx"),
        scatter_dimension=0,
        tiled=True,
    )
    output_grad = jnp.sum(
        exchange(
            lambda j: lax.dynamic_slice_in_dim(output_plane, j * features, features, 1)
        ).astype(F32),
        axis=0,
    )

    query_part = t_dot(normed, jnp.concatenate(grad_queries, axis=0))
    kv_part = t_dot(normed, grad_kv_raw)
    query_kv = plane_sum(jnp.concatenate([query_part, kv_part], axis=1))
    query_grad = query_kv[:, :features]
    kv_rows = query_kv.shape[0] // groups
    kv_plane = query_kv[:, features:].astype(BF16)
    kv_blocks = exchange(
        lambda j: lax.dynamic_slice_in_dim(kv_plane, j * kv_rows, kv_rows, 0)
    ).astype(F32)
    key_heads, value_heads = [], []
    for h in range(kv_count):
        members = [g for g in range(groups) if kv_pick[g] == h]
        total = jnp.zeros((kv_rows, 2 * HD), F32)
        for g in members:
            total = total + kv_blocks[g]
        key_heads.append(total[:, :HD])
        value_heads.append(total[:, HD:])
    key_grad = jnp.concatenate(key_heads, axis=1)
    value_grad = jnp.concatenate(value_heads, axis=1)

    gains = lax.psum(jnp.stack([attn_gain, mlp_gain]), ("dp", "ctx", "tensor"))
    plane = lax.axis_size("dp") * n_ctx
    plane_index = lax.axis_index("dp") * n_ctx + ctx_index
    gains = lax.dynamic_slice_in_dim(gains, plane_index * (width // plane), width // plane, 1)
    return (
        mixed,
        tokens_grad,
        gains[0],
        query_grad,
        key_grad,
        value_grad,
        output_grad,
        gains[1],
        gate_grad,
        up_grad,
        down_grad,
    )


def solution(mesh):
    placed = (
        P(("dp", "ctx"), None),
        P(("dp", "ctx"), None),
        P("dp", None),
        P(),
        P(None, "tensor"),
        P(),
        P(),
        P(None, "tensor"),
        P(),
        P(None, "tensor"),
        P(None, "tensor"),
        P(None, "tensor"),
    )
    return jax.shard_map(
        body,
        mesh=mesh,
        in_specs=placed,
        out_specs=(
            P(("dp", "ctx"), None),
            P(("dp", "ctx"), None),
            P(("dp", "ctx")),
            P(("dp", "ctx"), "tensor"),
            P(("dp", "ctx", "tensor"), None),
            P(("dp", "ctx", "tensor"), None),
            P(("dp", "ctx"), "tensor"),
            P(("dp", "ctx")),
            P(("dp", "ctx"), "tensor"),
            P(("dp", "ctx"), "tensor"),
            P(("dp", "ctx"), "tensor"),
        ),
        check_vma=False,
    )
```

time: 3400 us -> 1450 us (0.43)
  waiting for transfers between devices: 1760 us -> 311 us
  matrix products: 989 us -> 266 us
  other arithmetic: 441 us -> 165 us
  Pallas kernels: 0 us -> 260 us
  starting transfers between devices: 1.18 us -> 224 us
  blocking collectives: 15.1 us -> 52.4 us
    psum x3 -> x0, waiting for transfers between devices: 1420 us -> none  [the longest x1 565 us: body(): lax.psum(mlp_part.astype(jnp.bfloat16), 'tensor').astype(jnp.float32)]
    dot_general x49 -> x28, matrix products: 989 us -> 266 us  [the longest x8 87 us: dot(): return jnp.dot(a, b, preferred_element_type=F32)]
    reduce_scatter x8 -> x5, waiting for transfers between devices: 336 us -> 0.05 us  [the longest x4 0.05 us: plane_sum(): lax.psum_scatter(gradient.astype(BF16), ('dp', 'ctx'), scatter_dimension=...]
    ppermute x0 -> x86, waiting for transfers between devices: none -> 304 us  [the longest x18 114 us: line_gather(): lax.ppermute(lefts[-1], 'tensor', [(i, i - 1) for i in range(1, size - st...]
    pallas_call x0 -> x4, Pallas kernels: none -> 260 us  [the longest x2 160 us: attend_back(): pl.pallas_call(bwd_kernel, grid_spec=pltpu.PrefetchScalarGridSpec(num_sca...]
    ppermute x0 -> x86, starting transfers between devices: none -> 223 us  [the longest x24 92.8 us: exchange(): lax.ppermute(pick(lax.rem(me + shift, size)), 'tensor', [(i, (i + shift)...]
    convert_element_type x13 -> x8, other arithmetic: 258 us -> 35.3 us  [the longest x1 11.4 us: body(): inputs = tokens.astype(F32)]
    reduce_sum x8 -> x4, other arithmetic: 126 us -> 9.57 us  [the longest x1 5.23 us: body(): jnp.mean(inputs * inputs, axis=-1, keepdims=True) + EPSILON]
  transfers between devices with their start and end apart: 12 -> 95, of which waited for: 9 -> 37; matrix products, arithmetic and copies ran while one was open for 7% -> 39% of each run, Pallas kernels for 0% -> 18%
where the time goes in v1:
time: 1450 us; the launch traced here: 1440 us
  waiting for transfers between devices  311 us (21%)
  matrix products  266 us (18%)
  Pallas kernels  260 us (18%)
  starting transfers between devices  224 us (15%)
  other arithmetic  165 us (11%)
  local copies, waits for them, and re-layouts  140 us (10%)
  blocking collectives  52.4 us (4%)
  between operations  16.4 us (1%)
    pallas_call x2, Pallas kernels, attend_back(): pl.pallas_call(bwd_kernel, grid_spec=pltpu.PrefetchScalarGridSpec(num_sca...  160 us
    ppermute x18, waiting for transfers between devices, line_gather(): lax.ppermute(lefts[-1], 'tensor', [(i, i - 1) for i in range(1, size - st...  114 us
    pallas_call x2, Pallas kernels, attend(): pl.pallas_call(fwd_kernel, grid_spec=pltpu.PrefetchScalarGridSpec(num_sca...  100 us
    ppermute x12, waiting for transfers between devices, line_scatter(): right = lax.ppermute(send, 'tensor', [(i, i + 1) for i in range(step)])  97 us
    ppermute x24, starting transfers between devices, exchange(): lax.ppermute(pick(lax.rem(me + shift, size)), 'tensor', [(i, (i + shift)...  92.8 us
    dot_general x8, matrix products, dot(): return jnp.dot(a, b, preferred_element_type=F32)  87 us
    ppermute x24, waiting for transfers between devices, exchange(): lax.ppermute(pick(lax.rem(me + shift, size)), 'tensor', [(i, (i + shift)...  71.4 us
    dot_general x6, matrix products, dot_t(): return jnp.einsum('rf,df->rd', a, b, preferred_element_type=F32)  64.4 us
  transfers between devices with their start and end apart: 95, of which 37 were waited for; matrix products, arithmetic and copies ran while one was open for 39% of the time, Pallas kernels for 18%

profile of v1, /device:TPU:0, one launch (start us, length us, event | category | flops | bytes accessed | tf_op | source)
XLA Modules:
  0.0 1435.3 jit_solution(13319537843660688557)
XLA Ops:
  22.4 5.4 fusion.34
  34.3 6.6 all-gather.9.cloned.1.call-done
  60.3 12.1 fusion.13
  86.8 44.1 %attend.2 = (bf16[1024,512]{1,0:T(8,128)(2,1)}, f32[4,8,1024]{2,1,0:T(8,128)}) custom-call(s32[5]{0:T(128)} %get-tuple-element.203.meta, bf16[1024,512]{1,0:T(8,128)(2,1)} %get-tuple-element.127.q_ref, bf16[4096,128]{1,0:T(8,128)(2,1)} %get-tuple-element.106.ka_ref, bf16[4096,128]{1,0:T(8,128)(2,1)} %concatenate.116.kb_ref, bf16[80,4096]{1,0:T(8,128)(2,1)} %copy.143.vt_ref), custom_call_target="tpu_custom_call" | custom-call | flops 20615843840 | bytes 8388608 | tf_op jit(solution)/shard_map/attend/pallas_call | solution.py:69
  136.6 56.4 %attend.3 = (bf16[1024,512]{1,0:T(8,128)(2,1)}, f32[4,8,1024]{2,1,0:T(8,128)}) custom-call(s32[5]{0:T(128)} %get-tuple-element.202.meta, bf16[1024,512]{1,0:T(8,128)(2,1)} %get-tuple-element.126.q_ref, bf16[4096,128]{1,0:T(8,128)(2,1)} %get-tuple-element.106.ka_ref, bf16[4096,128]{1,0:T(8,128)(2,1)} %concatenate.116.kb_ref, bf16[80,4096]{1,0:T(8,128)(2,1)} %copy.143.vt_ref), custom_call_target="tpu_custom_call" | custom-call | flops 20615843840 | bytes 8388608 | tf_op jit(solution)/shard_map/attend/pallas_call | solution.py:69
  193.0 5.8 collective-permute-start.19
  198.8 11.3 fusion.62
  214.2 6.0 fusion.63
  224.3 11.4 convert_element_type.162
  250.5 10.2 collective-permute-done.3
  268.9 14.2 collective-permute-done.21
  291.1 11.9 collective-permute-done.4
  326.3 7.7 copy.148
  333.9 15.9 %multiply_reduce_fusion.2 = (f32[1024]{0:T(1024)S(1)}, f32[1024,2048]{1,0:T(8,128)}) fusion(bf16[4,1024,512]{1,2,0:T(8,128)(2,1)} %constant_dynamic-update-slice_fusion.12, bf16[4,2048,512]{2,1,0:T(8,128)(2,1)} %bitcast.247, f32[2048,2048]{1,0:T(8,128)} %convert_element_type.162), kind=kOutput, calls=%fused_computation.10 | convolution fusion | flops 8596225024 | bytes 29364224 | tf_op jit(solution)/shard_map/trq,tdq->rd/dot_general | solution.py:431
  349.8 14.2 multiply_reduce_fusion.1
  364.1 8.6 multiply_convert_fusion.1
  372.7 11.8 fusion.81
  384.5 8.4 fusion.82
  393.0 15.1 %multiply_convert_fusion.3 = (bf16[1024,1408]{1,0:T(8,128)(2,1)}, bf16[1024,1408]{1,0:T(8,128)(2,1)S(1)}, bf16[1024,1408]{1,0:T(8,128)(2,1)}) fusion(f32[1024,1408]{1,0:T(8,128)} %fusion.81, f32[1024,1408]{1,0:T(8,128)} %fusion.82, bf16[2048,1408]{1,0:T(8,128)(2,1)} %param.23, bf16[2048,2048]{1,0:T(8,128)(2,1)S(1)} %bitcast.244), kind=kOutput, calls=%fused_computation.24 | convolution fusion | flops 5928648704 | bytes 30146560 | tf_op jit(solution)/shard_map/dot_general | solution.py:308
  408.1 11.8 fusion.84
  419.9 10.5 fusion.79
  430.4 8.4 fusion.80
  438.8 15.3 %multiply_convert_fusion.5 = (bf16[1024,1408]{1,0:T(8,128)(2,1)}, bf16[1024,1408]{1,0:T(8,128)(2,1)}, bf16[1024,1408]{1,0:T(8,128)(2,1)}) fusion(f32[1024,1408]{1,0:T(8,128)} %fusion.79, f32[1024,1408]{1,0:T(8,128)} %fusion.80, bf16[2048,1408]{1,0:T(8,128)(2,1)} %param.23, bf16[2048,2048]{1,0:T(8,128)(2,1)S(1)} %bitcast.244), kind=kOutput, calls=%fused_computation.26 | convolution fusion | flops 5928648704 | bytes 30146560 | tf_op jit(solution)/shard_map/dot_general | solution.py:308
  454.2 17.6 %convolution_convert_fusion.1 = bf16[2048,1408]{1,0:T(8,128)(2,1)} fusion(bf16[1024,1408]{1,0:T(8,128)(2,1)S(1)} %copy-done.85, bf16[1024,1408]{1,0:T(8,128)(2,1)} %get-tuple-element.108, bf16[1024,2048]{1,0:T(8,128)(2,1)S(1)} %get-tuple-element.200, bf16[1024,2048]{1,0:T(8,128)(2,1)} %get-tuple-element.201), kind=kOutput, calls=%fused_computation.12 | convolution fusion | flops 11842355200 | bytes 19922944 | tf_op jit(solution)/shard_map/rd,rf->df/dot_general | solution.py:316
  471.8 12.0 add_convert_fusion
  486.3 11.1 fusion.83
  497.4 11.0 add_convert_fusion.1
  512.0 16.6 %convolution_convert_fusion.2 = bf16[2048,1408]{1,0:T(8,128)(2,1)} fusion(bf16[1024,1408]{1,0:T(8,128)(2,1)} %copy-done.83, bf16[1024,1408]{1,0:T(8,128)(2,1)} %get-tuple-element.109, bf16[1024,2048]{1,0:T(8,128)(2,1)S(1)} %copy-done.34, bf16[1024,2048]{1,0:T(8,128)(2,1)S(1)} %copy-done.36), kind=kOutput, calls=%fused_computation.13 | convolution fusion | flops 11842355200 | bytes 19922944 | tf_op jit(solution)/shard_map/rd,rf->df/dot_general | solution.py:316
  528.6 18.4 %fusion = bf16[2048,1408]{0,1:T(8,128)(2,1)} fusion(bf16[2048,2048]{1,0:T(8,128)(2,1)} %param.13, bf16[1024,1408]{1,0:T(8,128)(2,1)} %get-tuple-element.113, bf16[1024,1408]{1,0:T(8,128)(2,1)} %get-tuple-element.110), kind=kOutput, calls=%fused_computation.14 | convolution fusion | flops 11825577984 | bytes 19922944 | tf_op jit(solution)/shard_map/rd,rf->df/dot_general | solution.py:316
  547.0 9.8 convolution_convert_fusion.4
  562.6 8.7 convolution_convert_fusion.5
  574.2 29.7 %collective-permute-done.38 = bf16[256,2048]{1,0:T(8,128)(2,1)S(1)} collective-permute-done((bf16[256,2048]{1,0:T(8,128)(2,1)S(1)}, bf16[256,2048]{1,0:T(8,128)(2,1)S(1)}, u32[]{:S(2)}, u32[]{:S(2)}) %collective-permute-start.38) | collective-permute-done | bytes 1048608 | tf_op jit(solution)/shard_map/ppermute | solution.py:267
  609.3 13.8 collective-permute-done.7
  624.4 5.4 collective-permute-start.8
  639.0 13.7 collective-permute-done.8
  666.7 8.4 collective-permute-done.25
  679.0 6.0 collective-permute-start.26
  687.7 31.4 %collective-permute-done.39 = bf16[256,2048]{1,0:T(8,128)(2,1)S(1)} collective-permute-done((bf16[256,2048]{1,0:T(8,128)(2,1)}, bf16[256,2048]{1,0:T(8,128)(2,1)S(1)}, u32[]{:S(2)}, u32[]{:S(2)}) %collective-permute-start.39) | collective-permute-done | bytes 1048608 | tf_op jit(solution)/shard_map/ppermute | solution.py:267
  735.8 29.7 %collective-permute-start.44 = (bf16[256,512]{1,0:T(8,128)(2,1)S(1)}, bf16[256,512]{1,0:T(8,128)(2,1)S(1)}, u32[]{:S(2)}, u32[]{:S(2)}) collective-permute-start(bf16[256,512]{1,0:T(8,128)(2,1)S(1)} %get-tuple-element.162), channel_id=1, source_target_pairs={{0,2},{1,3},{2,0},{3,1},{4,6},{5,7},{6,4},{7,5},{8,10},{9,11},{10,... | collective-permute-start | bytes 786440 | tf_op jit(solution)/shard_map/ppermute | solution.py:285
  774.4 9.1 collective-permute-done.43
  791.0 68.7 %attend_back.2 = (bf16[1024,512]{1,0:T(8,128)(2,1)}, f32[4096,128]{1,0:T(8,128)}, f32[4096,128]{1,0:T(8,128)}) custom-call(s32[5]{0:T(128)} %get-tuple-element.203.meta, bf16[1024,512]{1,0:T(8,128)(2,1)} %get-tuple-element.127.q_ref, bf16[1024,512]{1,0:T(8,128)(2,1)} %get-tuple-element.21.o_ref, bf16[1024,512]{1,0:T(8,128)(2,1)} %bitcast.264, ...), custom_call_target="tpu_custom_call" | custom-call | flops 51539607552 | bytes 16777216 | tf_op jit(solution)/shard_map/attend_back/pallas_call | solution.py:198
  860.8 91.1 %attend_back.3 = (bf16[1024,512]{1,0:T(8,128)(2,1)}, f32[4096,128]{1,0:T(8,128)}, f32[4096,128]{1,0:T(8,128)}) custom-call(s32[5]{0:T(128)} %get-tuple-element.202.meta, bf16[1024,512]{1,0:T(8,128)(2,1)} %get-tuple-element.126.q_ref, bf16[1024,512]{1,0:T(8,128)(2,1)} %get-tuple-element.22.o_ref, bf16[1024,512]{1,0:T(8,128)(2,1)} %bitcast.265, ...), custom_call_target="tpu_custom_call" | custom-call | flops 51539607552 | bytes 16777216 | tf_op jit(solution)/shard_map/attend_back/pallas_call | solution.py:198
  958.0 5.4 convolution_convert_fusion.6
  990.8 7.7 copy.157
  1003.1 5.7 collective-permute-done.12
  1019.3 10.5 collective-permute-start.13
  1029.8 6.7 convolution_convert_fusion.3
  1036.6 12.3 copy.163
  1072.1 6.5 collective-permute-done.46
  1116.6 6.9 multiply_reduce_fusion.5
  1136.9 5.6 collective-permute-start.27
  1149.4 8.2 collective-permute-done.15
  1160.9 52.4 %psum.7 = f32[2,2048]{1,0:T(2,128)S(1)} all-reduce(f32[2,2048]{1,0:T(2,128)S(1)} %pad_maximum_fusion.16), channel_id=1, replica_groups=mesh['dp'=4,'ctx'=2,'tensor'=4] {'dp','ctx','tensor'}, use_global_device_ids=true, to_apply=%region_12.13 | all-reduce | flops 4096 | bytes 32768 | tf_op jit(solution)/shard_map/psum | solution.py:616
  1227.4 14.5 %collective-permute-done.30 = bf16[256,2048]{1,0:T(8,128)(2,1)S(1)} collective-permute-done((bf16[256,2048]{1,0:T(8,128)(2,1)S(1)}, bf16[256,2048]{1,0:T(8,128)(2,1)S(1)}, u32[]{:S(2)}, u32[]{:S(2)}) %collective-permute-start.30) | collective-permute-done | bytes 1048608 | tf_op jit(solution)/shard_map/ppermute | solution.py:271
  1247.5 5.7 collective-permute-start.31
  1277.6 5.5 collective-permute-start.74
  1293.2 8.4 collective-permute-done.80
  1301.6 10.5 collective-permute-start.82
  1313.2 10.2 collective-permute-done.81
  1325.2 6.8 collective-permute-done.82
  1339.0 21.2 %collective-permute-done.76 = bf16[256,2048]{1,0:T(8,128)(2,1)S(1)} collective-permute-done((bf16[256,2048]{1,0:T(8,128)(2,1)S(1)}, bf16[256,2048]{1,0:T(8,128)(2,1)S(1)}, u32[]{:S(2)}, u32[]{:S(2)}) %collective-permute-start.76) | collective-permute-done | bytes 1048608 | tf_op jit(solution)/shard_map/ppermute | solution.py:245
  1363.1 19.5 %collective-permute-done.34 = bf16[256,2048]{1,0:T(8,128)(2,1)S(1)} collective-permute-done((bf16[256,2048]{1,0:T(8,128)(2,1)}, bf16[256,2048]{1,0:T(8,128)(2,1)S(1)}, u32[]{:S(2)}, u32[]{:S(2)}) %collective-permute-start.34) | collective-permute-done | bytes 1048608 | tf_op jit(solution)/shard_map/ppermute | solution.py:245
  1390.7 11.6 collective-permute-done.77
  1420.1 7.5 collective-permute-done.84
  (600 shorter events, 434.1 us)
Async XLA Ops:
  7.2 33.6 %all-gather.9.cloned.1.call-start = ((), (), s32[]{:S(2)}) async-start(), calls=%async_computation.10 | async-start | bytes 1310720 | tf_op jit(solution)/shard_map/all_gather | solution.py:297
  9.5 255.9 %all-gather.13.cloned.1.call-start = ((), (), s32[]{:S(2)}) async-start(), calls=%async_computation.12 | async-start | bytes 1310720 | tf_op jit(solution)/shard_map/all_gather | solution.py:297
  11.3 315.0 %all-gather.11.cloned.1.call-start = ((), (), s32[]{:S(2)}) async-start(), calls=%async_computation.11 | async-start | bytes 9437184 | tf_op jit(solution)/shard_map/all_gather | solution.py:298
  40.9 949.9 %all-gather.15.cloned.1.call-start = ((), (), s32[]{:S(2)}) async-start(), calls=%async_computation.13 | async-start | bytes 9437184 | tf_op jit(solution)/shard_map/all_gather | solution.py:298
  49.1 30.6 %collective-permute-start = (bf16[2048,128]{1,0:T(8,128)(2,1)}, bf16[2048,128]{1,0:T(8,128)(2,1)}, u32[]{:S(2)}, u32[]{:S(2)}) collective-permute-start(bf16[2048,128]{1,0:T(8,128)(2,1)} %pad_maximum_fusion.11), channel_id=1, source_target_pairs={{0,4},{4,0},{1,5},{5,1},{2,6},{6,2},{3,7},{7,3},{8,12},{12,8},{9,1... | collective-permute-start | bytes 1572872 | tf_op jit(solution)/shard_map/ppermute | solution.py:381
  130.9 81.7 %collective-permute-start.1 = (bf16[1024,512]{1,0:T(8,128)(2,1)}, bf16[1024,512]{1,0:T(8,128)(2,1)}, u32[]{:S(2)}, u32[]{:S(2)}) collective-permute-start(bf16[1024,512]{1,0:T(8,128)(2,1)} %get-tuple-element.21.o_ref), channel_id=1, source_target_pairs={{0,1},{1,2},{2,3},{4,5},{5,6},{6,7},{8,9},{9,10},{10,11},{12,13},{... | collective-permute-start | bytes 3145736 | tf_op jit(solution)/shard_map/ppermute | solution.py:242
  135.3 85.0 %collective-permute-start.2 = (bf16[1024,512]{1,0:T(8,128)(2,1)}, bf16[1024,512]{1,0:T(8,128)(2,1)}, u32[]{:S(2)}, u32[]{:S(2)}) collective-permute-start(bf16[1024,512]{1,0:T(8,128)(2,1)} %get-tuple-element.21.o_ref), channel_id=1, source_target_pairs={{1,0},{2,1},{3,2},{5,4},{6,5},{7,6},{9,8},{10,9},{11,10},{13,12},{... | collective-permute-start | bytes 3145736 | tf_op jit(solution)/shard_map/ppermute | solution.py:245
  193.0 28.6 %collective-permute-start.19 = (bf16[1024,512]{1,0:T(8,128)(2,1)}, bf16[1024,512]{1,0:T(8,128)(2,1)}, u32[]{:S(2)}, u32[]{:S(2)}) collective-permute-start(bf16[1024,512]{1,0:T(8,128)(2,1)} %get-tuple-element.22.o_ref), channel_id=1, source_target_pairs={{0,1},{1,2},{2,3},{4,5},{5,6},{6,7},{8,9},{9,10},{10,11},{12,13},{... | collective-permute-start | bytes 3145736 | tf_op jit(solution)/shard_map/ppermute | solution.py:242
  220.3 40.3 %collective-permute-start.3 = (bf16[1024,512]{1,0:T(8,128)(2,1)}, bf16[1024,512]{1,0:T(8,128)(2,1)}, u32[]{:S(2)}, u32[]{:S(2)}) collective-permute-start(bf16[1024,512]{1,0:T(8,128)(2,1)} %collective-permute-done.2), channel_id=1, source_target_pairs={{1,0},{2,1},{5,4},{6,5},{9,8},{10,9},{13,12},{14,13},{17,16},{18,1... | collective-permute-start | bytes 3145736 | tf_op jit(solution)/shard_map/ppermute | solution.py:245
  221.6 44.0 %collective-permute-start.23 = (bf16[1024,512]{1,0:T(8,128)(2,1)}, bf16[1024,512]{1,0:T(8,128)(2,1)}, u32[]{:S(2)}, u32[]{:S(2)}) collective-permute-start(bf16[1024,512]{1,0:T(8,128)(2,1)} %collective-permute-done.19), channel_id=1, source_target_pairs={{1,2},{2,3},{5,6},{6,7},{9,10},{10,11},{13,14},{14,15},{17,18},{18... | collective-permute-start | bytes 3145736 | tf_op jit(solution)/shard_map/ppermute | solution.py:242
  238.2 44.9 %collective-permute-start.21 = (bf16[1024,512]{1,0:T(8,128)(2,1)}, bf16[1024,512]{1,0:T(8,128)(2,1)}, u32[]{:S(2)}, u32[]{:S(2)}) collective-permute-start(bf16[1024,512]{1,0:T(8,128)(2,1)} %collective-permute-done.20), channel_id=1, source_target_pairs={{1,0},{2,1},{5,4},{6,5},{9,8},{10,9},{13,12},{14,13},{17,16},{18,1... | collective-permute-start | bytes 3145736 | tf_op jit(solution)/shard_map/ppermute | solution.py:245
  239.5 48.7 %collective-permute-start.6 = (bf16[1024,512]{1,0:T(8,128)(2,1)}, bf16[1024,512]{1,0:T(8,128)(2,1)}, u32[]{:S(2)}, u32[]{:S(2)}) collective-permute-start(bf16[1024,512]{1,0:T(8,128)(2,1)} %collective-permute-done.5), channel_id=1, source_target_pairs={{2,3},{6,7},{10,11},{14,15},{18,19},{22,23},{26,27},{30,31}} | collective-permute-start | bytes 3145736 | tf_op jit(solution)/shard_map/ppermute | solution.py:242
  260.6 42.4 %collective-permute-start.4 = (bf16[1024,512]{1,0:T(8,128)(2,1)}, bf16[1024,512]{1,0:T(8,128)(2,1)}, u32[]{:S(2)}, u32[]{:S(2)}) collective-permute-start(bf16[1024,512]{1,0:T(8,128)(2,1)} %collective-permute-done.3), channel_id=1, source_target_pairs={{1,0},{5,4},{9,8},{13,12},{17,16},{21,20},{25,24},{29,28}} | collective-permute-start | bytes 3145736 | tf_op jit(solution)/shard_map/ppermute | solution.py:245
  265.5 987.7 %reduce-scatter.12.cloned.1.call-start = ((), (), s32[]{:S(2)}) async-start(), calls=%async_computation.8 | async-start | bytes 6488064 | tf_op jit(solution)/shard_map/reduce_scatter | solution.py:481
  265.5 40.5 %collective-permute-start.24 = (bf16[1024,512]{1,0:T(8,128)(2,1)}, bf16[1024,512]{1,0:T(8,128)(2,1)}, u32[]{:S(2)}, u32[]{:S(2)}) collective-permute-start(bf16[1024,512]{1,0:T(8,128)(2,1)} %collective-permute-done.23), channel_id=1, source_target_pairs={{2,3},{6,7},{10,11},{14,15},{18,19},{22,23},{26,27},{30,31}} | collective-permute-start | bytes 3145736 | tf_op jit(solution)/shard_map/ppermute | solution.py:242
  283.1 31.2 %collective-permute-start.22 = (bf16[1024,512]{1,0:T(8,128)(2,1)}, bf16[1024,512]{1,0:T(8,128)(2,1)}, u32[]{:S(2)}, u32[]{:S(2)}) collective-permute-start(bf16[1024,512]{1,0:T(8,128)(2,1)} %collective-permute-done.21), channel_id=1, source_target_pairs={{1,0},{5,4},{9,8},{13,12},{17,16},{21,20},{25,24},{29,28}} | collective-permute-start | bytes 3145736 | tf_op jit(solution)/shard_map/ppermute | solution.py:245
  471.8 783.8 %reduce-scatter.10.cloned.1.call-start = ((), (), s32[]{:S(2)}) async-start(), calls=%async_computation.7 | async-start | bytes 6488064 | tf_op jit(solution)/shard_map/reduce_scatter | solution.py:481
  484.0 72.7 %collective-permute-start.49 = (bf16[256,2048]{1,0:T(8,128)(2,1)S(1)}, bf16[256,2048]{1,0:T(8,128)(2,1)}, u32[]{:S(2)}, u32[]{:S(2)}) collective-permute-start(bf16[256,2048]{1,0:T(8,128)(2,1)S(1)} %constant_dynamic-slice_fusion.13), channel_id=1, source_target_pairs={{0,1},{4,5},{8,9},{12,13},{16,17},{20,21},{24,25},{28,29}} | collective-permute-start | bytes 3145736 | tf_op jit(solution)/shard_map/ppermute | solution.py:267
  510.6 50.3 %collective-permute-start.37 = (bf16[256,2048]{1,0:T(8,128)(2,1)S(1)}, bf16[256,2048]{1,0:T(8,128)(2,1)S(1)}, u32[]{:S(2)}, u32[]{:S(2)}) collective-permute-start(bf16[256,2048]{1,0:T(8,128)(2,1)S(1)} %constant_dynamic-slice_fusion.20), channel_id=1, source_target_pairs={{0,1},{4,5},{8,9},{12,13},{16,17},{20,21},{24,25},{28,29}} | collective-permute-start | bytes 3145736 | tf_op jit(solution)/shard_map/ppermute | solution.py:267
  528.5 729.3 %reduce-scatter.14.cloned.1.call-start = ((), (), s32[]{:S(2)}) async-start(), calls=%async_computation.9 | async-start | bytes 6488064 | tf_op jit(solution)/shard_map/reduce_scatter | solution.py:481
  559.3 46.9 %collective-permute-start.50 = (bf16[256,2048]{1,0:T(8,128)(2,1)S(1)}, bf16[256,2048]{1,0:T(8,128)(2,1)S(1)}, u32[]{:S(2)}, u32[]{:S(2)}) collective-permute-start(bf16[256,2048]{1,0:T(8,128)(2,1)S(1)} %dynamic-slice_add_fusion.2), channel_id=1, source_target_pairs={{0,1},{1,2},{4,5},{5,6},{8,9},{9,10},{12,13},{13,14},{16,17},{17,1... | collective-permute-start | bytes 3145736 | tf_op jit(solution)/shard_map/ppermute | solution.py:267
  561.3 42.6 %collective-permute-start.38 = (bf16[256,2048]{1,0:T(8,128)(2,1)S(1)}, bf16[256,2048]{1,0:T(8,128)(2,1)S(1)}, u32[]{:S(2)}, u32[]{:S(2)}) collective-permute-start(bf16[256,2048]{1,0:T(8,128)(2,1)S(1)} %dynamic-slice_add_fusion.6), channel_id=1, source_target_pairs={{0,1},{1,2},{4,5},{5,6},{8,9},{9,10},{12,13},{13,14},{16,17},{17,1... | collective-permute-start | bytes 3145736 | tf_op jit(solution)/shard_map/ppermute | solution.py:267
  572.3 50.8 %collective-permute-start.7 = (bf16[256,2048]{1,0:T(8,128)(2,1)S(1)}, bf16[256,2048]{1,0:T(8,128)(2,1)S(1)}, u32[]{:S(2)}, u32[]{:S(2)}) collective-permute-start(bf16[256,2048]{1,0:T(8,128)(2,1)S(1)} %constant_dynamic-slice_fusion.24), channel_id=1, source_target_pairs={{0,1},{4,5},{8,9},{12,13},{16,17},{20,21},{24,25},{28,29}} | collective-permute-start | bytes 3145736 | tf_op jit(solution)/shard_map/ppermute | solution.py:267
  624.4 28.3 %collective-permute-start.8 = (bf16[256,2048]{1,0:T(8,128)(2,1)}, bf16[256,2048]{1,0:T(8,128)(2,1)}, u32[]{:S(2)}, u32[]{:S(2)}) collective-permute-start(bf16[256,2048]{1,0:T(8,128)(2,1)} %dynamic-slice_add_fusion.14), channel_id=1, source_target_pairs={{0,1},{1,2},{4,5},{5,6},{8,9},{9,10},{12,13},{13,14},{16,17},{17,1... | collective-permute-start | bytes 3145736 | tf_op jit(solution)/shard_map/ppermute | solution.py:267
  631.2 30.1 %collective-permute-start.41 = (bf16[256,2048]{1,0:T(8,128)(2,1)}, bf16[256,2048]{1,0:T(8,128)(2,1)}, u32[]{:S(2)}, u32[]{:S(2)}) collective-permute-start(bf16[256,2048]{1,0:T(8,128)(2,1)} %dynamic-slice_add_fusion.4), channel_id=1, source_target_pairs={{2,1},{3,2},{6,5},{7,6},{10,9},{11,10},{14,13},{15,14},{18,17},{19... | collective-permute-start | bytes 3145736 | tf_op jit(solution)/shard_map/ppermute | solution.py:271
  634.2 29.5 %collective-permute-start.53 = (bf16[256,2048]{1,0:T(8,128)(2,1)}, bf16[256,2048]{1,0:T(8,128)(2,1)}, u32[]{:S(2)}, u32[]{:S(2)}) collective-permute-start(bf16[256,2048]{1,0:T(8,128)(2,1)} %dynamic-slice_add_fusion), channel_id=1, source_target_pairs={{2,1},{3,2},{6,5},{7,6},{10,9},{11,10},{14,13},{15,14},{18,17},{19... | collective-permute-start | bytes 3145736 | tf_op jit(solution)/shard_map/ppermute | solution.py:271
  636.0 39.1 %collective-permute-start.25 = (bf16[256,2048]{1,0:T(8,128)(2,1)S(1)}, bf16[256,2048]{1,0:T(8,128)(2,1)S(1)}, u32[]{:S(2)}, u32[]{:S(2)}) collective-permute-start(bf16[256,2048]{1,0:T(8,128)(2,1)S(1)} %constant_dynamic-slice_fusion.22), channel_id=1, source_target_pairs={{0,1},{4,5},{8,9},{12,13},{16,17},{20,21},{24,25},{28,29}} | collective-permute-start | bytes 3145736 | tf_op jit(solution)/shard_map/ppermute | solution.py:267
  637.3 651.0 %reduce-scatter.6.cloned.1.call-start = ((), (), s32[]{:S(2)}) async-start(), calls=%async_computation.5 | async-start | bytes 2949120 | tf_op jit(solution)/shard_map/reduce_scatter | solution.py:481
  637.4 86.7 %collective-permute-start.51 = (bf16[256,2048]{1,0:T(8,128)(2,1)}, bf16[256,2048]{1,0:T(8,128)(2,1)S(1)}, u32[]{:S(2)}, u32[]{:S(2)}) collective-permute-start(bf16[256,2048]{1,0:T(8,128)(2,1)} %get-tuple-element.120), channel_id=1, source_target_pairs={{0,1},{1,2},{2,3},{4,5},{5,6},{6,7},{8,9},{9,10},{10,11},{12,13},{... | collective-permute-start | bytes 3145736 | tf_op jit(solution)/shard_map/ppermute | solution.py:267
  652.7 66.4 %collective-permute-start.39 = (bf16[256,2048]{1,0:T(8,128)(2,1)}, bf16[256,2048]{1,0:T(8,128)(2,1)S(1)}, u32[]{:S(2)}, u32[]{:S(2)}) collective-permute-start(bf16[256,2048]{1,0:T(8,128)(2,1)} %get-tuple-element.118), channel_id=1, source_target_pairs={{0,1},{1,2},{2,3},{4,5},{5,6},{6,7},{8,9},{9,10},{10,11},{12,13},{... | collective-permute-start | bytes 3145736 | tf_op jit(solution)/shard_map/ppermute | solution.py:267
  663.8 57.0 %collective-permute-start.42 = (bf16[256,2048]{1,0:T(8,128)(2,1)S(1)}, bf16[256,2048]{1,0:T(8,128)(2,1)S(1)}, u32[]{:S(2)}, u32[]{:S(2)}) collective-permute-start(bf16[256,2048]{1,0:T(8,128)(2,1)S(1)} %dynamic-slice_add_fusion.5), channel_id=1, source_target_pairs={{1,0},{2,1},{3,2},{5,4},{6,5},{7,6},{9,8},{10,9},{11,10},{13,12},{... | collective-permute-start | bytes 3145736 | tf_op jit(solution)/shard_map/ppermute | solution.py:271
  675.1 49.0 %collective-permute-start.54 = (bf16[256,2048]{1,0:T(8,128)(2,1)S(1)}, bf16[256,2048]{1,0:T(8,128)(2,1)S(1)}, u32[]{:S(2)}, u32[]{:S(2)}) collective-permute-start(bf16[256,2048]{1,0:T(8,128)(2,1)S(1)} %dynamic-slice_add_fusion.1), channel_id=1, source_target_pairs={{1,0},{2,1},{3,2},{5,4},{6,5},{7,6},{9,8},{10,9},{11,10},{13,12},{... | collective-permute-start | bytes 3145736 | tf_op jit(solution)/shard_map/ppermute | solution.py:271
  679.0 295.0 %collective-permute-start.26 = (bf16[256,2048]{1,0:T(8,128)(2,1)}, bf16[256,2048]{1,0:T(8,128)(2,1)}, u32[]{:S(2)}, u32[]{:S(2)}) collective-permute-start(bf16[256,2048]{1,0:T(8,128)(2,1)} %dynamic-slice_add_fusion.10), channel_id=1, source_target_pairs={{0,1},{1,2},{4,5},{5,6},{8,9},{9,10},{12,13},{13,14},{16,17},{17,1... | collective-permute-start | bytes 3145736 | tf_op jit(solution)/shard_map/ppermute | solution.py:267
  719.2 262.6 %collective-permute-start.11 = (bf16[256,2048]{1,0:T(8,128)(2,1)}, bf16[256,2048]{1,0:T(8,128)(2,1)}, u32[]{:S(2)}, u32[]{:S(2)}) collective-permute-start(bf16[256,2048]{1,0:T(8,128)(2,1)} %dynamic-slice_add_fusion.12), channel_id=1, source_target_pairs={{2,1},{3,2},{6,5},{7,6},{10,9},{11,10},{14,13},{15,14},{18,17},{19... | collective-permute-start | bytes 3145736 | tf_op jit(solution)/shard_map/ppermute | solution.py:271
  731.8 51.7 %collective-permute-start.43 = (bf16[256,512]{1,0:T(8,128)(2,1)S(1)}, bf16[256,512]{1,0:T(8,128)(2,1)S(1)}, u32[]{:S(2)}, u32[]{:S(2)}) collective-permute-start(bf16[256,512]{1,0:T(8,128)(2,1)S(1)} %get-tuple-element.163), channel_id=1, source_target_pairs={{0,1},{1,2},{2,3},{3,0},{4,5},{5,6},{6,7},{7,4},{8,9},{9,10},{10,1... | collective-permute-start | bytes 786440 | tf_op jit(solution)/shard_map/ppermute | solution.py:285
  735.8 48.2 %collective-permute-start.44 = (bf16[256,512]{1,0:T(8,128)(2,1)S(1)}, bf16[256,512]{1,0:T(8,128)(2,1)S(1)}, u32[]{:S(2)}, u32[]{:S(2)}) collective-permute-start(bf16[256,512]{1,0:T(8,128)(2,1)S(1)} %get-tuple-element.162), channel_id=1, source_target_pairs={{0,2},{1,3},{2,0},{3,1},{4,6},{5,7},{6,4},{7,5},{8,10},{9,11},{10,... | collective-permute-start | bytes 786440 | tf_op jit(solution)/shard_map/ppermute | solution.py:285
  783.5 76.2 %collective-permute-start.55 = (bf16[256,512]{1,0:T(8,128)(2,1)S(1)}, bf16[256,512]{1,0:T(8,128)(2,1)S(1)}, u32[]{:S(2)}, u32[]{:S(2)}) collective-permute-start(bf16[256,512]{1,0:T(8,128)(2,1)S(1)} %get-tuple-element.172), channel_id=1, source_target_pairs={{0,1},{1,2},{2,3},{3,0},{4,5},{5,6},{6,7},{7,4},{8,9},{9,10},{10,1... | collective-permute-start | bytes 786440 | tf_op jit(solution)/shard_map/ppermute | solution.py:285
  784.0 75.8 %collective-permute-start.56 = (bf16[256,512]{1,0:T(8,128)(2,1)S(1)}, bf16[256,512]{1,0:T(8,128)(2,1)S(1)}, u32[]{:S(2)}, u32[]{:S(2)}) collective-permute-start(bf16[256,512]{1,0:T(8,128)(2,1)S(1)} %get-tuple-element.171), channel_id=1, source_target_pairs={{0,2},{1,3},{2,0},{3,1},{4,6},{5,7},{6,4},{7,5},{8,10},{9,11},{10,... | collective-permute-start | bytes 786440 | tf_op jit(solution)/shard_map/ppermute | solution.py:285
  784.2 75.6 %collective-permute-start.57 = (bf16[256,512]{1,0:T(8,128)(2,1)S(1)}, bf16[256,512]{1,0:T(8,128)(2,1)S(1)}, u32[]{:S(2)}, u32[]{:S(2)}) collective-permute-start(bf16[256,512]{1,0:T(8,128)(2,1)S(1)} %get-tuple-element.170), channel_id=1, source_target_pairs={{0,3},{1,0},{2,1},{3,2},{4,7},{5,4},{6,5},{7,6},{8,11},{9,8},{10,9... | collective-permute-start | bytes 786440 | tf_op jit(solution)/shard_map/ppermute | solution.py:285
  971.4 436.2 %reduce-scatter.8.cloned.1.call-start = ((), (), s32[]{:S(2)}) async-start(), calls=%async_computation.6 | async-start | bytes 9437184 | tf_op jit(solution)/shard_map/reduce_scatter | solution.py:583
  1001.4 135.5 %collective-permute-start.29 = (bf16[256,2048]{1,0:T(8,128)(2,1)}, bf16[256,2048]{1,0:T(8,128)(2,1)}, u32[]{:S(2)}, u32[]{:S(2)}) collective-permute-start(bf16[256,2048]{1,0:T(8,128)(2,1)} %dynamic-slice_add_fusion.8), channel_id=1, source_target_pairs={{2,1},{3,2},{6,5},{7,6},{10,9},{11,10},{14,13},{15,14},{18,17},{19... | collective-permute-start | bytes 3145736 | tf_op jit(solution)/shard_map/ppermute | solution.py:271
  1018.1 117.5 %collective-permute-start.14 = (bf16[256,2048]{1,0:T(8,128)(2,1)}, bf16[256,2048]{1,0:T(8,128)(2,1)}, u32[]{:S(2)}, u32[]{:S(2)}) collective-permute-start(bf16[256,2048]{1,0:T(8,128)(2,1)} %get-tuple-element.105), channel_id=1, source_target_pairs={{1,0},{2,1},{3,2},{5,4},{6,5},{7,6},{9,8},{10,9},{11,10},{13,12},{... | collective-permute-start | bytes 3145736 | tf_op jit(solution)/shard_map/ppermute | solution.py:245
  1019.3 123.1 %collective-permute-start.13 = (bf16[256,2048]{1,0:T(8,128)(2,1)}, bf16[256,2048]{1,0:T(8,128)(2,1)}, u32[]{:S(2)}, u32[]{:S(2)}) collective-permute-start(bf16[256,2048]{1,0:T(8,128)(2,1)} %get-tuple-element.105), channel_id=1, source_target_pairs={{0,1},{1,2},{2,3},{4,5},{5,6},{6,7},{8,9},{9,10},{10,11},{12,13},{... | collective-permute-start | bytes 3145736 | tf_op jit(solution)/shard_map/ppermute | solution.py:242
  1136.9 90.5 %collective-permute-start.27 = (bf16[256,2048]{1,0:T(8,128)(2,1)}, bf16[256,2048]{1,0:T(8,128)(2,1)}, u32[]{:S(2)}, u32[]{:S(2)}) collective-permute-start(bf16[256,2048]{1,0:T(8,128)(2,1)} %get-tuple-element.122), channel_id=1, source_target_pairs={{0,1},{1,2},{2,3},{4,5},{5,6},{6,7},{8,9},{9,10},{10,11},{12,13},{... | collective-permute-start | bytes 3145736 | tf_op jit(solution)/shard_map/ppermute | solution.py:267
  1142.5 71.5 %collective-permute-start.17 = (bf16[256,2048]{1,0:T(8,128)(2,1)}, bf16[256,2048]{1,0:T(8,128)(2,1)}, u32[]{:S(2)}, u32[]{:S(2)}) collective-permute-start(bf16[256,2048]{1,0:T(8,128)(2,1)} %collective-permute-done.13), channel_id=1, source_target_pairs={{1,2},{2,3},{5,6},{6,7},{9,10},{10,11},{13,14},{14,15},{17,18},{18... | collective-permute-start | bytes 3145736 | tf_op jit(solution)/shard_map/ppermute | solution.py:242
  1146.3 69.0 %collective-permute-start.64 = (bf16[256,2048]{1,0:T(8,128)(2,1)S(1)}, bf16[256,2048]{1,0:T(8,128)(2,1)}, u32[]{:S(2)}, u32[]{:S(2)}) collective-permute-start(bf16[256,2048]{1,0:T(8,128)(2,1)S(1)} %collective-permute-done.63), channel_id=1, source_target_pairs={{1,0},{2,1},{5,4},{6,5},{9,8},{10,9},{13,12},{14,13},{17,16},{18,1... | collective-permute-start | bytes 3145736 | tf_op jit(solution)/shard_map/ppermute | solution.py:245
  1147.8 68.3 %collective-permute-start.66 = (bf16[256,2048]{1,0:T(8,128)(2,1)S(1)}, bf16[256,2048]{1,0:T(8,128)(2,1)}, u32[]{:S(2)}, u32[]{:S(2)}) collective-permute-start(bf16[256,2048]{1,0:T(8,128)(2,1)S(1)} %collective-permute-done.62), channel_id=1, source_target_pairs={{1,2},{2,3},{5,6},{6,7},{9,10},{10,11},{13,14},{14,15},{17,18},{18... | collective-permute-start | bytes 3145736 | tf_op jit(solution)/shard_map/ppermute | solution.py:242
  1157.6 59.7 %collective-permute-start.16 = (bf16[256,2048]{1,0:T(8,128)(2,1)}, bf16[256,2048]{1,0:T(8,128)(2,1)}, u32[]{:S(2)}, u32[]{:S(2)}) collective-permute-start(bf16[256,2048]{1,0:T(8,128)(2,1)} %collective-permute-done.15), channel_id=1, source_target_pairs={{1,0},{5,4},{9,8},{13,12},{17,16},{21,20},{25,24},{29,28}} | collective-permute-start | bytes 3145736 | tf_op jit(solution)/shard_map/ppermute | solution.py:245
  1214.0 28.0 %collective-permute-start.30 = (bf16[256,2048]{1,0:T(8,128)(2,1)S(1)}, bf16[256,2048]{1,0:T(8,128)(2,1)S(1)}, u32[]{:S(2)}, u32[]{:S(2)}) collective-permute-start(bf16[256,2048]{1,0:T(8,128)(2,1)S(1)} %dynamic-slice_add_fusion.9), channel_id=1, source_target_pairs={{1,0},{2,1},{3,2},{5,4},{6,5},{7,6},{9,8},{10,9},{11,10},{13,12},{... | collective-permute-start | bytes 3145736 | tf_op jit(solution)/shard_map/ppermute | solution.py:271
  1216.1 48.5 %collective-permute-start.65 = (bf16[256,2048]{1,0:T(8,128)(2,1)}, bf16[256,2048]{1,0:T(8,128)(2,1)}, u32[]{:S(2)}, u32[]{:S(2)}) collective-permute-start(bf16[256,2048]{1,0:T(8,128)(2,1)} %collective-permute-done.64), channel_id=1, source_target_pairs={{1,0},{5,4},{9,8},{13,12},{17,16},{21,20},{25,24},{29,28}} | collective-permute-start | bytes 3145736 | tf_op jit(solution)/shard_map/ppermute | solution.py:245
  1217.4 53.2 %collective-permute-start.67 = (bf16[256,2048]{1,0:T(8,128)(2,1)}, bf16[256,2048]{1,0:T(8,128)(2,1)}, u32[]{:S(2)}, u32[]{:S(2)}) collective-permute-start(bf16[256,2048]{1,0:T(8,128)(2,1)} %collective-permute-done.66), channel_id=1, source_target_pairs={{2,3},{6,7},{10,11},{14,15},{18,19},{22,23},{26,27},{30,31}} | collective-permute-start | bytes 3145736 | tf_op jit(solution)/shard_map/ppermute | solution.py:242
  1246.2 40.8 %collective-permute-start.32 = (bf16[256,2048]{1,0:T(8,128)(2,1)}, bf16[256,2048]{1,0:T(8,128)(2,1)}, u32[]{:S(2)}, u32[]{:S(2)}) collective-permute-start(bf16[256,2048]{1,0:T(8,128)(2,1)} %get-tuple-element.103), channel_id=1, source_target_pairs={{1,0},{2,1},{3,2},{5,4},{6,5},{7,6},{9,8},{10,9},{11,10},{13,12},{... | collective-permute-start | bytes 3145736 | tf_op jit(solution)/shard_map/ppermute | solution.py:245
  1247.5 45.6 %collective-permute-start.31 = (bf16[256,2048]{1,0:T(8,128)(2,1)}, bf16[256,2048]{1,0:T(8,128)(2,1)}, u32[]{:S(2)}, u32[]{:S(2)}) collective-permute-start(bf16[256,2048]{1,0:T(8,128)(2,1)} %get-tuple-element.103), channel_id=1, source_target_pairs={{0,1},{1,2},{2,3},{4,5},{5,6},{6,7},{8,9},{9,10},{10,11},{12,13},{... | collective-permute-start | bytes 3145736 | tf_op jit(solution)/shard_map/ppermute | solution.py:242
  1276.3 55.9 %collective-permute-start.75 = (bf16[256,2048]{1,0:T(8,128)(2,1)S(1)}, bf16[256,2048]{1,0:T(8,128)(2,1)S(1)}, u32[]{:S(2)}, u32[]{:S(2)}) collective-permute-start(bf16[256,2048]{1,0:T(8,128)(2,1)S(1)} %get-tuple-element.95), channel_id=1, source_target_pairs={{1,0},{2,1},{3,2},{5,4},{6,5},{7,6},{9,8},{10,9},{11,10},{13,12},{... | collective-permute-start | bytes 3145736 | tf_op jit(solution)/shard_map/ppermute | solution.py:245
  1277.6 55.9 %collective-permute-start.74 = (bf16[256,2048]{1,0:T(8,128)(2,1)S(1)}, bf16[256,2048]{1,0:T(8,128)(2,1)}, u32[]{:S(2)}, u32[]{:S(2)}) collective-permute-start(bf16[256,2048]{1,0:T(8,128)(2,1)S(1)} %get-tuple-element.95), channel_id=1, source_target_pairs={{0,1},{1,2},{2,3},{4,5},{5,6},{6,7},{8,9},{9,10},{10,11},{12,13},{... | collective-permute-start | bytes 3145736 | tf_op jit(solution)/shard_map/ppermute | solution.py:242
  1287.0 48.2 %collective-permute-start.33 = (bf16[256,2048]{1,0:T(8,128)(2,1)}, bf16[256,2048]{1,0:T(8,128)(2,1)}, u32[]{:S(2)}, u32[]{:S(2)}) collective-permute-start(bf16[256,2048]{1,0:T(8,128)(2,1)} %collective-permute-done.32), channel_id=1, source_target_pairs={{1,0},{2,1},{5,4},{6,5},{9,8},{10,9},{13,12},{14,13},{17,16},{18,1... | collective-permute-start | bytes 3145736 | tf_op jit(solution)/shard_map/ppermute | solution.py:245
  1293.1 30.3 %collective-permute-start.81 = (bf16[64,128]{0,1:T(8,128)(2,1)S(1)}, bf16[64,128]{0,1:T(8,128)(2,1)S(1)}, u32[]{:S(2)}, u32[]{:S(2)}) collective-permute-start(bf16[64,128]{0,1:T(8,128)(2,1)S(1)} %get-tuple-element.178), channel_id=1, source_target_pairs={{0,2},{1,3},{2,0},{3,1},{4,6},{5,7},{6,4},{7,5},{8,10},{9,11},{10,... | collective-permute-start | bytes 49160 | tf_op jit(solution)/shard_map/ppermute | solution.py:285
  1301.6 30.4 %collective-permute-start.82 = (bf16[64,128]{0,1:T(8,128)(2,1)S(1)}, bf16[64,128]{0,1:T(8,128)(2,1)S(1)}, u32[]{:S(2)}, u32[]{:S(2)}) collective-permute-start(bf16[64,128]{0,1:T(8,128)(2,1)S(1)} %get-tuple-element.177), channel_id=1, source_target_pairs={{0,3},{1,0},{2,1},{3,2},{4,7},{5,4},{6,5},{7,6},{8,11},{9,8},{10,9... | collective-permute-start | bytes 49160 | tf_op jit(solution)/shard_map/ppermute | solution.py:285
  1332.2 28.0 %collective-permute-start.76 = (bf16[256,2048]{1,0:T(8,128)(2,1)S(1)}, bf16[256,2048]{1,0:T(8,128)(2,1)S(1)}, u32[]{:S(2)}, u32[]{:S(2)}) collective-permute-start(bf16[256,2048]{1,0:T(8,128)(2,1)S(1)} %collective-permute-done.75), channel_id=1, source_target_pairs={{1,0},{2,1},{5,4},{6,5},{9,8},{10,9},{13,12},{14,13},{17,16},{18,1... | collective-permute-start | bytes 3145736 | tf_op jit(solution)/shard_map/ppermute | solution.py:245
  1333.5 28.0 %collective-permute-start.78 = (bf16[256,2048]{1,0:T(8,128)(2,1)}, bf16[256,2048]{1,0:T(8,128)(2,1)}, u32[]{:S(2)}, u32[]{:S(2)}) collective-permute-start(bf16[256,2048]{1,0:T(8,128)(2,1)} %collective-permute-done.74), channel_id=1, source_target_pairs={{1,2},{2,3},{5,6},{6,7},{9,10},{10,11},{13,14},{14,15},{17,18},{18... | collective-permute-start | bytes 3145736 | tf_op jit(solution)/shard_map/ppermute | solution.py:242
  1335.2 47.4 %collective-permute-start.34 = (bf16[256,2048]{1,0:T(8,128)(2,1)}, bf16[256,2048]{1,0:T(8,128)(2,1)S(1)}, u32[]{:S(2)}, u32[]{:S(2)}) collective-permute-start(bf16[256,2048]{1,0:T(8,128)(2,1)} %collective-permute-done.33), channel_id=1, source_target_pairs={{1,0},{5,4},{9,8},{13,12},{17,16},{21,20},{25,24},{29,28}} | collective-permute-start | bytes 3145736 | tf_op jit(solution)/shard_map/ppermute | solution.py:245
  1338.3 49.9 %collective-permute-start.36 = (bf16[256,2048]{1,0:T(8,128)(2,1)}, bf16[256,2048]{1,0:T(8,128)(2,1)S(1)}, u32[]{:S(2)}, u32[]{:S(2)}) collective-permute-start(bf16[256,2048]{1,0:T(8,128)(2,1)} %collective-permute-done.35), channel_id=1, source_target_pairs={{2,3},{6,7},{10,11},{14,15},{18,19},{22,23},{26,27},{30,31}} | collective-permute-start | bytes 3145736 | tf_op jit(solution)/shard_map/ppermute | solution.py:242
  1360.2 42.1 %collective-permute-start.77 = (bf16[256,2048]{1,0:T(8,128)(2,1)S(1)}, bf16[256,2048]{1,0:T(8,128)(2,1)S(1)}, u32[]{:S(2)}, u32[]{:S(2)}) collective-permute-start(bf16[256,2048]{1,0:T(8,128)(2,1)S(1)} %collective-permute-done.76), channel_id=1, source_target_pairs={{1,0},{5,4},{9,8},{13,12},{17,16},{21,20},{25,24},{29,28}} | collective-permute-start | bytes 3145736 | tf_op jit(solution)/shard_map/ppermute | solution.py:245
  1361.5 47.5 %collective-permute-start.79 = (bf16[256,2048]{1,0:T(8,128)(2,1)}, bf16[256,2048]{1,0:T(8,128)(2,1)}, u32[]{:S(2)}, u32[]{:S(2)}) collective-permute-start(bf16[256,2048]{1,0:T(8,128)(2,1)} %collective-permute-done.78), channel_id=1, source_target_pairs={{2,3},{6,7},{10,11},{14,15},{18,19},{22,23},{26,27},{30,31}} | collective-permute-start | bytes 3145736 | tf_op jit(solution)/shard_map/ppermute | solution.py:242
  (135 other events, 2071.5 us)
Sparse Core Ops, SparseCore 0:
  10.2 30.6 all-gather.8
  42.4 27.4 all-gather.12
  71.8 53.8 all-gather.10
  265.6 53.7 all-gather.14
  471.9 54.9 reduce-scatter.11
  530.5 59.0 reduce-scatter.9
  637.5 69.2 reduce-scatter.13
  971.5 41.2 reduce-scatter.5
  1049.0 72.4 reduce-scatter.7

commit v2 on v0

v2 whole, which is shorter than its diff:
```python
import jax
import jax.numpy as jnp
import numpy as np
from jax import lax
from jax.experimental import pallas as pl
from jax.experimental.pallas import tpu as pltpu
from jax.sharding import PartitionSpec as P

NT = (((1,), (1,)), ((), ()))
F32 = jnp.float32
BF16 = jnp.bfloat16
HD = 64
GROUP = 256
EPSILON = 1e-05
LIGHT = pl.CostEstimate(flops=1, bytes_accessed=1, transcendentals=0)


def turn(values, cos, sin):
    low = (lax.broadcasted_iota(jnp.int32, values.shape, 1) % HD) < HD // 2
    other = jnp.where(
        low, pltpu.roll(values, 128 - HD // 2, 1), pltpu.roll(values, HD // 2, 1)
    )
    return values * cos + other * sin


def project_kernel(
    tokens_ref, gain_ref, kv_weight, q_weight, cos_ref, sin_ref, kv_ref, q_ref, normed_ref
):
    inputs = tokens_ref[...].astype(F32)
    inverse = lax.rsqrt(jnp.mean(inputs * inputs, axis=-1, keepdims=True) + EPSILON)
    normed = (inputs * inverse * gain_ref[...]).astype(BF16)
    normed_ref[...] = normed
    cos, sin = cos_ref[...], sin_ref[...]
    pair = jnp.dot(normed, kv_weight[...], preferred_element_type=F32)
    is_key = lax.broadcasted_iota(jnp.int32, pair.shape, 1) < HD
    kv_ref[...] = jnp.where(is_key, turn(pair, cos, sin), pair).astype(BF16)
    raw = jnp.dot(normed, q_weight[...], preferred_element_type=F32)
    for first in range(0, q_ref.shape[1], 128):
        pair = raw[:, first : first + 128]
        q_ref[:, first : first + 128] = (turn(pair, cos, sin) * HD**-0.5).astype(BF16)


def project(tokens, gain, kv_weight, q_weight, cos, sin):
    rows, width = tokens.shape
    columns = q_weight.shape[1]
    block = 256
    return pl.pallas_call(
        project_kernel,
        grid=(rows // block,),
        in_specs=[
            pl.BlockSpec((block, width), lambda i: (i, 0)),
            pl.BlockSpec((1, width), lambda i: (0, 0)),
            pl.BlockSpec((width, 128), lambda i: (0, 0)),
            pl.BlockSpec((width, columns), lambda i: (0, 0)),
            pl.BlockSpec((block, 128), lambda i: (i, 0)),
            pl.BlockSpec((block, 128), lambda i: (i, 0)),
        ],
        out_specs=[
            pl.BlockSpec((block, 128), lambda i: (i, 0)),
            pl.BlockSpec((block, columns), lambda i: (i, 0)),
            pl.BlockSpec((block, width), lambda i: (i, 0)),
        ],
        out_shape=[
            jax.ShapeDtypeStruct((rows, 128), BF16),
            jax.ShapeDtypeStruct((rows, columns), BF16),
            jax.ShapeDtypeStruct((rows, width), BF16),
        ],
        compiler_params=pltpu.CompilerParams(vmem_limit_bytes=48 * 2**20),
        cost_estimate=LIGHT,
        name="project",
    )(tokens, gain.reshape(1, width), kv_weight, q_weight, cos, sin)


def fwd_kernel(offsets, meta, q_ref, ka_ref, kb_ref, vt_ref, o_ref, lse_ref):
    half = q_ref.shape[0] // 2
    span = 2 * half
    group = min(GROUP, half)
    pairs = q_ref.shape[1] // 128
    for part, offset in enumerate(offsets):
        at = slice(part * half, part * half + half)
        queries = [q_ref[at, p * 128 : p * 128 + 128] for p in range(pairs)]
        chains = [(p, keys_ref) for p in range(pairs) for keys_ref in (ka_ref, kb_ref)]
        seen = meta[part]
        own = pl.multiple_of(meta[2 + seen] * span, span)
        heads = []
        for p, keys_ref in chains:
            tops, sums = [], []
            for first in range(0, half, group):
                count = offset + first + group
                rows = pl.ds(own, count)
                scores = lax.dot_general(
                    keys_ref[rows, :],
                    queries[p][first : first + group],
                    NT,
                    preferred_element_type=F32,
                )
                key_at = lax.broadcasted_iota(jnp.int32, scores.shape, 0)
                row_at = lax.broadcasted_iota(jnp.int32, scores.shape, 1) + (offset + first)
                scores = jnp.where(key_at <= row_at, scores, -1e30)
                top = jnp.max(scores, axis=0, keepdims=True)
                weights = jnp.exp(scores - top).astype(BF16)
                tops.append(top)
                sums.append(jnp.dot(vt_ref[:, rows], weights, preferred_element_type=F32))
            heads += [jnp.concatenate(tops, axis=1), jnp.concatenate(sums, axis=1)]

        def step(index, carry):
            rows = pl.ds(pl.multiple_of(meta[2 + index] * span, span), span)
            out = []
            for chain, (p, keys_ref) in enumerate(chains):
                top, total = carry[2 * chain : 2 * chain + 2]
                scores = lax.dot_general(
                    keys_ref[rows, :], queries[p], NT, preferred_element_type=F32
                )
                new_top = jnp.maximum(top, jnp.max(scores, axis=0, keepdims=True))
                weights = jnp.exp(scores - new_top).astype(BF16)
                total = total * jnp.exp(top - new_top) + jnp.dot(
                    vt_ref[:, rows], weights, preferred_element_type=F32
                )
                out += [new_top, total]
            return tuple(out)

        heads = lax.fori_loop(0, seen, step, tuple(heads))
        for p in range(pairs):
            top0, total0, top1, total1 = heads[4 * p : 4 * p + 4]
            norm0, norm1 = total0[HD : HD + 1], total1[HD : HD + 1]
            o_ref[at, p * 128 : p * 128 + 128] = (
                jnp.concatenate([total0[:HD] / norm0, total1[:HD] / norm1], axis=0).T.astype(BF16)
            )
            lse_ref[p, :, at] = jnp.concatenate(
                [top0 + jnp.log(norm0), top1 + jnp.log(norm1), jnp.zeros((6, half), F32)], axis=0
            )


def spread(kv_refs, ka_ref, kb_ref, va_ref, vb_ref, kt_ref, vt_ref):
    at = 0
    for kv_ref in kv_refs:
        rows = kv_ref.shape[0]
        block = min(512, rows)
        for first in range(0, rows, block):
            here = slice(at + first, at + first + block)
            pair = kv_ref[first : first + block, :].astype(F32)
            other = pltpu.roll(pair, HD, 1)
            left = lax.broadcasted_iota(jnp.int32, pair.shape, 1) < HD
            ka_ref[here, :] = jnp.where(left, pair, 0.0).astype(BF16)
            vb_ref[here, :] = jnp.where(left, 0.0, pair).astype(BF16)
            va_ref[here, :] = jnp.where(left, other, 0.0).astype(BF16)
            kb_ref[here, :] = jnp.where(left, 0.0, other).astype(BF16)
            turned = pair.T
            kt_ref[:, here] = turned[:HD].astype(BF16)
            ones = jnp.where(lax.broadcasted_iota(jnp.int32, (16, block), 0) == 0, 1.0, 0.0)
            vt_ref[:, here] = jnp.concatenate([turned[HD:], ones], axis=0).astype(BF16)
        at += rows


def attend_first(meta, offsets, queries, kv_own, kv_other):
    rows, width = queries.shape
    pairs = width // 128
    together = 2 if pairs % 2 == 0 else 1
    length = 2 * kv_own.shape[0]

    def whole(shape):
        return pl.BlockSpec(shape, lambda p, m: (0, 0))

    def kernel(meta, q_ref, own, other, o_ref, lse_ref, ka, kb, va, vb, kt, vt):
        @pl.when(pl.program_id(0) == 0)
        def _():
            spread((own, other), ka, kb, va, vb, kt, vt)

        fwd_kernel(offsets, meta, q_ref, ka, kb, vt, o_ref, lse_ref)

    wide = (length, 128)
    forms = [wide, wide, wide, wide, (HD, length), (HD + 16, length)]
    return pl.pallas_call(
        kernel,
        grid_spec=pltpu.PrefetchScalarGridSpec(
            num_scalar_prefetch=1,
            grid=(pairs // together,),
            in_specs=[
                pl.BlockSpec((rows, 128 * together), lambda p, m: (0, p)),
                whole(kv_own.shape),
                whole(kv_other.shape),
            ],
            out_specs=[
                pl.BlockSpec((rows, 128 * together), lambda p, m: (0, p)),
                pl.BlockSpec((together, 8, rows), lambda p, m: (p, 0, 0)),
            ]
            + [whole(form) for form in forms],
        ),
        out_shape=[
            jax.ShapeDtypeStruct((rows, width), BF16),
            jax.ShapeDtypeStruct((pairs, 8, rows), F32),
        ]
        + [jax.ShapeDtypeStruct(form, BF16) for form in forms],
        compiler_params=pltpu.CompilerParams(vmem_limit_bytes=58 * 2**20),
        cost_estimate=LIGHT,
        name="attend_first",
    )(meta, queries, kv_own, kv_other)


def attend(meta, offsets, queries, keys_a, keys_b, values_t):
    rows, width = queries.shape
    pairs = width // 128
    together = 2 if pairs % 2 == 0 else 1
    length = keys_a.shape[0]
    whole = pl.BlockSpec((length, 128), lambda p, m: (0, 0))

    def kernel(*refs):
        fwd_kernel(offsets, *refs)

    return pl.pallas_call(
        kernel,
        grid_spec=pltpu.PrefetchScalarGridSpec(
            num_scalar_prefetch=1,
            grid=(pairs // together,),
            in_specs=[
                pl.BlockSpec((rows, 128 * together), lambda p, m: (0, p)),
                whole,
                whole,
                pl.BlockSpec(values_t.shape, lambda p, m: (0, 0)),
            ],
            out_specs=[
                pl.BlockSpec((rows, 128 * together), lambda p, m: (0, p)),
                pl.BlockSpec((together, 8, rows), lambda p, m: (p, 0, 0)),
            ],
        ),
        out_shape=[
            jax.ShapeDtypeStruct((rows, width), BF16),
            jax.ShapeDtypeStruct((pairs, 8, rows), F32),
        ],
        compiler_params=pltpu.CompilerParams(vmem_limit_bytes=58 * 2**20),
        cost_estimate=LIGHT,
        name="attend",
    )(meta, queries, keys_a, keys_b, values_t)


def bwd_kernel(
    offsets,
    meta,
    q_ref,
    o_ref,
    g_ref,
    lse_ref,
    ka_ref,
    kb_ref,
    va_ref,
    vb_ref,
    kt_ref,
    cos_ref,
    sin_ref,
    dq_ref,
    dk_ref,
    dv_ref,
):
    half = q_ref.shape[0] // 2
    span = 2 * half
    group = min(GROUP, half)

    for part, offset in enumerate(offsets):
        at = slice(part * half, part * half + half)
        queries, grads = q_ref[at, :], g_ref[at, :]
        left = lax.broadcasted_iota(jnp.int32, (half, 128), 1) < HD
        products = (grads.astype(F32) * o_ref[at, :].astype(F32)).T
        zero = jnp.zeros_like(queries)
        sides = []
        for side, (keys_ref, values_ref) in enumerate(((ka_ref, va_ref), (kb_ref, vb_ref))):
            mine = left if side == 0 else jnp.logical_not(left)
            delta = jnp.sum(products[side * HD : side * HD + HD], axis=0, keepdims=True)
            sides.append(
                (
                    keys_ref,
                    values_ref,
                    jnp.where(mine, queries, zero),
                    jnp.where(mine, grads, zero),
                    lse_ref[0, side : side + 1, at],
                    delta,
                )
            )

        def block(rows, first, count, masked):
            cut = slice(first, first + count)
            dqs = []
            dk_add = dv_add = None
            for keys_ref, values_ref, q_mine, g_mine, lse, delta in sides:
                scores = lax.dot_general(
                    keys_ref[rows, :], queries[cut], NT, preferred_element_type=F32
                )
                probs = jnp.exp(scores - lse[:, cut])
                if masked:
                    key_at = lax.broadcasted_iota(jnp.int32, scores.shape, 0)
                    row_at = lax.broadcasted_iota(jnp.int32, scores.shape, 1) + (offset + first)
                    probs = jnp.where(key_at <= row_at, probs, 0.0)
                grad_probs = lax.dot_general(
                    values_ref[rows, :], grads[cut], NT, preferred_element_type=F32
                )
                grad_scores = (probs * (grad_probs - delta[:, cut])).astype(BF16)
                dv_new = jnp.dot(probs.astype(BF16), g_mine[cut], preferred_element_type=F32)
                dk_new = jnp.dot(grad_scores, q_mine[cut], preferred_element_type=F32)
                dv_add = dv_new if dv_add is None else dv_add + dv_new
                dk_add = dk_new if dk_add is None else dk_add + dk_new
                dqs.append(jnp.dot(kt_ref[:, rows], grad_scores, preferred_element_type=F32))
            dv_ref[rows, :] += dv_add
            dk_ref[rows, :] += dk_add
            return jnp.concatenate(dqs, axis=0)

        own = pl.multiple_of(meta[2 + meta[part]] * span, span)
        start = jnp.concatenate(
            [
                block(pl.ds(own, offset + first + group), first, group, True)
                for first in range(0, half, group)
            ],
            axis=1,
        )

        def step(index, total):
            rows = pl.ds(pl.multiple_of(meta[2 + index] * span, span), span)
            return total + block(rows, 0, half, False)

        dq = lax.fori_loop(0, meta[part], step, start).T * (HD**-0.5)
        dq_ref[at, :] = turn(dq, cos_ref[at, :], -sin_ref[at, :]).astype(BF16)


def back_specs(queries, forms):
    rows, width = queries.shape
    pair = pl.BlockSpec((rows, 128), lambda p, m: (0, p))
    table = pl.BlockSpec((rows, 128), lambda p, m: (0, 0))
    specs = [pair, pair, pair, pl.BlockSpec((1, 8, rows), lambda p, m: (p, 0, 0))]
    specs += [pl.BlockSpec(form.shape, lambda p, m: (0, 0)) for form in forms]
    return pair, specs + [table, table]


def attend_back_first(meta, offsets, queries, outputs, grads, lse, forms, cos, sin):
    length = forms[0].shape[0]
    pair, specs = back_specs(queries, forms)
    whole = pl.BlockSpec((length, 128), lambda p, m: (0, 0))

    def kernel(*refs):
        dk_ref, dv_ref = refs[-2:]

        @pl.when(pl.program_id(0) == 0)
        def _():
            dk_ref[...] = jnp.zeros(dk_ref.shape, F32)
            dv_ref[...] = jnp.zeros(dv_ref.shape, F32)

        bwd_kernel(offsets, *refs)

    return pl.pallas_call(
        kernel,
        grid_spec=pltpu.PrefetchScalarGridSpec(
            num_scalar_prefetch=1,
            grid=(queries.shape[1] // 128,),
            in_specs=specs,
            out_specs=[pair, whole, whole],
        ),
        out_shape=[
            jax.ShapeDtypeStruct(queries.shape, BF16),
            jax.ShapeDtypeStruct((length, 128), F32),
            jax.ShapeDtypeStruct((length, 128), F32),
        ],
        compiler_params=pltpu.CompilerParams(vmem_limit_bytes=58 * 2**20),
        cost_estimate=LIGHT,
        name="attend_back_first",
    )(meta, queries, outputs, grads, lse, *forms, cos, sin)


def attend_back_last(
    meta, offsets, queries, outputs, grads, lse, forms, cos, sin, dk, dv, all_cos, all_sin
):
    length = forms[0].shape[0]
    near = length // 2
    pair, specs = back_specs(queries, forms)
    whole = pl.BlockSpec((length, 128), lambda p, m: (0, 0))
    half = pl.BlockSpec((near, 128), lambda p, m: (0, 0))

    def kernel(*refs):
        dk_in, dv_in, cos_ref, sin_ref, dq_ref, near_ref, far_ref, dk_ref, dv_ref = refs[-9:]

        @pl.when(pl.program_id(0) == 0)
        def _():
            dk_ref[...] = dk_in[...]
            dv_ref[...] = dv_in[...]

        bwd_kernel(offsets, *refs[:-9], dq_ref, dk_ref, dv_ref)

        @pl.when(pl.program_id(0) == pl.num_programs(0) - 1)
        def _():
            block = min(512, near)
            for first in range(0, length, block):
                here = slice(first, first + block)
                dk_block, dv_block = dk_ref[here, :], dv_ref[here, :]
                dk_block = dk_block + pltpu.roll(dk_block, HD, 1)
                dv_block = dv_block + pltpu.roll(dv_block, HD, 1)
                left = lax.broadcasted_iota(jnp.int32, dk_block.shape, 1) < HD
                both = jnp.where(
                    left, turn(dk_block, cos_ref[here, :], -sin_ref[here, :]), dv_block
                )
                if first < near:
                    near_ref[here, :] = both
                else:
                    far_ref[first - near : first - near + block, :] = both.astype(BF16)

    return pl.pallas_call(
        kernel,
        grid_spec=pltpu.PrefetchScalarGridSpec(
            num_scalar_prefetch=1,
            grid=(queries.shape[1] // 128,),
            in_specs=specs + [whole] * 4,
            out_specs=[pair, half, half],
            scratch_shapes=[pltpu.VMEM((length, 128), F32), pltpu.VMEM((length, 128), F32)],
        ),
        out_shape=[
            jax.ShapeDtypeStruct(queries.shape, BF16),
            jax.ShapeDtypeStruct((near, 128), F32),
            jax.ShapeDtypeStruct((near, 128), BF16),
        ],
        compiler_params=pltpu.CompilerParams(vmem_limit_bytes=60 * 2**20),
        cost_estimate=LIGHT,
        name="attend_back_last",
    )(meta, queries, outputs, grads, lse, *forms, cos, sin, dk, dv, all_cos, all_sin)


def feed_kernel(
    gathered_ref,
    tokens_ref,
    cotangent_ref,
    gain_ref,
    output_weight,
    gate_weight,
    up_weight,
    down_weight,
    *refs,
):
    middle_ref, normed_ref, hidden_ref, gates_ref, down_ref, grad_ref = refs[-6:]
    middle = tokens_ref[...].astype(F32)
    for source in range(gathered_ref.shape[0]):
        middle = middle + lax.dot_general(
            gathered_ref[source], output_weight[source], NT, preferred_element_type=F32
        )
    middle_ref[...] = middle
    inverse = lax.rsqrt(jnp.mean(middle * middle, axis=-1, keepdims=True) + EPSILON)
    normed = (middle * inverse * gain_ref[...]).astype(BF16)
    normed_ref[...] = normed
    gate = jnp.dot(normed, gate_weight[...], preferred_element_type=F32)
    up = jnp.dot(normed, up_weight[...], preferred_element_type=F32)
    grad_hidden = jnp.dot(cotangent_ref[...], down_weight[...], preferred_element_type=F32)
    sigmoid = jax.nn.sigmoid(gate)
    hidden = (gate * sigmoid * up).astype(BF16)
    hidden_ref[...] = hidden
    grad_gate = (grad_hidden * up * sigmoid * (1.0 + gate * (1.0 - sigmoid))).astype(BF16)
    grad_up = (grad_hidden * gate * sigmoid).astype(BF16)
    units = hidden.shape[1]
    gates_ref[:, :units] = grad_gate
    gates_ref[:, units:] = grad_up
    down_ref[...] = lax.dot_general(
        hidden, down_weight[...], NT, preferred_element_type=F32
    ).astype(BF16)
    grad_ref[...] = (
        lax.dot_general(grad_gate, gate_weight[...], NT, preferred_element_type=F32)
        + lax.dot_general(grad_up, up_weight[...], NT, preferred_element_type=F32)
    ).astype(BF16)


def feed_forward(c, gathered, tokens, cotangent, gain, output_weight, weights, earlier):
    rows, width = tokens.shape
    units = weights[0].shape[1]
    block = min(256, rows // 4)
    quarter = rows // 4 // block
    if c:
        place = lambda i: (i + quarter, 0)
    else:
        place = lambda i: (jnp.where(i < quarter, i, i + 2 * quarter), 0)
    once = pl.Buffered(1)

    def natural(columns):
        return pl.BlockSpec((block, columns), place)

    def whole(array):
        zeros = (0,) * array.ndim
        return pl.BlockSpec(array.shape, lambda i: zeros, pipeline_mode=once)

    shapes = [
        jax.ShapeDtypeStruct((rows, width), F32),
        jax.ShapeDtypeStruct((rows, width), BF16),
        jax.ShapeDtypeStruct((rows, units), BF16),
        jax.ShapeDtypeStruct((rows, 2 * units), BF16),
        jax.ShapeDtypeStruct((rows, width), BF16),
    ]
    gain = gain.reshape(1, width)
    return pl.pallas_call(
        feed_kernel,
        grid=(2 * quarter,),
        in_specs=[
            pl.BlockSpec((gathered.shape[0], block, gathered.shape[2]), lambda i: (0, i, 0)),
            natural(width),
            natural(width),
            whole(gain),
            whole(output_weight),
        ]
        + [whole(weight) for weight in weights]
        + [pl.BlockSpec(memory_space=pl.ANY) for _ in earlier],
        out_specs=[natural(shape.shape[1]) for shape in shapes]
        + [pl.BlockSpec((block, width), lambda i: (i, 0))],
        out_shape=shapes + [jax.ShapeDtypeStruct((rows // 2, width), BF16)],
        input_output_aliases={8 + k: k for k in range(len(earlier))},
        compiler_params=pltpu.CompilerParams(vmem_limit_bytes=60 * 2**20),
        cost_estimate=LIGHT,
        name="feed_forward",
    )(gathered, tokens, cotangent, gain, output_weight, *weights, *earlier)


def quarter_row(row, c, half, span):
    if c:
        return half + row
    return row if row < half else row + span


def after(value, *earlier):
    return lax.optimization_barrier((value, earlier))[0]


def line_steps(size):
    return [
        (
            [(i, i + 1) for i in range(step - 1, size - 1)],
            [(i, i - 1) for i in range(1, size - step + 1)],
        )
        for step in range(1, size)
    ]


class Gather:
    def __init__(self, piece):
        self.piece = piece
        self.rights, self.lefts = [piece], [piece]
        self.hops = line_steps(lax.axis_size("tensor"))

    def step(self):
        done = len(self.rights) - 1
        if done < len(self.hops):
            to_right, to_left = self.hops[done]
            self.rights.append(lax.ppermute(self.rights[-1], "tensor", to_right))
            self.lefts.append(lax.ppermute(self.lefts[-1], "tensor", to_left))
        return self.rights[-1], self.lefts[-1]

    def held(self, pair):
        self.rights[-1], self.lefts[-1] = pair

    def collect(self, place, target):
        size = lax.axis_size("tensor")
        me = lax.axis_index("tensor")
        while len(self.rights) <= len(self.hops):
            self.step()
        target = place(target, self.piece, me)
        for step in range(1, size):
            arrived = self.rights[step] + self.lefts[size - step]
            target = place(target, arrived, lax.rem(me - step + size, size))
        return target


def send_blocks(pick, across=False):
    size = lax.axis_size("tensor")
    me = lax.axis_index("tensor")
    arrived = []
    for shift in range(size):
        block = pick(lax.rem(me + shift, size))
        if across:
            block = lax.ppermute(
                block,
                ("ctx", "tensor"),
                [
                    (c * size + i, (1 - c) * size + (i + shift) % size)
                    for c in range(2)
                    for i in range(size)
                ],
            )
        elif shift:
            block = lax.ppermute(block, "tensor", [(i, (i + shift) % size) for i in range(size)])
        arrived.append(block)
    return tuple(arrived)


def stack_blocks(arrived):
    size = len(arrived)
    me = lax.axis_index("tensor")
    out = jnp.zeros((size, *arrived[0].shape), arrived[0].dtype)
    for shift, block in enumerate(arrived):
        out = lax.dynamic_update_index_in_dim(out, block, lax.rem(me - shift + size, size), 0)
    return out


def pairwise(value, axis, step):
    size = lax.axis_size(axis)
    return value + lax.ppermute(value, axis, [(i, i ^ step) for i in range(size)])


def pair_steps():
    steps = []
    for axis in ("dp", "ctx", "tensor"):
        step = 1
        while step < lax.axis_size(axis):
            steps.append((axis, step))
            step *= 2
    return steps


def hold(*values):
    return lax.optimization_barrier(values)


def in_order(mine, other, upper):
    return jnp.concatenate(
        [jnp.where(upper == 0, mine, other), jnp.where(upper == 0, other, mine)], axis=1
    )


def rows_part(weight, index, count):
    rows = weight.shape[0] // count
    return lax.dynamic_slice_in_dim(weight, index * rows, rows, 0)


def by_source(target, piece, source):
    return lax.dynamic_update_index_in_dim(target, piece, source, 0)


def dot(a, b):
    return jnp.dot(a, b, preferred_element_type=F32)


def dot_t(a, b):
    return jnp.einsum("rf,df->rd", a, b, preferred_element_type=F32)


def t_dot(a, b):
    return jnp.einsum("rd,rf->df", a, b, preferred_element_type=F32)


def body(
    tokens,
    cotangent,
    span_order,
    norm_attn,
    w_query,
    w_key,
    w_value,
    w_output,
    norm_mlp,
    w_gate,
    w_up,
    w_down,
):
    tok_rows, width = tokens.shape
    groups = lax.axis_size("tensor")
    member = lax.axis_index("tensor")
    n_ctx = lax.axis_size("ctx")
    assert n_ctx == 2
    ctx_index = lax.axis_index("ctx")
    features = w_query.shape[1]
    kv_count = w_key.shape[1] // HD
    kv_pick = np.arange(groups) * kv_count // groups
    kv_start = member * kv_count // groups * HD
    key_weight = lax.dynamic_slice_in_dim(w_key, kv_start, HD, 1)
    value_weight = lax.dynamic_slice_in_dim(w_value, kv_start, HD, 1)
    span = tok_rows // 2
    half = span // 2
    share = span // groups
    over = [(0, 1), (1, 0)]
    chunks = range(2)

    def chunk(array, c):
        if c:
            return array[half : half + span]
        return jnp.concatenate([array[:half], array[half + span :]], axis=0)

    def natural(first, second):
        return jnp.concatenate([first[:half], second, first[half:]], axis=0)

    order = jnp.roll(span_order[0], -2 * ctx_index)
    places = jnp.arange(4, dtype=jnp.int32)
    slot_of = jnp.sum(
        jnp.where(order[None, :] == places[:, None], places[None, :], 0), axis=1, dtype=jnp.int32
    )
    metas = [jnp.concatenate([order[2 * c : 2 * c + 2], slot_of]) for c in chunks]
    offsets = [(0, half), (half, 0)]

    positions = (order[:, None] * span + jnp.arange(span, dtype=jnp.int32)[None, :]).reshape(-1)
    frequency = 10000.0 ** (-jnp.arange(HD // 2, dtype=F32) / (HD // 2))

    def table(positions):
        angles = frequency[:, None] * positions.astype(F32)[None, :]
        cos_part, sin_part = hold(jnp.cos(angles), jnp.sin(angles))
        cos_part, sin_part = cos_part.T, sin_part.T
        return (
            jnp.concatenate([cos_part] * 4, axis=1),
            jnp.concatenate([-sin_part, sin_part] * 2, axis=1),
        )

    cos_near, sin_near = table(positions[:tok_rows])

    upper = lax.axis_index("dp") % 2
    half_output = lax.all_gather(rows_part(w_output, upper, 2), "tensor", axis=0, tiled=False)
    beside = [(i, i ^ 1) for i in range(lax.axis_size("dp"))]

    kv_own, queries, normed = project(
        tokens,
        norm_attn,
        jnp.concatenate([key_weight, value_weight], axis=1),
        w_query,
        cos_near,
        sin_near,
    )
    kv_other = lax.ppermute(kv_own, "ctx", over)
    kv_own, kv_other, sent, kept, normed = hold(
        kv_own, kv_other, chunk(queries, 1), chunk(queries, 0), normed
    )
    length = 2 * tok_rows

    foreign = lax.ppermute(sent, "ctx", over)
    first, first_log, *forms = attend_first(metas[0], offsets[0], kept, kv_own, kv_other)
    first, first_log, foreign, forms = hold(first, first_log, foreign, forms)
    *forms, values_t = forms
    first_whole = lax.all_gather(first, "tensor", axis=0, tiled=False)

    other_output = lax.ppermute(half_output, "dp", beside)
    second, second_log = attend(metas[1], offsets[1], foreign, forms[0], forms[1], values_t)
    second, second_log, other_output, half_output = hold(
        second, second_log, other_output, half_output
    )
    output_whole = in_order(half_output, other_output, upper)

    cos_far, sin_far = table(after(positions[tok_rows:], second))
    cos_pair = jnp.concatenate([cos_near, cos_far], axis=0)
    sin_pair = jnp.concatenate([sin_near, sin_far], axis=0)
    tables = [(chunk(cos_near, 0), chunk(sin_near, 0)), (chunk(cos_far, 1), chunk(sin_far, 1))]
    second_home = lax.ppermute(second, "ctx", over)
    second_home, first_whole, output_whole, tables, cos_pair, sin_pair = hold(
        second_home, first_whole, output_whole, tables, cos_pair, sin_pair
    )
    second_whole = lax.all_gather(second_home, "tensor", axis=0, tiled=False)
    queries = [kept, foreign]
    attention = [first, second]
    log_totals = [first_log, second_log]

    row_of = [
        jnp.asarray([quarter_row(i * share, c, half, span) for i in range(groups)], jnp.int32)
        for c in chunks
    ]

    def own_rows(array, c):
        return lax.dynamic_slice_in_dim(array, row_of[c][member], share, 0)

    def to_attention(c, middle, grad_share):
        middle = own_rows(middle, c)
        inverse_two = lax.rsqrt(jnp.mean(middle * middle, axis=-1, keepdims=True) + EPSILON)
        grad_normed_mlp = grad_share.astype(F32)
        gain = jnp.sum(grad_normed_mlp * middle * inverse_two, axis=0)
        scaled_two = grad_normed_mlp * norm_mlp
        grad_middle = (
            own_rows(cotangent, c).astype(F32)
            + inverse_two * scaled_two
            - middle * inverse_two**3 * jnp.mean(scaled_two * middle, axis=-1, keepdims=True)
        )
        grad_low = grad_middle.astype(BF16)
        blocks = jnp.einsum(
            "rd,tdq->trq", grad_low, output_whole, preferred_element_type=F32
        ).astype(BF16)
        return gain, grad_middle, grad_low, blocks

    def block_of(blocks):
        return lambda j: lax.dynamic_index_in_dim(blocks, j, 0, keepdims=False)

    def rows_of(array):
        return lambda j: lax.dynamic_slice_in_dim(array, j * share, share, 0)

    def line_sum(array):
        return lax.psum_scatter(array, "tensor", scatter_dimension=0, tiled=True)

    def plane_sum(gradient):
        return lax.psum_scatter(
            gradient.astype(BF16), ("dp", "ctx"), scatter_dimension=0, tiled=True
        )

    query_gather = Gather(after(rows_part(w_query, 2 * upper + ctx_index, 4), first_whole))
    hop = query_gather.step()
    weights = (w_gate, w_up, w_down)
    fixed = (tokens, cotangent, norm_mlp, output_whole, weights)
    *fed, grad_first = feed_forward(0, first_whole, *fixed, ())
    fed, grad_first, second_whole, hop = hold(fed, grad_first, second_whole, hop)
    query_gather.held(hop)

    share_first = line_sum(grad_first)
    hop = query_gather.step()
    *fed, grad_second = feed_forward(1, second_whole, *fixed, fed)
    fed, grad_second, hop = hold(fed, grad_second, hop)
    query_gather.held(hop)
    middle, normed_mlp, hidden, gates, mlp_part = fed

    share_second = line_sum(grad_second)
    hop = query_gather.step()
    w_gates = t_dot(normed_mlp, gates).astype(BF16)
    w_gates, hop = hold(w_gates, hop)
    query_gather.held(hop)
    mlp_share = line_sum(after(mlp_part, w_gates))

    query_part = query_gather.collect(
        by_source, jnp.zeros((groups, w_query.shape[0] // 4, features), BF16)
    )
    part_over = lax.ppermute(query_part, "ctx", over)
    w_downs = t_dot(after(cotangent, w_gates), hidden).astype(BF16)
    w_downs, share_first, query_part, part_over = hold(
        w_downs, share_first, query_part, part_over
    )

    gain_first, middle_first, low_first, blocks = to_attention(0, middle, share_first)
    query_half = in_order(query_part, part_over, ctx_index)
    gain_first, middle_first, low_first, blocks, query_half = hold(
        gain_first, middle_first, low_first, blocks, query_half
    )

    came_first = send_blocks(block_of(blocks))
    other_half = lax.ppermute(query_half, "dp", beside)
    attention_rows = jnp.concatenate(
        [
            lax.dynamic_slice_in_dim(whole, member * share, share, 1)
            for whole in (first_whole, second_whole)
        ],
        axis=1,
    )
    attention_rows = jnp.swapaxes(attention_rows, 0, 1).reshape(2 * share, groups * features)
    n_part = tok_rows // groups
    middle_own = lax.dynamic_slice_in_dim(middle, member * n_part, n_part, 0)
    came_first, attention_rows, middle_own, query_half, other_half = hold(
        came_first, attention_rows, middle_own, query_half, other_half
    )
    query_whole = in_order(query_half, other_half, upper)
    grads_first = stack_blocks(came_first).reshape(span, features)
    query_whole, grads_first, share_second = hold(query_whole, grads_first, share_second)

    gain_second, middle_second, low_second, blocks = to_attention(1, middle, share_second)
    gain_second, middle_second, low_second, blocks = hold(
        gain_second, middle_second, low_second, blocks
    )

    def back_arguments(c, grads):
        return metas[c], offsets[c], queries[c], attention[c], grads, log_totals[c], forms, *tables[c]

    came_second = send_blocks(block_of(blocks), across=True)
    dq_first, dk, dv = attend_back_first(*back_arguments(0, grads_first))
    dq_first, dk, dv, came_second = hold(dq_first, dk, dv, came_second)

    rows_first = send_blocks(rows_of(dq_first))
    grads_second = stack_blocks(came_second).reshape(span, features)
    dq_second, kv_near, kv_far = attend_back_last(
        *back_arguments(1, grads_second), dk, dv, cos_pair, sin_pair
    )
    dq_second, kv_near, kv_far, rows_first, mlp_share = hold(
        dq_second, kv_near, kv_far, rows_first, mlp_share
    )
    gate_up_grad = plane_sum(after(w_gates, mlp_share))

    kv_sent = lax.ppermute(kv_far, "ctx", over)
    rows_second = send_blocks(rows_of(dq_second), across=True)
    dq_home = lax.ppermute(dq_second, "ctx", over)
    first_part = jnp.einsum(
        "trq,tdq->rd", stack_blocks(rows_first), query_whole, preferred_element_type=F32
    )
    kv_near, kv_sent, rows_second, first_part, dq_home = hold(
        kv_near, kv_sent, rows_second, first_part, dq_home
    )
    mixed_gather = Gather((middle_own + mlp_share.astype(F32)).astype(BF16))
    mixed_hop = mixed_gather.step()
    grad_kv_raw = (kv_near + kv_sent.astype(F32)).astype(BF16)
    kv_rows = send_blocks(
        lambda j: jnp.concatenate(
            [lax.dynamic_slice_in_dim(grad_kv_raw, row_of[c][j], share, 0) for c in chunks], axis=0
        )
    )
    second_part = jnp.einsum(
        "trq,tdq->rd", stack_blocks(rows_second), query_whole, preferred_element_type=F32
    )
    first_part, second_part, kv_rows, grad_kv_raw = hold(
        first_part, second_part, kv_rows, grad_kv_raw
    )
    kv_whole = jnp.stack(
        [
            jnp.concatenate(
                [w_key[:, h * HD : (h + 1) * HD], w_value[:, h * HD : (h + 1) * HD]], axis=1
            )
            for h in kv_pick
        ]
    )

    grad_normed = jnp.concatenate([first_part, second_part], axis=0) + jnp.einsum(
        "trq,tdq->rd", stack_blocks(kv_rows), kv_whole, preferred_element_type=F32
    )
    inputs_own = jnp.concatenate([own_rows(tokens, c) for c in chunks], axis=0).astype(F32)
    inverse_own = lax.rsqrt(jnp.mean(inputs_own * inputs_own, axis=-1, keepdims=True) + EPSILON)
    attn_gain = jnp.sum(grad_normed * inputs_own * inverse_own, axis=0)
    scaled_one = grad_normed * norm_attn
    grad_inputs = (
        jnp.concatenate([middle_first, middle_second], axis=0)
        + inverse_own * scaled_one
        - inputs_own * inverse_own**3 * jnp.mean(scaled_one * inputs_own, axis=-1, keepdims=True)
    ).astype(BF16)

    def put_rows(target, piece, source):
        for c in chunks:
            target = lax.dynamic_update_slice_in_dim(
                target, piece[c * share : (c + 1) * share], row_of[c][source], 0
            )
        return target

    gains = jnp.stack([attn_gain, gain_first + gain_second])
    grad_inputs, gains, low_first = hold(grad_inputs, gains, low_first)

    tokens_gather = Gather(grad_inputs)
    hop = tokens_gather.step()
    w_outs = t_dot(jnp.concatenate([low_first, low_second], axis=0), attention_rows).astype(BF16)
    query_kv = t_dot(
        normed, jnp.concatenate([natural(dq_first, dq_home), grad_kv_raw], axis=1)
    ).astype(BF16)
    rest = jnp.concatenate([w_downs, w_outs, query_kv], axis=1)
    hop, mixed_hop, rest, gate_up_grad = hold(hop, mixed_hop, rest, gate_up_grad)
    tokens_gather.held(hop)
    mixed_gather.held(mixed_hop)
    rest = plane_sum(rest)

    steps = pair_steps()
    hop, mixed_hop = tokens_gather.step(), mixed_gather.step()
    for axis, step in steps[:2]:
        gains = pairwise(gains, axis, step)
    hop, mixed_hop, gains = hold(hop, mixed_hop, gains)
    tokens_gather.held(hop)
    mixed_gather.held(mixed_hop)

    hop, mixed_hop = tokens_gather.step(), mixed_gather.step()
    for axis, step in steps[2:]:
        gains = pairwise(gains, axis, step)
    hop, mixed_hop, gains, rest = hold(hop, mixed_hop, gains, rest)
    tokens_gather.held(hop)
    mixed_gather.held(mixed_hop)

    tokens_grad = tokens_gather.collect(put_rows, jnp.zeros((tok_rows, width), BF16))
    hidden_units = w_down.shape[1]
    down_grad = rest[:, :hidden_units]
    rest = rest[:, hidden_units:]
    output_plane, query_kv = rest[:, : groups * features], rest[:, groups * features :]
    query_grad, kv_plane = query_kv[:, :features].astype(F32), query_kv[:, features:]
    output_rows = send_blocks(
        lambda j: lax.dynamic_slice_in_dim(output_plane, j * features, features, 1)
    )
    kv_share = query_kv.shape[0] // groups
    kv_blocks = send_blocks(
        lambda j: lax.dynamic_slice_in_dim(kv_plane, j * kv_share, kv_share, 0)
    )
    mixed = mixed_gather.collect(
        lambda target, piece, source: lax.dynamic_update_slice_in_dim(
            target, piece, source * n_part, 0
        ),
        jnp.zeros((tok_rows, width), BF16),
    )
    output_grad = jnp.sum(stack_blocks(output_rows).astype(F32), axis=0)

    kv_blocks = stack_blocks(kv_blocks).astype(F32)
    key_heads, value_heads = [], []
    for h in range(kv_count):
        total = jnp.zeros((kv_share, 2 * HD), F32)
        for g in range(groups):
            if kv_pick[g] == h:
                total = total + kv_blocks[g]
        key_heads.append(total[:, :HD])
        value_heads.append(total[:, HD:])
    key_grad = jnp.concatenate(key_heads, axis=1)
    value_grad = jnp.concatenate(value_heads, axis=1)

    plane = lax.axis_size("dp") * n_ctx
    plane_index = lax.axis_index("dp") * n_ctx + ctx_index
    gains = lax.dynamic_slice_in_dim(gains, plane_index * (width // plane), width // plane, 1)
    return (
        mixed,
        tokens_grad,
        gains[0],
        query_grad,
        key_grad,
        value_grad,
        output_grad,
        gains[1],
        gate_up_grad[:, :hidden_units].astype(F32),
        gate_up_grad[:, hidden_units:].astype(F32),
        down_grad.astype(F32),
    )


def solution(mesh):
    placed = (
        P(("dp", "ctx"), None),
        P(("dp", "ctx"), None),
        P("dp", None),
        P(),
        P(None, "tensor"),
        P(),
        P(),
        P(None, "tensor"),
        P(),
        P(None, "tensor"),
        P(None, "tensor"),
        P(None, "tensor"),
    )
    return jax.shard_map(
        body,
        mesh=mesh,
        in_specs=placed,
        out_specs=(
            P(("dp", "ctx"), None),
            P(("dp", "ctx"), None),
            P(("dp", "ctx")),
            P(("dp", "ctx"), "tensor"),
            P(("dp", "ctx", "tensor"), None),
            P(("dp", "ctx", "tensor"), None),
            P(("dp", "ctx"), "tensor"),
            P(("dp", "ctx")),
            P(("dp", "ctx"), "tensor"),
            P(("dp", "ctx"), "tensor"),
            P(("dp", "ctx"), "tensor"),
        ),
        check_vma=False,
    )
```

time: 3400 us -> 1230 us (0.36)
  waiting for transfers between devices: 1760 us -> 443 us
  matrix products: 989 us -> 83.2 us
  Pallas kernels: 0 us -> 340 us
  other arithmetic: 441 us -> 127 us
  starting transfers between devices: 1.18 us -> 113 us
  local copies, waits for them, and re-layouts: 170 us -> 82.8 us
    psum x3 -> x0, waiting for transfers between devices: 1420 us -> none  [the longest x1 565 us: body(): lax.psum(mlp_part.astype(jnp.bfloat16), 'tensor').astype(jnp.float32)]
    dot_general x49 -> x9, matrix products: 989 us -> 83.2 us  [the longest x4 63 us: t_dot(): return jnp.einsum('rd,rf->df', a, b, preferred_element_type=F32)]
    ppermute x0 -> x54, waiting for transfers between devices: none -> 346 us  [the longest x9 88.1 us: step(): self.lefts.append(lax.ppermute(self.lefts[-1], 'tensor', to_left))]
    pallas_call x0 -> x7, Pallas kernels: none -> 340 us  [the longest x2 125 us: feed_forward(): pl.pallas_call(feed_kernel, grid=(2 * quarter,), in_specs=[pl.BlockSpec((...]
    reduce_scatter x8 -> x5, waiting for transfers between devices: 336 us -> 0.03 us  [the longest x2 0.02 us: plane_sum(): lax.psum_scatter(gradient.astype(BF16), ('dp', 'ctx'), scatter_dimension=...]
    convert_element_type x13 -> x9, other arithmetic: 258 us -> 16.3 us  [the longest x2 8.12 us: to_attention(): grad_low = grad_middle.astype(BF16)]
    reduce_sum x8 -> x6, other arithmetic: 126 us -> 11.1 us  [the longest x2 5.38 us: to_attention(): jnp.mean(scaled_two * middle, axis=-1, keepdims=True)]
    ppermute x0 -> x54, starting transfers between devices: none -> 112 us  [the longest x8 35.4 us: send_blocks(): lax.ppermute(block, ('ctx', 'tensor'), [(c * size + i, (1 - c) * size + (...]
  transfers between devices with their start and end apart: 12 -> 62, of which waited for: 9 -> 17; matrix products, arithmetic and copies ran while one was open for 7% -> 22% of each run, Pallas kernels for 0% -> 28%
where the time goes in v2:
time: 1230 us; the launch traced here: 1220 us
  waiting for transfers between devices  443 us (36%)
  Pallas kernels  340 us (28%)
  other arithmetic  127 us (10%)
  starting transfers between devices  113 us (9%)
  matrix products  83.2 us (7%)
  local copies, waits for them, and re-layouts  82.8 us (7%)
  between operations  35.1 us (3%)
    pallas_call x2, Pallas kernels, feed_forward(): pl.pallas_call(feed_kernel, grid=(2 * quarter,), in_specs=[pl.BlockSpec((...  125 us
    ppermute x9, waiting for transfers between devices, step(): self.lefts.append(lax.ppermute(self.lefts[-1], 'tensor', to_left))  88.1 us
    ppermute x5, waiting for transfers between devices, pairwise(): lax.ppermute(value, axis, [(i, i ^ step) for i in range(size)])  80.9 us
    ppermute x15, waiting for transfers between devices, send_blocks(): lax.ppermute(block, 'tensor', [(i, (i + shift) % size) for i in range(siz...  68.1 us
    pallas_call x1, Pallas kernels, attend_back_first(): pl.pallas_call(kernel, grid_spec=pltpu.PrefetchScalarGridSpec(num_scalar_...  66.9 us
    dot_general x4, matrix products, t_dot(): return jnp.einsum('rd,rf->df', a, b, preferred_element_type=F32)  63 us
    ppermute x8, waiting for transfers between devices, send_blocks(): lax.ppermute(block, ('ctx', 'tensor'), [(c * size + i, (1 - c) * size + (...  54.8 us
    all_gather x1, waiting for transfers between devices, body(): lax.all_gather(rows_part(w_output, upper, 2), 'tensor', axis=0, tiled=False)  51.9 us
  transfers between devices with their start and end apart: 62, of which 17 were waited for; matrix products, arithmetic and copies ran while one was open for 22% of the time, Pallas kernels for 28%

profile of v2, /device:TPU:0, one launch (start us, length us, event | category | flops | bytes accessed | tf_op | source)
XLA Modules:
  0.0 1224.3 jit_solution(6619617528016622882)
XLA Ops:
  11.0 5.4 multiply_sine_fusion.1
  16.4 2.9 fusion.52
  22.3 15.2 %project.1 = (bf16[2048,128]{1,0:T(8,128)(2,1)S(1)}, bf16[2048,512]{1,0:T(8,128)(2,1)S(1)}, bf16[2048,2048]{1,0:T(8,128)(2,1)}) custom-call(bf16[2048,2048]{1,0:T(8,128)(2,1)} %tokens_ref.5, f32[1,2048]{1,0:T(1,128)S(1)} %bitcast.152, bf16[2048,128]{1,0:T(8,128)(2,1)S(1)} %pad_maximum_fusion.14.kv_weight, bf16[2048,512]{1,0:T(8,128)(2,1)} %q_weight.1, ...), custom_call_target="tpu_custom_call" | custom-call | flops 1 | bytes 1 | tf_op jit(solution)/shard_map/project/pallas_call | solution.py:47
  38.9 2.9 collective-permute-start
  41.8 51.9 %all-gather.7.cloned.1.call-done = bf16[4096,512]{1,0:T(8,128)(2,1)} async-done(((bf16[1024,512]{1,0:T(8,128)(2,1)}), bf16[4096,512]{1,0:T(8,128)(2,1)}) %all-gather.7.cloned.1.call-update) | async-done | bytes 4194320 | tf_op jit(solution)/shard_map/all_gather | solution.py:699
  99.6 51.5 %attend_first.1 = (bf16[1024,512]{1,0:T(8,128)(2,1)}, f32[4,8,1024]{2,1,0:T(8,128)}, bf16[4096,128]{1,0:T(8,128)(2,1)}, bf16[4096,128]{1,0:T(8,128)(2,1)}, bf16[...) custom-call(s32[6]{0:T(128)} %get-tuple-element.478.meta.refs_0_, ...), custom_call_target="tpu_custom_call" | custom-call | flops 1 | bytes 1 | tf_op jit(solution)/shard_map/attend_first/pallas_call | solution.py:173
  153.0 33.3 %attend.1 = (bf16[1024,512]{1,0:T(8,128)(2,1)}, f32[4,8,1024]{2,1,0:T(8,128)}) custom-call(s32[6]{0:T(128)} %get-tuple-element.479.refs_0_, bf16[1024,512]{1,0:T(8,128)(2,1)} %collective-permute-done.1.refs_1_, bf16[4096,128]{1,0:T(8,128)(2,1)} %get-tuple-element.190.refs_2_.refs_5_, bf16[4096,128]{1,0:T(8,128)(2,1)} %get-tuple-element.191.refs_3_.refs_6_, ...), custom_call_target="tpu_custom_call" | custom-call | flops 1 | bytes 1 | tf_op jit(solution)/shard_map/attend/pallas_call | solution.py:210
  186.9 3.7 multiply_sine_fusion
  191.8 5.8 broadcast_select_fusion.3
  197.7 7.5 pad_maximum_fusion.1.output_weight
  206.9 3.0 maximum_maximum_fusion.1.refs_15_
  209.9 3.0 maximum_maximum_fusion.refs_14_
  212.9 24.5 %all-gather.9.cloned.1.call-done = bf16[4096,512]{1,0:T(8,128)(2,1)} async-done(((bf16[1024,512]{1,0:T(8,128)(2,1)}), bf16[4096,512]{1,0:T(8,128)(2,1)}) %all-gather.9.cloned.1.call-update) | async-done | bytes 4194320 | tf_op jit(solution)/shard_map/all_gather | solution.py:720
  241.1 62.6 %feed_forward.2 = (f32[2048,2048]{1,0:T(8,128)}, bf16[2048,2048]{1,0:T(8,128)(2,1)}, bf16[2048,1408]{1,0:T(8,128)(2,1)}, bf16[2048,2816]{1,0:T(8,128)(2,1)}, bf1...) custom-call(bf16[4,1024,512]{2,1,0:T(8,128)(2,1)} %bitcast.167, bf16[2048,2048]{1,0:T(8,128)(2,1)} %tokens_ref.5, ...), custom_call_target="tpu_custom_call" | custom-call | flops 1 | bytes 1 | tf_op jit(solution)/shard_map/feed_forward/pallas_call | solution.py:488
  303.7 21.0 %all-gather.11.cloned.1.call-done = bf16[4096,512]{1,0:T(8,128)(2,1)} async-done(((bf16[1024,512]{1,0:T(8,128)(2,1)}), bf16[4096,512]{1,0:T(8,128)(2,1)}) %all-gather.11.cloned.1.call-update) | async-done | bytes 4194320 | tf_op jit(solution)/shard_map/all_gather | solution.py:737
  326.8 62.0 %feed_forward.3 = (f32[2048,2048]{1,0:T(8,128)}, bf16[2048,2048]{1,0:T(8,128)(2,1)}, bf16[2048,1408]{1,0:T(8,128)(2,1)}, bf16[2048,2816]{1,0:T(8,128)(2,1)}, bf1...) custom-call(bf16[4,1024,512]{2,1,0:T(8,128)(2,1)} %bitcast.169, ...), custom_call_target="tpu_custom_call", output_to_operand_aliasing={{0}: (8, {}), {1}: (9, {}), {2}: (10, {}), {3}: (11, {}), {... | custom-call | flops 1 | bytes 1 | tf_op jit(solution)/shard_map/feed_forward/pallas_call | solution.py:488
  391.0 31.7 %convolution_convert_fusion = bf16[2048,2816]{1,0:T(8,128)(2,1)} fusion(bf16[2048,2048]{1,0:T(8,128)(2,1)} %get-tuple-element.226, bf16[2048,2816]{1,0:T(8,128)(2,1)} %get-tuple-element.227), kind=kOutput, calls=%fused_computation.1 | convolution fusion | flops 23628087296 | bytes 31457280 | tf_op jit(solution)/shard_map/rd,rf->df/dot_general | solution.py:633
  428.6 2.9 multiply_reduce_fusion
  435.3 17.9 %convolution_convert_fusion.2 = bf16[2048,1408]{1,0:T(8,128)(2,1)} fusion(bf16[2048,2048]{1,0:T(8,128)(2,1)} %cotangent_ref.3, bf16[2048,1408]{1,0:T(8,128)(2,1)S(1)} %bitcast.172), kind=kOutput, calls=%fused_computation.5 | convolution fusion | flops 11814043648 | bytes 19922944 | tf_op jit(solution)/shard_map/rd,rf->df/dot_general | solution.py:633
  453.2 28.3 %collective-permute-done.10 = bf16[4,512,512]{2,1,0:T(8,128)(2,1)} collective-permute-done((bf16[4,512,512]{2,1,0:T(8,128)(2,1)S(1)}, bf16[4,512,512]{2,1,0:T(8,128)(2,1)}, u32[]{:S(2)}, u32[]{:S(2)}) %collective-permute-start.10) | collective-permute-done | bytes 2097184 | tf_op jit(solution)/shard_map/ppermute | solution.py:806
  485.9 2.9 fusion.23
  488.8 3.9 fusion.48
  504.7 3.4 collective-permute-start.13
  508.1 4.8 constant_dynamic-slice_fusion.31
  513.1 20.6 %collective-permute-done.12 = bf16[256,512]{1,0:T(8,128)(2,1)S(1)} collective-permute-done((bf16[256,512]{1,0:T(8,128)(2,1)S(1)}, bf16[256,512]{1,0:T(8,128)(2,1)S(1)}, u32[]{:S(2)}, u32[]{:S(2)}) %collective-permute-start.12) | collective-permute-done | bytes 262176 | tf_op jit(solution)/shard_map/ppermute | solution.py:576
  534.0 6.1 broadcast_select_fusion.1
  540.2 7.4 pad_maximum_fusion.2
  550.1 4.2 fusion.46
  554.3 6.2 fusion.39
  562.7 22.8 %collective-permute-start.16 = (bf16[256,512]{1,0:T(8,128)(2,1)S(1)}, bf16[256,512]{1,0:T(8,128)(2,1)S(1)}, u32[]{:S(2)}, u32[]{:S(2)}) collective-permute-start(bf16[256,512]{1,0:T(8,128)(2,1)S(1)} %bitcast.183), channel_id=1, source_target_pairs={{0,5},{1,6},{2,7},{3,4},{4,1},{5,2},{6,3},{7,0},{8,13},{9,14},{10,... | collective-permute-start | bytes 786440 | tf_op jit(solution)/shard_map/ppermute | solution.py:566
  585.9 3.6 collective-permute-start.18
  589.4 66.9 %attend_back_first.1 = (bf16[1024,512]{1,0:T(8,128)(2,1)}, f32[4096,128]{1,0:T(8,128)}, f32[4096,128]{1,0:T(8,128)}) custom-call(s32[6]{0:T(128)} %get-tuple-element.478.meta.refs_0_, bf16[1024,512]{1,0:T(8,128)(2,1)} %pad_maximum_fusion.7.q_ref.refs_1_, bf16[1024,512]{1,0:T(8,128)(2,1)} %get-tuple-element.196.refs_2_, bf16[1024,512]{1,0:T(8,128)(2,1)} %bitcast.175, ...), custom_call_target="tpu_custom_call" | custom-call | flops 1 | bytes 1 | tf_op jit(solution)/shard_map/attend_back_first/pallas_call | solution.py:346
  662.9 48.9 %attend_back_last.1 = (bf16[1024,512]{1,0:T(8,128)(2,1)}, f32[2048,128]{1,0:T(8,128)}, bf16[2048,128]{1,0:T(8,128)(2,1)}) custom-call(s32[6]{0:T(128)} %get-tuple-element.479.refs_0_, bf16[1024,512]{1,0:T(8,128)(2,1)} %collective-permute-done.1.refs_1_, bf16[1024,512]{1,0:T(8,128)(2,1)} %get-tuple-element.195.refs_2_, bf16[1024,512]{1,0:T(8,128)(2,1)} %bitcast.176, ...), custom_call_target="tpu_custom_call" | custom-call | flops 1 | bytes 1 | tf_op jit(solution)/shard_map/attend_back_last/pallas_call | solution.py:401
  730.7 2.6 maximum_bitcast_fusion.1
  733.3 2.5 maximum_bitcast_fusion.2
  738.0 8.4 copy.74
  748.7 4.3 collective-permute-start.27
  754.3 3.4 collective-permute-start.24
  757.7 3.7 collective-permute-start.26
  762.6 7.1 convolution_bitcast_fusion.1
  769.7 54.8 %collective-permute-done.23 = bf16[256,512]{1,0:T(8,128)(2,1)S(1)} collective-permute-done((bf16[256,512]{1,0:T(8,128)(2,1)S(1)}, bf16[256,512]{1,0:T(8,128)(2,1)S(1)}, u32[]{:S(2)}, u32[]{:S(2)}) %collective-permute-start.23) | collective-permute-done | bytes 262176 | tf_op jit(solution)/shard_map/ppermute | solution.py:566
  825.0 4.5 broadcast.113.clone
  829.4 3.1 constant_dynamic-update-slice_fusion.7
  832.5 5.7 collective-permute-start.33
  839.6 2.5 collective-permute-done.22
  842.3 3.9 collective-permute-start.30
  851.9 40.4 %collective-permute-done.30 = bf16[512,128]{1,0:T(8,128)(2,1)S(1)} collective-permute-done((bf16[512,128]{1,0:T(8,128)(2,1)S(1)}, bf16[512,128]{1,0:T(8,128)(2,1)S(1)}, u32[]{:S(2)}, u32[]{:S(2)}) %collective-permute-start.30) | collective-permute-done | bytes 131104 | tf_op jit(solution)/shard_map/ppermute | solution.py:576
  892.3 7.0 collective-permute-done.29
  901.8 3.4 fusion.3
  908.1 8.6 convolution_convert_fusion.3
  916.7 4.8 convolution_convert_fusion.1
  921.6 7.6 pad_maximum_fusion
  929.2 22.9 %collective-permute-done.31 = bf16[512,2048]{1,0:T(8,128)(2,1)S(1)} collective-permute-done((bf16[512,2048]{1,0:T(8,128)(2,1)}, bf16[512,2048]{1,0:T(8,128)(2,1)S(1)}, u32[]{:S(2)}, u32[]{:S(2)}) %collective-permute-start.31) | collective-permute-done | bytes 2097184 | tf_op jit(solution)/shard_map/ppermute | solution.py:540
  952.0 4.2 collective-permute-done.32
  968.0 41.0 %collective-permute-done.36 = bf16[512,2048]{1,0:T(8,128)(2,1)} collective-permute-done((bf16[512,2048]{1,0:T(8,128)(2,1)}, bf16[512,2048]{1,0:T(8,128)(2,1)}, u32[]{:S(2)}, u32[]{:S(2)}) %collective-permute-start.36) | collective-permute-done | bytes 2097184 | tf_op jit(solution)/shard_map/ppermute | solution.py:541
  1009.0 42.8 %collective-permute-done.38 = bf16[512,2048]{1,0:T(8,128)(2,1)} collective-permute-done((bf16[512,2048]{1,0:T(8,128)(2,1)}, bf16[512,2048]{1,0:T(8,128)(2,1)}, u32[]{:S(2)}, u32[]{:S(2)}) %collective-permute-start.38) | collective-permute-done | bytes 2097184 | tf_op jit(solution)/shard_map/ppermute | solution.py:541
  1062.7 5.3 collective-permute-start.46
  1069.3 77.5 %collective-permute-done.46 = f32[2,2048]{1,0:T(2,128)S(1)} collective-permute-done((f32[2,2048]{1,0:T(2,128)S(1)}, f32[2,2048]{1,0:T(2,128)S(1)}, u32[]{:S(2)}, u32[]{:S(2)}) %collective-permute-start.46) | collective-permute-done | bytes 16416 | tf_op jit(solution)/shard_map/ppermute | solution.py:592
  1148.6 3.1 add.462
  1158.9 2.9 collective-permute-start.52
  1168.4 3.0 add.463
  1180.1 4.4 add_dynamic-update-slice_fusion.2
  1184.6 4.5 add_dynamic-update-slice_fusion.1
  1192.1 4.4 add_dynamic-update-slice_fusion
  (398 shorter events, 156.3 us)
Async XLA Ops:
  7.2 86.5 %all-gather.7.cloned.1.call-start = ((), (), s32[]{:S(2)}) async-start(), calls=%async_computation.10 | async-start | bytes 5242880 | tf_op jit(solution)/shard_map/all_gather | solution.py:699
  9.8 227.5 %all-gather.9.cloned.1.call-start = ((), (), s32[]{:S(2)}) async-start(), calls=%async_computation.11 | async-start | bytes 5242880 | tf_op jit(solution)/shard_map/all_gather | solution.py:720
  38.9 58.4 %collective-permute-start = (bf16[2048,128]{1,0:T(8,128)(2,1)S(1)}, bf16[2048,128]{1,0:T(8,128)(2,1)S(1)}, u32[]{:S(2)}, u32[]{:S(2)}) collective-permute-start(bf16[2048,128]{1,0:T(8,128)(2,1)S(1)} %get-tuple-element.178.own), channel_id=1, source_target_pairs={{0,4},{4,0},{1,5},{5,1},{2,6},{6,2},{3,7},{7,3},{8,12},{12,8},{9,1... | collective-permute-start | bytes 1572872 | tf_op jit(solution)/shard_map/ppermute | solution.py:710
  93.7 92.6 %collective-permute-start.2 = (bf16[4,1024,512]{2,1,0:T(8,128)(2,1)}, bf16[4,1024,512]{2,1,0:T(8,128)(2,1)}, u32[]{:S(2)}, u32[]{:S(2)}) collective-permute-start(bf16[4,1024,512]{2,1,0:T(8,128)(2,1)} %bitcast.173), channel_id=1, source_target_pairs={{0,8},{8,0},{16,24},{24,16},{1,9},{9,1},{17,25},{25,17},{2,10},{10... | collective-permute-start | bytes 12582920 | tf_op jit(solution)/shard_map/ppermute | solution.py:722
  97.3 53.8 %collective-permute-start.1 = (bf16[1024,512]{1,0:T(8,128)(2,1)S(1)}, bf16[1024,512]{1,0:T(8,128)(2,1)}, u32[]{:S(2)}, u32[]{:S(2)}) collective-permute-start(bf16[1024,512]{1,0:T(8,128)(2,1)S(1)} %slice.166), channel_id=1, source_target_pairs={{0,4},{4,0},{1,5},{5,1},{2,6},{6,2},{3,7},{7,3},{8,12},{12,8},{9,1... | collective-permute-start | bytes 3145736 | tf_op jit(solution)/shard_map/ppermute | solution.py:716
  151.2 173.6 %all-gather.11.cloned.1.call-start = ((), (), s32[]{:S(2)}) async-start(), calls=%async_computation.12 | async-start | bytes 5242880 | tf_op jit(solution)/shard_map/all_gather | solution.py:737
  186.3 51.0 %collective-permute-start.3 = (bf16[1024,512]{1,0:T(8,128)(2,1)}, bf16[1024,512]{1,0:T(8,128)(2,1)}, u32[]{:S(2)}, u32[]{:S(2)}) collective-permute-start(bf16[1024,512]{1,0:T(8,128)(2,1)} %get-tuple-element.195.refs_2_), channel_id=1, source_target_pairs={{0,4},{4,0},{1,5},{5,1},{2,6},{6,2},{3,7},{7,3},{8,12},{12,8},{9,1... | collective-permute-start | bytes 3145736 | tf_op jit(solution)/shard_map/ppermute | solution.py:733
  237.4 244.2 %reduce-scatter.6.cloned.1.call-start = ((), (), s32[]{:S(2)}) async-start(), calls=%async_computation.5 | async-start | bytes 5242880 | tf_op jit(solution)/shard_map/reduce_scatter | solution.py:774
  238.5 65.2 %collective-permute-start.4 = (bf16[512,512]{1,0:T(8,128)(2,1)S(1)}, bf16[512,512]{1,0:T(8,128)(2,1)S(1)}, u32[]{:S(2)}, u32[]{:S(2)}) collective-permute-start(bf16[512,512]{1,0:T(8,128)(2,1)S(1)} %constant_dynamic-slice_fusion.38), channel_id=1, source_target_pairs={{0,1},{1,2},{2,3},{4,5},{5,6},{6,7},{8,9},{9,10},{10,11},{12,13},{... | collective-permute-start | bytes 1572872 | tf_op jit(solution)/shard_map/ppermute | solution.py:540
  239.8 63.9 %collective-permute-start.5 = (bf16[512,512]{1,0:T(8,128)(2,1)S(1)}, bf16[512,512]{1,0:T(8,128)(2,1)S(1)}, u32[]{:S(2)}, u32[]{:S(2)}) collective-permute-start(bf16[512,512]{1,0:T(8,128)(2,1)S(1)} %constant_dynamic-slice_fusion.38), channel_id=1, source_target_pairs={{1,0},{2,1},{3,2},{5,4},{6,5},{7,6},{9,8},{10,9},{11,10},{13,12},{... | collective-permute-start | bytes 1572872 | tf_op jit(solution)/shard_map/ppermute | solution.py:541
  303.7 85.1 %copy-start.42 = (bf16[512,512]{1,0:T(8,128)(2,1)}, bf16[512,512]{1,0:T(8,128)(2,1)S(1)}, u32[]{:S(2)}) copy-start(bf16[512,512]{1,0:T(8,128)(2,1)S(1)} %collective-permute-done.4) | copy-start | bytes 1572868
  324.8 222.7 %reduce-scatter.8.cloned.1.call-start = ((), (), s32[]{:S(2)}) async-start(), calls=%async_computation.6 | async-start | bytes 5242880 | tf_op jit(solution)/shard_map/reduce_scatter | solution.py:774
  324.8 64.0 %collective-permute-start.6 = (bf16[512,512]{1,0:T(8,128)(2,1)S(1)}, bf16[512,512]{1,0:T(8,128)(2,1)S(1)}, u32[]{:S(2)}, u32[]{:S(2)}) collective-permute-start(bf16[512,512]{1,0:T(8,128)(2,1)S(1)} %collective-permute-done.4), channel_id=1, source_target_pairs={{1,2},{2,3},{5,6},{6,7},{9,10},{10,11},{13,14},{14,15},{17,18},{18... | collective-permute-start | bytes 1572872 | tf_op jit(solution)/shard_map/ppermute | solution.py:540
  325.5 63.3 %collective-permute-start.7 = (bf16[512,512]{1,0:T(8,128)(2,1)S(1)}, bf16[512,512]{1,0:T(8,128)(2,1)S(1)}, u32[]{:S(2)}, u32[]{:S(2)}) collective-permute-start(bf16[512,512]{1,0:T(8,128)(2,1)S(1)} %collective-permute-done.5), channel_id=1, source_target_pairs={{1,0},{2,1},{5,4},{6,5},{9,8},{10,9},{13,12},{14,13},{17,16},{18,1... | collective-permute-start | bytes 1572872 | tf_op jit(solution)/shard_map/ppermute | solution.py:541
  388.9 33.8 %collective-permute-start.8 = (bf16[512,512]{1,0:T(8,128)(2,1)S(1)}, bf16[512,512]{1,0:T(8,128)(2,1)S(1)}, u32[]{:S(2)}, u32[]{:S(2)}) collective-permute-start(bf16[512,512]{1,0:T(8,128)(2,1)S(1)} %collective-permute-done.6), channel_id=1, source_target_pairs={{2,3},{6,7},{10,11},{14,15},{18,19},{22,23},{26,27},{30,31}} | collective-permute-start | bytes 1572872 | tf_op jit(solution)/shard_map/ppermute | solution.py:540
  389.6 33.1 %collective-permute-start.9 = (bf16[512,512]{1,0:T(8,128)(2,1)S(1)}, bf16[512,512]{1,0:T(8,128)(2,1)S(1)}, u32[]{:S(2)}, u32[]{:S(2)}) collective-permute-start(bf16[512,512]{1,0:T(8,128)(2,1)S(1)} %collective-permute-done.7), channel_id=1, source_target_pairs={{1,0},{5,4},{9,8},{13,12},{17,16},{21,20},{25,24},{29,28}} | collective-permute-start | bytes 1572872 | tf_op jit(solution)/shard_map/ppermute | solution.py:541
  390.9 321.6 %reduce-scatter.10.cloned.1.call-start = ((), (), s32[]{:S(2)}) async-start(), calls=%async_computation.7 | async-start | bytes 10485760 | tf_op jit(solution)/shard_map/reduce_scatter | solution.py:774
  423.7 532.6 %reduce-scatter.12.cloned.1.call-start = ((), (), s32[]{:S(2)}) async-start(), calls=%async_computation.8 | async-start | bytes 12976128 | tf_op jit(solution)/shard_map/reduce_scatter | solution.py:777
  433.6 47.9 %collective-permute-start.10 = (bf16[4,512,512]{2,1,0:T(8,128)(2,1)S(1)}, bf16[4,512,512]{2,1,0:T(8,128)(2,1)}, u32[]{:S(2)}, u32[]{:S(2)}) collective-permute-start(bf16[4,512,512]{2,1,0:T(8,128)(2,1)S(1)} %bitcast_dynamic-update-slice_fusion), channel_id=1, source_target_pairs={{0,4},{4,0},{1,5},{5,1},{2,6},{6,2},{3,7},{7,3},{8,12},{12,8},{9,1... | collective-permute-start | bytes 6291464 | tf_op jit(solution)/shard_map/ppermute | solution.py:806
  495.1 38.7 %collective-permute-start.14 = (bf16[4,1024,512]{2,1,0:T(8,128)(2,1)}, bf16[4,1024,512]{2,1,0:T(8,128)(2,1)}, u32[]{:S(2)}, u32[]{:S(2)}) collective-permute-start(bf16[4,1024,512]{2,1,0:T(8,128)(2,1)} %pad_maximum_fusion.3), channel_id=1, source_target_pairs={{0,8},{8,0},{16,24},{24,16},{1,9},{9,1},{17,25},{25,17},{2,10},{10... | collective-permute-start | bytes 12582920 | tf_op jit(solution)/shard_map/ppermute | solution.py:819
  500.6 12.5 %collective-permute-start.11 = (bf16[256,512]{1,0:T(8,128)(2,1)S(1)}, bf16[256,512]{1,0:T(8,128)(2,1)S(1)}, u32[]{:S(2)}, u32[]{:S(2)}) collective-permute-start(bf16[256,512]{1,0:T(8,128)(2,1)S(1)} %bitcast.186), channel_id=1, source_target_pairs={{0,1},{1,2},{2,3},{3,0},{4,5},{5,6},{6,7},{7,4},{8,9},{9,10},{10,1... | collective-permute-start | bytes 786440 | tf_op jit(solution)/shard_map/ppermute | solution.py:576
  503.2 30.5 %collective-permute-start.12 = (bf16[256,512]{1,0:T(8,128)(2,1)S(1)}, bf16[256,512]{1,0:T(8,128)(2,1)S(1)}, u32[]{:S(2)}, u32[]{:S(2)}) collective-permute-start(bf16[256,512]{1,0:T(8,128)(2,1)S(1)} %bitcast.187), channel_id=1, source_target_pairs={{0,2},{1,3},{2,0},{3,1},{4,6},{5,7},{6,4},{7,5},{8,10},{9,11},{10,... | collective-permute-start | bytes 786440 | tf_op jit(solution)/shard_map/ppermute | solution.py:576
  504.7 29.1 %collective-permute-start.13 = (bf16[256,512]{1,0:T(8,128)(2,1)S(1)}, bf16[256,512]{1,0:T(8,128)(2,1)S(1)}, u32[]{:S(2)}, u32[]{:S(2)}) collective-permute-start(bf16[256,512]{1,0:T(8,128)(2,1)S(1)} %bitcast.188), channel_id=1, source_target_pairs={{0,3},{1,0},{2,1},{3,2},{4,7},{5,4},{6,5},{7,6},{8,11},{9,8},{10,9... | collective-permute-start | bytes 786440 | tf_op jit(solution)/shard_map/ppermute | solution.py:576
  560.7 95.6 %collective-permute-start.15 = (bf16[256,512]{1,0:T(8,128)(2,1)S(1)}, bf16[256,512]{1,0:T(8,128)(2,1)S(1)}, u32[]{:S(2)}, u32[]{:S(2)}) collective-permute-start(bf16[256,512]{1,0:T(8,128)(2,1)S(1)} %bitcast.182), channel_id=1, source_target_pairs={{0,4},{1,5},{2,6},{3,7},{4,0},{5,1},{6,2},{7,3},{8,12},{9,13},{10,... | collective-permute-start | bytes 786440 | tf_op jit(solution)/shard_map/ppermute | solution.py:566
  562.7 93.7 %collective-permute-start.16 = (bf16[256,512]{1,0:T(8,128)(2,1)S(1)}, bf16[256,512]{1,0:T(8,128)(2,1)S(1)}, u32[]{:S(2)}, u32[]{:S(2)}) collective-permute-start(bf16[256,512]{1,0:T(8,128)(2,1)S(1)} %bitcast.183), channel_id=1, source_target_pairs={{0,5},{1,6},{2,7},{3,4},{4,1},{5,2},{6,3},{7,0},{8,13},{9,14},{10,... | collective-permute-start | bytes 786440 | tf_op jit(solution)/shard_map/ppermute | solution.py:566
  585.6 70.7 %collective-permute-start.17 = (bf16[256,512]{1,0:T(8,128)(2,1)S(1)}, bf16[256,512]{1,0:T(8,128)(2,1)S(1)}, u32[]{:S(2)}, u32[]{:S(2)}) collective-permute-start(bf16[256,512]{1,0:T(8,128)(2,1)S(1)} %bitcast.184), channel_id=1, source_target_pairs={{0,6},{1,7},{2,4},{3,5},{4,2},{5,3},{6,0},{7,1},{8,14},{9,15},{10,... | collective-permute-start | bytes 786440 | tf_op jit(solution)/shard_map/ppermute | solution.py:566
  585.9 70.5 %collective-permute-start.18 = (bf16[256,512]{1,0:T(8,128)(2,1)S(1)}, bf16[256,512]{1,0:T(8,128)(2,1)S(1)}, u32[]{:S(2)}, u32[]{:S(2)}) collective-permute-start(bf16[256,512]{1,0:T(8,128)(2,1)S(1)} %bitcast.185), channel_id=1, source_target_pairs={{0,7},{1,4},{2,5},{3,6},{4,3},{5,0},{6,1},{7,2},{8,15},{9,12},{10,... | collective-permute-start | bytes 786440 | tf_op jit(solution)/shard_map/ppermute | solution.py:566
  657.7 54.1 %collective-permute-start.19 = (bf16[256,512]{1,0:T(8,128)(2,1)S(1)}, bf16[256,512]{1,0:T(8,128)(2,1)S(1)}, u32[]{:S(2)}, u32[]{:S(2)}) collective-permute-start(bf16[256,512]{1,0:T(8,128)(2,1)S(1)} %get-tuple-element.416), channel_id=1, source_target_pairs={{0,1},{1,2},{2,3},{3,0},{4,5},{5,6},{6,7},{7,4},{8,9},{9,10},{10,1... | collective-permute-start | bytes 786440 | tf_op jit(solution)/shard_map/ppermute | solution.py:576
  657.8 54.1 %collective-permute-start.20 = (bf16[256,512]{1,0:T(8,128)(2,1)S(1)}, bf16[256,512]{1,0:T(8,128)(2,1)S(1)}, u32[]{:S(2)}, u32[]{:S(2)}) collective-permute-start(bf16[256,512]{1,0:T(8,128)(2,1)S(1)} %get-tuple-element.415), channel_id=1, source_target_pairs={{0,2},{1,3},{2,0},{3,1},{4,6},{5,7},{6,4},{7,5},{8,10},{9,11},{10,... | collective-permute-start | bytes 786440 | tf_op jit(solution)/shard_map/ppermute | solution.py:576
  660.1 52.4 %collective-permute-start.21 = (bf16[256,512]{1,0:T(8,128)(2,1)S(1)}, bf16[256,512]{1,0:T(8,128)(2,1)}, u32[]{:S(2)}, u32[]{:S(2)}) collective-permute-start(bf16[256,512]{1,0:T(8,128)(2,1)S(1)} %get-tuple-element.414), channel_id=1, source_target_pairs={{0,3},{1,0},{2,1},{3,2},{4,7},{5,4},{6,5},{7,6},{8,11},{9,8},{10,9... | collective-permute-start | bytes 786440 | tf_op jit(solution)/shard_map/ppermute | solution.py:576
  712.6 439.9 %reduce-scatter.14.cloned.1.call-start = ((), (), s32[]{:S(2)}) async-start(), calls=%async_computation.9 | async-start | bytes 18874368 | tf_op jit(solution)/shard_map/reduce_scatter | solution.py:777
  748.7 93.3 %collective-permute-start.27 = (bf16[1024,512]{1,0:T(8,128)(2,1)}, bf16[1024,512]{1,0:T(8,128)(2,1)}, u32[]{:S(2)}, u32[]{:S(2)}) collective-permute-start(bf16[1024,512]{1,0:T(8,128)(2,1)} %get-tuple-element.284), channel_id=1, source_target_pairs={{0,4},{4,0},{1,5},{5,1},{2,6},{6,2},{3,7},{7,3},{8,12},{12,8},{9,1... | collective-permute-start | bytes 3145736 | tf_op jit(solution)/shard_map/ppermute | solution.py:861
  754.3 70.2 %collective-permute-start.23 = (bf16[256,512]{1,0:T(8,128)(2,1)S(1)}, bf16[256,512]{1,0:T(8,128)(2,1)S(1)}, u32[]{:S(2)}, u32[]{:S(2)}) collective-permute-start(bf16[256,512]{1,0:T(8,128)(2,1)S(1)} %get-tuple-element.413), channel_id=1, source_target_pairs={{0,4},{1,5},{2,6},{3,7},{4,0},{5,1},{6,2},{7,3},{8,12},{9,13},{10,... | collective-permute-start | bytes 786440 | tf_op jit(solution)/shard_map/ppermute | solution.py:566
  754.3 78.2 %collective-permute-start.24 = (bf16[256,512]{1,0:T(8,128)(2,1)S(1)}, bf16[256,512]{1,0:T(8,128)(2,1)S(1)}, u32[]{:S(2)}, u32[]{:S(2)}) collective-permute-start(bf16[256,512]{1,0:T(8,128)(2,1)S(1)} %get-tuple-element.412), channel_id=1, source_target_pairs={{0,5},{1,6},{2,7},{3,4},{4,1},{5,2},{6,3},{7,0},{8,13},{9,14},{10,... | collective-permute-start | bytes 786440 | tf_op jit(solution)/shard_map/ppermute | solution.py:566
  757.7 80.5 %collective-permute-start.25 = (bf16[256,512]{1,0:T(8,128)(2,1)S(1)}, bf16[256,512]{1,0:T(8,128)(2,1)S(1)}, u32[]{:S(2)}, u32[]{:S(2)}) collective-permute-start(bf16[256,512]{1,0:T(8,128)(2,1)S(1)} %get-tuple-element.411), channel_id=1, source_target_pairs={{0,6},{1,7},{2,4},{3,5},{4,2},{5,3},{6,0},{7,1},{8,14},{9,15},{10,... | collective-permute-start | bytes 786440 | tf_op jit(solution)/shard_map/ppermute | solution.py:566
  757.7 81.8 %collective-permute-start.26 = (bf16[256,512]{1,0:T(8,128)(2,1)S(1)}, bf16[256,512]{1,0:T(8,128)(2,1)S(1)}, u32[]{:S(2)}, u32[]{:S(2)}) collective-permute-start(bf16[256,512]{1,0:T(8,128)(2,1)S(1)} %get-tuple-element.410), channel_id=1, source_target_pairs={{0,7},{1,4},{2,5},{3,6},{4,3},{5,0},{6,1},{7,2},{8,15},{9,12},{10,... | collective-permute-start | bytes 786440 | tf_op jit(solution)/shard_map/ppermute | solution.py:566
  824.5 17.6 %collective-permute-start.22 = (bf16[2048,128]{1,0:T(8,128)(2,1)S(1)}, bf16[2048,128]{1,0:T(8,128)(2,1)S(1)}, u32[]{:S(2)}, u32[]{:S(2)}) collective-permute-start(bf16[2048,128]{1,0:T(8,128)(2,1)S(1)} %copy-done.58), channel_id=1, source_target_pairs={{0,4},{4,0},{1,5},{5,1},{2,6},{6,2},{3,7},{7,3},{8,12},{12,8},{9,1... | collective-permute-start | bytes 1572872 | tf_op jit(solution)/shard_map/ppermute | solution.py:859
  832.5 96.6 %collective-permute-start.33 = (bf16[512,2048]{1,0:T(8,128)(2,1)}, bf16[512,2048]{1,0:T(8,128)(2,1)}, u32[]{:S(2)}, u32[]{:S(2)}) collective-permute-start(bf16[512,2048]{1,0:T(8,128)(2,1)} %get-tuple-element.375), channel_id=1, source_target_pairs={{0,1},{1,2},{2,3},{4,5},{5,6},{6,7},{8,9},{9,10},{10,11},{12,13},{... | collective-permute-start | bytes 6291464 | tf_op jit(solution)/shard_map/ppermute | solution.py:540
  838.3 90.9 %collective-permute-start.34 = (bf16[512,2048]{1,0:T(8,128)(2,1)}, bf16[512,2048]{1,0:T(8,128)(2,1)}, u32[]{:S(2)}, u32[]{:S(2)}) collective-permute-start(bf16[512,2048]{1,0:T(8,128)(2,1)} %get-tuple-element.375), channel_id=1, source_target_pairs={{1,0},{2,1},{3,2},{5,4},{6,5},{7,6},{9,8},{10,9},{11,10},{13,12},{... | collective-permute-start | bytes 6291464 | tf_op jit(solution)/shard_map/ppermute | solution.py:541
  842.3 49.9 %collective-permute-start.30 = (bf16[512,128]{1,0:T(8,128)(2,1)S(1)}, bf16[512,128]{1,0:T(8,128)(2,1)S(1)}, u32[]{:S(2)}, u32[]{:S(2)}) collective-permute-start(bf16[512,128]{1,0:T(8,128)(2,1)S(1)} %pad_maximum_fusion.20), channel_id=1, source_target_pairs={{0,3},{1,0},{2,1},{3,2},{4,7},{5,4},{6,5},{7,6},{8,11},{9,8},{10,9... | collective-permute-start | bytes 393224 | tf_op jit(solution)/shard_map/ppermute | solution.py:576
  846.2 53.0 %collective-permute-start.29 = (bf16[512,128]{1,0:T(8,128)(2,1)S(1)}, bf16[512,128]{1,0:T(8,128)(2,1)S(1)}, u32[]{:S(2)}, u32[]{:S(2)}) collective-permute-start(bf16[512,128]{1,0:T(8,128)(2,1)S(1)} %pad_maximum_fusion.19), channel_id=1, source_target_pairs={{0,2},{1,3},{2,0},{3,1},{4,6},{5,7},{6,4},{7,5},{8,10},{9,11},{10,... | collective-permute-start | bytes 393224 | tf_op jit(solution)/shard_map/ppermute | solution.py:576
  847.8 51.5 %collective-permute-start.28 = (bf16[512,128]{1,0:T(8,128)(2,1)S(1)}, bf16[512,128]{1,0:T(8,128)(2,1)S(1)}, u32[]{:S(2)}, u32[]{:S(2)}) collective-permute-start(bf16[512,128]{1,0:T(8,128)(2,1)S(1)} %pad_maximum_fusion.18), channel_id=1, source_target_pairs={{0,1},{1,2},{2,3},{3,0},{4,5},{5,6},{6,7},{7,4},{8,9},{9,10},{10,1... | collective-permute-start | bytes 393224 | tf_op jit(solution)/shard_map/ppermute | solution.py:576
  905.1 46.9 %collective-permute-start.31 = (bf16[512,2048]{1,0:T(8,128)(2,1)}, bf16[512,2048]{1,0:T(8,128)(2,1)S(1)}, u32[]{:S(2)}, u32[]{:S(2)}) collective-permute-start(bf16[512,2048]{1,0:T(8,128)(2,1)} %fusion.3), channel_id=1, source_target_pairs={{0,1},{1,2},{2,3},{4,5},{5,6},{6,7},{8,9},{9,10},{10,11},{12,13},{... | collective-permute-start | bytes 6291464 | tf_op jit(solution)/shard_map/ppermute | solution.py:540
  906.7 49.6 %collective-permute-start.32 = (bf16[512,2048]{1,0:T(8,128)(2,1)}, bf16[512,2048]{1,0:T(8,128)(2,1)}, u32[]{:S(2)}, u32[]{:S(2)}) collective-permute-start(bf16[512,2048]{1,0:T(8,128)(2,1)} %fusion.3), channel_id=1, source_target_pairs={{1,0},{2,1},{3,2},{5,4},{6,5},{7,6},{9,8},{10,9},{11,10},{13,12},{... | collective-permute-start | bytes 6291464 | tf_op jit(solution)/shard_map/ppermute | solution.py:541
  956.3 11.7 collective-permute-start.35
  958.3 50.8 %collective-permute-start.36 = (bf16[512,2048]{1,0:T(8,128)(2,1)}, bf16[512,2048]{1,0:T(8,128)(2,1)}, u32[]{:S(2)}, u32[]{:S(2)}) collective-permute-start(bf16[512,2048]{1,0:T(8,128)(2,1)} %collective-permute-done.32), channel_id=1, source_target_pairs={{1,0},{2,1},{5,4},{6,5},{9,8},{10,9},{13,12},{14,13},{17,16},{18,1... | collective-permute-start | bytes 6291464 | tf_op jit(solution)/shard_map/ppermute | solution.py:541
  959.6 49.5 %collective-permute-start.37 = (bf16[512,2048]{1,0:T(8,128)(2,1)}, bf16[512,2048]{1,0:T(8,128)(2,1)}, u32[]{:S(2)}, u32[]{:S(2)}) collective-permute-start(bf16[512,2048]{1,0:T(8,128)(2,1)} %collective-permute-done.33), channel_id=1, source_target_pairs={{1,2},{2,3},{5,6},{6,7},{9,10},{10,11},{13,14},{14,15},{17,18},{18... | collective-permute-start | bytes 6291464 | tf_op jit(solution)/shard_map/ppermute | solution.py:540
  961.6 90.2 %collective-permute-start.38 = (bf16[512,2048]{1,0:T(8,128)(2,1)}, bf16[512,2048]{1,0:T(8,128)(2,1)}, u32[]{:S(2)}, u32[]{:S(2)}) collective-permute-start(bf16[512,2048]{1,0:T(8,128)(2,1)} %collective-permute-done.34), channel_id=1, source_target_pairs={{1,0},{2,1},{5,4},{6,5},{9,8},{10,9},{13,12},{14,13},{17,16},{18,1... | collective-permute-start | bytes 6291464 | tf_op jit(solution)/shard_map/ppermute | solution.py:541
  962.9 1.2 collective-permute-start.39
  964.2 3.8 collective-permute-start.40
  1051.9 100.5 %collective-permute-start.41 = (bf16[512,2048]{1,0:T(8,128)(2,1)}, bf16[512,2048]{1,0:T(8,128)(2,1)}, u32[]{:S(2)}, u32[]{:S(2)}) collective-permute-start(bf16[512,2048]{1,0:T(8,128)(2,1)} %collective-permute-done.35), channel_id=1, source_target_pairs={{2,3},{6,7},{10,11},{14,15},{18,19},{22,23},{26,27},{30,31}} | collective-permute-start | bytes 6291464 | tf_op jit(solution)/shard_map/ppermute | solution.py:540
  1053.8 98.6 %collective-permute-start.42 = (bf16[512,2048]{1,0:T(8,128)(2,1)}, bf16[512,2048]{1,0:T(8,128)(2,1)}, u32[]{:S(2)}, u32[]{:S(2)}) collective-permute-start(bf16[512,2048]{1,0:T(8,128)(2,1)} %collective-permute-done.36), channel_id=1, source_target_pairs={{1,0},{5,4},{9,8},{13,12},{17,16},{21,20},{25,24},{29,28}} | collective-permute-start | bytes 6291464 | tf_op jit(solution)/shard_map/ppermute | solution.py:541
  1055.1 97.3 %collective-permute-start.43 = (bf16[512,2048]{1,0:T(8,128)(2,1)}, bf16[512,2048]{1,0:T(8,128)(2,1)}, u32[]{:S(2)}, u32[]{:S(2)}) collective-permute-start(bf16[512,2048]{1,0:T(8,128)(2,1)} %collective-permute-done.37), channel_id=1, source_target_pairs={{2,3},{6,7},{10,11},{14,15},{18,19},{22,23},{26,27},{30,31}} | collective-permute-start | bytes 6291464 | tf_op jit(solution)/shard_map/ppermute | solution.py:540
  1057.1 95.3 %collective-permute-start.44 = (bf16[512,2048]{1,0:T(8,128)(2,1)}, bf16[512,2048]{1,0:T(8,128)(2,1)}, u32[]{:S(2)}, u32[]{:S(2)}) collective-permute-start(bf16[512,2048]{1,0:T(8,128)(2,1)} %collective-permute-done.38), channel_id=1, source_target_pairs={{1,0},{5,4},{9,8},{13,12},{17,16},{21,20},{25,24},{29,28}} | collective-permute-start | bytes 6291464 | tf_op jit(solution)/shard_map/ppermute | solution.py:541
  1058.5 4.2 collective-permute-start.45
  1061.2 85.7 %copy-start.30 = (bf16[256,2816]{1,0:T(8,128)(2,1)S(1)}, bf16[256,2816]{1,0:T(8,128)(2,1)}, u32[]{:S(2)}) copy-start(bf16[256,2816]{1,0:T(8,128)(2,1)} %reduce-scatter.12.cloned.1.call-done) | copy-start | bytes 4325380
  1062.7 84.0 %collective-permute-start.46 = (f32[2,2048]{1,0:T(2,128)S(1)}, f32[2,2048]{1,0:T(2,128)S(1)}, u32[]{:S(2)}, u32[]{:S(2)}) collective-permute-start(f32[2,2048]{1,0:T(2,128)S(1)} %add.452), channel_id=1, source_target_pairs={{0,1},{1,0},{2,3},{3,2},{4,5},{5,4},{6,7},{7,6},{8,9},{9,8},{10,11... | collective-permute-start | bytes 49160 | tf_op jit(solution)/shard_map/ppermute | solution.py:592
  1146.8 5.0 collective-permute-start.47
  1158.9 51.5 %collective-permute-start.51 = (bf16[256,512]{0,1:T(8,128)(2,1)}, bf16[256,512]{0,1:T(8,128)(2,1)}, u32[]{:S(2)}, u32[]{:S(2)}) collective-permute-start(bf16[256,512]{0,1:T(8,128)(2,1)} %get-tuple-element.396), channel_id=1, source_target_pairs={{0,1},{1,2},{2,3},{3,0},{4,5},{5,6},{6,7},{7,4},{8,9},{9,10},{10,1... | collective-permute-start | bytes 786440 | tf_op jit(solution)/shard_map/ppermute | solution.py:576
  1158.9 52.6 %collective-permute-start.52 = (bf16[256,512]{0,1:T(8,128)(2,1)}, bf16[256,512]{0,1:T(8,128)(2,1)}, u32[]{:S(2)}, u32[]{:S(2)}) collective-permute-start(bf16[256,512]{0,1:T(8,128)(2,1)} %get-tuple-element.395), channel_id=1, source_target_pairs={{0,2},{1,3},{2,0},{3,1},{4,6},{5,7},{6,4},{7,5},{8,10},{9,11},{10,... | collective-permute-start | bytes 786440 | tf_op jit(solution)/shard_map/ppermute | solution.py:576
  1164.3 37.2 %collective-permute-start.48 = (bf16[64,128]{0,1:T(8,128)(2,1)}, bf16[64,128]{0,1:T(8,128)(2,1)}, u32[]{:S(2)}, u32[]{:S(2)}) collective-permute-start(bf16[64,128]{0,1:T(8,128)(2,1)} %get-tuple-element.444), channel_id=1, source_target_pairs={{0,1},{1,2},{2,3},{3,0},{4,5},{5,6},{6,7},{7,4},{8,9},{9,10},{10,1... | collective-permute-start | bytes 49160 | tf_op jit(solution)/shard_map/ppermute | solution.py:576
  1165.8 38.5 %collective-permute-start.49 = (bf16[64,128]{0,1:T(8,128)(2,1)}, bf16[64,128]{0,1:T(8,128)(2,1)}, u32[]{:S(2)}, u32[]{:S(2)}) collective-permute-start(bf16[64,128]{0,1:T(8,128)(2,1)} %get-tuple-element.443), channel_id=1, source_target_pairs={{0,2},{1,3},{2,0},{3,1},{4,6},{5,7},{6,4},{7,5},{8,10},{9,11},{10,... | collective-permute-start | bytes 49160 | tf_op jit(solution)/shard_map/ppermute | solution.py:576
  1167.8 37.3 %collective-permute-start.50 = (bf16[64,128]{0,1:T(8,128)(2,1)}, bf16[64,128]{0,1:T(8,128)(2,1)}, u32[]{:S(2)}, u32[]{:S(2)}) collective-permute-start(bf16[64,128]{0,1:T(8,128)(2,1)} %get-tuple-element.442), channel_id=1, source_target_pairs={{0,3},{1,0},{2,1},{3,2},{4,7},{5,4},{6,5},{7,6},{8,11},{9,8},{10,9... | collective-permute-start | bytes 49160 | tf_op jit(solution)/shard_map/ppermute | solution.py:576
  1201.5 11.2 collective-permute-start.53
  (67 other events, 1022.4 us)
Sparse Core Ops, SparseCore 0:
  10.2 83.4 all-gather.6
  151.3 86.0 all-gather.8
  238.9 85.7 all-gather.10
  326.9 94.5 reduce-scatter.5
  423.8 75.1 reduce-scatter.7
  501.2 201.3 reduce-scatter.9
  712.7 143.6 reduce-scatter.11
  956.4 114.1 reduce-scatter.13

commit v3 on v2

--- a/solution.py
+++ b/solution.py
@@ -152,6 +152,12 @@
         at += rows
 
 
+def attend_cost(rows, length, width):
+    return pl.CostEstimate(
+        flops=8 * rows * length * width, bytes_accessed=2**23, transcendentals=0
+    )
+
+
 def attend_first(meta, offsets, queries, kv_own, kv_other):
     rows, width = queries.shape
     pairs = width // 128
@@ -192,7 +198,7 @@
         ]
         + [jax.ShapeDtypeStruct(form, BF16) for form in forms],
         compiler_params=pltpu.CompilerParams(vmem_limit_bytes=58 * 2**20),
-        cost_estimate=LIGHT,
+        cost_estimate=attend_cost(rows, length, width),
         name="attend_first",
     )(meta, queries, kv_own, kv_other)
 
@@ -228,7 +234,7 @@
             jax.ShapeDtypeStruct((pairs, 8, rows), F32),
         ],
         compiler_params=pltpu.CompilerParams(vmem_limit_bytes=58 * 2**20),
-        cost_estimate=LIGHT,
+        cost_estimate=attend_cost(rows, length, width),
         name="attend",
     )(meta, queries, keys_a, keys_b, values_t)
 
@@ -507,6 +513,89 @@
     )(gathered, tokens, cotangent, gain, output_weight, *weights, *earlier)
 
 
+def join_kernel(order, rows_ref, near_ref, far_ref, out_ref):
+    piece = pl.program_id(0)
+
+    def total(weight_ref):
+        result = None
+        for source in range(rows_ref.shape[0]):
+            part = lax.dot_general(
+                rows_ref[source], weight_ref[0, source], NT, preferred_element_type=F32
+            )
+            result = part if result is None else result + part
+        out_ref[...] = result
+
+    @pl.when(piece < 2)
+    def _():
+        total(near_ref)
+
+    @pl.when(piece >= 2)
+    def _():
+        total(far_ref)
+
+
+def join(order, rows, near, far):
+    size, count, features = rows.shape
+    columns = near.shape[2]
+    return pl.pallas_call(
+        join_kernel,
+        grid_spec=pltpu.PrefetchScalarGridSpec(
+            num_scalar_prefetch=1,
+            grid=(4,),
+            in_specs=[
+                pl.BlockSpec(rows.shape, lambda p, order: (0, 0, 0)),
+                pl.BlockSpec(
+                    (1, size, columns, features), lambda p, order: (jnp.minimum(p, 1), 0, 0, 0)
+                ),
+                pl.BlockSpec(
+                    (1, size, columns, features), lambda p, order: (jnp.maximum(p - 2, 0), 0, 0, 0)
+                ),
+            ],
+            out_specs=pl.BlockSpec((count, columns), lambda p, order: (0, order[p])),
+        ),
+        out_shape=jax.ShapeDtypeStruct((count, 4 * columns), F32),
+        compiler_params=pltpu.CompilerParams(vmem_limit_bytes=32 * 2**20),
+        cost_estimate=LIGHT,
+        name="join",
+    )(order, rows, near, far)
+
+
+def arrange_kernel(order, near_ref, far_ref, out_ref):
+    piece = pl.program_id(0)
+
+    @pl.when(piece < 2)
+    def _():
+        out_ref[...] = near_ref[0]
+
+    @pl.when(piece >= 2)
+    def _():
+        out_ref[...] = far_ref[0]
+
+
+def arrange(order, near, far):
+    size, rows, features = near.shape[1:]
+    return pl.pallas_call(
+        arrange_kernel,
+        grid_spec=pltpu.PrefetchScalarGridSpec(
+            num_scalar_prefetch=1,
+            grid=(4,),
+            in_specs=[
+                pl.BlockSpec(
+                    (1, size, rows, features), lambda p, order: (jnp.minimum(p, 1), 0, 0, 0)
+                ),
+                pl.BlockSpec(
+                    (1, size, rows, features), lambda p, order: (jnp.maximum(p - 2, 0), 0, 0, 0)
+                ),
+            ],
+            out_specs=pl.BlockSpec((size, rows, features), lambda p, order: (0, order[p], 0)),
+        ),
+        out_shape=jax.ShapeDtypeStruct((size, 4 * rows, features), near.dtype),
+        compiler_params=pltpu.CompilerParams(vmem_limit_bytes=32 * 2**20),
+        cost_estimate=LIGHT,
+        name="arrange",
+    )(order, near, far)
+
+
 def quarter_row(row, c, half, span):
     if c:
         return half + row
@@ -544,15 +633,29 @@
     def held(self, pair):
         self.rights[-1], self.lefts[-1] = pair
 
-    def collect(self, place, target):
+    def place_hop(self, place, target, hop):
         size = lax.axis_size("tensor")
         me = lax.axis_index("tensor")
+        if hop == 0:
+            return place(target, self.piece, me)
+        right, left = self.rights[hop], self.lefts[hop]
+        from_left, from_right = me >= hop, me + hop < size
+        if 2 * hop >= size:
+            piece = jnp.where(from_left, right, jnp.where(from_right, left, self.piece))
+            source = jnp.where(from_left, me - hop, jnp.where(from_right, me + hop, me))
+            return place(target, piece, source)
+        target = place(
+            target, jnp.where(from_left, right, self.piece), jnp.where(from_left, me - hop, me)
+        )
+        return place(
+            target, jnp.where(from_right, left, self.piece), jnp.where(from_right, me + hop, me)
+        )
+
+    def collect(self, place, target):
         while len(self.rights) <= len(self.hops):
             self.step()
-        target = place(target, self.piece, me)
-        for step in range(1, size):
-            arrived = self.rights[step] + self.lefts[size - step]
-            target = place(target, arrived, lax.rem(me - step + size, size))
+        for hop in range(len(self.rights)):
+            target = self.place_hop(place, target, hop)
         return target
 
 
@@ -604,12 +707,6 @@
 
 def hold(*values):
     return lax.optimization_barrier(values)
-
-
-def in_order(mine, other, upper):
-    return jnp.concatenate(
-        [jnp.where(upper == 0, mine, other), jnp.where(upper == 0, other, mine)], axis=1
-    )
 
 
 def rows_part(weight, index, count):
@@ -696,8 +793,24 @@
     cos_near, sin_near = table(positions[:tok_rows])
 
     upper = lax.axis_index("dp") % 2
-    half_output = lax.all_gather(rows_part(w_output, upper, 2), "tensor", axis=0, tiled=False)
     beside = [(i, i ^ 1) for i in range(lax.axis_size("dp"))]
+    quarters = jnp.stack(
+        [
+            2 * upper + ctx_index,
+            2 * upper + 1 - ctx_index,
+            2 - 2 * upper + ctx_index,
+            3 - 2 * upper - ctx_index,
+        ]
+    ).astype(jnp.int32)
+
+    def quarter_gather(weight):
+        return Gather(rows_part(weight, 2 * upper + ctx_index, 4))
+
+    def quarter_collect(gather):
+        return gather.collect(by_source, jnp.zeros((groups, *gather.piece.shape), BF16))
+
+    output_gather = quarter_gather(w_output)
+    hop = output_gather.step()
 
     kv_own, queries, normed = project(
         tokens,
@@ -707,34 +820,44 @@
         cos_near,
         sin_near,
     )
+    kv_own, queries, normed, hop, quarters = hold(kv_own, queries, normed, hop, quarters)
+    output_gather.held(hop)
     kv_other = lax.ppermute(kv_own, "ctx", over)
-    kv_own, kv_other, sent, kept, normed = hold(
-        kv_own, kv_other, chunk(queries, 1), chunk(queries, 0), normed
-    )
+    hop = output_gather.step()
+    kv_own, kv_other, sent, kept, normed, hop = hold(
+        kv_own, kv_other, chunk(queries, 1), chunk(queries, 0), normed, hop
+    )
+    output_gather.held(hop)
     length = 2 * tok_rows
 
     foreign = lax.ppermute(sent, "ctx", over)
+    hop = output_gather.step()
     first, first_log, *forms = attend_first(metas[0], offsets[0], kept, kv_own, kv_other)
-    first, first_log, foreign, forms = hold(first, first_log, foreign, forms)
+    first, first_log, foreign, forms, hop = hold(first, first_log, foreign, forms, hop)
+    output_gather.held(hop)
     *forms, values_t = forms
     first_whole = lax.all_gather(first, "tensor", axis=0, tiled=False)
 
-    other_output = lax.ppermute(half_output, "dp", beside)
+    output_part = quarter_collect(output_gather)
+    output_over = lax.ppermute(output_part, "ctx", over)
     second, second_log = attend(metas[1], offsets[1], foreign, forms[0], forms[1], values_t)
-    second, second_log, other_output, half_output = hold(
-        second, second_log, other_output, half_output
-    )
-    output_whole = in_order(half_output, other_output, upper)
-
+    second, second_log, output_part, output_over = hold(
+        second, second_log, output_part, output_over
+    )
+
+    output_near = jnp.stack([output_part, output_over])
+    output_far = lax.ppermute(output_near, "dp", beside)
     cos_far, sin_far = table(after(positions[tok_rows:], second))
     cos_pair = jnp.concatenate([cos_near, cos_far], axis=0)
     sin_pair = jnp.concatenate([sin_near, sin_far], axis=0)
     tables = [(chunk(cos_near, 0), chunk(sin_near, 0)), (chunk(cos_far, 1), chunk(sin_far, 1))]
     second_home = lax.ppermute(second, "ctx", over)
-    second_home, first_whole, output_whole, tables, cos_pair, sin_pair = hold(
-        second_home, first_whole, output_whole, tables, cos_pair, sin_pair
+    second_home, output_near, output_far, tables, cos_pair, sin_pair = hold(
+        second_home, output_near, output_far, tables, cos_pair, sin_pair
     )
     second_whole = lax.all_gather(second_home, "tensor", axis=0, tiled=False)
+    output_whole = arrange(quarters, output_near, output_far)
+    output_whole, first_whole = hold(output_whole, first_whole)
     queries = [kept, foreign]
     attention = [first, second]
     log_totals = [first_log, second_log]
@@ -778,7 +901,7 @@
             gradient.astype(BF16), ("dp", "ctx"), scatter_dimension=0, tiled=True
         )
 
-    query_gather = Gather(after(rows_part(w_query, 2 * upper + ctx_index, 4), first_whole))
+    query_gather = quarter_gather(after(w_query, first_whole))
     hop = query_gather.step()
     weights = (w_gate, w_up, w_down)
     fixed = (tokens, cotangent, norm_mlp, output_whole, weights)
@@ -796,27 +919,41 @@
     share_second = line_sum(grad_second)
     hop = query_gather.step()
     w_gates = t_dot(normed_mlp, gates).astype(BF16)
-    w_gates, hop = hold(w_gates, hop)
+    w_gates, hop, share_first = hold(w_gates, hop, share_first)
     query_gather.held(hop)
-    mlp_share = line_sum(after(mlp_part, w_gates))
-
-    query_part = query_gather.collect(
-        by_source, jnp.zeros((groups, w_query.shape[0] // 4, features), BF16)
-    )
-    part_over = lax.ppermute(query_part, "ctx", over)
-    w_downs = t_dot(after(cotangent, w_gates), hidden).astype(BF16)
-    w_downs, share_first, query_part, part_over = hold(
-        w_downs, share_first, query_part, part_over
-    )
 
     gain_first, middle_first, low_first, blocks = to_attention(0, middle, share_first)
-    query_half = in_order(query_part, part_over, ctx_index)
-    gain_first, middle_first, low_first, blocks, query_half = hold(
-        gain_first, middle_first, low_first, blocks, query_half
+    gain_first, middle_first, low_first, blocks, hidden = hold(
+        gain_first, middle_first, low_first, blocks, hidden
     )
 
     came_first = send_blocks(block_of(blocks))
-    other_half = lax.ppermute(query_half, "dp", beside)
+    query_part = quarter_collect(query_gather)
+    query_over = lax.ppermute(query_part, "ctx", over)
+    w_downs = t_dot(cotangent, hidden).astype(BF16)
+    n_part = tok_rows // groups
+    middle_own = lax.dynamic_slice_in_dim(middle, member * n_part, n_part, 0)
+    came_first, middle_own, query_part, query_over, w_downs = hold(
+        came_first, middle_own, query_part, query_over, w_downs
+    )
+
+    def back_arguments(c, grads):
+        return metas[c], offsets[c], queries[c], attention[c], grads, log_totals[c], forms, *tables[c]
+
+    query_near = jnp.stack([query_part, query_over])
+    query_far = lax.ppermute(query_near, "dp", beside)
+    grads_first = stack_blocks(came_first).reshape(span, features)
+    dq_first, dk, dv = attend_back_first(*back_arguments(0, grads_first))
+    dq_first, dk, dv, query_near, query_far, share_second = hold(
+        dq_first, dk, dv, query_near, query_far, share_second
+    )
+
+    gain_second, middle_second, low_second, blocks = to_attention(1, middle, share_second)
+    gain_second, middle_second, low_second, blocks = hold(
+        gain_second, middle_second, low_second, blocks
+    )
+
+    came_second = send_blocks(block_of(blocks), across=True)
     attention_rows = jnp.concatenate(
         [
             lax.dynamic_slice_in_dim(whole, member * share, share, 1)
@@ -825,57 +962,28 @@
         axis=1,
     )
     attention_rows = jnp.swapaxes(attention_rows, 0, 1).reshape(2 * share, groups * features)
-    n_part = tok_rows // groups
-    middle_own = lax.dynamic_slice_in_dim(middle, member * n_part, n_part, 0)
-    came_first, attention_rows, middle_own, query_half, other_half = hold(
-        came_first, attention_rows, middle_own, query_half, other_half
-    )
-    query_whole = in_order(query_half, other_half, upper)
-    grads_first = stack_blocks(came_first).reshape(span, features)
-    query_whole, grads_first, share_second = hold(query_whole, grads_first, share_second)
-
-    gain_second, middle_second, low_second, blocks = to_attention(1, middle, share_second)
-    gain_second, middle_second, low_second, blocks = hold(
-        gain_second, middle_second, low_second, blocks
-    )
-
-    def back_arguments(c, grads):
-        return metas[c], offsets[c], queries[c], attention[c], grads, log_totals[c], forms, *tables[c]
-
-    came_second = send_blocks(block_of(blocks), across=True)
-    dq_first, dk, dv = attend_back_first(*back_arguments(0, grads_first))
-    dq_first, dk, dv, came_second = hold(dq_first, dk, dv, came_second)
+    w_outs = t_dot(jnp.concatenate([low_first, low_second], axis=0), attention_rows).astype(BF16)
+    came_second, w_outs = hold(came_second, w_outs)
+    mlp_share = line_sum(after(mlp_part, came_second))
 
     rows_first = send_blocks(rows_of(dq_first))
     grads_second = stack_blocks(came_second).reshape(span, features)
     dq_second, kv_near, kv_far = attend_back_last(
         *back_arguments(1, grads_second), dk, dv, cos_pair, sin_pair
     )
-    dq_second, kv_near, kv_far, rows_first, mlp_share = hold(
-        dq_second, kv_near, kv_far, rows_first, mlp_share
-    )
-    gate_up_grad = plane_sum(after(w_gates, mlp_share))
+    dq_second, kv_near, kv_far, rows_first = hold(dq_second, kv_near, kv_far, rows_first)
 
     kv_sent = lax.ppermute(kv_far, "ctx", over)
     rows_second = send_blocks(rows_of(dq_second), across=True)
-    dq_home = lax.ppermute(dq_second, "ctx", over)
-    first_part = jnp.einsum(
-        "trq,tdq->rd", stack_blocks(rows_first), query_whole, preferred_element_type=F32
-    )
-    kv_near, kv_sent, rows_second, first_part, dq_home = hold(
-        kv_near, kv_sent, rows_second, first_part, dq_home
-    )
-    mixed_gather = Gather((middle_own + mlp_share.astype(F32)).astype(BF16))
-    mixed_hop = mixed_gather.step()
+    first_part = join(quarters, stack_blocks(rows_first), query_near, query_far)
+    kv_near, kv_sent, rows_second, first_part = hold(kv_near, kv_sent, rows_second, first_part)
     grad_kv_raw = (kv_near + kv_sent.astype(F32)).astype(BF16)
     kv_rows = send_blocks(
         lambda j: jnp.concatenate(
             [lax.dynamic_slice_in_dim(grad_kv_raw, row_of[c][j], share, 0) for c in chunks], axis=0
         )
     )
-    second_part = jnp.einsum(
-        "trq,tdq->rd", stack_blocks(rows_second), query_whole, preferred_element_type=F32
-    )
+    second_part = join(quarters, stack_blocks(rows_second), query_near, query_far)
     first_part, second_part, kv_rows, grad_kv_raw = hold(
         first_part, second_part, kv_rows, grad_kv_raw
     )
@@ -909,16 +1017,27 @@
         return target
 
     gains = jnp.stack([attn_gain, gain_first + gain_second])
-    grad_inputs, gains, low_first = hold(grad_inputs, gains, low_first)
-
-    tokens_gather = Gather(grad_inputs)
-    hop = tokens_gather.step()
-    w_outs = t_dot(jnp.concatenate([low_first, low_second], axis=0), attention_rows).astype(BF16)
+    mixed_share = (middle_own + mlp_share.astype(F32)).astype(BF16)
+    grad_inputs, gains, dq_second, mixed_share, w_gates = hold(
+        grad_inputs, gains, dq_second, mixed_share, w_gates
+    )
+    gate_up_grad = plane_sum(w_gates)
+
+    def put_share(target, piece, source):
+        return lax.dynamic_update_slice_in_dim(target, piece, source * n_part, 0)
+
+    tokens_gather, mixed_gather = Gather(grad_inputs), Gather(mixed_share)
+    tokens_grad = jnp.zeros((tok_rows, width), BF16)
+    mixed = jnp.zeros((tok_rows, width), BF16)
+    hop, mixed_hop = tokens_gather.step(), mixed_gather.step()
+    dq_home = lax.ppermute(dq_second, "ctx", over)
     query_kv = t_dot(
         normed, jnp.concatenate([natural(dq_first, dq_home), grad_kv_raw], axis=1)
     ).astype(BF16)
     rest = jnp.concatenate([w_downs, w_outs, query_kv], axis=1)
-    hop, mixed_hop, rest, gate_up_grad = hold(hop, mixed_hop, rest, gate_up_grad)
+    tokens_grad = tokens_gather.place_hop(put_rows, tokens_grad, 0)
+    mixed = mixed_gather.place_hop(put_share, mixed, 0)
+    hop, mixed_hop, rest, tokens_grad, mixed = hold(hop, mixed_hop, rest, tokens_grad, mixed)
     tokens_gather.held(hop)
     mixed_gather.held(mixed_hop)
     rest = plane_sum(rest)
@@ -927,18 +1046,17 @@
     hop, mixed_hop = tokens_gather.step(), mixed_gather.step()
     for axis, step in steps[:2]:
         gains = pairwise(gains, axis, step)
-    hop, mixed_hop, gains = hold(hop, mixed_hop, gains)
+    tokens_grad = tokens_gather.place_hop(put_rows, tokens_grad, 1)
+    mixed = mixed_gather.place_hop(put_share, mixed, 1)
+    hop, mixed_hop, gains, tokens_grad, mixed = hold(hop, mixed_hop, gains, tokens_grad, mixed)
     tokens_gather.held(hop)
     mixed_gather.held(mixed_hop)
 
     hop, mixed_hop = tokens_gather.step(), mixed_gather.step()
     for axis, step in steps[2:]:
         gains = pairwise(gains, axis, step)
-    hop, mixed_hop, gains, rest = hold(hop, mixed_hop, gains, rest)
-    tokens_gather.held(hop)
-    mixed_gather.held(mixed_hop)
-
-    tokens_grad = tokens_gather.collect(put_rows, jnp.zeros((tok_rows, width), BF16))
+    tokens_grad = tokens_gather.place_hop(put_rows, tokens_grad, 2)
+    mixed = mixed_gather.place_hop(put_share, mixed, 2)
     hidden_units = w_down.shape[1]
     down_grad = rest[:, :hidden_units]
     rest = rest[:, hidden_units:]
@@ -951,12 +1069,17 @@
     kv_blocks = send_blocks(
         lambda j: lax.dynamic_slice_in_dim(kv_plane, j * kv_share, kv_share, 0)
     )
-    mixed = mixed_gather.collect(
-        lambda target, piece, source: lax.dynamic_update_slice_in_dim(
-            target, piece, source * n_part, 0
-        ),
-        jnp.zeros((tok_rows, width), BF16),
-    )
+    hop, mixed_hop, gains, tokens_grad, mixed, output_rows, kv_blocks = hold(
+        hop, mixed_hop, gains, tokens_grad, mixed, output_rows, kv_blocks
+    )
+    tokens_gather.held(hop)
+    mixed_gather.held(mixed_hop)
+    for hop in range(3, groups):
+        while len(tokens_gather.rights) <= hop:
+            tokens_gather.step()
+            mixed_gather.step()
+        tokens_grad = tokens_gather.place_hop(put_rows, tokens_grad, hop)
+        mixed = mixed_gather.place_hop(put_share, mixed, hop)
     output_grad = jnp.sum(stack_blocks(output_rows).astype(F32), axis=0)
 
     kv_blocks = stack_blocks(kv_blocks).astype(F32)

time: 1230 us -> 1200 us (0.976)
  waiting for transfers between devices: 443 us -> 302 us
  starting transfers between devices: 113 us -> 217 us
  local copies, waits for them, and re-layouts: 82.8 us -> 63.4 us
  Pallas kernels: 340 us -> 359 us
  other arithmetic: 127 us -> 110 us
  between operations: 35.1 us -> 50.8 us
    all_gather x1 -> x0, waiting for transfers between devices: 51.9 us -> none  [body(): lax.all_gather(rows_part(w_output, upper, 2), 'tensor', axis=0, tiled=False)]
    ppermute x8, starting transfers between devices: 35.4 us -> 75.9 us  [send_blocks(): lax.ppermute(block, ('ctx', 'tensor'), [(c * size + i, (1 - c) * size + (...]
    ppermute x8, waiting for transfers between devices: 54.8 us -> 15.1 us  [send_blocks(): lax.ppermute(block, ('ctx', 'tensor'), [(c * size + i, (1 - c) * size + (...]
    ppermute x15, waiting for transfers between devices: 68.1 us -> 34.6 us  [send_blocks(): lax.ppermute(block, 'tensor', [(i, (i + shift) % size) for i in range(siz...]
    pallas_call x1, Pallas kernels: 48.9 us -> 81.8 us  [attend_back_last(): pl.pallas_call(kernel, grid_spec=pltpu.PrefetchScalarGridSpec(num_scalar_...]
    ppermute x3 -> x4, starting transfers between devices: 1.79 us -> 34.4 us  [the longest x1 32.9 us: body(): output_over = lax.ppermute(output_part, 'ctx', over)]
    pallas_call x1, Pallas kernels: 66.9 us -> 34.5 us  [attend_back_first(): pl.pallas_call(kernel, grid_spec=pltpu.PrefetchScalarGridSpec(num_scalar_...]
    ppermute x1, waiting for transfers between devices: 0.01 us -> 28.8 us  [body(): dq_home = lax.ppermute(dq_second, 'ctx', over)]
  transfers between devices with their start and end apart: 62 -> 68, of which waited for: 17 -> 21; matrix products, arithmetic and copies ran while one was open for 22% -> 18% of each run, Pallas kernels for 28% -> 30%
where the time goes in v3:
time: 1200 us; the launch traced here: 1190 us
  Pallas kernels  359 us (30%)
  waiting for transfers between devices  302 us (25%)
  starting transfers between devices  217 us (18%)
  other arithmetic  110 us (9%)
  matrix products  84.1 us (7%)
  local copies, waits for them, and re-layouts  63.4 us (5%)
  between operations  50.8 us (4%)
    pallas_call x2, Pallas kernels, feed_forward(): pl.pallas_call(feed_kernel, grid=(2 * quarter,), in_specs=[pl.BlockSpec((...  123 us
    ppermute x12, waiting for transfers between devices, step(): self.lefts.append(lax.ppermute(self.lefts[-1], 'tensor', to_left))  89.3 us
    pallas_call x1, Pallas kernels, attend_back_last(): pl.pallas_call(kernel, grid_spec=pltpu.PrefetchScalarGridSpec(num_scalar_...  81.8 us
    ppermute x5, waiting for transfers between devices, pairwise(): lax.ppermute(value, axis, [(i, i ^ step) for i in range(size)])  81.6 us
    ppermute x8, starting transfers between devices, send_blocks(): lax.ppermute(block, ('ctx', 'tensor'), [(c * size + i, (1 - c) * size + (...  75.9 us
    dot_general x4, matrix products, t_dot(): return jnp.einsum('rd,rf->df', a, b, preferred_element_type=F32)  69.6 us
    pallas_call x1, Pallas kernels, attend(): pl.pallas_call(kernel, grid_spec=pltpu.PrefetchScalarGridSpec(num_scalar_...  57.1 us
    ppermute x15, starting transfers between devices, send_blocks(): lax.ppermute(block, 'tensor', [(i, (i + shift) % size) for i in range(siz...  43.5 us
  transfers between devices with their start and end apart: 68, of which 21 were waited for; matrix products, arithmetic and copies ran while one was open for 18% of the time, Pallas kernels for 30%

profile of v3, /device:TPU:0, one launch (start us, length us, event | category | flops | bytes accessed | tf_op | source)
XLA Modules:
  0.0 1187.7 jit_solution(13027811895520014843)
XLA Ops:
  10.6 5.7 collective-permute-start
  18.0 5.4 multiply_sine_fusion.1
  24.5 4.8 fusion.53
  29.6 5.7 pad_maximum_fusion.4
  35.3 15.3 %project.1 = (bf16[2048,128]{1,0:T(8,128)(2,1)S(1)}, bf16[2048,512]{1,0:T(8,128)(2,1)S(1)}, bf16[2048,2048]{1,0:T(8,128)(2,1)}) custom-call(bf16[2048,2048]{1,0:T(8,128)(2,1)} %tokens_ref.5, f32[1,2048]{1,0:T(1,128)S(1)} %bitcast.179, bf16[2048,128]{1,0:T(8,128)(2,1)S(1)} %pad_maximum_fusion.13.kv_weight, bf16[2048,512]{1,0:T(8,128)(2,1)} %q_weight.1, ...), custom_call_target="tpu_custom_call" | custom-call | flops 1 | bytes 1 | tf_op jit(solution)/shard_map/project/pallas_call | solution.py:47
  59.2 5.9 collective-permute-done.2.other
  65.1 6.3 collective-permute-done.4
  74.0 27.7 %attend_first.1 = (bf16[1024,512]{1,0:T(8,128)(2,1)}, f32[4,8,1024]{2,1,0:T(8,128)}, bf16[4096,128]{1,0:T(8,128)(2,1)}, bf16[4096,128]{1,0:T(8,128)(2,1)}, bf16[...) custom-call(s32[6]{0:T(128)} %get-tuple-element.492.meta.refs_0_, ...), custom_call_target="tpu_custom_call" | custom-call | flops 17179869184 | bytes 8388608 | tf_op jit(solution)/shard_map/attend_first/pallas_call | solution.py:179
  105.6 32.9 %collective-permute-start.8 = (bf16[4,512,512]{2,1,0:T(8,128)(2,1)}, bf16[4,512,512]{2,1,0:T(8,128)(2,1)}, u32[]{:S(2)}, u32[]{:S(2)}) collective-permute-start(bf16[4,512,512]{2,1,0:T(8,128)(2,1)} %bitcast_dynamic-update-slice_fusion.5), channel_id=1, source_target_pairs={{0,4},{4,0},{1,5},{5,1},{2,6},{6,2},{3,7},{7,3},{8,12},{12,8},{9,1... | collective-permute-start | bytes 6291464 | tf_op jit(solution)/shard_map/ppermute | solution.py:842
  138.6 57.1 %attend.1 = (bf16[1024,512]{1,0:T(8,128)(2,1)}, f32[4,8,1024]{2,1,0:T(8,128)}) custom-call(s32[6]{0:T(128)} %get-tuple-element.491.refs_0_, bf16[1024,512]{1,0:T(8,128)(2,1)} %collective-permute-done.5.refs_1_, bf16[4096,128]{1,0:T(8,128)(2,1)} %get-tuple-element.218.refs_2_.refs_5_, bf16[4096,128]{1,0:T(8,128)(2,1)} %get-tuple-element.219.refs_3_.refs_6_, ...), custom_call_target="tpu_custom_call" | custom-call | flops 17179869184 | bytes 8388608 | tf_op jit(solution)/shard_map/attend/pallas_call | solution.py:216
  195.7 4.6 pad_maximum_fusion.1.near_ref
  202.1 3.7 multiply_sine_fusion
  208.8 3.0 maximum_maximum_fusion.1.refs_15_
  211.8 3.1 maximum_maximum_fusion.refs_14_
  214.8 12.9 %collective-permute-done.9 = bf16[1024,512]{1,0:T(8,128)(2,1)S(1)} collective-permute-done((bf16[1024,512]{1,0:T(8,128)(2,1)S(1)}, bf16[1024,512]{1,0:T(8,128)(2,1)S(1)}, u32[]{:S(2)}, u32[]{:S(2)}) %collective-permute-start.9) | collective-permute-done | bytes 1048608 | tf_op jit(solution)/shard_map/ppermute | solution.py:854
  228.7 5.8 arrange.1.output_weight
  234.6 3.4 copy-done
  239.3 3.6 collective-permute-start.11
  248.8 61.4 %feed_forward.2 = (f32[2048,2048]{1,0:T(8,128)}, bf16[2048,2048]{1,0:T(8,128)(2,1)}, bf16[2048,1408]{1,0:T(8,128)(2,1)}, bf16[2048,2816]{1,0:T(8,128)(2,1)}, bf1...) custom-call(bf16[4,1024,512]{2,1,0:T(8,128)(2,1)} %bitcast.191, bf16[2048,2048]{1,0:T(8,128)(2,1)} %tokens_ref.5, ...), custom_call_target="tpu_custom_call" | custom-call | flops 1 | bytes 1 | tf_op jit(solution)/shard_map/feed_forward/pallas_call | solution.py:494
  310.2 7.8 all-gather.7.cloned.1.call-done
  320.8 62.0 %feed_forward.3 = (f32[2048,2048]{1,0:T(8,128)}, bf16[2048,2048]{1,0:T(8,128)(2,1)}, bf16[2048,1408]{1,0:T(8,128)(2,1)}, bf16[2048,2816]{1,0:T(8,128)(2,1)}, bf1...) custom-call(bf16[4,1024,512]{2,1,0:T(8,128)(2,1)} %bitcast.193, ...), custom_call_target="tpu_custom_call", output_to_operand_aliasing={{0}: (8, {}), {1}: (9, {}), {2}: (10, {}), {3}: (11, {}), {... | custom-call | flops 1 | bytes 1 | tf_op jit(solution)/shard_map/feed_forward/pallas_call | solution.py:494
  387.5 32.0 %convolution_convert_fusion = bf16[2048,2816]{1,0:T(8,128)(2,1)} fusion(bf16[2048,2048]{1,0:T(8,128)(2,1)} %get-tuple-element.258, bf16[2048,2816]{1,0:T(8,128)(2,1)} %get-tuple-element.259), kind=kOutput, calls=%fused_computation.1 | convolution fusion | flops 23628087296 | bytes 31457280 | tf_op jit(solution)/shard_map/rd,rf->df/dot_general | solution.py:730
  422.2 4.7 constant_dynamic-slice_fusion.33
  432.1 3.9 fusion.49
  435.9 6.2 fusion.39
  443.1 3.3 collective-permute-start.17
  453.0 19.2 %fusion = bf16[2048,1408]{1,0:T(8,128)(2,1)} fusion(bf16[2048,1408]{1,0:T(8,128)(2,1)} %get-tuple-element.270, bf16[2048,2048]{1,0:T(8,128)(2,1)} %cotangent_ref.3), kind=kOutput, calls=%fused_computation.8 | convolution fusion | flops 11814043648 | bytes 19922944 | tf_op jit(solution)/shard_map/rd,rf->df/dot_general | solution.py:730
  472.3 8.1 collective-permute-done.18
  480.8 4.1 pad_maximum_fusion.2.near_ref
  492.0 34.5 %attend_back_first.1 = (bf16[1024,512]{1,0:T(8,128)(2,1)}, f32[4096,128]{1,0:T(8,128)}, f32[4096,128]{1,0:T(8,128)}) custom-call(s32[6]{0:T(128)} %get-tuple-element.492.meta.refs_0_, bf16[1024,512]{1,0:T(8,128)(2,1)} %pad_maximum_fusion.6.q_ref.refs_1_, bf16[1024,512]{1,0:T(8,128)(2,1)} %get-tuple-element.233.refs_2_, bf16[1024,512]{1,0:T(8,128)(2,1)} %bitcast.197, ...), custom_call_target="tpu_custom_call" | custom-call | flops 1 | bytes 1 | tf_op jit(solution)/shard_map/attend_back_first/pallas_call | solution.py:352
  529.2 3.9 fusion.47
  533.1 6.1 fusion.40
  539.5 45.0 %collective-permute-start.22 = (bf16[256,512]{1,0:T(8,128)(2,1)S(1)}, bf16[256,512]{1,0:T(8,128)(2,1)S(1)}, u32[]{:S(2)}, u32[]{:S(2)}) collective-permute-start(bf16[256,512]{1,0:T(8,128)(2,1)S(1)} %bitcast.203), channel_id=1, source_target_pairs={{0,4},{1,5},{2,6},{3,7},{4,0},{5,1},{6,2},{7,3},{8,12},{9,13},{10,... | collective-permute-start | bytes 786440 | tf_op jit(solution)/shard_map/ppermute | solution.py:669
  585.4 19.1 %collective-permute-start.23 = (bf16[256,512]{1,0:T(8,128)(2,1)}, bf16[256,512]{1,0:T(8,128)(2,1)S(1)}, u32[]{:S(2)}, u32[]{:S(2)}) collective-permute-start(bf16[256,512]{1,0:T(8,128)(2,1)} %bitcast.204), channel_id=1, source_target_pairs={{0,5},{1,6},{2,7},{3,4},{4,1},{5,2},{6,3},{7,0},{8,13},{9,14},{10,... | collective-permute-start | bytes 786440 | tf_op jit(solution)/shard_map/ppermute | solution.py:669
  605.3 4.4 collective-permute-start.24
  610.5 8.4 convolution_convert_fusion.1
  649.3 81.8 %attend_back_last.1 = (bf16[1024,512]{1,0:T(8,128)(2,1)}, f32[2048,128]{1,0:T(8,128)}, bf16[2048,128]{1,0:T(8,128)(2,1)}) custom-call(s32[6]{0:T(128)} %get-tuple-element.491.refs_0_, bf16[1024,512]{1,0:T(8,128)(2,1)} %collective-permute-done.5.refs_1_, bf16[1024,512]{1,0:T(8,128)(2,1)} %get-tuple-element.225.refs_2_, bf16[1024,512]{1,0:T(8,128)(2,1)} %bitcast.198, ...), custom_call_target="tpu_custom_call" | custom-call | flops 1 | bytes 1 | tf_op jit(solution)/shard_map/attend_back_last/pallas_call | solution.py:407
  736.0 3.8 collective-permute-start.33
  743.0 7.0 join.2
  750.0 12.6 %collective-permute-done.32 = bf16[256,512]{1,0:T(8,128)(2,1)S(1)} collective-permute-done((bf16[256,512]{1,0:T(8,128)(2,1)S(1)}, bf16[256,512]{1,0:T(8,128)(2,1)S(1)}, u32[]{:S(2)}, u32[]{:S(2)}) %collective-permute-start.32) | collective-permute-done | bytes 262176 | tf_op jit(solution)/shard_map/ppermute | solution.py:669
  763.9 24.6 %collective-permute-start.36 = (bf16[512,128]{1,0:T(8,128)(2,1)S(1)}, bf16[512,128]{1,0:T(8,128)(2,1)S(1)}, u32[]{:S(2)}, u32[]{:S(2)}) collective-permute-start(bf16[512,128]{1,0:T(8,128)(2,1)S(1)} %pad_maximum_fusion.19), channel_id=1, source_target_pairs={{0,3},{1,0},{2,1},{3,2},{4,7},{5,4},{6,5},{7,6},{8,11},{9,8},{10,9... | collective-permute-start | bytes 393224 | tf_op jit(solution)/shard_map/ppermute | solution.py:679
  789.5 6.8 join.3
  796.4 9.8 collective-permute-done.35
  808.7 3.4 fusion.4
  813.0 3.5 add_convert_fusion
  818.7 10.6 collective-permute-start.37
  830.6 5.9 collective-permute-start.39
  846.7 28.8 %collective-permute-done.41 = bf16[1024,512]{1,0:T(8,128)(2,1)} collective-permute-done((bf16[1024,512]{1,0:T(8,128)(2,1)S(1)}, bf16[1024,512]{1,0:T(8,128)(2,1)}, u32[]{:S(2)}, u32[]{:S(2)}) %collective-permute-start.41) | collective-permute-done | bytes 1048608 | tf_op jit(solution)/shard_map/ppermute | solution.py:1033
  875.6 9.9 convolution_convert_fusion.3
  885.6 7.0 pad_maximum_fusion
  892.6 25.3 %collective-permute-done.39 = bf16[512,2048]{1,0:T(8,128)(2,1)} collective-permute-done((bf16[512,2048]{1,0:T(8,128)(2,1)S(1)}, bf16[512,2048]{1,0:T(8,128)(2,1)}, u32[]{:S(2)}, u32[]{:S(2)}) %collective-permute-start.39) | collective-permute-done | bytes 2097184 | tf_op jit(solution)/shard_map/ppermute | solution.py:629
  918.0 5.6 collective-permute-done.40
  956.2 3.7 select_dynamic-update-slice_fusion.2
  959.9 33.2 %collective-permute-done.43 = bf16[512,2048]{1,0:T(8,128)(2,1)} collective-permute-done((bf16[512,2048]{1,0:T(8,128)(2,1)}, bf16[512,2048]{1,0:T(8,128)(2,1)}, u32[]{:S(2)}, u32[]{:S(2)}) %collective-permute-start.43) | collective-permute-done | bytes 2097184 | tf_op jit(solution)/shard_map/ppermute | solution.py:630
  993.1 44.1 %collective-permute-done.45 = bf16[512,2048]{1,0:T(8,128)(2,1)} collective-permute-done((bf16[512,2048]{1,0:T(8,128)(2,1)}, bf16[512,2048]{1,0:T(8,128)(2,1)}, u32[]{:S(2)}, u32[]{:S(2)}) %collective-permute-start.45) | collective-permute-done | bytes 2097184 | tf_op jit(solution)/shard_map/ppermute | solution.py:630
  1047.2 4.2 select_dynamic-update-slice_fusion.1
  1051.4 5.4 collective-permute-start.53
  1057.8 76.9 %collective-permute-done.53 = f32[2,2048]{1,0:T(2,128)S(1)} collective-permute-done((f32[2,2048]{1,0:T(2,128)S(1)}, f32[2,2048]{1,0:T(2,128)S(1)}, u32[]{:S(2)}, u32[]{:S(2)}) %collective-permute-start.53) | collective-permute-done | bytes 16416 | tf_op jit(solution)/shard_map/ppermute | solution.py:695
  1135.9 3.5 collective-permute-done.54
  1139.5 3.1 slice_convert_fusion.1
  1144.1 3.8 collective-permute-start.57
  1151.1 11.9 collective-permute-done.58
  1164.1 4.3 collective-permute-done.59
  1176.2 4.1 select_dynamic-update-slice_fusion
  (394 shorter events, 150.9 us)
Async XLA Ops:
  7.2 230.8 %all-gather.5.cloned.1.call-start = ((), (), s32[]{:S(2)}) async-start(), calls=%async_computation.10 | async-start | bytes 5242880 | tf_op jit(solution)/shard_map/all_gather | solution.py:839
  10.6 40.9 %collective-permute-start = (bf16[512,512]{1,0:T(8,128)(2,1)S(1)}, bf16[512,512]{1,0:T(8,128)(2,1)}, u32[]{:S(2)}, u32[]{:S(2)}) collective-permute-start(bf16[512,512]{1,0:T(8,128)(2,1)S(1)} %get-tuple-element.388), channel_id=1, source_target_pairs={{0,1},{1,2},{2,3},{4,5},{5,6},{6,7},{8,9},{9,10},{10,11},{12,13},{... | collective-permute-start | bytes 1572872 | tf_op jit(solution)/shard_map/ppermute | solution.py:629
  16.4 35.2 %collective-permute-start.1 = (bf16[512,512]{1,0:T(8,128)(2,1)S(1)}, bf16[512,512]{1,0:T(8,128)(2,1)}, u32[]{:S(2)}, u32[]{:S(2)}) collective-permute-start(bf16[512,512]{1,0:T(8,128)(2,1)S(1)} %get-tuple-element.388), channel_id=1, source_target_pairs={{1,0},{2,1},{3,2},{5,4},{6,5},{7,6},{9,8},{10,9},{11,10},{13,12},{... | collective-permute-start | bytes 1572872 | tf_op jit(solution)/shard_map/ppermute | solution.py:630
  51.7 13.4 %collective-permute-start.2 = (bf16[2048,128]{1,0:T(8,128)(2,1)S(1)}, bf16[2048,128]{1,0:T(8,128)(2,1)S(1)}, u32[]{:S(2)}, u32[]{:S(2)}) collective-permute-start(bf16[2048,128]{1,0:T(8,128)(2,1)S(1)} %get-tuple-element.204.own), channel_id=1, source_target_pairs={{0,4},{4,0},{1,5},{5,1},{2,6},{6,2},{3,7},{7,3},{8,12},{12,8},{9,1... | collective-permute-start | bytes 1572872 | tf_op jit(solution)/shard_map/ppermute | solution.py:825
  53.2 11.9 %collective-permute-start.3 = (bf16[512,512]{1,0:T(8,128)(2,1)}, bf16[512,512]{1,0:T(8,128)(2,1)S(1)}, u32[]{:S(2)}, u32[]{:S(2)}) collective-permute-start(bf16[512,512]{1,0:T(8,128)(2,1)} %collective-permute-done), channel_id=1, source_target_pairs={{1,2},{2,3},{5,6},{6,7},{9,10},{10,11},{13,14},{14,15},{17,18},{18... | collective-permute-start | bytes 1572872 | tf_op jit(solution)/shard_map/ppermute | solution.py:629
  53.9 17.5 %collective-permute-start.4 = (bf16[512,512]{1,0:T(8,128)(2,1)}, bf16[512,512]{1,0:T(8,128)(2,1)S(1)}, u32[]{:S(2)}, u32[]{:S(2)}) collective-permute-start(bf16[512,512]{1,0:T(8,128)(2,1)} %collective-permute-done.1), channel_id=1, source_target_pairs={{1,0},{2,1},{5,4},{6,5},{9,8},{10,9},{13,12},{14,13},{17,16},{18,1... | collective-permute-start | bytes 1572872 | tf_op jit(solution)/shard_map/ppermute | solution.py:630
  71.5 31.2 %collective-permute-start.5 = (bf16[1024,512]{1,0:T(8,128)(2,1)S(1)}, bf16[1024,512]{1,0:T(8,128)(2,1)}, u32[]{:S(2)}, u32[]{:S(2)}) collective-permute-start(bf16[1024,512]{1,0:T(8,128)(2,1)S(1)} %slice.172), channel_id=1, source_target_pairs={{0,4},{4,0},{1,5},{5,1},{2,6},{6,2},{3,7},{7,3},{8,12},{12,8},{9,1... | collective-permute-start | bytes 3145736 | tf_op jit(solution)/shard_map/ppermute | solution.py:833
  72.0 30.7 %collective-permute-start.6 = (bf16[512,512]{1,0:T(8,128)(2,1)S(1)}, bf16[512,512]{1,0:T(8,128)(2,1)S(1)}, u32[]{:S(2)}, u32[]{:S(2)}) collective-permute-start(bf16[512,512]{1,0:T(8,128)(2,1)S(1)} %collective-permute-done.3), channel_id=1, source_target_pairs={{2,3},{6,7},{10,11},{14,15},{18,19},{22,23},{26,27},{30,31}} | collective-permute-start | bytes 1572872 | tf_op jit(solution)/shard_map/ppermute | solution.py:629
  72.7 30.0 %collective-permute-start.7 = (bf16[512,512]{1,0:T(8,128)(2,1)S(1)}, bf16[512,512]{1,0:T(8,128)(2,1)S(1)}, u32[]{:S(2)}, u32[]{:S(2)}) collective-permute-start(bf16[512,512]{1,0:T(8,128)(2,1)S(1)} %collective-permute-done.4), channel_id=1, source_target_pairs={{1,0},{5,4},{9,8},{13,12},{17,16},{21,20},{25,24},{29,28}} | collective-permute-start | bytes 1572872 | tf_op jit(solution)/shard_map/ppermute | solution.py:630
  105.6 90.1 %collective-permute-start.8 = (bf16[4,512,512]{2,1,0:T(8,128)(2,1)}, bf16[4,512,512]{2,1,0:T(8,128)(2,1)}, u32[]{:S(2)}, u32[]{:S(2)}) collective-permute-start(bf16[4,512,512]{2,1,0:T(8,128)(2,1)} %bitcast_dynamic-update-slice_fusion.5), channel_id=1, source_target_pairs={{0,4},{4,0},{1,5},{5,1},{2,6},{6,2},{3,7},{7,3},{8,12},{12,8},{9,1... | collective-permute-start | bytes 6291464 | tf_op jit(solution)/shard_map/ppermute | solution.py:842
  138.5 179.5 %all-gather.7.cloned.1.call-start = ((), (), s32[]{:S(2)}) async-start(), calls=%async_computation.11 | async-start | bytes 5242880 | tf_op jit(solution)/shard_map/all_gather | solution.py:858
  200.4 27.3 %collective-permute-start.10 = (bf16[2,4,512,512]{3,2,1,0:T(8,128)(2,1)}, bf16[2,4,512,512]{3,2,1,0:T(8,128)(2,1)}, u32[]{:S(2)}, u32[]{:S(2)}) collective-permute-start(bf16[2,4,512,512]{3,2,1,0:T(8,128)(2,1)} %pad_maximum_fusion.1.near_ref), channel_id=1, source_target_pairs={{0,8},{8,0},{16,24},{24,16},{1,9},{9,1},{17,25},{25,17},{2,10},{10... | collective-permute-start | bytes 12582920 | tf_op jit(solution)/shard_map/ppermute | solution.py:849
  202.1 25.6 %collective-permute-start.9 = (bf16[1024,512]{1,0:T(8,128)(2,1)S(1)}, bf16[1024,512]{1,0:T(8,128)(2,1)S(1)}, u32[]{:S(2)}, u32[]{:S(2)}) collective-permute-start(bf16[1024,512]{1,0:T(8,128)(2,1)S(1)} %copy-done.31), channel_id=1, source_target_pairs={{0,4},{4,0},{1,5},{5,1},{2,6},{6,2},{3,7},{7,3},{8,12},{12,8},{9,1... | collective-permute-start | bytes 3145736 | tf_op jit(solution)/shard_map/ppermute | solution.py:854
  228.7 198.3 %reduce-scatter.6.cloned.1.call-start = ((), (), s32[]{:S(2)}) async-start(), calls=%async_computation.5 | async-start | bytes 5242880 | tf_op jit(solution)/shard_map/reduce_scatter | solution.py:897
  239.3 70.9 %collective-permute-start.11 = (bf16[512,512]{1,0:T(8,128)(2,1)S(1)}, bf16[512,512]{1,0:T(8,128)(2,1)S(1)}, u32[]{:S(2)}, u32[]{:S(2)}) collective-permute-start(bf16[512,512]{1,0:T(8,128)(2,1)S(1)} %get-tuple-element.384), channel_id=1, source_target_pairs={{0,1},{1,2},{2,3},{4,5},{5,6},{6,7},{8,9},{9,10},{10,11},{12,13},{... | collective-permute-start | bytes 1572872 | tf_op jit(solution)/shard_map/ppermute | solution.py:629
  242.8 67.3 %collective-permute-start.12 = (bf16[512,512]{1,0:T(8,128)(2,1)S(1)}, bf16[512,512]{1,0:T(8,128)(2,1)}, u32[]{:S(2)}, u32[]{:S(2)}) collective-permute-start(bf16[512,512]{1,0:T(8,128)(2,1)S(1)} %get-tuple-element.384), channel_id=1, source_target_pairs={{1,0},{2,1},{3,2},{5,4},{6,5},{7,6},{9,8},{10,9},{11,10},{13,12},{... | collective-permute-start | bytes 1572872 | tf_op jit(solution)/shard_map/ppermute | solution.py:630
  318.0 66.2 %collective-permute-start.13 = (bf16[512,512]{1,0:T(8,128)(2,1)S(1)}, bf16[512,512]{1,0:T(8,128)(2,1)}, u32[]{:S(2)}, u32[]{:S(2)}) collective-permute-start(bf16[512,512]{1,0:T(8,128)(2,1)S(1)} %collective-permute-done.11), channel_id=1, source_target_pairs={{1,2},{2,3},{5,6},{6,7},{9,10},{10,11},{13,14},{14,15},{17,18},{18... | collective-permute-start | bytes 1572872 | tf_op jit(solution)/shard_map/ppermute | solution.py:629
  319.5 64.7 %collective-permute-start.14 = (bf16[512,512]{1,0:T(8,128)(2,1)}, bf16[512,512]{1,0:T(8,128)(2,1)}, u32[]{:S(2)}, u32[]{:S(2)}) collective-permute-start(bf16[512,512]{1,0:T(8,128)(2,1)} %collective-permute-done.12), channel_id=1, source_target_pairs={{1,0},{2,1},{5,4},{6,5},{9,8},{10,9},{13,12},{14,13},{17,16},{18,1... | collective-permute-start | bytes 1572872 | tf_op jit(solution)/shard_map/ppermute | solution.py:630
  320.8 205.8 %reduce-scatter.8.cloned.1.call-start = ((), (), s32[]{:S(2)}) async-start(), calls=%async_computation.6 | async-start | bytes 5242880 | tf_op jit(solution)/shard_map/reduce_scatter | solution.py:897
  384.2 42.7 %collective-permute-start.15 = (bf16[512,512]{1,0:T(8,128)(2,1)}, bf16[512,512]{1,0:T(8,128)(2,1)S(1)}, u32[]{:S(2)}, u32[]{:S(2)}) collective-permute-start(bf16[512,512]{1,0:T(8,128)(2,1)} %collective-permute-done.13), channel_id=1, source_target_pairs={{2,3},{6,7},{10,11},{14,15},{18,19},{22,23},{26,27},{30,31}} | collective-permute-start | bytes 1572872 | tf_op jit(solution)/shard_map/ppermute | solution.py:629
  384.9 42.0 %collective-permute-start.16 = (bf16[512,512]{1,0:T(8,128)(2,1)}, bf16[512,512]{1,0:T(8,128)(2,1)}, u32[]{:S(2)}, u32[]{:S(2)}) collective-permute-start(bf16[512,512]{1,0:T(8,128)(2,1)} %collective-permute-done.14), channel_id=1, source_target_pairs={{1,0},{5,4},{9,8},{13,12},{17,16},{21,20},{25,24},{29,28}} | collective-permute-start | bytes 1572872 | tf_op jit(solution)/shard_map/ppermute | solution.py:630
  419.6 393.5 %reduce-scatter.10.cloned.1.call-start = ((), (), s32[]{:S(2)}) async-start(), calls=%async_computation.7 | async-start | bytes 10485760 | tf_op jit(solution)/shard_map/reduce_scatter | solution.py:897
  428.3 52.5 %collective-permute-start.20 = (bf16[4,512,512]{2,1,0:T(8,128)(2,1)S(1)}, bf16[4,512,512]{2,1,0:T(8,128)(2,1)}, u32[]{:S(2)}, u32[]{:S(2)}) collective-permute-start(bf16[4,512,512]{2,1,0:T(8,128)(2,1)S(1)} %bitcast_dynamic-update-slice_fusion), channel_id=1, source_target_pairs={{0,4},{4,0},{1,5},{5,1},{2,6},{6,2},{3,7},{7,3},{8,12},{12,8},{9,1... | collective-permute-start | bytes 6291464 | tf_op jit(solution)/shard_map/ppermute | solution.py:932
  443.1 29.2 %collective-permute-start.17 = (bf16[256,512]{1,0:T(8,128)(2,1)}, bf16[256,512]{1,0:T(8,128)(2,1)S(1)}, u32[]{:S(2)}, u32[]{:S(2)}) collective-permute-start(bf16[256,512]{1,0:T(8,128)(2,1)} %bitcast.24), channel_id=1, source_target_pairs={{0,1},{1,2},{2,3},{3,0},{4,5},{5,6},{6,7},{7,4},{8,9},{9,10},{10,1... | collective-permute-start | bytes 786440 | tf_op jit(solution)/shard_map/ppermute | solution.py:679
  447.2 33.2 %collective-permute-start.18 = (bf16[256,512]{1,0:T(8,128)(2,1)}, bf16[256,512]{1,0:T(8,128)(2,1)S(1)}, u32[]{:S(2)}, u32[]{:S(2)}) collective-permute-start(bf16[256,512]{1,0:T(8,128)(2,1)} %bitcast.207), channel_id=1, source_target_pairs={{0,2},{1,3},{2,0},{3,1},{4,6},{5,7},{6,4},{7,5},{8,10},{9,11},{10,... | collective-permute-start | bytes 786440 | tf_op jit(solution)/shard_map/ppermute | solution.py:679
  450.1 30.8 %collective-permute-start.19 = (bf16[256,512]{1,0:T(8,128)(2,1)}, bf16[256,512]{1,0:T(8,128)(2,1)S(1)}, u32[]{:S(2)}, u32[]{:S(2)}) collective-permute-start(bf16[256,512]{1,0:T(8,128)(2,1)} %bitcast.26), channel_id=1, source_target_pairs={{0,3},{1,0},{2,1},{3,2},{4,7},{5,4},{6,5},{7,6},{8,11},{9,8},{10,9... | collective-permute-start | bytes 786440 | tf_op jit(solution)/shard_map/ppermute | solution.py:679
  484.9 41.7 %collective-permute-start.21 = (bf16[2,4,512,512]{3,2,1,0:T(8,128)(2,1)}, bf16[2,4,512,512]{3,2,1,0:T(8,128)(2,1)}, u32[]{:S(2)}, u32[]{:S(2)}) collective-permute-start(bf16[2,4,512,512]{3,2,1,0:T(8,128)(2,1)} %pad_maximum_fusion.2.near_ref), channel_id=1, source_target_pairs={{0,8},{8,0},{16,24},{24,16},{1,9},{9,1},{17,25},{25,17},{2,10},{10... | collective-permute-start | bytes 12582920 | tf_op jit(solution)/shard_map/ppermute | solution.py:944
  539.5 79.5 %collective-permute-start.22 = (bf16[256,512]{1,0:T(8,128)(2,1)S(1)}, bf16[256,512]{1,0:T(8,128)(2,1)S(1)}, u32[]{:S(2)}, u32[]{:S(2)}) collective-permute-start(bf16[256,512]{1,0:T(8,128)(2,1)S(1)} %bitcast.203), channel_id=1, source_target_pairs={{0,4},{1,5},{2,6},{3,7},{4,0},{5,1},{6,2},{7,3},{8,12},{9,13},{10,... | collective-permute-start | bytes 786440 | tf_op jit(solution)/shard_map/ppermute | solution.py:669
  585.4 33.6 %collective-permute-start.23 = (bf16[256,512]{1,0:T(8,128)(2,1)}, bf16[256,512]{1,0:T(8,128)(2,1)S(1)}, u32[]{:S(2)}, u32[]{:S(2)}) collective-permute-start(bf16[256,512]{1,0:T(8,128)(2,1)} %bitcast.204), channel_id=1, source_target_pairs={{0,5},{1,6},{2,7},{3,4},{4,1},{5,2},{6,3},{7,0},{8,13},{9,14},{10,... | collective-permute-start | bytes 786440 | tf_op jit(solution)/shard_map/ppermute | solution.py:669
  605.3 13.7 %collective-permute-start.24 = (bf16[256,512]{1,0:T(8,128)(2,1)}, bf16[256,512]{1,0:T(8,128)(2,1)S(1)}, u32[]{:S(2)}, u32[]{:S(2)}) collective-permute-start(bf16[256,512]{1,0:T(8,128)(2,1)} %bitcast.205), channel_id=1, source_target_pairs={{0,6},{1,7},{2,4},{3,5},{4,2},{5,3},{6,0},{7,1},{8,14},{9,15},{10,... | collective-permute-start | bytes 786440 | tf_op jit(solution)/shard_map/ppermute | solution.py:669
  621.2 518.3 %reduce-scatter.14.cloned.1.call-start = ((), (), s32[]{:S(2)}) async-start(), calls=%async_computation.9 | async-start | bytes 12976128 | tf_op jit(solution)/shard_map/reduce_scatter | solution.py:900
  644.2 86.9 %collective-permute-start.26 = (bf16[256,512]{1,0:T(8,128)(2,1)}, bf16[256,512]{1,0:T(8,128)(2,1)}, u32[]{:S(2)}, u32[]{:S(2)}) collective-permute-start(bf16[256,512]{1,0:T(8,128)(2,1)} %get-tuple-element.421), channel_id=1, source_target_pairs={{0,1},{1,2},{2,3},{3,0},{4,5},{5,6},{6,7},{7,4},{8,9},{9,10},{10,1... | collective-permute-start | bytes 786440 | tf_op jit(solution)/shard_map/ppermute | solution.py:679
  644.9 86.3 %collective-permute-start.27 = (bf16[256,512]{1,0:T(8,128)(2,1)S(1)}, bf16[256,512]{1,0:T(8,128)(2,1)}, u32[]{:S(2)}, u32[]{:S(2)}) collective-permute-start(bf16[256,512]{1,0:T(8,128)(2,1)S(1)} %get-tuple-element.420), channel_id=1, source_target_pairs={{0,2},{1,3},{2,0},{3,1},{4,6},{5,7},{6,4},{7,5},{8,10},{9,11},{10,... | collective-permute-start | bytes 786440 | tf_op jit(solution)/shard_map/ppermute | solution.py:679
  646.7 84.5 %collective-permute-start.28 = (bf16[256,512]{1,0:T(8,128)(2,1)S(1)}, bf16[256,512]{1,0:T(8,128)(2,1)}, u32[]{:S(2)}, u32[]{:S(2)}) collective-permute-start(bf16[256,512]{1,0:T(8,128)(2,1)S(1)} %get-tuple-element.419), channel_id=1, source_target_pairs={{0,3},{1,0},{2,1},{3,2},{4,7},{5,4},{6,5},{7,6},{8,11},{9,8},{10,9... | collective-permute-start | bytes 786440 | tf_op jit(solution)/shard_map/ppermute | solution.py:679
  732.5 17.5 %collective-permute-start.30 = (bf16[256,512]{1,0:T(8,128)(2,1)S(1)}, bf16[256,512]{1,0:T(8,128)(2,1)S(1)}, u32[]{:S(2)}, u32[]{:S(2)}) collective-permute-start(bf16[256,512]{1,0:T(8,128)(2,1)S(1)} %get-tuple-element.418), channel_id=1, source_target_pairs={{0,4},{1,5},{2,6},{3,7},{4,0},{5,1},{6,2},{7,3},{8,12},{9,13},{10,... | collective-permute-start | bytes 786440 | tf_op jit(solution)/shard_map/ppermute | solution.py:669
  732.6 17.4 %collective-permute-start.31 = (bf16[256,512]{1,0:T(8,128)(2,1)S(1)}, bf16[256,512]{1,0:T(8,128)(2,1)S(1)}, u32[]{:S(2)}, u32[]{:S(2)}) collective-permute-start(bf16[256,512]{1,0:T(8,128)(2,1)S(1)} %get-tuple-element.417), channel_id=1, source_target_pairs={{0,5},{1,6},{2,7},{3,4},{4,1},{5,2},{6,3},{7,0},{8,13},{9,14},{10,... | collective-permute-start | bytes 786440 | tf_op jit(solution)/shard_map/ppermute | solution.py:669
  734.7 28.0 %collective-permute-start.32 = (bf16[256,512]{1,0:T(8,128)(2,1)S(1)}, bf16[256,512]{1,0:T(8,128)(2,1)S(1)}, u32[]{:S(2)}, u32[]{:S(2)}) collective-permute-start(bf16[256,512]{1,0:T(8,128)(2,1)S(1)} %get-tuple-element.416), channel_id=1, source_target_pairs={{0,6},{1,7},{2,4},{3,5},{4,2},{5,3},{6,0},{7,1},{8,14},{9,15},{10,... | collective-permute-start | bytes 786440 | tf_op jit(solution)/shard_map/ppermute | solution.py:669
  736.0 27.6 %collective-permute-start.33 = (bf16[256,512]{1,0:T(8,128)(2,1)S(1)}, bf16[256,512]{1,0:T(8,128)(2,1)S(1)}, u32[]{:S(2)}, u32[]{:S(2)}) collective-permute-start(bf16[256,512]{1,0:T(8,128)(2,1)S(1)} %get-tuple-element.415), channel_id=1, source_target_pairs={{0,7},{1,4},{2,5},{3,6},{4,3},{5,0},{6,1},{7,2},{8,15},{9,12},{10,... | collective-permute-start | bytes 786440 | tf_op jit(solution)/shard_map/ppermute | solution.py:669
  739.8 23.8 %collective-permute-start.29 = (bf16[2048,128]{1,0:T(8,128)(2,1)S(1)}, bf16[2048,128]{1,0:T(8,128)(2,1)S(1)}, u32[]{:S(2)}, u32[]{:S(2)}) collective-permute-start(bf16[2048,128]{1,0:T(8,128)(2,1)S(1)} %copy-done.56), channel_id=1, source_target_pairs={{0,4},{4,0},{1,5},{5,1},{2,6},{6,2},{3,7},{7,3},{8,12},{12,8},{9,1... | collective-permute-start | bytes 1572872 | tf_op jit(solution)/shard_map/ppermute | solution.py:976
  763.9 32.5 %collective-permute-start.36 = (bf16[512,128]{1,0:T(8,128)(2,1)S(1)}, bf16[512,128]{1,0:T(8,128)(2,1)S(1)}, u32[]{:S(2)}, u32[]{:S(2)}) collective-permute-start(bf16[512,128]{1,0:T(8,128)(2,1)S(1)} %pad_maximum_fusion.19), channel_id=1, source_target_pairs={{0,3},{1,0},{2,1},{3,2},{4,7},{5,4},{6,5},{7,6},{8,11},{9,8},{10,9... | collective-permute-start | bytes 393224 | tf_op jit(solution)/shard_map/ppermute | solution.py:679
  788.5 17.7 %collective-permute-start.35 = (bf16[512,128]{1,0:T(8,128)(2,1)S(1)}, bf16[512,128]{1,0:T(8,128)(2,1)S(1)}, u32[]{:S(2)}, u32[]{:S(2)}) collective-permute-start(bf16[512,128]{1,0:T(8,128)(2,1)S(1)} %pad_maximum_fusion.18), channel_id=1, source_target_pairs={{0,2},{1,3},{2,0},{3,1},{4,6},{5,7},{6,4},{7,5},{8,10},{9,11},{10,... | collective-permute-start | bytes 393224 | tf_op jit(solution)/shard_map/ppermute | solution.py:679
  788.6 17.6 %collective-permute-start.34 = (bf16[512,128]{1,0:T(8,128)(2,1)S(1)}, bf16[512,128]{1,0:T(8,128)(2,1)S(1)}, u32[]{:S(2)}, u32[]{:S(2)}) collective-permute-start(bf16[512,128]{1,0:T(8,128)(2,1)S(1)} %pad_maximum_fusion.17), channel_id=1, source_target_pairs={{0,1},{1,2},{2,3},{3,0},{4,5},{5,6},{6,7},{7,4},{8,9},{9,10},{10,1... | collective-permute-start | bytes 393224 | tf_op jit(solution)/shard_map/ppermute | solution.py:679
  816.6 325.9 %reduce-scatter.12.cloned.1.call-start = ((), (), s32[]{:S(2)}) async-start(), calls=%async_computation.8 | async-start | bytes 18874368 | tf_op jit(solution)/shard_map/reduce_scatter | solution.py:900
  818.7 73.9 %collective-permute-start.37 = (bf16[512,2048]{1,0:T(8,128)(2,1)}, bf16[512,2048]{1,0:T(8,128)(2,1)}, u32[]{:S(2)}, u32[]{:S(2)}) collective-permute-start(bf16[512,2048]{1,0:T(8,128)(2,1)} %fusion.4), channel_id=1, source_target_pairs={{0,1},{1,2},{2,3},{4,5},{5,6},{6,7},{8,9},{9,10},{10,11},{12,13},{... | collective-permute-start | bytes 6291464 | tf_op jit(solution)/shard_map/ppermute | solution.py:629
  829.3 63.3 %collective-permute-start.38 = (bf16[512,2048]{1,0:T(8,128)(2,1)}, bf16[512,2048]{1,0:T(8,128)(2,1)}, u32[]{:S(2)}, u32[]{:S(2)}) collective-permute-start(bf16[512,2048]{1,0:T(8,128)(2,1)} %fusion.4), channel_id=1, source_target_pairs={{1,0},{2,1},{3,2},{5,4},{6,5},{7,6},{9,8},{10,9},{11,10},{13,12},{... | collective-permute-start | bytes 6291464 | tf_op jit(solution)/shard_map/ppermute | solution.py:630
  830.6 87.4 %collective-permute-start.39 = (bf16[512,2048]{1,0:T(8,128)(2,1)S(1)}, bf16[512,2048]{1,0:T(8,128)(2,1)}, u32[]{:S(2)}, u32[]{:S(2)}) collective-permute-start(bf16[512,2048]{1,0:T(8,128)(2,1)S(1)} %add_convert_fusion), channel_id=1, source_target_pairs={{0,1},{1,2},{2,3},{4,5},{5,6},{6,7},{8,9},{9,10},{10,11},{12,13},{... | collective-permute-start | bytes 6291464 | tf_op jit(solution)/shard_map/ppermute | solution.py:629
  836.4 87.1 %collective-permute-start.40 = (bf16[512,2048]{1,0:T(8,128)(2,1)S(1)}, bf16[512,2048]{1,0:T(8,128)(2,1)}, u32[]{:S(2)}, u32[]{:S(2)}) collective-permute-start(bf16[512,2048]{1,0:T(8,128)(2,1)S(1)} %add_convert_fusion), channel_id=1, source_target_pairs={{1,0},{2,1},{3,2},{5,4},{6,5},{7,6},{9,8},{10,9},{11,10},{13,12},{... | collective-permute-start | bytes 6291464 | tf_op jit(solution)/shard_map/ppermute | solution.py:630
  837.7 37.8 %collective-permute-start.41 = (bf16[1024,512]{1,0:T(8,128)(2,1)S(1)}, bf16[1024,512]{1,0:T(8,128)(2,1)}, u32[]{:S(2)}, u32[]{:S(2)}) collective-permute-start(bf16[1024,512]{1,0:T(8,128)(2,1)S(1)} %copy-done.32), channel_id=1, source_target_pairs={{0,4},{4,0},{1,5},{5,1},{2,6},{6,2},{3,7},{7,3},{8,12},{12,8},{9,1... | collective-permute-start | bytes 3145736 | tf_op jit(solution)/shard_map/ppermute | solution.py:1033
  924.8 15.6 %collective-permute-start.47 = (f32[2,2048]{1,0:T(2,128)S(1)}, f32[2,2048]{1,0:T(2,128)S(1)}, u32[]{:S(2)}, u32[]{:S(2)}) collective-permute-start(f32[2,2048]{1,0:T(2,128)S(1)} %add.489), channel_id=1, source_target_pairs={{0,16},{8,24},{16,0},{24,8},{1,17},{9,25},{17,1},{25,9},{2,18},{10... | collective-permute-start | bytes 49160 | tf_op jit(solution)/shard_map/ppermute | solution.py:695
  940.5 19.5 %collective-permute-start.42 = (bf16[512,2048]{1,0:T(8,128)(2,1)}, bf16[512,2048]{1,0:T(8,128)(2,1)}, u32[]{:S(2)}, u32[]{:S(2)}) collective-permute-start(bf16[512,2048]{1,0:T(8,128)(2,1)} %collective-permute-done.37), channel_id=1, source_target_pairs={{1,2},{2,3},{5,6},{6,7},{9,10},{10,11},{13,14},{14,15},{17,18},{18... | collective-permute-start | bytes 6291464 | tf_op jit(solution)/shard_map/ppermute | solution.py:629
  942.5 50.7 %collective-permute-start.43 = (bf16[512,2048]{1,0:T(8,128)(2,1)}, bf16[512,2048]{1,0:T(8,128)(2,1)}, u32[]{:S(2)}, u32[]{:S(2)}) collective-permute-start(bf16[512,2048]{1,0:T(8,128)(2,1)} %collective-permute-done.38), channel_id=1, source_target_pairs={{1,0},{2,1},{5,4},{6,5},{9,8},{10,9},{13,12},{14,13},{17,16},{18,1... | collective-permute-start | bytes 6291464 | tf_op jit(solution)/shard_map/ppermute | solution.py:630
  943.7 49.4 %collective-permute-start.44 = (bf16[512,2048]{1,0:T(8,128)(2,1)}, bf16[512,2048]{1,0:T(8,128)(2,1)}, u32[]{:S(2)}, u32[]{:S(2)}) collective-permute-start(bf16[512,2048]{1,0:T(8,128)(2,1)} %collective-permute-done.39), channel_id=1, source_target_pairs={{1,2},{2,3},{5,6},{6,7},{9,10},{10,11},{13,14},{14,15},{17,18},{18... | collective-permute-start | bytes 6291464 | tf_op jit(solution)/shard_map/ppermute | solution.py:629
  945.7 91.6 %collective-permute-start.45 = (bf16[512,2048]{1,0:T(8,128)(2,1)}, bf16[512,2048]{1,0:T(8,128)(2,1)}, u32[]{:S(2)}, u32[]{:S(2)}) collective-permute-start(bf16[512,2048]{1,0:T(8,128)(2,1)} %collective-permute-done.40), channel_id=1, source_target_pairs={{1,0},{2,1},{5,4},{6,5},{9,8},{10,9},{13,12},{14,13},{17,16},{18,1... | collective-permute-start | bytes 6291464 | tf_op jit(solution)/shard_map/ppermute | solution.py:630
  1037.3 14.1 %collective-permute-start.52 = (f32[2,2048]{1,0:T(2,128)S(1)}, f32[2,2048]{1,0:T(2,128)S(1)}, u32[]{:S(2)}, u32[]{:S(2)}) collective-permute-start(f32[2,2048]{1,0:T(2,128)S(1)} %add.490), channel_id=1, source_target_pairs={{0,4},{4,0},{1,5},{5,1},{2,6},{6,2},{3,7},{7,3},{8,12},{12,8},{9,1... | collective-permute-start | bytes 49160 | tf_op jit(solution)/shard_map/ppermute | solution.py:695
  1038.8 105.2 %collective-permute-start.48 = (bf16[512,2048]{1,0:T(8,128)(2,1)}, bf16[512,2048]{1,0:T(8,128)(2,1)}, u32[]{:S(2)}, u32[]{:S(2)}) collective-permute-start(bf16[512,2048]{1,0:T(8,128)(2,1)} %collective-permute-done.42), channel_id=1, source_target_pairs={{2,3},{6,7},{10,11},{14,15},{18,19},{22,23},{26,27},{30,31}} | collective-permute-start | bytes 6291464 | tf_op jit(solution)/shard_map/ppermute | solution.py:629
  1040.7 103.4 %collective-permute-start.49 = (bf16[512,2048]{1,0:T(8,128)(2,1)}, bf16[512,2048]{1,0:T(8,128)(2,1)}, u32[]{:S(2)}, u32[]{:S(2)}) collective-permute-start(bf16[512,2048]{1,0:T(8,128)(2,1)} %collective-permute-done.43), channel_id=1, source_target_pairs={{1,0},{5,4},{9,8},{13,12},{17,16},{21,20},{25,24},{29,28}} | collective-permute-start | bytes 6291464 | tf_op jit(solution)/shard_map/ppermute | solution.py:630
  1042.0 105.9 %collective-permute-start.50 = (bf16[512,2048]{1,0:T(8,128)(2,1)}, bf16[512,2048]{1,0:T(8,128)(2,1)}, u32[]{:S(2)}, u32[]{:S(2)}) collective-permute-start(bf16[512,2048]{1,0:T(8,128)(2,1)} %collective-permute-done.44), channel_id=1, source_target_pairs={{2,3},{6,7},{10,11},{14,15},{18,19},{22,23},{26,27},{30,31}} | collective-permute-start | bytes 6291464 | tf_op jit(solution)/shard_map/ppermute | solution.py:629
  1044.0 105.7 %collective-permute-start.51 = (bf16[512,2048]{1,0:T(8,128)(2,1)}, bf16[512,2048]{1,0:T(8,128)(2,1)}, u32[]{:S(2)}, u32[]{:S(2)}) collective-permute-start(bf16[512,2048]{1,0:T(8,128)(2,1)} %collective-permute-done.45), channel_id=1, source_target_pairs={{1,0},{5,4},{9,8},{13,12},{17,16},{21,20},{25,24},{29,28}} | collective-permute-start | bytes 6291464 | tf_op jit(solution)/shard_map/ppermute | solution.py:630
  1051.4 83.4 %collective-permute-start.53 = (f32[2,2048]{1,0:T(2,128)S(1)}, f32[2,2048]{1,0:T(2,128)S(1)}, u32[]{:S(2)}, u32[]{:S(2)}) collective-permute-start(f32[2,2048]{1,0:T(2,128)S(1)} %add.497), channel_id=1, source_target_pairs={{0,1},{1,0},{2,3},{3,2},{4,5},{5,4},{6,7},{7,6},{8,9},{9,8},{10,11... | collective-permute-start | bytes 49160 | tf_op jit(solution)/shard_map/ppermute | solution.py:695
  1143.9 24.5 %collective-permute-start.55 = (bf16[256,512]{1,0:T(8,128)(2,1)S(1)}, bf16[256,512]{1,0:T(8,128)(2,1)S(1)}, u32[]{:S(2)}, u32[]{:S(2)}) collective-permute-start(bf16[256,512]{1,0:T(8,128)(2,1)S(1)} %get-tuple-element.401), channel_id=1, source_target_pairs={{0,1},{1,2},{2,3},{3,0},{4,5},{5,6},{6,7},{7,4},{8,9},{9,10},{10,1... | collective-permute-start | bytes 786440 | tf_op jit(solution)/shard_map/ppermute | solution.py:679
  1144.0 24.4 %collective-permute-start.56 = (bf16[256,512]{1,0:T(8,128)(2,1)S(1)}, bf16[256,512]{1,0:T(8,128)(2,1)S(1)}, u32[]{:S(2)}, u32[]{:S(2)}) collective-permute-start(bf16[256,512]{1,0:T(8,128)(2,1)S(1)} %get-tuple-element.400), channel_id=1, source_target_pairs={{0,2},{1,3},{2,0},{3,1},{4,6},{5,7},{6,4},{7,5},{8,10},{9,11},{10,... | collective-permute-start | bytes 786440 | tf_op jit(solution)/shard_map/ppermute | solution.py:679
  1144.1 24.4 %collective-permute-start.57 = (bf16[256,512]{1,0:T(8,128)(2,1)S(1)}, bf16[256,512]{1,0:T(8,128)(2,1)S(1)}, u32[]{:S(2)}, u32[]{:S(2)}) collective-permute-start(bf16[256,512]{1,0:T(8,128)(2,1)S(1)} %get-tuple-element.399), channel_id=1, source_target_pairs={{0,3},{1,0},{2,1},{3,2},{4,7},{5,4},{6,5},{7,6},{8,11},{9,8},{10,9... | collective-permute-start | bytes 786440 | tf_op jit(solution)/shard_map/ppermute | solution.py:679
  1147.9 15.0 %collective-permute-start.58 = (bf16[64,128]{1,0:T(8,128)(2,1)S(1)}, bf16[64,128]{1,0:T(8,128)(2,1)S(1)}, u32[]{:S(2)}, u32[]{:S(2)}) collective-permute-start(bf16[64,128]{1,0:T(8,128)(2,1)S(1)} %get-tuple-element.449), channel_id=1, source_target_pairs={{0,1},{1,2},{2,3},{3,0},{4,5},{5,6},{6,7},{7,4},{8,9},{9,10},{10,1... | collective-permute-start | bytes 49160 | tf_op jit(solution)/shard_map/ppermute | solution.py:679
  1149.7 18.7 %collective-permute-start.59 = (bf16[64,128]{1,0:T(8,128)(2,1)S(1)}, bf16[64,128]{1,0:T(8,128)(2,1)S(1)}, u32[]{:S(2)}, u32[]{:S(2)}) collective-permute-start(bf16[64,128]{1,0:T(8,128)(2,1)S(1)} %get-tuple-element.448), channel_id=1, source_target_pairs={{0,2},{1,3},{2,0},{3,1},{4,6},{5,7},{6,4},{7,5},{8,10},{9,11},{10,... | collective-permute-start | bytes 49160 | tf_op jit(solution)/shard_map/ppermute | solution.py:679
  (69 other events, 624.4 us)
Sparse Core Ops, SparseCore 0:
  138.7 78.1 all-gather.4
  228.8 89.1 all-gather.6
  320.9 91.7 reduce-scatter.5
  419.7 96.6 reduce-scatter.7
  620.6 192.3 reduce-scatter.9
  816.7 101.3 reduce-scatter.13
  923.7 113.9 reduce-scatter.11

commit v4 on v3

--- a/solution.py
+++ b/solution.py
@@ -24,42 +24,51 @@
 
 
 def project_kernel(
-    tokens_ref, gain_ref, kv_weight, q_weight, cos_ref, sin_ref, kv_ref, q_ref, normed_ref
+    head, tokens_ref, gain_ref, k_weight, v_weight, q_weight, cos_ref, sin_ref, kv_ref, q_ref, normed_ref
 ):
     inputs = tokens_ref[...].astype(F32)
     inverse = lax.rsqrt(jnp.mean(inputs * inputs, axis=-1, keepdims=True) + EPSILON)
     normed = (inputs * inverse * gain_ref[...]).astype(BF16)
     normed_ref[...] = normed
     cos, sin = cos_ref[...], sin_ref[...]
-    pair = jnp.dot(normed, kv_weight[...], preferred_element_type=F32)
-    is_key = lax.broadcasted_iota(jnp.int32, pair.shape, 1) < HD
-    kv_ref[...] = jnp.where(is_key, turn(pair, cos, sin), pair).astype(BF16)
+    first = head[0] % 2 == 0
+    key = jnp.dot(normed, k_weight[...], preferred_element_type=F32)
+    value = jnp.dot(normed, v_weight[...], preferred_element_type=F32)
+    key = jnp.where(first, key, pltpu.roll(key, HD, 1))
+    value = jnp.where(first, pltpu.roll(value, HD, 1), value)
+    is_key = lax.broadcasted_iota(jnp.int32, key.shape, 1) < HD
+    kv_ref[...] = jnp.where(is_key, turn(key, cos, sin), value).astype(BF16)
     raw = jnp.dot(normed, q_weight[...], preferred_element_type=F32)
-    for first in range(0, q_ref.shape[1], 128):
-        pair = raw[:, first : first + 128]
-        q_ref[:, first : first + 128] = (turn(pair, cos, sin) * HD**-0.5).astype(BF16)
-
-
-def project(tokens, gain, kv_weight, q_weight, cos, sin):
+    for start in range(0, q_ref.shape[1], 128):
+        pair = raw[:, start : start + 128]
+        q_ref[:, start : start + 128] = (turn(pair, cos, sin) * HD**-0.5).astype(BF16)
+
+
+def project(head, tokens, gain, k_weight, v_weight, q_weight, cos, sin):
     rows, width = tokens.shape
     columns = q_weight.shape[1]
     block = 256
+    two_heads = pl.BlockSpec((width, 128), lambda i, head: (0, head[0] // 2))
     return pl.pallas_call(
         project_kernel,
-        grid=(rows // block,),
-        in_specs=[
-            pl.BlockSpec((block, width), lambda i: (i, 0)),
-            pl.BlockSpec((1, width), lambda i: (0, 0)),
-            pl.BlockSpec((width, 128), lambda i: (0, 0)),
-            pl.BlockSpec((width, columns), lambda i: (0, 0)),
-            pl.BlockSpec((block, 128), lambda i: (i, 0)),
-            pl.BlockSpec((block, 128), lambda i: (i, 0)),
-        ],
-        out_specs=[
-            pl.BlockSpec((block, 128), lambda i: (i, 0)),
-            pl.BlockSpec((block, columns), lambda i: (i, 0)),
-            pl.BlockSpec((block, width), lambda i: (i, 0)),
-        ],
+        grid_spec=pltpu.PrefetchScalarGridSpec(
+            num_scalar_prefetch=1,
+            grid=(rows // block,),
+            in_specs=[
+                pl.BlockSpec((block, width), lambda i, head: (i, 0)),
+                pl.BlockSpec((1, width), lambda i, head: (0, 0)),
+                two_heads,
+                two_heads,
+                pl.BlockSpec((width, columns), lambda i, head: (0, 0)),
+                pl.BlockSpec((block, 128), lambda i, head: (i, 0)),
+                pl.BlockSpec((block, 128), lambda i, head: (i, 0)),
+            ],
+            out_specs=[
+                pl.BlockSpec((block, 128), lambda i, head: (i, 0)),
+                pl.BlockSpec((block, columns), lambda i, head: (i, 0)),
+                pl.BlockSpec((block, width), lambda i, head: (i, 0)),
+            ],
+        ),
         out_shape=[
             jax.ShapeDtypeStruct((rows, 128), BF16),
             jax.ShapeDtypeStruct((rows, columns), BF16),
@@ -68,7 +77,7 @@
         compiler_params=pltpu.CompilerParams(vmem_limit_bytes=48 * 2**20),
         cost_estimate=LIGHT,
         name="project",
-    )(tokens, gain.reshape(1, width), kv_weight, q_weight, cos, sin)
+    )(head, tokens, gain.reshape(1, width), k_weight, v_weight, q_weight, cos, sin)
 
 
 def fwd_kernel(offsets, meta, q_ref, ka_ref, kb_ref, vt_ref, o_ref, lse_ref):
@@ -513,87 +522,67 @@
     )(gathered, tokens, cotangent, gain, output_weight, *weights, *earlier)
 
 
-def join_kernel(order, rows_ref, near_ref, far_ref, out_ref):
-    piece = pl.program_id(0)
-
-    def total(weight_ref):
-        result = None
-        for source in range(rows_ref.shape[0]):
-            part = lax.dot_general(
-                rows_ref[source], weight_ref[0, source], NT, preferred_element_type=F32
-            )
-            result = part if result is None else result + part
-        out_ref[...] = result
-
-    @pl.when(piece < 2)
-    def _():
-        total(near_ref)
-
-    @pl.when(piece >= 2)
-    def _():
-        total(far_ref)
-
-
-def join(order, rows, near, far):
+def part_specs(shape):
+    return [pl.BlockSpec(shape, lambda p, order: (0, 0, 0)) for _ in range(4)]
+
+
+def join_kernel(order, rows_ref, *refs):
+    out_ref = refs[4]
+    for part, weight_ref in enumerate(refs[:4]):
+
+        @pl.when(pl.program_id(0) == part)
+        def _():
+            result = None
+            for source in range(rows_ref.shape[0]):
+                term = lax.dot_general(
+                    rows_ref[source], weight_ref[source], NT, preferred_element_type=F32
+                )
+                result = term if result is None else result + term
+            out_ref[...] = result
+
+
+def join(order, rows, parts):
     size, count, features = rows.shape
-    columns = near.shape[2]
+    columns = parts[0].shape[1]
     return pl.pallas_call(
         join_kernel,
         grid_spec=pltpu.PrefetchScalarGridSpec(
             num_scalar_prefetch=1,
             grid=(4,),
-            in_specs=[
-                pl.BlockSpec(rows.shape, lambda p, order: (0, 0, 0)),
-                pl.BlockSpec(
-                    (1, size, columns, features), lambda p, order: (jnp.minimum(p, 1), 0, 0, 0)
-                ),
-                pl.BlockSpec(
-                    (1, size, columns, features), lambda p, order: (jnp.maximum(p - 2, 0), 0, 0, 0)
-                ),
-            ],
+            in_specs=[pl.BlockSpec(rows.shape, lambda p, order: (0, 0, 0))]
+            + part_specs(parts[0].shape),
             out_specs=pl.BlockSpec((count, columns), lambda p, order: (0, order[p])),
         ),
         out_shape=jax.ShapeDtypeStruct((count, 4 * columns), F32),
-        compiler_params=pltpu.CompilerParams(vmem_limit_bytes=32 * 2**20),
+        compiler_params=pltpu.CompilerParams(vmem_limit_bytes=48 * 2**20),
         cost_estimate=LIGHT,
         name="join",
-    )(order, rows, near, far)
-
-
-def arrange_kernel(order, near_ref, far_ref, out_ref):
-    piece = pl.program_id(0)
-
-    @pl.when(piece < 2)
-    def _():
-        out_ref[...] = near_ref[0]
-
-    @pl.when(piece >= 2)
-    def _():
-        out_ref[...] = far_ref[0]
-
-
-def arrange(order, near, far):
-    size, rows, features = near.shape[1:]
+    )(order, rows, *parts)
+
+
+def arrange_kernel(order, *refs):
+    for part, weight_ref in enumerate(refs[:4]):
+
+        @pl.when(pl.program_id(0) == part)
+        def _():
+            refs[4][...] = weight_ref[...]
+
+
+def arrange(order, parts):
+    size, rows, features = parts[0].shape
     return pl.pallas_call(
         arrange_kernel,
         grid_spec=pltpu.PrefetchScalarGridSpec(
             num_scalar_prefetch=1,
             grid=(4,),
-            in_specs=[
-                pl.BlockSpec(
-                    (1, size, rows, features), lambda p, order: (jnp.minimum(p, 1), 0, 0, 0)
-                ),
-                pl.BlockSpec(
-                    (1, size, rows, features), lambda p, order: (jnp.maximum(p - 2, 0), 0, 0, 0)
-                ),
-            ],
+            in_specs=part_specs(parts[0].shape),
             out_specs=pl.BlockSpec((size, rows, features), lambda p, order: (0, order[p], 0)),
         ),
-        out_shape=jax.ShapeDtypeStruct((size, 4 * rows, features), near.dtype),
-        compiler_params=pltpu.CompilerParams(vmem_limit_bytes=32 * 2**20),
+        out_shape=jax.ShapeDtypeStruct((size, 4 * rows, features), parts[0].dtype),
+        compiler_params=pltpu.CompilerParams(vmem_limit_bytes=48 * 2**20),
         cost_estimate=LIGHT,
         name="arrange",
-    )(order, near, far)
+    )(order, *parts)
 
 
 def quarter_row(row, c, half, span):
@@ -688,21 +677,6 @@
     for shift, block in enumerate(arrived):
         out = lax.dynamic_update_index_in_dim(out, block, lax.rem(me - shift + size, size), 0)
     return out
-
-
-def pairwise(value, axis, step):
-    size = lax.axis_size(axis)
-    return value + lax.ppermute(value, axis, [(i, i ^ step) for i in range(size)])
-
-
-def pair_steps():
-    steps = []
-    for axis in ("dp", "ctx", "tensor"):
-        step = 1
-        while step < lax.axis_size(axis):
-            steps.append((axis, step))
-            step *= 2
-    return steps
 
 
 def hold(*values):
@@ -753,9 +727,7 @@
     features = w_query.shape[1]
     kv_count = w_key.shape[1] // HD
     kv_pick = np.arange(groups) * kv_count // groups
-    kv_start = member * kv_count // groups * HD
-    key_weight = lax.dynamic_slice_in_dim(w_key, kv_start, HD, 1)
-    value_weight = lax.dynamic_slice_in_dim(w_value, kv_start, HD, 1)
+    head = (member * kv_count // groups).astype(jnp.int32).reshape(1)
     span = tok_rows // 2
     half = span // 2
     share = span // groups
@@ -790,7 +762,6 @@
             jnp.concatenate([-sin_part, sin_part] * 2, axis=1),
         )
 
-    cos_near, sin_near = table(positions[:tok_rows])
 
     upper = lax.axis_index("dp") % 2
     beside = [(i, i ^ 1) for i in range(lax.axis_size("dp"))]
@@ -811,16 +782,15 @@
 
     output_gather = quarter_gather(w_output)
     hop = output_gather.step()
+    cos_near, sin_near = table(positions[:tok_rows])
+    cos_near, sin_near, hop, quarters, head = hold(cos_near, sin_near, hop, quarters, head)
+    output_gather.held(hop)
+    hop = output_gather.step()
 
     kv_own, queries, normed = project(
-        tokens,
-        norm_attn,
-        jnp.concatenate([key_weight, value_weight], axis=1),
-        w_query,
-        cos_near,
-        sin_near,
-    )
-    kv_own, queries, normed, hop, quarters = hold(kv_own, queries, normed, hop, quarters)
+        head, tokens, norm_attn, w_key, w_value, w_query, cos_near, sin_near
+    )
+    kv_own, queries, normed, hop = hold(kv_own, queries, normed, hop)
     output_gather.held(hop)
     kv_other = lax.ppermute(kv_own, "ctx", over)
     hop = output_gather.step()
@@ -831,33 +801,31 @@
     length = 2 * tok_rows
 
     foreign = lax.ppermute(sent, "ctx", over)
-    hop = output_gather.step()
+    output_part = quarter_collect(output_gather)
+    output_over = lax.ppermute(output_part, "ctx", over)
     first, first_log, *forms = attend_first(metas[0], offsets[0], kept, kv_own, kv_other)
-    first, first_log, foreign, forms, hop = hold(first, first_log, foreign, forms, hop)
-    output_gather.held(hop)
+    first, first_log, foreign, forms, output_near = hold(
+        first, first_log, foreign, forms, (output_part, output_over)
+    )
     *forms, values_t = forms
     first_whole = lax.all_gather(first, "tensor", axis=0, tiled=False)
 
-    output_part = quarter_collect(output_gather)
-    output_over = lax.ppermute(output_part, "ctx", over)
+    output_far = tuple(lax.ppermute(part, "dp", beside) for part in output_near)
     second, second_log = attend(metas[1], offsets[1], foreign, forms[0], forms[1], values_t)
-    second, second_log, output_part, output_over = hold(
-        second, second_log, output_part, output_over
-    )
-
-    output_near = jnp.stack([output_part, output_over])
-    output_far = lax.ppermute(output_near, "dp", beside)
+    second, second_log, output_near, output_far = hold(
+        second, second_log, output_near, output_far
+    )
+
     cos_far, sin_far = table(after(positions[tok_rows:], second))
     cos_pair = jnp.concatenate([cos_near, cos_far], axis=0)
     sin_pair = jnp.concatenate([sin_near, sin_far], axis=0)
     tables = [(chunk(cos_near, 0), chunk(sin_near, 0)), (chunk(cos_far, 1), chunk(sin_far, 1))]
     second_home = lax.ppermute(second, "ctx", over)
-    second_home, output_near, output_far, tables, cos_pair, sin_pair = hold(
-        second_home, output_near, output_far, tables, cos_pair, sin_pair
+    output_whole = arrange(quarters, output_near + output_far)
+    second_home, output_whole, tables, cos_pair, sin_pair = hold(
+        second_home, output_whole, tables, cos_pair, sin_pair
     )
     second_whole = lax.all_gather(second_home, "tensor", axis=0, tiled=False)
-    output_whole = arrange(quarters, output_near, output_far)
-    output_whole, first_whole = hold(output_whole, first_whole)
     queries = [kept, foreign]
     attention = [first, second]
     log_totals = [first_log, second_log]
@@ -940,8 +908,8 @@
     def back_arguments(c, grads):
         return metas[c], offsets[c], queries[c], attention[c], grads, log_totals[c], forms, *tables[c]
 
-    query_near = jnp.stack([query_part, query_over])
-    query_far = lax.ppermute(query_near, "dp", beside)
+    query_near = (query_part, query_over)
+    query_far = tuple(lax.ppermute(part, "dp", beside) for part in query_near)
     grads_first = stack_blocks(came_first).reshape(span, features)
     dq_first, dk, dv = attend_back_first(*back_arguments(0, grads_first))
     dq_first, dk, dv, query_near, query_far, share_second = hold(
@@ -973,20 +941,24 @@
     )
     dq_second, kv_near, kv_far, rows_first = hold(dq_second, kv_near, kv_far, rows_first)
 
-    kv_sent = lax.ppermute(kv_far, "ctx", over)
-    rows_second = send_blocks(rows_of(dq_second), across=True)
-    first_part = join(quarters, stack_blocks(rows_first), query_near, query_far)
-    kv_near, kv_sent, rows_second, first_part = hold(kv_near, kv_sent, rows_second, first_part)
-    grad_kv_raw = (kv_near + kv_sent.astype(F32)).astype(BF16)
-    kv_rows = send_blocks(
-        lambda j: jnp.concatenate(
-            [lax.dynamic_slice_in_dim(grad_kv_raw, row_of[c][j], share, 0) for c in chunks], axis=0
-        )
-    )
-    second_part = join(quarters, stack_blocks(rows_second), query_near, query_far)
-    first_part, second_part, kv_rows, grad_kv_raw = hold(
-        first_part, second_part, kv_rows, grad_kv_raw
-    )
+    def kv_share_of(array, j):
+        return [lax.dynamic_slice_in_dim(array, row_of[c][j], share, 0) for c in chunks]
+
+    kv_low = kv_near.astype(BF16)
+    near_blocks = send_blocks(lambda j: jnp.concatenate(kv_share_of(kv_low, j), axis=1))
+    far_blocks = send_blocks(
+        lambda j: jnp.concatenate([rows_of(dq_second)(j), *kv_share_of(kv_far, j)], axis=1),
+        across=True,
+    )
+    query_parts = query_near + query_far
+    first_part = join(quarters, stack_blocks(rows_first), query_parts)
+    near_blocks, far_blocks, first_part = hold(near_blocks, far_blocks, first_part)
+    far_blocks = stack_blocks(far_blocks)
+    kv_blocks = (
+        stack_blocks(near_blocks).astype(F32) + far_blocks[:, :, features:].astype(F32)
+    ).astype(BF16)
+    kv_blocks = jnp.concatenate([kv_blocks[:, :, : 2 * HD], kv_blocks[:, :, 2 * HD :]], axis=1)
+    second_part = join(quarters, far_blocks[:, :, :features], query_parts)
     kv_whole = jnp.stack(
         [
             jnp.concatenate(
@@ -997,7 +969,7 @@
     )
 
     grad_normed = jnp.concatenate([first_part, second_part], axis=0) + jnp.einsum(
-        "trq,tdq->rd", stack_blocks(kv_rows), kv_whole, preferred_element_type=F32
+        "trq,tdq->rd", kv_blocks, kv_whole, preferred_element_type=F32
     )
     inputs_own = jnp.concatenate([own_rows(tokens, c) for c in chunks], axis=0).astype(F32)
     inverse_own = lax.rsqrt(jnp.mean(inputs_own * inputs_own, axis=-1, keepdims=True) + EPSILON)
@@ -1016,73 +988,80 @@
             )
         return target
 
-    gains = jnp.stack([attn_gain, gain_first + gain_second])
-    mixed_share = (middle_own + mlp_share.astype(F32)).astype(BF16)
-    grad_inputs, gains, dq_second, mixed_share, w_gates = hold(
-        grad_inputs, gains, dq_second, mixed_share, w_gates
+    gains = jnp.stack([attn_gain, gain_first + gain_second], axis=1).astype(BF16)
+    grad_inputs, gains, dq_second, kv_far, kv_near, w_gates = hold(
+        grad_inputs, gains, dq_second, kv_far, kv_near, w_gates
     )
     gate_up_grad = plane_sum(w_gates)
 
     def put_share(target, piece, source):
         return lax.dynamic_update_slice_in_dim(target, piece, source * n_part, 0)
 
-    tokens_gather, mixed_gather = Gather(grad_inputs), Gather(mixed_share)
+    tokens_gather = Gather(grad_inputs)
     tokens_grad = jnp.zeros((tok_rows, width), BF16)
     mixed = jnp.zeros((tok_rows, width), BF16)
-    hop, mixed_hop = tokens_gather.step(), mixed_gather.step()
+    hop = tokens_gather.step()
+    kv_sent = lax.ppermute(kv_far, "ctx", over)
     dq_home = lax.ppermute(dq_second, "ctx", over)
+    grad_kv_raw = (kv_near + kv_sent.astype(F32)).astype(BF16)
     query_kv = t_dot(
         normed, jnp.concatenate([natural(dq_first, dq_home), grad_kv_raw], axis=1)
     ).astype(BF16)
-    rest = jnp.concatenate([w_downs, w_outs, query_kv], axis=1)
+    gains = jnp.pad(gains, ((0, 0), (0, 126)))
+    rest = jnp.concatenate([w_downs, w_outs, query_kv, gains], axis=1)
     tokens_grad = tokens_gather.place_hop(put_rows, tokens_grad, 0)
+    hop, rest, tokens_grad = hold(hop, rest, tokens_grad)
+    tokens_gather.held(hop)
+    rest = plane_sum(rest)
+
+    mixed_gather = Gather((middle_own + after(mlp_share, hop).astype(F32)).astype(BF16))
+    hop, mixed_hop = tokens_gather.step(), mixed_gather.step()
+    tokens_grad = tokens_gather.place_hop(put_rows, tokens_grad, 1)
     mixed = mixed_gather.place_hop(put_share, mixed, 0)
-    hop, mixed_hop, rest, tokens_grad, mixed = hold(hop, mixed_hop, rest, tokens_grad, mixed)
+    hop, mixed_hop, tokens_grad, mixed, mixed_gather.piece = hold(
+        hop, mixed_hop, tokens_grad, mixed, mixed_gather.piece
+    )
     tokens_gather.held(hop)
     mixed_gather.held(mixed_hop)
-    rest = plane_sum(rest)
-
-    steps = pair_steps()
+
     hop, mixed_hop = tokens_gather.step(), mixed_gather.step()
-    for axis, step in steps[:2]:
-        gains = pairwise(gains, axis, step)
-    tokens_grad = tokens_gather.place_hop(put_rows, tokens_grad, 1)
+    tokens_grad = tokens_gather.place_hop(put_rows, tokens_grad, 2)
     mixed = mixed_gather.place_hop(put_share, mixed, 1)
-    hop, mixed_hop, gains, tokens_grad, mixed = hold(hop, mixed_hop, gains, tokens_grad, mixed)
+    hidden_units = w_down.shape[1]
+    rest = after(rest, tokens_gather.rights[-2])
+    down_grad = rest[:, :hidden_units]
+    output_plane = rest[:, hidden_units : hidden_units + groups * features]
+    query_plane = rest[:, hidden_units + groups * features :]
+    query_grad, small = query_plane[:, :features].astype(F32), query_plane[:, features:]
+    blocks = send_blocks(
+        lambda j: jnp.concatenate(
+            [lax.dynamic_slice_in_dim(output_plane, j * features, features, 1), small], axis=1
+        )
+    )
+    hop, mixed_hop, tokens_grad, mixed, blocks = hold(hop, mixed_hop, tokens_grad, mixed, blocks)
     tokens_gather.held(hop)
     mixed_gather.held(mixed_hop)
 
-    hop, mixed_hop = tokens_gather.step(), mixed_gather.step()
-    for axis, step in steps[2:]:
-        gains = pairwise(gains, axis, step)
-    tokens_grad = tokens_gather.place_hop(put_rows, tokens_grad, 2)
+    hop = mixed_gather.step()
+    if groups > 3:
+        tokens_grad = tokens_gather.place_hop(put_rows, tokens_grad, 3)
     mixed = mixed_gather.place_hop(put_share, mixed, 2)
-    hidden_units = w_down.shape[1]
-    down_grad = rest[:, :hidden_units]
-    rest = rest[:, hidden_units:]
-    output_plane, query_kv = rest[:, : groups * features], rest[:, groups * features :]
-    query_grad, kv_plane = query_kv[:, :features].astype(F32), query_kv[:, features:]
-    output_rows = send_blocks(
-        lambda j: lax.dynamic_slice_in_dim(output_plane, j * features, features, 1)
-    )
-    kv_share = query_kv.shape[0] // groups
-    kv_blocks = send_blocks(
-        lambda j: lax.dynamic_slice_in_dim(kv_plane, j * kv_share, kv_share, 0)
-    )
-    hop, mixed_hop, gains, tokens_grad, mixed, output_rows, kv_blocks = hold(
-        hop, mixed_hop, gains, tokens_grad, mixed, output_rows, kv_blocks
-    )
-    tokens_gather.held(hop)
-    mixed_gather.held(mixed_hop)
-    for hop in range(3, groups):
-        while len(tokens_gather.rights) <= hop:
+    blocks = stack_blocks(blocks).astype(F32)
+    output_grad = jnp.sum(blocks[:, :, :features], axis=0)
+    kv_share = blocks.shape[1] // groups
+    kv_blocks = lax.dynamic_slice_in_dim(
+        blocks[:, :, features : features + 2 * HD], member * kv_share, kv_share, 1
+    )
+    gains = jnp.sum(blocks[:, :, features + 2 * HD : features + 2 * HD + 2], axis=0).T
+    hop, tokens_grad, mixed = hold(hop, tokens_grad, mixed)
+    mixed_gather.held(hop)
+    for count in range(3, groups):
+        mixed = mixed_gather.place_hop(put_share, mixed, count)
+        if count + 1 < groups:
             tokens_gather.step()
             mixed_gather.step()
-        tokens_grad = tokens_gather.place_hop(put_rows, tokens_grad, hop)
-        mixed = mixed_gather.place_hop(put_share, mixed, hop)
-    output_grad = jnp.sum(stack_blocks(output_rows).astype(F32), axis=0)
-
-    kv_blocks = stack_blocks(kv_blocks).astype(F32)
+            tokens_grad = tokens_gather.place_hop(put_rows, tokens_grad, count + 1)
+
     key_heads, value_heads = [], []
     for h in range(kv_count):
         total = jnp.zeros((kv_share, 2 * HD), F32)
@@ -1094,9 +1073,6 @@
     key_grad = jnp.concatenate(key_heads, axis=1)
     value_grad = jnp.concatenate(value_heads, axis=1)
 
-    plane = lax.axis_size("dp") * n_ctx
-    plane_index = lax.axis_index("dp") * n_ctx + ctx_index
-    gains = lax.dynamic_slice_in_dim(gains, plane_index * (width // plane), width // plane, 1)
     return (
         mixed,
         tokens_grad,

time: 1200 us -> 1160 us (0.967)
  starting transfers between devices: 217 us -> 127 us
  waiting for transfers between devices: 302 us -> 340 us
    ppermute x7 -> x4, waiting for transfers between devices: 81.6 us -> 0.01 us  [the longest x2 0.01 us: body(): query_far = tuple((lax.ppermute(part, 'dp', beside) for part in query_near))]
    ppermute x15 -> x12, waiting for transfers between devices: 34.6 us -> 92.9 us  [send_blocks(): lax.ppermute(block, 'tensor', [(i, (i + shift) % size) for i in range(siz...]
    reduce_scatter x2, waiting for transfers between devices: 0.02 us -> 44.4 us  [plane_sum(): lax.psum_scatter(gradient.astype(BF16), ('dp', 'ctx'), scatter_dimension=...]
    ppermute x12, waiting for transfers between devices: 89.3 us -> 129 us  [step(): self.lefts.append(lax.ppermute(self.lefts[-1], 'tensor', to_left))]
    ppermute x1, starting transfers between devices: 32.9 us -> 0.55 us  [body(): output_over = lax.ppermute(output_part, 'ctx', over)]
    ppermute x1, waiting for transfers between devices: 0.01 us -> 29.6 us  [body(): foreign = lax.ppermute(sent, 'ctx', over)]
    ppermute x12, waiting for transfers between devices: 25.4 us -> 0.03 us  [step(): self.rights.append(lax.ppermute(self.rights[-1], 'tensor', to_right))]
    ppermute x8, starting transfers between devices: 75.9 us -> 52.1 us  [send_blocks(): lax.ppermute(block, ('ctx', 'tensor'), [(c * size + i, (1 - c) * size + (...]
  transfers between devices with their start and end apart: 68 -> 62, of which waited for: 21 -> 18; matrix products, arithmetic and copies ran while one was open for 18% -> 20% of each run, Pallas kernels for 30% -> 32%
where the time goes in v4:
time: 1160 us; the launch traced here: 1140 us
  Pallas kernels  363 us (31%)
  waiting for transfers between devices  340 us (29%)
  starting transfers between devices  127 us (11%)
  other arithmetic  101 us (9%)
  matrix products  85.7 us (7%)
  local copies, waits for them, and re-layouts  71.5 us (6%)
  between operations  49.3 us (4%)
    ppermute x12, waiting for transfers between devices, step(): self.lefts.append(lax.ppermute(self.lefts[-1], 'tensor', to_left))  129 us
    pallas_call x2, Pallas kernels, feed_forward(): pl.pallas_call(feed_kernel, grid=(2 * quarter,), in_specs=[pl.BlockSpec((...  124 us
    ppermute x12, waiting for transfers between devices, send_blocks(): lax.ppermute(block, 'tensor', [(i, (i + shift) % size) for i in range(siz...  92.9 us
    dot_general x4, matrix products, t_dot(): return jnp.einsum('rd,rf->df', a, b, preferred_element_type=F32)  71.2 us
    pallas_call x1, Pallas kernels, attend_back_last(): pl.pallas_call(kernel, grid_spec=pltpu.PrefetchScalarGridSpec(num_scalar_...  70.7 us
    ppermute x8, starting transfers between devices, send_blocks(): lax.ppermute(block, ('ctx', 'tensor'), [(c * size + i, (1 - c) * size + (...  52.1 us
    pallas_call x1, Pallas kernels, attend(): pl.pallas_call(kernel, grid_spec=pltpu.PrefetchScalarGridSpec(num_scalar_...  49.3 us
    pallas_call x1, Pallas kernels, attend_back_first(): pl.pallas_call(kernel, grid_spec=pltpu.PrefetchScalarGridSpec(num_scalar_...  45.5 us
  transfers between devices with their start and end apart: 62, of which 18 were waited for; matrix products, arithmetic and copies ran while one was open for 20% of the time, Pallas kernels for 32%

profile of v4, /device:TPU:0, one launch (start us, length us, event | category | flops | bytes accessed | tf_op | source)
XLA Modules:
  0.0 1138.0 jit_solution(7102724166447871170)
XLA Ops:
  10.7 5.0 collective-permute-start
  17.3 5.4 multiply_sine_fusion.1
  24.0 5.6 pad_maximum_fusion.1
  33.1 17.5 %project.1 = (bf16[2048,128]{1,0:T(8,128)(2,1)S(1)}, bf16[2048,512]{1,0:T(8,128)(2,1)}, bf16[2048,2048]{1,0:T(8,128)(2,1)}) custom-call(s32[1]{0:T(128)} %bitcast.7.head, bf16[2048,2048]{1,0:T(8,128)(2,1)} %tokens_ref.5, f32[1,2048]{1,0:T(1,128)S(1)} %bitcast.164, bf16[2048,256]{1,0:T(8,128)(2,1)S(1)} %copy-done, bf16[2048,256]{1,0:T(8,128)(2,1)S(1)} %copy-done.2, ...), custom_call_target="tpu_custom_call" | custom-call | flops 1 | bytes 1 | tf_op jit(solution)/shard_map/project/pallas_call | solution.py:52
  59.3 6.8 collective-permute-done.4.other
  66.1 6.3 collective-permute-done.6
  76.2 35.4 %attend_first.1 = (bf16[1024,512]{1,0:T(8,128)(2,1)}, f32[4,8,1024]{2,1,0:T(8,128)}, bf16[4096,128]{1,0:T(8,128)(2,1)}, bf16[4096,128]{1,0:T(8,128)(2,1)}, bf16[...) custom-call(s32[6]{0:T(128)} %get-tuple-element.502.meta.refs_0_, ...), custom_call_target="tpu_custom_call" | custom-call | flops 17179869184 | bytes 8388608 | tf_op jit(solution)/shard_map/attend_first/pallas_call | solution.py:188
  111.6 29.6 %collective-permute-done.7.refs_1_ = bf16[1024,512]{1,0:T(8,128)(2,1)S(1)} collective-permute-done((bf16[1024,512]{1,0:T(8,128)(2,1)S(1)}, bf16[1024,512]{1,0:T(8,128)(2,1)S(1)}, u32[]{:S(2)}, u32[]{:S(2)}) %collective-permute-start.7) | collective-permute-done | bytes 1048608 | tf_op jit(solution)/shard_map/ppermute | solution.py:803
  143.7 49.3 %attend.1 = (bf16[1024,512]{1,0:T(8,128)(2,1)}, f32[4,8,1024]{2,1,0:T(8,128)}) custom-call(s32[6]{0:T(128)} %get-tuple-element.501.refs_0_, bf16[1024,512]{1,0:T(8,128)(2,1)} %copy-done.27, bf16[4096,128]{1,0:T(8,128)(2,1)} %get-tuple-element.223.refs_2_.refs_5_, bf16[4096,128]{1,0:T(8,128)(2,1)} %get-tuple-element.224.refs_3_.refs_6_, ...), custom_call_target="tpu_custom_call" | custom-call | flops 17179869184 | bytes 8388608 | tf_op jit(solution)/shard_map/attend/pallas_call | solution.py:225
  193.1 3.7 multiply_sine_fusion
  199.4 7.6 arrange.1.output_weight
  212.5 8.1 all-gather.5.cloned.1.call-done
  224.6 62.3 %feed_forward.2 = (f32[2048,2048]{1,0:T(8,128)}, bf16[2048,2048]{1,0:T(8,128)(2,1)}, bf16[2048,1408]{1,0:T(8,128)(2,1)}, bf16[2048,2816]{1,0:T(8,128)(2,1)}, bf1...) custom-call(bf16[4,1024,512]{2,1,0:T(8,128)(2,1)} %bitcast.172, bf16[2048,2048]{1,0:T(8,128)(2,1)} %tokens_ref.5, ...), custom_call_target="tpu_custom_call" | custom-call | flops 1 | bytes 1 | tf_op jit(solution)/shard_map/feed_forward/pallas_call | solution.py:503
  286.9 21.3 %all-gather.7.cloned.1.call-done = bf16[4096,512]{1,0:T(8,128)(2,1)} async-done(((bf16[1024,512]{1,0:T(8,128)(2,1)}), bf16[4096,512]{1,0:T(8,128)(2,1)}) %all-gather.7.cloned.1.call-update) | async-done | bytes 4194320 | tf_op jit(solution)/shard_map/all_gather | solution.py:828
  315.2 61.3 %feed_forward.3 = (f32[2048,2048]{1,0:T(8,128)}, bf16[2048,2048]{1,0:T(8,128)(2,1)}, bf16[2048,1408]{1,0:T(8,128)(2,1)}, bf16[2048,2816]{1,0:T(8,128)(2,1)}, bf1...) custom-call(bf16[4,1024,512]{2,1,0:T(8,128)(2,1)} %bitcast.174, ...), custom_call_target="tpu_custom_call", output_to_operand_aliasing={{0}: (8, {}), {1}: (9, {}), {2}: (10, {}), {3}: (11, {}), {... | custom-call | flops 1 | bytes 1 | tf_op jit(solution)/shard_map/feed_forward/pallas_call | solution.py:503
  380.8 31.9 %convolution_convert_fusion = bf16[2048,2816]{1,0:T(8,128)(2,1)} fusion(bf16[2048,2048]{1,0:T(8,128)(2,1)} %get-tuple-element.262, bf16[2048,2816]{1,0:T(8,128)(2,1)} %get-tuple-element.263), kind=kOutput, calls=%fused_computation.3 | convolution fusion | flops 23628087296 | bytes 31457280 | tf_op jit(solution)/shard_map/rd,rf->df/dot_general | solution.py:704
  412.7 2.6 multiply_reduce_fusion
  416.6 4.7 constant_dynamic-slice_fusion.36
  426.6 3.9 fusion.54
  430.5 6.2 fusion.41
  437.7 2.7 collective-permute-start.18
  443.5 2.9 collective-permute-start.20
  446.5 19.1 %fusion.2 = bf16[2048,1408]{1,0:T(8,128)(2,1)} fusion(bf16[2048,1408]{1,0:T(8,128)(2,1)} %get-tuple-element.274, bf16[2048,2048]{1,0:T(8,128)(2,1)} %cotangent_ref.3), kind=kOutput, calls=%fused_computation.10 | convolution fusion | flops 11814043648 | bytes 19922944 | tf_op jit(solution)/shard_map/rd,rf->df/dot_general | solution.py:704
  465.7 9.0 collective-permute-done.19
  479.8 4.2 copy.82
  485.2 45.5 %attend_back_first.1 = (bf16[1024,512]{1,0:T(8,128)(2,1)}, f32[4096,128]{1,0:T(8,128)}, f32[4096,128]{1,0:T(8,128)}) custom-call(s32[6]{0:T(128)} %get-tuple-element.502.meta.refs_0_, bf16[1024,512]{1,0:T(8,128)(2,1)} %pad_maximum_fusion.3.q_ref.refs_1_, bf16[1024,512]{1,0:T(8,128)(2,1)} %get-tuple-element.221.refs_2_, bf16[1024,512]{1,0:T(8,128)(2,1)} %bitcast.179, ...), custom_call_target="tpu_custom_call" | custom-call | flops 1 | bytes 1 | tf_op jit(solution)/shard_map/attend_back_first/pallas_call | solution.py:361
  530.8 2.6 fusion.23
  533.4 3.9 fusion.52
  537.3 6.1 fusion.42
  543.7 22.8 %collective-permute-start.24 = (bf16[256,512]{1,0:T(8,128)(2,1)S(1)}, bf16[256,512]{1,0:T(8,128)(2,1)S(1)}, u32[]{:S(2)}, u32[]{:S(2)}) collective-permute-start(bf16[256,512]{1,0:T(8,128)(2,1)S(1)} %bitcast.185), channel_id=1, source_target_pairs={{0,4},{1,5},{2,6},{3,7},{4,0},{5,1},{6,2},{7,3},{8,12},{9,13},{10,... | collective-permute-start | bytes 786440 | tf_op jit(solution)/shard_map/ppermute | solution.py:658
  567.3 19.4 %collective-permute-start.25 = (bf16[256,512]{1,0:T(8,128)(2,1)}, bf16[256,512]{1,0:T(8,128)(2,1)S(1)}, u32[]{:S(2)}, u32[]{:S(2)}) collective-permute-start(bf16[256,512]{1,0:T(8,128)(2,1)} %bitcast.186), channel_id=1, source_target_pairs={{0,5},{1,6},{2,7},{3,4},{4,1},{5,2},{6,3},{7,0},{8,13},{9,14},{10,... | collective-permute-start | bytes 786440 | tf_op jit(solution)/shard_map/ppermute | solution.py:658
  587.6 3.6 collective-permute-start.26
  592.3 10.2 convolution_convert_fusion.1
  629.6 2.3 collective-permute-start.30
  635.9 70.7 %attend_back_last.1 = (bf16[1024,512]{1,0:T(8,128)(2,1)}, f32[2048,128]{1,0:T(8,128)}, bf16[2048,128]{1,0:T(8,128)(2,1)}) custom-call(s32[6]{0:T(128)} %get-tuple-element.501.refs_0_, bf16[1024,512]{1,0:T(8,128)(2,1)} %copy-done.27, bf16[1024,512]{1,0:T(8,128)(2,1)} %get-tuple-element.230.refs_2_, bf16[1024,512]{1,0:T(8,128)(2,1)} %bitcast.50.refs_3_, ...), custom_call_target="tpu_custom_call" | custom-call | flops 1 | bytes 1 | tf_op jit(solution)/shard_map/attend_back_last/pallas_call | solution.py:416
  709.3 2.7 collective-permute-start.36
  712.6 3.7 collective-permute-start.33
  718.5 43.2 %collective-permute-done.33 = bf16[256,256]{1,0:T(8,128)(2,1)S(1)} collective-permute-done((bf16[256,256]{1,0:T(8,128)(2,1)S(1)}, bf16[256,256]{1,0:T(8,128)(2,1)S(1)}, u32[]{:S(2)}, u32[]{:S(2)}) %collective-permute-start.33) | collective-permute-done | bytes 131104 | tf_op jit(solution)/shard_map/ppermute | solution.py:668
  761.7 2.9 collective-permute-start.34
  764.7 36.1 %collective-permute-done.32 = bf16[256,256]{1,0:T(8,128)(2,1)S(1)} collective-permute-done((bf16[256,256]{1,0:T(8,128)(2,1)S(1)}, bf16[256,256]{1,0:T(8,128)(2,1)S(1)}, u32[]{:S(2)}, u32[]{:S(2)}) %collective-permute-start.32) | collective-permute-done | bytes 131104 | tf_op jit(solution)/shard_map/ppermute | solution.py:668
  801.7 6.6 join.2
  808.8 6.6 join.3
  819.5 2.5 fusion.6
  824.2 3.5 collective-permute-start.38
  831.3 6.1 broadcast.128.clone
  842.6 8.2 collective-permute-done.40
  850.8 10.0 convolution_convert_fusion.3
  860.9 6.9 fusion.1
  885.5 4.0 broadcast_select_fusion
  889.5 4.8 broadcast.128
  894.3 3.0 constant_dynamic-update-slice_fusion
  897.3 10.7 collective-permute-start.44
  915.0 3.1 slice_convert_fusion
  918.1 20.1 %collective-permute-done.43 = bf16[512,2048]{1,0:T(8,128)(2,1)} collective-permute-done((bf16[512,2048]{1,0:T(8,128)(2,1)}, bf16[512,2048]{1,0:T(8,128)(2,1)}, u32[]{:S(2)}, u32[]{:S(2)}) %collective-permute-start.43) | collective-permute-done | bytes 2097184 | tf_op jit(solution)/shard_map/ppermute | solution.py:619
  938.2 38.0 %collective-permute-done.45 = bf16[512,2048]{1,0:T(8,128)(2,1)} collective-permute-done((bf16[512,2048]{1,0:T(8,128)(2,1)}, bf16[512,2048]{1,0:T(8,128)(2,1)}, u32[]{:S(2)}, u32[]{:S(2)}) %collective-permute-start.45) | collective-permute-done | bytes 2097184 | tf_op jit(solution)/shard_map/ppermute | solution.py:619
  982.7 3.8 select_dynamic-update-slice_fusion.3
  990.6 3.9 select_dynamic-update-slice_fusion.2
  994.5 42.8 %reduce-scatter.12.cloned.1.call-done = bf16[256,4224]{1,0:T(8,128)(2,1)} async-done(((bf16[2048,4224]{1,0:T(8,128)(2,1)}), bf16[256,4224]{1,0:T(8,128)(2,1)}) %reduce-scatter.12.cloned.1.call-update) | async-done | bytes 2162704 | tf_op jit(solution)/shard_map/reduce_scatter | solution.py:868
  1041.1 2.4 collective-permute-start.51
  1046.2 32.4 %collective-permute-done.49 = bf16[512,2048]{1,0:T(8,128)(2,1)} collective-permute-done((bf16[512,2048]{1,0:T(8,128)(2,1)}, bf16[512,2048]{1,0:T(8,128)(2,1)}, u32[]{:S(2)}, u32[]{:S(2)}) %collective-permute-start.49) | collective-permute-done | bytes 2097184 | tf_op jit(solution)/shard_map/ppermute | solution.py:619
  1078.6 4.1 collective-permute-done.52
  1093.3 4.3 select_dynamic-update-slice_fusion.1
  1097.6 30.5 %collective-permute-done.54 = bf16[512,2048]{1,0:T(8,128)(2,1)S(1)} collective-permute-done((bf16[512,2048]{1,0:T(8,128)(2,1)}, bf16[512,2048]{1,0:T(8,128)(2,1)S(1)}, u32[]{:S(2)}, u32[]{:S(2)}) %collective-permute-start.54) | collective-permute-done | bytes 2097184 | tf_op jit(solution)/shard_map/ppermute | solution.py:619
  1128.1 2.6 select_dynamic-update-slice_fusion
  (363 shorter events, 139.6 us)
Async XLA Ops:
  7.2 213.5 %all-gather.5.cloned.1.call-start = ((), (), s32[]{:S(2)}) async-start(), calls=%async_computation.10 | async-start | bytes 5242880 | tf_op jit(solution)/shard_map/all_gather | solution.py:811
  10.7 18.8 %collective-permute-start = (bf16[512,512]{1,0:T(8,128)(2,1)S(1)}, bf16[512,512]{1,0:T(8,128)(2,1)S(1)}, u32[]{:S(2)}, u32[]{:S(2)}) collective-permute-start(bf16[512,512]{1,0:T(8,128)(2,1)S(1)} %get-tuple-element.392), channel_id=1, source_target_pairs={{0,1},{1,2},{2,3},{4,5},{5,6},{6,7},{8,9},{9,10},{10,11},{12,13},{... | collective-permute-start | bytes 1572872 | tf_op jit(solution)/shard_map/ppermute | solution.py:618
  15.7 15.4 %collective-permute-start.1 = (bf16[512,512]{1,0:T(8,128)(2,1)S(1)}, bf16[512,512]{1,0:T(8,128)(2,1)}, u32[]{:S(2)}, u32[]{:S(2)}) collective-permute-start(bf16[512,512]{1,0:T(8,128)(2,1)S(1)} %get-tuple-element.392), channel_id=1, source_target_pairs={{1,0},{2,1},{3,2},{5,4},{6,5},{7,6},{9,8},{10,9},{11,10},{13,12},{... | collective-permute-start | bytes 1572872 | tf_op jit(solution)/shard_map/ppermute | solution.py:619
  31.1 22.6 %collective-permute-start.2 = (bf16[512,512]{1,0:T(8,128)(2,1)S(1)}, bf16[512,512]{1,0:T(8,128)(2,1)S(1)}, u32[]{:S(2)}, u32[]{:S(2)}) collective-permute-start(bf16[512,512]{1,0:T(8,128)(2,1)S(1)} %collective-permute-done), channel_id=1, source_target_pairs={{1,2},{2,3},{5,6},{6,7},{9,10},{10,11},{13,14},{14,15},{17,18},{18... | collective-permute-start | bytes 1572872 | tf_op jit(solution)/shard_map/ppermute | solution.py:618
  31.8 21.9 %collective-permute-start.3 = (bf16[512,512]{1,0:T(8,128)(2,1)}, bf16[512,512]{1,0:T(8,128)(2,1)S(1)}, u32[]{:S(2)}, u32[]{:S(2)}) collective-permute-start(bf16[512,512]{1,0:T(8,128)(2,1)} %collective-permute-done.1), channel_id=1, source_target_pairs={{1,0},{2,1},{5,4},{6,5},{9,8},{10,9},{13,12},{14,13},{17,16},{18,1... | collective-permute-start | bytes 1572872 | tf_op jit(solution)/shard_map/ppermute | solution.py:619
  53.6 12.5 %collective-permute-start.4 = (bf16[2048,128]{1,0:T(8,128)(2,1)S(1)}, bf16[2048,128]{1,0:T(8,128)(2,1)S(1)}, u32[]{:S(2)}, u32[]{:S(2)}) collective-permute-start(bf16[2048,128]{1,0:T(8,128)(2,1)S(1)} %get-tuple-element.208.own), channel_id=1, source_target_pairs={{0,4},{4,0},{1,5},{5,1},{2,6},{6,2},{3,7},{7,3},{8,12},{12,8},{9,1... | collective-permute-start | bytes 1572872 | tf_op jit(solution)/shard_map/ppermute | solution.py:795
  55.1 11.0 collective-permute-start.5
  55.8 16.6 %collective-permute-start.6 = (bf16[512,512]{1,0:T(8,128)(2,1)S(1)}, bf16[512,512]{1,0:T(8,128)(2,1)S(1)}, u32[]{:S(2)}, u32[]{:S(2)}) collective-permute-start(bf16[512,512]{1,0:T(8,128)(2,1)S(1)} %collective-permute-done.3), channel_id=1, source_target_pairs={{1,0},{5,4},{9,8},{13,12},{17,16},{21,20},{25,24},{29,28}} | collective-permute-start | bytes 1572872 | tf_op jit(solution)/shard_map/ppermute | solution.py:619
  73.4 67.9 %collective-permute-start.8 = (bf16[4,512,512]{2,1,0:T(8,128)(2,1)}, bf16[4,512,512]{2,1,0:T(8,128)(2,1)}, u32[]{:S(2)}, u32[]{:S(2)}) collective-permute-start(bf16[4,512,512]{2,1,0:T(8,128)(2,1)} %bitcast_dynamic-update-slice_fusion.5.refs_0_), channel_id=1, source_target_pairs={{0,4},{4,0},{1,5},{5,1},{2,6},{6,2},{3,7},{7,3},{8,12},{12,8},{9,1... | collective-permute-start | bytes 6291464 | tf_op jit(solution)/shard_map/ppermute | solution.py:805
  74.7 66.5 %collective-permute-start.7 = (bf16[1024,512]{1,0:T(8,128)(2,1)S(1)}, bf16[1024,512]{1,0:T(8,128)(2,1)S(1)}, u32[]{:S(2)}, u32[]{:S(2)}) collective-permute-start(bf16[1024,512]{1,0:T(8,128)(2,1)S(1)} %slice.189), channel_id=1, source_target_pairs={{0,4},{4,0},{1,5},{5,1},{2,6},{6,2},{3,7},{7,3},{8,12},{12,8},{9,1... | collective-permute-start | bytes 3145736 | tf_op jit(solution)/shard_map/ppermute | solution.py:803
  141.3 166.9 %all-gather.7.cloned.1.call-start = ((), (), s32[]{:S(2)}) async-start(), calls=%async_computation.11 | async-start | bytes 5242880 | tf_op jit(solution)/shard_map/all_gather | solution.py:828
  141.4 51.6 %collective-permute-start.10 = (bf16[4,512,512]{2,1,0:T(8,128)(2,1)}, bf16[4,512,512]{2,1,0:T(8,128)(2,1)S(1)}, u32[]{:S(2)}, u32[]{:S(2)}) collective-permute-start(bf16[4,512,512]{2,1,0:T(8,128)(2,1)} %collective-permute-done.8.refs_1_), channel_id=1, source_target_pairs={{0,8},{8,0},{16,24},{24,16},{1,9},{9,1},{17,25},{25,17},{2,10},{10... | collective-permute-start | bytes 6291464 | tf_op jit(solution)/shard_map/ppermute | solution.py:813
  141.5 51.6 %collective-permute-start.9 = (bf16[4,512,512]{2,1,0:T(8,128)(2,1)}, bf16[4,512,512]{2,1,0:T(8,128)(2,1)}, u32[]{:S(2)}, u32[]{:S(2)}) collective-permute-start(bf16[4,512,512]{2,1,0:T(8,128)(2,1)} %bitcast_dynamic-update-slice_fusion.5.refs_0_), channel_id=1, source_target_pairs={{0,8},{8,0},{16,24},{24,16},{1,9},{9,1},{17,25},{25,17},{2,10},{10... | collective-permute-start | bytes 6291464 | tf_op jit(solution)/shard_map/ppermute | solution.py:813
  193.0 18.4 %collective-permute-start.11 = (bf16[1024,512]{1,0:T(8,128)(2,1)}, bf16[1024,512]{1,0:T(8,128)(2,1)S(1)}, u32[]{:S(2)}, u32[]{:S(2)}) collective-permute-start(bf16[1024,512]{1,0:T(8,128)(2,1)} %get-tuple-element.230.refs_2_), channel_id=1, source_target_pairs={{0,4},{4,0},{1,5},{5,1},{2,6},{6,2},{3,7},{7,3},{8,12},{12,8},{9,1... | collective-permute-start | bytes 3145736 | tf_op jit(solution)/shard_map/ppermute | solution.py:823
  212.5 208.8 %reduce-scatter.6.cloned.1.call-start = ((), (), s32[]{:S(2)}) async-start(), calls=%async_computation.5 | async-start | bytes 5242880 | tf_op jit(solution)/shard_map/reduce_scatter | solution.py:865
  222.0 65.0 %collective-permute-start.12 = (bf16[512,512]{1,0:T(8,128)(2,1)S(1)}, bf16[512,512]{1,0:T(8,128)(2,1)S(1)}, u32[]{:S(2)}, u32[]{:S(2)}) collective-permute-start(bf16[512,512]{1,0:T(8,128)(2,1)S(1)} %get-tuple-element.388), channel_id=1, source_target_pairs={{0,1},{1,2},{2,3},{4,5},{5,6},{6,7},{8,9},{9,10},{10,11},{12,13},{... | collective-permute-start | bytes 1572872 | tf_op jit(solution)/shard_map/ppermute | solution.py:618
  223.3 63.6 %collective-permute-start.13 = (bf16[512,512]{1,0:T(8,128)(2,1)S(1)}, bf16[512,512]{1,0:T(8,128)(2,1)}, u32[]{:S(2)}, u32[]{:S(2)}) collective-permute-start(bf16[512,512]{1,0:T(8,128)(2,1)S(1)} %get-tuple-element.388), channel_id=1, source_target_pairs={{1,0},{2,1},{3,2},{5,4},{6,5},{7,6},{9,8},{10,9},{11,10},{13,12},{... | collective-permute-start | bytes 1572872 | tf_op jit(solution)/shard_map/ppermute | solution.py:619
  308.2 222.5 %reduce-scatter.8.cloned.1.call-start = ((), (), s32[]{:S(2)}) async-start(), calls=%async_computation.6 | async-start | bytes 5242880 | tf_op jit(solution)/shard_map/reduce_scatter | solution.py:865
  313.2 64.6 %collective-permute-start.14 = (bf16[512,512]{1,0:T(8,128)(2,1)S(1)}, bf16[512,512]{1,0:T(8,128)(2,1)S(1)}, u32[]{:S(2)}, u32[]{:S(2)}) collective-permute-start(bf16[512,512]{1,0:T(8,128)(2,1)S(1)} %collective-permute-done.12), channel_id=1, source_target_pairs={{1,2},{2,3},{5,6},{6,7},{9,10},{10,11},{13,14},{14,15},{17,18},{18... | collective-permute-start | bytes 1572872 | tf_op jit(solution)/shard_map/ppermute | solution.py:618
  313.9 64.7 %collective-permute-start.15 = (bf16[512,512]{1,0:T(8,128)(2,1)}, bf16[512,512]{1,0:T(8,128)(2,1)}, u32[]{:S(2)}, u32[]{:S(2)}) collective-permute-start(bf16[512,512]{1,0:T(8,128)(2,1)} %collective-permute-done.13), channel_id=1, source_target_pairs={{1,0},{2,1},{5,4},{6,5},{9,8},{10,9},{13,12},{14,13},{17,16},{18,1... | collective-permute-start | bytes 1572872 | tf_op jit(solution)/shard_map/ppermute | solution.py:619
  378.7 42.6 %collective-permute-start.16 = (bf16[512,512]{1,0:T(8,128)(2,1)}, bf16[512,512]{1,0:T(8,128)(2,1)S(1)}, u32[]{:S(2)}, u32[]{:S(2)}) collective-permute-start(bf16[512,512]{1,0:T(8,128)(2,1)} %copy-done.35), channel_id=1, source_target_pairs={{2,3},{6,7},{10,11},{14,15},{18,19},{22,23},{26,27},{30,31}} | collective-permute-start | bytes 1572872 | tf_op jit(solution)/shard_map/ppermute | solution.py:618
  379.4 41.9 %collective-permute-start.17 = (bf16[512,512]{1,0:T(8,128)(2,1)}, bf16[512,512]{1,0:T(8,128)(2,1)}, u32[]{:S(2)}, u32[]{:S(2)}) collective-permute-start(bf16[512,512]{1,0:T(8,128)(2,1)} %collective-permute-done.15), channel_id=1, source_target_pairs={{1,0},{5,4},{9,8},{13,12},{17,16},{21,20},{25,24},{29,28}} | collective-permute-start | bytes 1572872 | tf_op jit(solution)/shard_map/ppermute | solution.py:619
  380.7 508.8 %reduce-scatter.10.cloned.1.call-start = ((), (), s32[]{:S(2)}) async-start(), calls=%async_computation.7 | async-start | bytes 10485760 | tf_op jit(solution)/shard_map/reduce_scatter | solution.py:865
  422.7 52.5 %collective-permute-start.21 = (bf16[4,512,512]{2,1,0:T(8,128)(2,1)S(1)}, bf16[4,512,512]{2,1,0:T(8,128)(2,1)}, u32[]{:S(2)}, u32[]{:S(2)}) collective-permute-start(bf16[4,512,512]{2,1,0:T(8,128)(2,1)S(1)} %bitcast_dynamic-update-slice_fusion.refs_0_), channel_id=1, source_target_pairs={{0,4},{4,0},{1,5},{5,1},{2,6},{6,2},{3,7},{7,3},{8,12},{12,8},{9,1... | collective-permute-start | bytes 6291464 | tf_op jit(solution)/shard_map/ppermute | solution.py:900
  437.7 28.0 %collective-permute-start.18 = (bf16[256,512]{1,0:T(8,128)(2,1)}, bf16[256,512]{1,0:T(8,128)(2,1)S(1)}, u32[]{:S(2)}, u32[]{:S(2)}) collective-permute-start(bf16[256,512]{1,0:T(8,128)(2,1)} %bitcast.23), channel_id=1, source_target_pairs={{0,1},{1,2},{2,3},{3,0},{4,5},{5,6},{6,7},{7,4},{8,9},{9,10},{10,1... | collective-permute-start | bytes 786440 | tf_op jit(solution)/shard_map/ppermute | solution.py:668
  441.3 33.5 %collective-permute-start.19 = (bf16[256,512]{1,0:T(8,128)(2,1)}, bf16[256,512]{1,0:T(8,128)(2,1)S(1)}, u32[]{:S(2)}, u32[]{:S(2)}) collective-permute-start(bf16[256,512]{1,0:T(8,128)(2,1)} %bitcast.24), channel_id=1, source_target_pairs={{0,2},{1,3},{2,0},{3,1},{4,6},{5,7},{6,4},{7,5},{8,10},{9,11},{10,... | collective-permute-start | bytes 786440 | tf_op jit(solution)/shard_map/ppermute | solution.py:668
  443.5 31.7 %collective-permute-start.20 = (bf16[256,512]{1,0:T(8,128)(2,1)}, bf16[256,512]{1,0:T(8,128)(2,1)S(1)}, u32[]{:S(2)}, u32[]{:S(2)}) collective-permute-start(bf16[256,512]{1,0:T(8,128)(2,1)} %bitcast.189), channel_id=1, source_target_pairs={{0,3},{1,0},{2,1},{3,2},{4,7},{5,4},{6,5},{7,6},{8,11},{9,8},{10,9... | collective-permute-start | bytes 786440 | tf_op jit(solution)/shard_map/ppermute | solution.py:668
  475.2 55.6 %collective-permute-start.22 = (bf16[4,512,512]{2,1,0:T(8,128)(2,1)S(1)}, bf16[4,512,512]{2,1,0:T(8,128)(2,1)}, u32[]{:S(2)}, u32[]{:S(2)}) collective-permute-start(bf16[4,512,512]{2,1,0:T(8,128)(2,1)S(1)} %bitcast_dynamic-update-slice_fusion.refs_0_), channel_id=1, source_target_pairs={{0,8},{8,0},{16,24},{24,16},{1,9},{9,1},{17,25},{25,17},{2,10},{10... | collective-permute-start | bytes 6291464 | tf_op jit(solution)/shard_map/ppermute | solution.py:912
  475.2 55.6 %collective-permute-start.23 = (bf16[4,512,512]{2,1,0:T(8,128)(2,1)}, bf16[4,512,512]{2,1,0:T(8,128)(2,1)}, u32[]{:S(2)}, u32[]{:S(2)}) collective-permute-start(bf16[4,512,512]{2,1,0:T(8,128)(2,1)} %collective-permute-done.21.refs_1_), channel_id=1, source_target_pairs={{0,8},{8,0},{16,24},{24,16},{1,9},{9,1},{17,25},{25,17},{2,10},{10... | collective-permute-start | bytes 6291464 | tf_op jit(solution)/shard_map/ppermute | solution.py:912
  543.7 58.7 %collective-permute-start.24 = (bf16[256,512]{1,0:T(8,128)(2,1)S(1)}, bf16[256,512]{1,0:T(8,128)(2,1)S(1)}, u32[]{:S(2)}, u32[]{:S(2)}) collective-permute-start(bf16[256,512]{1,0:T(8,128)(2,1)S(1)} %bitcast.185), channel_id=1, source_target_pairs={{0,4},{1,5},{2,6},{3,7},{4,0},{5,1},{6,2},{7,3},{8,12},{9,13},{10,... | collective-permute-start | bytes 786440 | tf_op jit(solution)/shard_map/ppermute | solution.py:658
  567.3 35.1 %collective-permute-start.25 = (bf16[256,512]{1,0:T(8,128)(2,1)}, bf16[256,512]{1,0:T(8,128)(2,1)S(1)}, u32[]{:S(2)}, u32[]{:S(2)}) collective-permute-start(bf16[256,512]{1,0:T(8,128)(2,1)} %bitcast.186), channel_id=1, source_target_pairs={{0,5},{1,6},{2,7},{3,4},{4,1},{5,2},{6,3},{7,0},{8,13},{9,14},{10,... | collective-permute-start | bytes 786440 | tf_op jit(solution)/shard_map/ppermute | solution.py:658
  587.6 14.8 %collective-permute-start.26 = (bf16[256,512]{1,0:T(8,128)(2,1)}, bf16[256,512]{1,0:T(8,128)(2,1)S(1)}, u32[]{:S(2)}, u32[]{:S(2)}) collective-permute-start(bf16[256,512]{1,0:T(8,128)(2,1)} %bitcast.187), channel_id=1, source_target_pairs={{0,6},{1,7},{2,4},{3,5},{4,2},{5,3},{6,0},{7,1},{8,14},{9,15},{10,... | collective-permute-start | bytes 786440 | tf_op jit(solution)/shard_map/ppermute | solution.py:658
  592.1 10.4 collective-permute-start.27
  603.4 311.6 %reduce-scatter.14.cloned.1.call-start = ((), (), s32[]{:S(2)}) async-start(), calls=%async_computation.9 | async-start | bytes 12976128 | tf_op jit(solution)/shard_map/reduce_scatter | solution.py:868
  627.6 79.0 %collective-permute-start.28 = (bf16[256,512]{1,0:T(8,128)(2,1)}, bf16[256,512]{1,0:T(8,128)(2,1)}, u32[]{:S(2)}, u32[]{:S(2)}) collective-permute-start(bf16[256,512]{1,0:T(8,128)(2,1)} %get-tuple-element.423), channel_id=1, source_target_pairs={{0,1},{1,2},{2,3},{3,0},{4,5},{5,6},{6,7},{7,4},{8,9},{9,10},{10,1... | collective-permute-start | bytes 786440 | tf_op jit(solution)/shard_map/ppermute | solution.py:668
  628.9 77.7 %collective-permute-start.29 = (bf16[256,512]{1,0:T(8,128)(2,1)S(1)}, bf16[256,512]{1,0:T(8,128)(2,1)}, u32[]{:S(2)}, u32[]{:S(2)}) collective-permute-start(bf16[256,512]{1,0:T(8,128)(2,1)S(1)} %get-tuple-element.422), channel_id=1, source_target_pairs={{0,2},{1,3},{2,0},{3,1},{4,6},{5,7},{6,4},{7,5},{8,10},{9,11},{10,... | collective-permute-start | bytes 786440 | tf_op jit(solution)/shard_map/ppermute | solution.py:668
  629.6 77.0 %collective-permute-start.30 = (bf16[256,512]{1,0:T(8,128)(2,1)S(1)}, bf16[256,512]{1,0:T(8,128)(2,1)}, u32[]{:S(2)}, u32[]{:S(2)}) collective-permute-start(bf16[256,512]{1,0:T(8,128)(2,1)S(1)} %get-tuple-element.421), channel_id=1, source_target_pairs={{0,3},{1,0},{2,1},{3,2},{4,7},{5,4},{6,5},{7,6},{8,11},{9,8},{10,9... | collective-permute-start | bytes 786440 | tf_op jit(solution)/shard_map/ppermute | solution.py:668
  709.2 99.2 %collective-permute-start.37 = (bf16[256,768]{1,0:T(8,128)(2,1)S(1)}, bf16[256,768]{1,0:T(8,128)(2,1)S(1)}, u32[]{:S(2)}, u32[]{:S(2)}) collective-permute-start(bf16[256,768]{1,0:T(8,128)(2,1)S(1)} %pad_maximum_fusion.19), channel_id=1, source_target_pairs={{0,7},{1,4},{2,5},{3,6},{4,3},{5,0},{6,1},{7,2},{8,15},{9,12},{10,... | collective-permute-start | bytes 1179656 | tf_op jit(solution)/shard_map/ppermute | solution.py:658
  709.3 99.1 %collective-permute-start.36 = (bf16[256,768]{1,0:T(8,128)(2,1)S(1)}, bf16[256,768]{1,0:T(8,128)(2,1)S(1)}, u32[]{:S(2)}, u32[]{:S(2)}) collective-permute-start(bf16[256,768]{1,0:T(8,128)(2,1)S(1)} %pad_maximum_fusion.18), channel_id=1, source_target_pairs={{0,6},{1,7},{2,4},{3,5},{4,2},{5,3},{6,0},{7,1},{8,14},{9,15},{10,... | collective-permute-start | bytes 1179656 | tf_op jit(solution)/shard_map/ppermute | solution.py:658
  712.1 96.3 %collective-permute-start.35 = (bf16[256,768]{1,0:T(8,128)(2,1)S(1)}, bf16[256,768]{1,0:T(8,128)(2,1)S(1)}, u32[]{:S(2)}, u32[]{:S(2)}) collective-permute-start(bf16[256,768]{1,0:T(8,128)(2,1)S(1)} %pad_maximum_fusion.17), channel_id=1, source_target_pairs={{0,5},{1,6},{2,7},{3,4},{4,1},{5,2},{6,3},{7,0},{8,13},{9,14},{10,... | collective-permute-start | bytes 1179656 | tf_op jit(solution)/shard_map/ppermute | solution.py:658
  712.6 49.1 %collective-permute-start.33 = (bf16[256,256]{1,0:T(8,128)(2,1)S(1)}, bf16[256,256]{1,0:T(8,128)(2,1)S(1)}, u32[]{:S(2)}, u32[]{:S(2)}) collective-permute-start(bf16[256,256]{1,0:T(8,128)(2,1)S(1)} %pad_maximum_fusion.23), channel_id=1, source_target_pairs={{0,3},{1,0},{2,1},{3,2},{4,7},{5,4},{6,5},{7,6},{8,11},{9,8},{10,9... | collective-permute-start | bytes 393224 | tf_op jit(solution)/shard_map/ppermute | solution.py:668
  716.3 84.4 %collective-permute-start.32 = (bf16[256,256]{1,0:T(8,128)(2,1)S(1)}, bf16[256,256]{1,0:T(8,128)(2,1)S(1)}, u32[]{:S(2)}, u32[]{:S(2)}) collective-permute-start(bf16[256,256]{1,0:T(8,128)(2,1)S(1)} %pad_maximum_fusion.22), channel_id=1, source_target_pairs={{0,2},{1,3},{2,0},{3,1},{4,6},{5,7},{6,4},{7,5},{8,10},{9,11},{10,... | collective-permute-start | bytes 393224 | tf_op jit(solution)/shard_map/ppermute | solution.py:668
  761.7 46.7 %collective-permute-start.34 = (bf16[256,768]{1,0:T(8,128)(2,1)S(1)}, bf16[256,768]{1,0:T(8,128)(2,1)S(1)}, u32[]{:S(2)}, u32[]{:S(2)}) collective-permute-start(bf16[256,768]{1,0:T(8,128)(2,1)S(1)} %pad_maximum_fusion.16), channel_id=1, source_target_pairs={{0,4},{1,5},{2,6},{3,7},{4,0},{5,1},{6,2},{7,3},{8,12},{9,13},{10,... | collective-permute-start | bytes 1179656 | tf_op jit(solution)/shard_map/ppermute | solution.py:658
  800.7 7.6 collective-permute-start.31
  822.0 215.3 %reduce-scatter.12.cloned.1.call-start = ((), (), s32[]{:S(2)}) async-start(), calls=%async_computation.8 | async-start | bytes 19464192 | tf_op jit(solution)/shard_map/reduce_scatter | solution.py:868
  824.2 43.6 %collective-permute-start.38 = (bf16[512,2048]{1,0:T(8,128)(2,1)S(1)}, bf16[512,2048]{1,0:T(8,128)(2,1)}, u32[]{:S(2)}, u32[]{:S(2)}) collective-permute-start(bf16[512,2048]{1,0:T(8,128)(2,1)S(1)} %fusion.6), channel_id=1, source_target_pairs={{0,1},{1,2},{2,3},{4,5},{5,6},{6,7},{8,9},{9,10},{10,11},{12,13},{... | collective-permute-start | bytes 6291464 | tf_op jit(solution)/shard_map/ppermute | solution.py:618
  827.7 40.1 %collective-permute-start.39 = (bf16[512,2048]{1,0:T(8,128)(2,1)S(1)}, bf16[512,2048]{1,0:T(8,128)(2,1)}, u32[]{:S(2)}, u32[]{:S(2)}) collective-permute-start(bf16[512,2048]{1,0:T(8,128)(2,1)S(1)} %fusion.6), channel_id=1, source_target_pairs={{1,0},{2,1},{3,2},{5,4},{6,5},{7,6},{9,8},{10,9},{11,10},{13,12},{... | collective-permute-start | bytes 6291464 | tf_op jit(solution)/shard_map/ppermute | solution.py:619
  829.2 11.3 collective-permute-start.41
  830.9 19.9 %collective-permute-start.40 = (bf16[1024,512]{1,0:T(8,128)(2,1)}, bf16[1024,512]{1,0:T(8,128)(2,1)}, u32[]{:S(2)}, u32[]{:S(2)}) collective-permute-start(bf16[1024,512]{1,0:T(8,128)(2,1)} %get-tuple-element.338), channel_id=1, source_target_pairs={{0,4},{4,0},{1,5},{5,1},{2,6},{6,2},{3,7},{7,3},{8,12},{12,8},{9,1... | collective-permute-start | bytes 3145736 | tf_op jit(solution)/shard_map/ppermute | solution.py:1005
  839.5 21.3 %slice-start.2 = ((s8[5767168]{0:T(1024)(128)(4,1)}), s8[4194304]{0:T(1024)(128)(4,1)S(1)}, s32[]{:S(2)}) async-start(s8[5767168]{0:T(1024)(128)(4,1)} %bitcast.176), calls=%async_computation.14 | async-start | bytes 8388608
  840.5 20.3 %slice-start = ((s8[8388608]{0:T(1024)(128)(4,1)}), s8[4194304]{0:T(1024)(128)(4,1)S(1)}, s32[]{:S(2)}) async-start(s8[8388608]{0:T(1024)(128)(4,1)} %bitcast.170), calls=%async_computation.12 | async-start | bytes 8388608
  882.2 36.0 %collective-permute-start.42 = (bf16[512,2048]{1,0:T(8,128)(2,1)}, bf16[512,2048]{1,0:T(8,128)(2,1)}, u32[]{:S(2)}, u32[]{:S(2)}) collective-permute-start(bf16[512,2048]{1,0:T(8,128)(2,1)} %collective-permute-done.38), channel_id=1, source_target_pairs={{1,2},{2,3},{5,6},{6,7},{9,10},{10,11},{13,14},{14,15},{17,18},{18... | collective-permute-start | bytes 6291464 | tf_op jit(solution)/shard_map/ppermute | solution.py:618
  884.2 54.1 %collective-permute-start.43 = (bf16[512,2048]{1,0:T(8,128)(2,1)}, bf16[512,2048]{1,0:T(8,128)(2,1)}, u32[]{:S(2)}, u32[]{:S(2)}) collective-permute-start(bf16[512,2048]{1,0:T(8,128)(2,1)} %collective-permute-done.39), channel_id=1, source_target_pairs={{1,0},{2,1},{5,4},{6,5},{9,8},{10,9},{13,12},{14,13},{17,16},{18,1... | collective-permute-start | bytes 6291464 | tf_op jit(solution)/shard_map/ppermute | solution.py:619
  897.3 41.0 %collective-permute-start.44 = (bf16[512,2048]{1,0:T(8,128)(2,1)}, bf16[512,2048]{1,0:T(8,128)(2,1)}, u32[]{:S(2)}, u32[]{:S(2)}) collective-permute-start(bf16[512,2048]{1,0:T(8,128)(2,1)} %get-tuple-element.355), channel_id=1, source_target_pairs={{0,1},{1,2},{2,3},{4,5},{5,6},{6,7},{8,9},{9,10},{10,11},{12,13},{... | collective-permute-start | bytes 6291464 | tf_op jit(solution)/shard_map/ppermute | solution.py:618
  907.9 68.3 %collective-permute-start.45 = (bf16[512,2048]{1,0:T(8,128)(2,1)}, bf16[512,2048]{1,0:T(8,128)(2,1)}, u32[]{:S(2)}, u32[]{:S(2)}) collective-permute-start(bf16[512,2048]{1,0:T(8,128)(2,1)} %get-tuple-element.355), channel_id=1, source_target_pairs={{1,0},{2,1},{3,2},{5,4},{6,5},{7,6},{9,8},{10,9},{11,10},{13,12},{... | collective-permute-start | bytes 6291464 | tf_op jit(solution)/shard_map/ppermute | solution.py:619
  976.3 64.9 %collective-permute-start.46 = (bf16[512,2048]{1,0:T(8,128)(2,1)}, bf16[512,2048]{1,0:T(8,128)(2,1)}, u32[]{:S(2)}, u32[]{:S(2)}) collective-permute-start(bf16[512,2048]{1,0:T(8,128)(2,1)} %collective-permute-done.42), channel_id=1, source_target_pairs={{2,3},{6,7},{10,11},{14,15},{18,19},{22,23},{26,27},{30,31}} | collective-permute-start | bytes 6291464 | tf_op jit(solution)/shard_map/ppermute | solution.py:618
  978.2 65.4 %collective-permute-start.47 = (bf16[512,2048]{1,0:T(8,128)(2,1)}, bf16[512,2048]{1,0:T(8,128)(2,1)}, u32[]{:S(2)}, u32[]{:S(2)}) collective-permute-start(bf16[512,2048]{1,0:T(8,128)(2,1)} %collective-permute-done.43), channel_id=1, source_target_pairs={{1,0},{5,4},{9,8},{13,12},{17,16},{21,20},{25,24},{29,28}} | collective-permute-start | bytes 6291464 | tf_op jit(solution)/shard_map/ppermute | solution.py:619
  979.5 66.7 %collective-permute-start.48 = (bf16[512,2048]{1,0:T(8,128)(2,1)}, bf16[512,2048]{1,0:T(8,128)(2,1)}, u32[]{:S(2)}, u32[]{:S(2)}) collective-permute-start(bf16[512,2048]{1,0:T(8,128)(2,1)} %collective-permute-done.44), channel_id=1, source_target_pairs={{1,2},{2,3},{5,6},{6,7},{9,10},{10,11},{13,14},{14,15},{17,18},{18... | collective-permute-start | bytes 6291464 | tf_op jit(solution)/shard_map/ppermute | solution.py:618
  981.4 97.2 %collective-permute-start.49 = (bf16[512,2048]{1,0:T(8,128)(2,1)}, bf16[512,2048]{1,0:T(8,128)(2,1)}, u32[]{:S(2)}, u32[]{:S(2)}) collective-permute-start(bf16[512,2048]{1,0:T(8,128)(2,1)} %collective-permute-done.45), channel_id=1, source_target_pairs={{1,0},{2,1},{5,4},{6,5},{9,8},{10,9},{13,12},{14,13},{17,16},{18,1... | collective-permute-start | bytes 6291464 | tf_op jit(solution)/shard_map/ppermute | solution.py:619
  1038.7 39.9 %collective-permute-start.50 = (bf16[256,768]{1,0:T(8,128)(2,1)S(1)}, bf16[256,768]{1,0:T(8,128)(2,1)S(1)}, u32[]{:S(2)}, u32[]{:S(2)}) collective-permute-start(bf16[256,768]{1,0:T(8,128)(2,1)S(1)} %get-tuple-element.460), channel_id=1, source_target_pairs={{0,1},{1,2},{2,3},{3,0},{4,5},{5,6},{6,7},{7,4},{8,9},{9,10},{10,1... | collective-permute-start | bytes 1179656 | tf_op jit(solution)/shard_map/ppermute | solution.py:668
  1041.1 37.5 %collective-permute-start.51 = (bf16[256,768]{1,0:T(8,128)(2,1)S(1)}, bf16[256,768]{1,0:T(8,128)(2,1)S(1)}, u32[]{:S(2)}, u32[]{:S(2)}) collective-permute-start(bf16[256,768]{1,0:T(8,128)(2,1)S(1)} %get-tuple-element.461), channel_id=1, source_target_pairs={{0,2},{1,3},{2,0},{3,1},{4,6},{5,7},{6,4},{7,5},{8,10},{9,11},{10,... | collective-permute-start | bytes 1179656 | tf_op jit(solution)/shard_map/ppermute | solution.py:668
  1043.6 39.2 %collective-permute-start.52 = (bf16[256,768]{1,0:T(8,128)(2,1)S(1)}, bf16[256,768]{1,0:T(8,128)(2,1)S(1)}, u32[]{:S(2)}, u32[]{:S(2)}) collective-permute-start(bf16[256,768]{1,0:T(8,128)(2,1)S(1)} %get-tuple-element.459), channel_id=1, source_target_pairs={{0,3},{1,0},{2,1},{3,2},{4,7},{5,4},{6,5},{7,6},{8,11},{9,8},{10,9... | collective-permute-start | bytes 1179656 | tf_op jit(solution)/shard_map/ppermute | solution.py:668
  1085.4 12.2 %collective-permute-start.53 = (bf16[512,2048]{1,0:T(8,128)(2,1)}, bf16[512,2048]{1,0:T(8,128)(2,1)S(1)}, u32[]{:S(2)}, u32[]{:S(2)}) collective-permute-start(bf16[512,2048]{1,0:T(8,128)(2,1)} %collective-permute-done.48), channel_id=1, source_target_pairs={{2,3},{6,7},{10,11},{14,15},{18,19},{22,23},{26,27},{30,31}} | collective-permute-start | bytes 6291464 | tf_op jit(solution)/shard_map/ppermute | solution.py:618
  1086.2 41.9 %collective-permute-start.54 = (bf16[512,2048]{1,0:T(8,128)(2,1)}, bf16[512,2048]{1,0:T(8,128)(2,1)S(1)}, u32[]{:S(2)}, u32[]{:S(2)}) collective-permute-start(bf16[512,2048]{1,0:T(8,128)(2,1)} %collective-permute-done.49), channel_id=1, source_target_pairs={{1,0},{5,4},{9,8},{13,12},{17,16},{21,20},{25,24},{29,28}} | collective-permute-start | bytes 6291464 | tf_op jit(solution)/shard_map/ppermute | solution.py:619
  (54 other events, 216.1 us)
Sparse Core Ops, SparseCore 0:
  141.4 79.2 all-gather.4
  222.2 85.9 all-gather.6
  310.5 94.9 reduce-scatter.5
  407.8 91.5 reduce-scatter.7
  602.6 202.4 reduce-scatter.9
  822.1 92.8 reduce-scatter.13
  918.7 118.5 reduce-scatter.11

commit v5 on v4

--- a/solution.py
+++ b/solution.py
@@ -24,13 +24,29 @@
 
 
 def project_kernel(
-    head, tokens_ref, gain_ref, k_weight, v_weight, q_weight, cos_ref, sin_ref, kv_ref, q_ref, normed_ref
+    head,
+    tokens_ref,
+    gain_ref,
+    k_weight,
+    v_weight,
+    q_weight,
+    cos_part,
+    sin_part,
+    kv_ref,
+    q_ref,
+    normed_ref,
+    cos_ref,
+    sin_ref,
 ):
     inputs = tokens_ref[...].astype(F32)
     inverse = lax.rsqrt(jnp.mean(inputs * inputs, axis=-1, keepdims=True) + EPSILON)
     normed = (inputs * inverse * gain_ref[...]).astype(BF16)
     normed_ref[...] = normed
-    cos, sin = cos_ref[...], sin_ref[...]
+    cos, sin = cos_part[...], sin_part[...]
+    cos = jnp.concatenate([cos, cos, cos, cos], axis=0).T
+    sin = jnp.concatenate([-sin, sin, -sin, sin], axis=0).T
+    cos_ref[...] = cos
+    sin_ref[...] = sin
     first = head[0] % 2 == 0
     key = jnp.dot(normed, k_weight[...], preferred_element_type=F32)
     value = jnp.dot(normed, v_weight[...], preferred_element_type=F32)
@@ -60,19 +76,23 @@
                 two_heads,
                 two_heads,
                 pl.BlockSpec((width, columns), lambda i, head: (0, 0)),
-                pl.BlockSpec((block, 128), lambda i, head: (i, 0)),
-                pl.BlockSpec((block, 128), lambda i, head: (i, 0)),
+                pl.BlockSpec((HD // 2, block), lambda i, head: (0, i)),
+                pl.BlockSpec((HD // 2, block), lambda i, head: (0, i)),
             ],
             out_specs=[
                 pl.BlockSpec((block, 128), lambda i, head: (i, 0)),
                 pl.BlockSpec((block, columns), lambda i, head: (i, 0)),
                 pl.BlockSpec((block, width), lambda i, head: (i, 0)),
+                pl.BlockSpec((block, 128), lambda i, head: (i, 0)),
+                pl.BlockSpec((block, 128), lambda i, head: (i, 0)),
             ],
         ),
         out_shape=[
             jax.ShapeDtypeStruct((rows, 128), BF16),
             jax.ShapeDtypeStruct((rows, columns), BF16),
             jax.ShapeDtypeStruct((rows, width), BF16),
+            jax.ShapeDtypeStruct((rows, 128), F32),
+            jax.ShapeDtypeStruct((rows, 128), F32),
         ],
         compiler_params=pltpu.CompilerParams(vmem_limit_bytes=48 * 2**20),
         cost_estimate=LIGHT,
@@ -561,24 +581,24 @@
 
 
 def arrange_kernel(order, *refs):
-    for part, weight_ref in enumerate(refs[:4]):
+    for part, weight_ref in enumerate(refs[:-1]):
 
         @pl.when(pl.program_id(0) == part)
         def _():
-            refs[4][...] = weight_ref[...]
-
-
-def arrange(order, parts):
-    size, rows, features = parts[0].shape
+            refs[-1][...] = weight_ref[...].reshape(refs[-1].shape)
+
+
+def arrange(order, parts, shape, block, place):
+    zeros = (0,) * parts[0].ndim
     return pl.pallas_call(
         arrange_kernel,
         grid_spec=pltpu.PrefetchScalarGridSpec(
             num_scalar_prefetch=1,
-            grid=(4,),
-            in_specs=part_specs(parts[0].shape),
-            out_specs=pl.BlockSpec((size, rows, features), lambda p, order: (0, order[p], 0)),
+            grid=(len(parts),),
+            in_specs=[pl.BlockSpec(parts[0].shape, lambda p, order: zeros) for _ in parts],
+            out_specs=pl.BlockSpec(block, lambda p, order: place(order[p])),
         ),
-        out_shape=jax.ShapeDtypeStruct((size, 4 * rows, features), parts[0].dtype),
+        out_shape=jax.ShapeDtypeStruct(shape, parts[0].dtype),
         compiler_params=pltpu.CompilerParams(vmem_limit_bytes=48 * 2**20),
         cost_estimate=LIGHT,
         name="arrange",
@@ -640,12 +660,25 @@
             target, jnp.where(from_right, left, self.piece), jnp.where(from_right, me + hop, me)
         )
 
-    def collect(self, place, target):
+    def whole(self):
+        size = lax.axis_size("tensor")
+        me = lax.axis_index("tensor")
         while len(self.rights) <= len(self.hops):
             self.step()
-        for hop in range(len(self.rights)):
-            target = self.place_hop(place, target, hop)
-        return target
+        parts, order = [self.piece], [me]
+        for hop in range(1, size):
+            for came, source in ((self.rights[hop], me - hop), (self.lefts[hop], me + hop)):
+                parts.append(came)
+                order.append(jnp.where((source >= 0) & (source < size), source, me))
+        parts, order = parts[::-1], order[::-1]
+        shape = self.piece.shape
+        return arrange(
+            jnp.stack(order).astype(jnp.int32),
+            parts,
+            (size, *shape),
+            (1, *shape),
+            lambda i: (i,) + (0,) * len(shape),
+        )
 
 
 def send_blocks(pick, across=False):
@@ -686,10 +719,6 @@
 def rows_part(weight, index, count):
     rows = weight.shape[0] // count
     return lax.dynamic_slice_in_dim(weight, index * rows, rows, 0)
-
-
-def by_source(target, piece, source):
-    return lax.dynamic_update_index_in_dim(target, piece, source, 0)
 
 
 def dot(a, b):
@@ -774,23 +803,14 @@
         ]
     ).astype(jnp.int32)
 
-    def quarter_gather(weight):
-        return Gather(rows_part(weight, 2 * upper + ctx_index, 4))
-
-    def quarter_collect(gather):
-        return gather.collect(by_source, jnp.zeros((groups, *gather.piece.shape), BF16))
-
-    output_gather = quarter_gather(w_output)
+    output_gather = Gather(rows_part(w_output, upper, 2))
     hop = output_gather.step()
-    cos_near, sin_near = table(positions[:tok_rows])
-    cos_near, sin_near, hop, quarters, head = hold(cos_near, sin_near, hop, quarters, head)
-    output_gather.held(hop)
-    hop = output_gather.step()
-
-    kv_own, queries, normed = project(
-        head, tokens, norm_attn, w_key, w_value, w_query, cos_near, sin_near
-    )
-    kv_own, queries, normed, hop = hold(kv_own, queries, normed, hop)
+    angles = frequency[:, None] * positions[:tok_rows].astype(F32)[None, :]
+    cos_part, sin_part = hold(jnp.cos(angles), jnp.sin(angles))
+    kv_own, queries, normed, cos_near, sin_near = project(
+        head, tokens, norm_attn, w_key, w_value, w_query, cos_part, sin_part
+    )
+    kv_own, queries, normed, hop, quarters = hold(kv_own, queries, normed, hop, quarters)
     output_gather.held(hop)
     kv_other = lax.ppermute(kv_own, "ctx", over)
     hop = output_gather.step()
@@ -801,16 +821,15 @@
     length = 2 * tok_rows
 
     foreign = lax.ppermute(sent, "ctx", over)
-    output_part = quarter_collect(output_gather)
-    output_over = lax.ppermute(output_part, "ctx", over)
+    hop = output_gather.step()
     first, first_log, *forms = attend_first(metas[0], offsets[0], kept, kv_own, kv_other)
-    first, first_log, foreign, forms, output_near = hold(
-        first, first_log, foreign, forms, (output_part, output_over)
-    )
+    first, first_log, foreign, forms, hop = hold(first, first_log, foreign, forms, hop)
+    output_gather.held(hop)
     *forms, values_t = forms
     first_whole = lax.all_gather(first, "tensor", axis=0, tiled=False)
 
-    output_far = tuple(lax.ppermute(part, "dp", beside) for part in output_near)
+    output_near = output_gather.whole()
+    output_far = lax.ppermute(output_near, "dp", beside)
     second, second_log = attend(metas[1], offsets[1], foreign, forms[0], forms[1], values_t)
     second, second_log, output_near, output_far = hold(
         second, second_log, output_near, output_far
@@ -821,7 +840,14 @@
     sin_pair = jnp.concatenate([sin_near, sin_far], axis=0)
     tables = [(chunk(cos_near, 0), chunk(sin_near, 0)), (chunk(cos_far, 1), chunk(sin_far, 1))]
     second_home = lax.ppermute(second, "ctx", over)
-    output_whole = arrange(quarters, output_near + output_far)
+    half_rows = output_near.shape[1]
+    output_whole = arrange(
+        jnp.stack([upper, 1 - upper]).astype(jnp.int32),
+        [output_near, output_far],
+        (groups, 2 * half_rows, features),
+        output_near.shape,
+        lambda i: (0, i, 0),
+    )
     second_home, output_whole, tables, cos_pair, sin_pair = hold(
         second_home, output_whole, tables, cos_pair, sin_pair
     )
@@ -869,7 +895,7 @@
             gradient.astype(BF16), ("dp", "ctx"), scatter_dimension=0, tiled=True
         )
 
-    query_gather = quarter_gather(after(w_query, first_whole))
+    query_gather = Gather(rows_part(after(w_query, first_whole), 2 * upper + ctx_index, 4))
     hop = query_gather.step()
     weights = (w_gate, w_up, w_down)
     fixed = (tokens, cotangent, norm_mlp, output_whole, weights)
@@ -890,13 +916,15 @@
     w_gates, hop, share_first = hold(w_gates, hop, share_first)
     query_gather.held(hop)
 
+    mlp_share = line_sum(after(mlp_part, w_gates))
+
     gain_first, middle_first, low_first, blocks = to_attention(0, middle, share_first)
-    gain_first, middle_first, low_first, blocks, hidden = hold(
-        gain_first, middle_first, low_first, blocks, hidden
+    query_part = query_gather.whole()
+    gain_first, middle_first, low_first, blocks, hidden, query_part = hold(
+        gain_first, middle_first, low_first, blocks, hidden, query_part
     )
 
     came_first = send_blocks(block_of(blocks))
-    query_part = quarter_collect(query_gather)
     query_over = lax.ppermute(query_part, "ctx", over)
     w_downs = t_dot(cotangent, hidden).astype(BF16)
     n_part = tok_rows // groups
@@ -905,23 +933,9 @@
         came_first, middle_own, query_part, query_over, w_downs
     )
 
-    def back_arguments(c, grads):
-        return metas[c], offsets[c], queries[c], attention[c], grads, log_totals[c], forms, *tables[c]
-
     query_near = (query_part, query_over)
     query_far = tuple(lax.ppermute(part, "dp", beside) for part in query_near)
     grads_first = stack_blocks(came_first).reshape(span, features)
-    dq_first, dk, dv = attend_back_first(*back_arguments(0, grads_first))
-    dq_first, dk, dv, query_near, query_far, share_second = hold(
-        dq_first, dk, dv, query_near, query_far, share_second
-    )
-
-    gain_second, middle_second, low_second, blocks = to_attention(1, middle, share_second)
-    gain_second, middle_second, low_second, blocks = hold(
-        gain_second, middle_second, low_second, blocks
-    )
-
-    came_second = send_blocks(block_of(blocks), across=True)
     attention_rows = jnp.concatenate(
         [
             lax.dynamic_slice_in_dim(whole, member * share, share, 1)
@@ -930,9 +944,21 @@
         axis=1,
     )
     attention_rows = jnp.swapaxes(attention_rows, 0, 1).reshape(2 * share, groups * features)
-    w_outs = t_dot(jnp.concatenate([low_first, low_second], axis=0), attention_rows).astype(BF16)
-    came_second, w_outs = hold(came_second, w_outs)
-    mlp_share = line_sum(after(mlp_part, came_second))
+    query_near, query_far, grads_first, attention_rows, share_second = hold(
+        query_near, query_far, grads_first, attention_rows, share_second
+    )
+
+    gain_second, middle_second, low_second, blocks = to_attention(1, middle, share_second)
+    gain_second, middle_second, low_second, blocks = hold(
+        gain_second, middle_second, low_second, blocks
+    )
+
+    def back_arguments(c, grads):
+        return metas[c], offsets[c], queries[c], attention[c], grads, log_totals[c], forms, *tables[c]
+
+    came_second = send_blocks(block_of(blocks), across=True)
+    dq_first, dk, dv = attend_back_first(*back_arguments(0, grads_first))
+    dq_first, dk, dv, came_second = hold(dq_first, dk, dv, came_second)
 
     rows_first = send_blocks(rows_of(dq_first))
     grads_second = stack_blocks(came_second).reshape(span, features)
@@ -952,7 +978,8 @@
     )
     query_parts = query_near + query_far
     first_part = join(quarters, stack_blocks(rows_first), query_parts)
-    near_blocks, far_blocks, first_part = hold(near_blocks, far_blocks, first_part)
+    w_outs = t_dot(jnp.concatenate([low_first, low_second], axis=0), attention_rows).astype(BF16)
+    near_blocks, far_blocks, first_part, w_outs = hold(near_blocks, far_blocks, first_part, w_outs)
     far_blocks = stack_blocks(far_blocks)
     kv_blocks = (
         stack_blocks(near_blocks).astype(F32) + far_blocks[:, :, features:].astype(F32)
@@ -997,10 +1024,11 @@
     def put_share(target, piece, source):
         return lax.dynamic_update_slice_in_dim(target, piece, source * n_part, 0)
 
-    tokens_gather = Gather(grad_inputs)
+    mixed_share = (middle_own + mlp_share.astype(F32)).astype(BF16)
+    tokens_gather, mixed_gather = Gather(grad_inputs), Gather(mixed_share)
     tokens_grad = jnp.zeros((tok_rows, width), BF16)
     mixed = jnp.zeros((tok_rows, width), BF16)
-    hop = tokens_gather.step()
+    hop, mixed_hop = tokens_gather.step(), mixed_gather.step()
     kv_sent = lax.ppermute(kv_far, "ctx", over)
     dq_home = lax.ppermute(dq_second, "ctx", over)
     grad_kv_raw = (kv_near + kv_sent.astype(F32)).astype(BF16)
@@ -1010,25 +1038,30 @@
     gains = jnp.pad(gains, ((0, 0), (0, 126)))
     rest = jnp.concatenate([w_downs, w_outs, query_kv, gains], axis=1)
     tokens_grad = tokens_gather.place_hop(put_rows, tokens_grad, 0)
-    hop, rest, tokens_grad = hold(hop, rest, tokens_grad)
+    mixed = mixed_gather.place_hop(put_share, mixed, 0)
+    hop, mixed_hop, rest, tokens_grad, mixed = hold(hop, mixed_hop, rest, tokens_grad, mixed)
     tokens_gather.held(hop)
+    mixed_gather.held(mixed_hop)
     rest = plane_sum(rest)
 
-    mixed_gather = Gather((middle_own + after(mlp_share, hop).astype(F32)).astype(BF16))
     hop, mixed_hop = tokens_gather.step(), mixed_gather.step()
     tokens_grad = tokens_gather.place_hop(put_rows, tokens_grad, 1)
-    mixed = mixed_gather.place_hop(put_share, mixed, 0)
-    hop, mixed_hop, tokens_grad, mixed, mixed_gather.piece = hold(
-        hop, mixed_hop, tokens_grad, mixed, mixed_gather.piece
-    )
+    mixed = mixed_gather.place_hop(put_share, mixed, 1)
+    hop, mixed_hop, tokens_grad, mixed = hold(hop, mixed_hop, tokens_grad, mixed)
     tokens_gather.held(hop)
     mixed_gather.held(mixed_hop)
 
-    hop, mixed_hop = tokens_gather.step(), mixed_gather.step()
+    hop = tokens_gather.step()
     tokens_grad = tokens_gather.place_hop(put_rows, tokens_grad, 2)
-    mixed = mixed_gather.place_hop(put_share, mixed, 1)
+    mixed = mixed_gather.place_hop(put_share, mixed, 2)
+    hop, tokens_grad, mixed = hold(hop, tokens_grad, mixed)
+    tokens_gather.held(hop)
+
+    mixed_hop = mixed_gather.step()
+    if groups > 3:
+        tokens_grad = tokens_gather.place_hop(put_rows, tokens_grad, 3)
     hidden_units = w_down.shape[1]
-    rest = after(rest, tokens_gather.rights[-2])
+    rest = after(rest, hop)
     down_grad = rest[:, :hidden_units]
     output_plane = rest[:, hidden_units : hidden_units + groups * features]
     query_plane = rest[:, hidden_units + groups * features :]
@@ -1038,14 +1071,8 @@
             [lax.dynamic_slice_in_dim(output_plane, j * features, features, 1), small], axis=1
         )
     )
-    hop, mixed_hop, tokens_grad, mixed, blocks = hold(hop, mixed_hop, tokens_grad, mixed, blocks)
-    tokens_gather.held(hop)
+    mixed_hop, tokens_grad, blocks = hold(mixed_hop, tokens_grad, blocks)
     mixed_gather.held(mixed_hop)
-
-    hop = mixed_gather.step()
-    if groups > 3:
-        tokens_grad = tokens_gather.place_hop(put_rows, tokens_grad, 3)
-    mixed = mixed_gather.place_hop(put_share, mixed, 2)
     blocks = stack_blocks(blocks).astype(F32)
     output_grad = jnp.sum(blocks[:, :, :features], axis=0)
     kv_share = blocks.shape[1] // groups
@@ -1053,8 +1080,6 @@
         blocks[:, :, features : features + 2 * HD], member * kv_share, kv_share, 1
     )
     gains = jnp.sum(blocks[:, :, features + 2 * HD : features + 2 * HD + 2], axis=0).T
-    hop, tokens_grad, mixed = hold(hop, tokens_grad, mixed)
-    mixed_gather.held(hop)
     for count in range(3, groups):
         mixed = mixed_gather.place_hop(put_share, mixed, count)
         if count + 1 < groups:

time: 1160 us -> 1140 us (0.983); the launches traced: 1140 us -> 1140 us
  local copies, waits for them, and re-layouts: 71.5 us -> 107 us
  waiting for transfers between devices: 340 us -> 322 us
  starting transfers between devices: 127 us -> 113 us
    ppermute x12, waiting for transfers between devices: 92.9 us -> 40.6 us  [send_blocks(): lax.ppermute(block, 'tensor', [(i, (i + shift) % size) for i in range(siz...]
    reduce_scatter x2, waiting for transfers between devices: 44.4 us -> 0.01 us  [plane_sum(): lax.psum_scatter(gradient.astype(BF16), ('dp', 'ctx'), scatter_dimension=...]
    ppermute x12, waiting for transfers between devices: 129 us -> 173 us  [step(): self.lefts.append(lax.ppermute(self.lefts[-1], 'tensor', to_left))]
    pallas_call x1, Pallas kernels: 70.7 us -> 38.1 us  [attend_back_last(): pl.pallas_call(kernel, grid_spec=pltpu.PrefetchScalarGridSpec(num_scalar_...]
    pallas_call x1, Pallas kernels: 45.5 us -> 78.1 us  [attend_back_first(): pl.pallas_call(kernel, grid_spec=pltpu.PrefetchScalarGridSpec(num_scalar_...]
    ppermute x1, waiting for transfers between devices: 29.6 us -> 0.01 us  [body(): foreign = lax.ppermute(sent, 'ctx', over)]
    ppermute x8, starting transfers between devices: 52.1 us -> 22.9 us  [send_blocks(): lax.ppermute(block, ('ctx', 'tensor'), [(c * size + i, (1 - c) * size + (...]
    ppermute x12, waiting for transfers between devices: 0.03 us -> 27.1 us  [step(): self.rights.append(lax.ppermute(self.rights[-1], 'tensor', to_right))]
  transfers between devices with their start and end apart: 62 -> 60, of which waited for: 18 -> 19; matrix products, arithmetic and copies ran while one was open for 20% -> 23% of each run, Pallas kernels for 32% -> 33%
where the time goes in v5:
time: 1140 us
  Pallas kernels  371 us (33%)
  waiting for transfers between devices  322 us (28%)
  starting transfers between devices  113 us (10%)
  local copies, waits for them, and re-layouts  107 us (9%)
  other arithmetic  91.9 us (8%)
  matrix products  85.4 us (7%)
  between operations  49 us (4%)
    ppermute x12, waiting for transfers between devices, step(): self.lefts.append(lax.ppermute(self.lefts[-1], 'tensor', to_left))  173 us
    pallas_call x2, Pallas kernels, feed_forward(): pl.pallas_call(feed_kernel, grid=(2 * quarter,), in_specs=[pl.BlockSpec((...  123 us
    pallas_call x1, Pallas kernels, attend_back_first(): pl.pallas_call(kernel, grid_spec=pltpu.PrefetchScalarGridSpec(num_scalar_...  78.1 us
    dot_general x4, matrix products, t_dot(): return jnp.einsum('rd,rf->df', a, b, preferred_element_type=F32)  71.4 us
    pallas_call x1, Pallas kernels, attend_first(): pl.pallas_call(kernel, grid_spec=pltpu.PrefetchScalarGridSpec(num_scalar_...  59.1 us
    ppermute x12, waiting for transfers between devices, send_blocks(): lax.ppermute(block, 'tensor', [(i, (i + shift) % size) for i in range(siz...  40.6 us
    pallas_call x1, Pallas kernels, attend_back_last(): pl.pallas_call(kernel, grid_spec=pltpu.PrefetchScalarGridSpec(num_scalar_...  38.1 us
    ppermute x1, waiting for transfers between devices, body(): dq_home = lax.ppermute(dq_second, 'ctx', over)  34.6 us
  transfers between devices with their start and end apart: 60, of which 19 were waited for; matrix products, arithmetic and copies ran while one was open for 23% of the time, Pallas kernels for 33%

profile of v5, /device:TPU:0, one launch (start us, length us, event | category | flops | bytes accessed | tf_op | source)
XLA Modules:
  0.0 1138.7 jit_solution(10210509099579159844)
XLA Ops:
  9.8 5.9 collective-permute-start
  17.4 5.4 multiply_sine_fusion.1
  26.3 17.5 %project.1 = (bf16[2048,128]{1,0:T(8,128)(2,1)S(1)}, bf16[2048,512]{1,0:T(8,128)(2,1)}, bf16[2048,2048]{1,0:T(8,128)(2,1)}, f32[2048,128]{1,0:T(8,128)S(1)}, f32[2048,128]{1,0:T(8,128)S(1)}) custom-call(s32[1]{0:T(128)} %bitcast.1.head, bf16[2048,2048]{1,0:T(8,128)(2,1)} %tokens_ref.5, f32[1,2048]{1,0:T(1,128)S(1)} %bitcast.150, ...), custom_call_target="tpu_custom_call" | custom-call | flops 1 | bytes 1 | tf_op jit(solution)/shard_map/project/pallas_call | solution.py:68
  53.4 8.0 collective-permute-done.2.other
  61.4 13.9 %collective-permute-done.4.refs_2_ = bf16[1024,512]{1,0:T(8,128)(2,1)S(1)} collective-permute-done((bf16[1024,512]{1,0:T(8,128)(2,1)}, bf16[1024,512]{1,0:T(8,128)(2,1)S(1)}, u32[]{:S(2)}, u32[]{:S(2)}) %collective-permute-start.4) | collective-permute-done | bytes 1048608 | tf_op jit(solution)/shard_map/ppermute | solution.py:639
  78.9 59.1 %attend_first.1 = (bf16[1024,512]{1,0:T(8,128)(2,1)}, f32[4,8,1024]{2,1,0:T(8,128)}, bf16[4096,128]{1,0:T(8,128)(2,1)}, bf16[4096,128]{1,0:T(8,128)(2,1)}, bf16[...) custom-call(s32[6]{0:T(128)} %get-tuple-element.490.meta.refs_0_, ...), custom_call_target="tpu_custom_call" | custom-call | flops 17179869184 | bytes 8388608 | tf_op jit(solution)/shard_map/attend_first/pallas_call | solution.py:208
  142.8 7.2 arrange.3.refs_0_
  151.8 25.7 %attend.1 = (bf16[1024,512]{1,0:T(8,128)(2,1)}, f32[4,8,1024]{2,1,0:T(8,128)}) custom-call(s32[6]{0:T(128)} %get-tuple-element.489.refs_0_, bf16[1024,512]{1,0:T(8,128)(2,1)} %collective-permute-done.5.refs_1_, bf16[4096,128]{1,0:T(8,128)(2,1)} %get-tuple-element.214.refs_2_.refs_5_, bf16[4096,128]{1,0:T(8,128)(2,1)} %get-tuple-element.215.refs_3_.refs_6_, ...), custom_call_target="tpu_custom_call" | custom-call | flops 17179869184 | bytes 8388608 | tf_op jit(solution)/shard_map/attend/pallas_call | solution.py:245
  177.5 14.2 %collective-permute-start.9 = (bf16[1024,512]{1,0:T(8,128)(2,1)}, bf16[1024,512]{1,0:T(8,128)(2,1)}, u32[]{:S(2)}, u32[]{:S(2)}) collective-permute-start(bf16[1024,512]{1,0:T(8,128)(2,1)} %get-tuple-element.221.refs_2_), channel_id=1, source_target_pairs={{0,4},{4,0},{1,5},{5,1},{2,6},{6,2},{3,7},{7,3},{8,12},{12,8},{9,1... | collective-permute-start | bytes 3145736 | tf_op jit(solution)/shard_map/ppermute | solution.py:842
  193.9 6.4 arrange.4.output_weight
  200.4 3.7 multiply_sine_fusion
  206.1 3.7 maximum_maximum_fusion
  209.8 4.2 collective-permute-done.9
  214.1 5.2 all-gather.5.cloned.1.call-done
  223.0 62.3 %feed_forward.2 = (f32[2048,2048]{1,0:T(8,128)}, bf16[2048,2048]{1,0:T(8,128)(2,1)}, bf16[2048,1408]{1,0:T(8,128)(2,1)}, bf16[2048,2816]{1,0:T(8,128)(2,1)}, bf1...) custom-call(bf16[4,1024,512]{2,1,0:T(8,128)(2,1)} %bitcast.155, bf16[2048,2048]{1,0:T(8,128)(2,1)} %tokens_ref.5, ...), custom_call_target="tpu_custom_call" | custom-call | flops 1 | bytes 1 | tf_op jit(solution)/shard_map/feed_forward/pallas_call | solution.py:523
  285.3 21.3 %all-gather.7.cloned.1.call-done = bf16[4096,512]{1,0:T(8,128)(2,1)} async-done(((bf16[1024,512]{1,0:T(8,128)(2,1)}), bf16[4096,512]{1,0:T(8,128)(2,1)}) %all-gather.7.cloned.1.call-update) | async-done | bytes 4194320 | tf_op jit(solution)/shard_map/all_gather | solution.py:854
  318.6 3.1 constant_dynamic-slice_fusion.33
  321.8 61.1 %feed_forward.3 = (f32[2048,2048]{1,0:T(8,128)}, bf16[2048,2048]{1,0:T(8,128)(2,1)}, bf16[2048,1408]{1,0:T(8,128)(2,1)}, bf16[2048,2816]{1,0:T(8,128)(2,1)}, bf1...) custom-call(bf16[4,1024,512]{2,1,0:T(8,128)(2,1)} %bitcast.157, ...), custom_call_target="tpu_custom_call", output_to_operand_aliasing={{0}: (8, {}), {1}: (9, {}), {2}: (10, {}), {3}: (11, {}), {... | custom-call | flops 1 | bytes 1 | tf_op jit(solution)/shard_map/feed_forward/pallas_call | solution.py:523
  388.0 31.6 %convolution_convert_fusion = bf16[2048,2816]{1,0:T(8,128)(2,1)} fusion(bf16[2048,2048]{1,0:T(8,128)(2,1)} %get-tuple-element.252, bf16[2048,2816]{1,0:T(8,128)(2,1)} %get-tuple-element.253), kind=kOutput, calls=%fused_computation.3 | convolution fusion | flops 23628087296 | bytes 31457280 | tf_op jit(solution)/shard_map/rd,rf->df/dot_general | solution.py:733
  419.6 4.7 constant_dynamic-slice_fusion.36
  428.4 4.1 fusion.54
  434.7 5.8 fusion.41
  443.7 3.2 collective-permute-start.16
  450.1 3.1 collective-permute-start.18
  453.2 18.9 %fusion.2 = bf16[2048,1408]{1,0:T(8,128)(2,1)} fusion(bf16[2048,1408]{1,0:T(8,128)(2,1)} %get-tuple-element.265, bf16[2048,2048]{1,0:T(8,128)(2,1)} %cotangent_ref.3), kind=kOutput, calls=%fused_computation.10 | convolution fusion | flops 11814043648 | bytes 19922944 | tf_op jit(solution)/shard_map/rd,rf->df/dot_general | solution.py:733
  473.9 4.8 collective-permute-done.17
  478.7 2.9 collective-permute-done.18
  481.7 6.5 collective-permute-done.19.refs_1_
  504.5 3.1 maximum_bitcast_fusion.3
  512.0 4.4 copy.85
  526.8 3.9 fusion.52
  530.7 6.1 fusion.42
  542.9 10.2 collective-permute-start.23
  554.9 4.0 collective-permute-start.24
  560.7 10.1 convolution_convert_fusion.1
  570.9 78.1 %attend_back_first.1 = (bf16[1024,512]{1,0:T(8,128)(2,1)}, f32[4096,128]{1,0:T(8,128)}, f32[4096,128]{1,0:T(8,128)}) custom-call(s32[6]{0:T(128)} %get-tuple-element.490.meta.refs_0_, bf16[1024,512]{1,0:T(8,128)(2,1)} %pad_maximum_fusion.1.q_ref.refs_1_, bf16[1024,512]{1,0:T(8,128)(2,1)} %get-tuple-element.212.refs_2_, bf16[1024,512]{1,0:T(8,128)(2,1)} %bitcast.33.refs_3_, ...), custom_call_target="tpu_custom_call" | custom-call | flops 1 | bytes 1 | tf_op jit(solution)/shard_map/attend_back_first/pallas_call | solution.py:381
  662.3 38.1 %attend_back_last.1 = (bf16[1024,512]{1,0:T(8,128)(2,1)}, f32[2048,128]{1,0:T(8,128)}, bf16[2048,128]{1,0:T(8,128)(2,1)}) custom-call(s32[6]{0:T(128)} %get-tuple-element.489.refs_0_, bf16[1024,512]{1,0:T(8,128)(2,1)} %collective-permute-done.5.refs_1_, bf16[1024,512]{1,0:T(8,128)(2,1)} %get-tuple-element.221.refs_2_, bf16[1024,512]{1,0:T(8,128)(2,1)} %bitcast.47.refs_3_, ...), custom_call_target="tpu_custom_call" | custom-call | flops 1 | bytes 1 | tf_op jit(solution)/shard_map/attend_back_last/pallas_call | solution.py:436
  703.0 5.2 collective-permute-start.35
  716.8 17.0 %collective-permute-done.31 = bf16[256,256]{1,0:T(8,128)(2,1)S(1)} collective-permute-done((bf16[256,256]{1,0:T(8,128)(2,1)S(1)}, bf16[256,256]{1,0:T(8,128)(2,1)S(1)}, u32[]{:S(2)}, u32[]{:S(2)}) %collective-permute-start.31) | collective-permute-done | bytes 131104 | tf_op jit(solution)/shard_map/ppermute | solution.py:701
  734.3 11.7 %collective-permute-done.30 = bf16[256,256]{1,0:T(8,128)(2,1)S(1)} collective-permute-done((bf16[256,256]{1,0:T(8,128)(2,1)S(1)}, bf16[256,256]{1,0:T(8,128)(2,1)S(1)}, u32[]{:S(2)}, u32[]{:S(2)}) %collective-permute-start.30) | collective-permute-done | bytes 131104 | tf_op jit(solution)/shard_map/ppermute | solution.py:701
  748.8 6.6 join.2
  755.9 6.6 join.3
  766.6 3.3 fusion.6
  772.2 3.3 collective-permute-start.36
  779.1 6.1 broadcast.124.clone.1
  793.1 34.6 %collective-permute-done.40 = bf16[1024,512]{1,0:T(8,128)(2,1)} collective-permute-done((bf16[1024,512]{1,0:T(8,128)(2,1)S(1)}, bf16[1024,512]{1,0:T(8,128)(2,1)}, u32[]{:S(2)}, u32[]{:S(2)}) %collective-permute-start.40) | collective-permute-done | bytes 1048608 | tf_op jit(solution)/shard_map/ppermute | solution.py:1033
  827.8 10.7 convolution_convert_fusion.3
  838.5 5.3 broadcast.124.clone
  843.8 4.1 constant_dynamic-update-slice_fusion
  847.9 8.0 collective-permute-start.38
  857.3 10.6 fusion.1
  867.9 27.1 %collective-permute-done.38 = bf16[512,2048]{1,0:T(8,128)(2,1)} collective-permute-done((bf16[512,2048]{1,0:T(8,128)(2,1)S(1)}, bf16[512,2048]{1,0:T(8,128)(2,1)}, u32[]{:S(2)}, u32[]{:S(2)}) %collective-permute-start.38) | collective-permute-done | bytes 2097184 | tf_op jit(solution)/shard_map/ppermute | solution.py:638
  894.9 5.5 collective-permute-done.39
  922.1 3.4 broadcast_select_fusion
  931.9 3.8 select_dynamic-update-slice_fusion.2
  935.7 34.2 %collective-permute-done.43 = bf16[512,2048]{1,0:T(8,128)(2,1)} collective-permute-done((bf16[512,2048]{1,0:T(8,128)(2,1)}, bf16[512,2048]{1,0:T(8,128)(2,1)}, u32[]{:S(2)}, u32[]{:S(2)}) %collective-permute-start.43) | collective-permute-done | bytes 2097184 | tf_op jit(solution)/shard_map/ppermute | solution.py:639
  969.9 38.0 %collective-permute-done.45 = bf16[512,2048]{1,0:T(8,128)(2,1)} collective-permute-done((bf16[512,2048]{1,0:T(8,128)(2,1)}, bf16[512,2048]{1,0:T(8,128)(2,1)}, u32[]{:S(2)}, u32[]{:S(2)}) %collective-permute-start.45) | collective-permute-done | bytes 2097184 | tf_op jit(solution)/shard_map/ppermute | solution.py:639
  1018.8 4.3 select_dynamic-update-slice_fusion.1
  1023.1 3.1 slice_convert_fusion
  1026.2 42.8 %collective-permute-done.47 = bf16[512,2048]{1,0:T(8,128)(2,1)} collective-permute-done((bf16[512,2048]{1,0:T(8,128)(2,1)}, bf16[512,2048]{1,0:T(8,128)(2,1)}, u32[]{:S(2)}, u32[]{:S(2)}) %collective-permute-start.47) | collective-permute-done | bytes 2097184 | tf_op jit(solution)/shard_map/ppermute | solution.py:639
  1074.7 3.7 collective-permute-start.52
  1080.5 38.3 %collective-permute-done.49 = bf16[512,2048]{1,0:T(8,128)(2,1)} collective-permute-done((bf16[512,2048]{1,0:T(8,128)(2,1)}, bf16[512,2048]{1,0:T(8,128)(2,1)}, u32[]{:S(2)}, u32[]{:S(2)}) %collective-permute-start.49) | collective-permute-done | bytes 2097184 | tf_op jit(solution)/shard_map/ppermute | solution.py:639
  1118.8 4.1 collective-permute-done.52
  1127.1 4.3 select_dynamic-update-slice_fusion
  (355 shorter events, 171.9 us)
Async XLA Ops:
  7.2 212.1 %all-gather.5.cloned.1.call-start = ((), (), s32[]{:S(2)}) async-start(), calls=%async_computation.10 | async-start | bytes 5242880 | tf_op jit(solution)/shard_map/all_gather | solution.py:829
  9.8 35.8 %collective-permute-start = (bf16[1024,512]{1,0:T(8,128)(2,1)}, bf16[1024,512]{1,0:T(8,128)(2,1)}, u32[]{:S(2)}, u32[]{:S(2)}) collective-permute-start(bf16[1024,512]{1,0:T(8,128)(2,1)} %constant_dynamic-slice_fusion.42.refs_6_), channel_id=1, source_target_pairs={{0,1},{1,2},{2,3},{4,5},{5,6},{6,7},{8,9},{9,10},{10,11},{12,13},{... | collective-permute-start | bytes 3145736 | tf_op jit(solution)/shard_map/ppermute | solution.py:638
  15.8 29.8 %collective-permute-start.1 = (bf16[1024,512]{1,0:T(8,128)(2,1)}, bf16[1024,512]{1,0:T(8,128)(2,1)}, u32[]{:S(2)}, u32[]{:S(2)}) collective-permute-start(bf16[1024,512]{1,0:T(8,128)(2,1)} %constant_dynamic-slice_fusion.42.refs_6_), channel_id=1, source_target_pairs={{1,0},{2,1},{3,2},{5,4},{6,5},{7,6},{9,8},{10,9},{11,10},{13,12},{... | collective-permute-start | bytes 3145736 | tf_op jit(solution)/shard_map/ppermute | solution.py:639
  45.6 15.8 %collective-permute-start.3 = (bf16[1024,512]{1,0:T(8,128)(2,1)}, bf16[1024,512]{1,0:T(8,128)(2,1)S(1)}, u32[]{:S(2)}, u32[]{:S(2)}) collective-permute-start(bf16[1024,512]{1,0:T(8,128)(2,1)} %collective-permute-done.refs_5_), channel_id=1, source_target_pairs={{1,2},{2,3},{5,6},{6,7},{9,10},{10,11},{13,14},{14,15},{17,18},{18... | collective-permute-start | bytes 3145736 | tf_op jit(solution)/shard_map/ppermute | solution.py:638
  46.5 28.9 %collective-permute-start.4 = (bf16[1024,512]{1,0:T(8,128)(2,1)}, bf16[1024,512]{1,0:T(8,128)(2,1)S(1)}, u32[]{:S(2)}, u32[]{:S(2)}) collective-permute-start(bf16[1024,512]{1,0:T(8,128)(2,1)} %collective-permute-done.1.refs_4_), channel_id=1, source_target_pairs={{1,0},{2,1},{5,4},{6,5},{9,8},{10,9},{13,12},{14,13},{17,16},{18,1... | collective-permute-start | bytes 3145736 | tf_op jit(solution)/shard_map/ppermute | solution.py:639
  47.8 13.6 %collective-permute-start.2 = (bf16[2048,128]{1,0:T(8,128)(2,1)}, bf16[2048,128]{1,0:T(8,128)(2,1)S(1)}, u32[]{:S(2)}, u32[]{:S(2)}) collective-permute-start(bf16[2048,128]{1,0:T(8,128)(2,1)} %copy-done.24), channel_id=1, source_target_pairs={{0,4},{4,0},{1,5},{5,1},{2,6},{6,2},{3,7},{7,3},{8,12},{12,8},{9,1... | collective-permute-start | bytes 1572872 | tf_op jit(solution)/shard_map/ppermute | solution.py:815
  61.4 76.5 %copy-start.8 = (bf16[1024,512]{1,0:T(8,128)(2,1)}, bf16[1024,512]{1,0:T(8,128)(2,1)S(1)}, u32[]{:S(2)}) copy-start(bf16[1024,512]{1,0:T(8,128)(2,1)S(1)} %collective-permute-done.3.refs_3_) | copy-start | bytes 3145732
  75.4 62.6 %copy-start.10 = (bf16[1024,512]{1,0:T(8,128)(2,1)}, bf16[1024,512]{1,0:T(8,128)(2,1)S(1)}, u32[]{:S(2)}) copy-start(bf16[1024,512]{1,0:T(8,128)(2,1)S(1)} %collective-permute-done.4.refs_2_) | copy-start | bytes 3145732
  75.4 62.6 %collective-permute-start.5 = (bf16[1024,512]{1,0:T(8,128)(2,1)}, bf16[1024,512]{1,0:T(8,128)(2,1)}, u32[]{:S(2)}, u32[]{:S(2)}) collective-permute-start(bf16[1024,512]{1,0:T(8,128)(2,1)} %slice.189), channel_id=1, source_target_pairs={{0,4},{4,0},{1,5},{5,1},{2,6},{6,2},{3,7},{7,3},{8,12},{12,8},{9,1... | collective-permute-start | bytes 3145736 | tf_op jit(solution)/shard_map/ppermute | solution.py:823
  76.8 61.1 %collective-permute-start.6 = (bf16[1024,512]{1,0:T(8,128)(2,1)S(1)}, bf16[1024,512]{1,0:T(8,128)(2,1)S(1)}, u32[]{:S(2)}, u32[]{:S(2)}) collective-permute-start(bf16[1024,512]{1,0:T(8,128)(2,1)S(1)} %collective-permute-done.3.refs_3_), channel_id=1, source_target_pairs={{2,3},{6,7},{10,11},{14,15},{18,19},{22,23},{26,27},{30,31}} | collective-permute-start | bytes 3145736 | tf_op jit(solution)/shard_map/ppermute | solution.py:638
  77.6 61.4 %collective-permute-start.7 = (bf16[1024,512]{1,0:T(8,128)(2,1)S(1)}, bf16[1024,512]{1,0:T(8,128)(2,1)}, u32[]{:S(2)}, u32[]{:S(2)}) collective-permute-start(bf16[1024,512]{1,0:T(8,128)(2,1)S(1)} %collective-permute-done.4.refs_2_), channel_id=1, source_target_pairs={{1,0},{5,4},{9,8},{13,12},{17,16},{21,20},{25,24},{29,28}} | collective-permute-start | bytes 3145736 | tf_op jit(solution)/shard_map/ppermute | solution.py:639
  139.0 167.7 %all-gather.7.cloned.1.call-start = ((), (), s32[]{:S(2)}) async-start(), calls=%async_computation.11 | async-start | bytes 5242880 | tf_op jit(solution)/shard_map/all_gather | solution.py:854
  150.0 27.5 %collective-permute-start.8 = (bf16[4,1024,512]{2,1,0:T(8,128)(2,1)}, bf16[4,1024,512]{2,1,0:T(8,128)(2,1)}, u32[]{:S(2)}, u32[]{:S(2)}) collective-permute-start(bf16[4,1024,512]{2,1,0:T(8,128)(2,1)} %arrange.3.refs_0_), channel_id=1, source_target_pairs={{0,8},{8,0},{16,24},{24,16},{1,9},{9,1},{17,25},{25,17},{2,10},{10... | collective-permute-start | bytes 12582920 | tf_op jit(solution)/shard_map/ppermute | solution.py:832
  177.5 36.5 %collective-permute-start.9 = (bf16[1024,512]{1,0:T(8,128)(2,1)}, bf16[1024,512]{1,0:T(8,128)(2,1)}, u32[]{:S(2)}, u32[]{:S(2)}) collective-permute-start(bf16[1024,512]{1,0:T(8,128)(2,1)} %get-tuple-element.221.refs_2_), channel_id=1, source_target_pairs={{0,4},{4,0},{1,5},{5,1},{2,6},{6,2},{3,7},{7,3},{8,12},{12,8},{9,1... | collective-permute-start | bytes 3145736 | tf_op jit(solution)/shard_map/ppermute | solution.py:842
  214.0 210.3 %reduce-scatter.6.cloned.1.call-start = ((), (), s32[]{:S(2)}) async-start(), calls=%async_computation.5 | async-start | bytes 5242880 | tf_op jit(solution)/shard_map/reduce_scatter | solution.py:891
  220.4 64.9 %collective-permute-start.10 = (bf16[512,512]{1,0:T(8,128)(2,1)S(1)}, bf16[512,512]{1,0:T(8,128)(2,1)S(1)}, u32[]{:S(2)}, u32[]{:S(2)}) collective-permute-start(bf16[512,512]{1,0:T(8,128)(2,1)S(1)} %constant_dynamic-slice_fusion.41.refs_6_), channel_id=1, source_target_pairs={{0,1},{1,2},{2,3},{4,5},{5,6},{6,7},{8,9},{9,10},{10,11},{12,13},{... | collective-permute-start | bytes 1572872 | tf_op jit(solution)/shard_map/ppermute | solution.py:638
  221.7 63.6 %collective-permute-start.11 = (bf16[512,512]{1,0:T(8,128)(2,1)S(1)}, bf16[512,512]{1,0:T(8,128)(2,1)}, u32[]{:S(2)}, u32[]{:S(2)}) collective-permute-start(bf16[512,512]{1,0:T(8,128)(2,1)S(1)} %constant_dynamic-slice_fusion.41.refs_6_), channel_id=1, source_target_pairs={{1,0},{2,1},{3,2},{5,4},{6,5},{7,6},{9,8},{10,9},{11,10},{13,12},{... | collective-permute-start | bytes 1572872 | tf_op jit(solution)/shard_map/ppermute | solution.py:639
  306.7 217.5 %reduce-scatter.8.cloned.1.call-start = ((), (), s32[]{:S(2)}) async-start(), calls=%async_computation.6 | async-start | bytes 5242880 | tf_op jit(solution)/shard_map/reduce_scatter | solution.py:891
  314.9 68.0 %collective-permute-start.12 = (bf16[512,512]{1,0:T(8,128)(2,1)S(1)}, bf16[512,512]{1,0:T(8,128)(2,1)S(1)}, u32[]{:S(2)}, u32[]{:S(2)}) collective-permute-start(bf16[512,512]{1,0:T(8,128)(2,1)S(1)} %collective-permute-done.10.refs_5_), channel_id=1, source_target_pairs={{1,2},{2,3},{5,6},{6,7},{9,10},{10,11},{13,14},{14,15},{17,18},{18... | collective-permute-start | bytes 1572872 | tf_op jit(solution)/shard_map/ppermute | solution.py:638
  315.6 67.3 %collective-permute-start.13 = (bf16[512,512]{1,0:T(8,128)(2,1)}, bf16[512,512]{1,0:T(8,128)(2,1)S(1)}, u32[]{:S(2)}, u32[]{:S(2)}) collective-permute-start(bf16[512,512]{1,0:T(8,128)(2,1)} %collective-permute-done.11.refs_4_), channel_id=1, source_target_pairs={{1,0},{2,1},{5,4},{6,5},{9,8},{10,9},{13,12},{14,13},{17,16},{18,1... | collective-permute-start | bytes 1572872 | tf_op jit(solution)/shard_map/ppermute | solution.py:639
  382.9 41.4 %collective-permute-start.14 = (bf16[512,512]{1,0:T(8,128)(2,1)S(1)}, bf16[512,512]{1,0:T(8,128)(2,1)S(1)}, u32[]{:S(2)}, u32[]{:S(2)}) collective-permute-start(bf16[512,512]{1,0:T(8,128)(2,1)S(1)} %collective-permute-done.12.refs_3_), channel_id=1, source_target_pairs={{2,3},{6,7},{10,11},{14,15},{18,19},{22,23},{26,27},{30,31}} | collective-permute-start | bytes 1572872 | tf_op jit(solution)/shard_map/ppermute | solution.py:638
  383.6 40.7 %collective-permute-start.15 = (bf16[512,512]{1,0:T(8,128)(2,1)S(1)}, bf16[512,512]{1,0:T(8,128)(2,1)S(1)}, u32[]{:S(2)}, u32[]{:S(2)}) collective-permute-start(bf16[512,512]{1,0:T(8,128)(2,1)S(1)} %collective-permute-done.13.refs_2_), channel_id=1, source_target_pairs={{1,0},{5,4},{9,8},{13,12},{17,16},{21,20},{25,24},{29,28}} | collective-permute-start | bytes 1572872 | tf_op jit(solution)/shard_map/ppermute | solution.py:639
  387.5 450.9 %reduce-scatter.10.cloned.1.call-start = ((), (), s32[]{:S(2)}) async-start(), calls=%async_computation.7 | async-start | bytes 10485760 | tf_op jit(solution)/shard_map/reduce_scatter | solution.py:891
  427.2 595.9 %reduce-scatter.14.cloned.1.call-start = ((), (), s32[]{:S(2)}) async-start(), calls=%async_computation.9 | async-start | bytes 12976128 | tf_op jit(solution)/shard_map/reduce_scatter | solution.py:894
  440.5 47.7 %collective-permute-start.19 = (bf16[4,512,512]{2,1,0:T(8,128)(2,1)S(1)}, bf16[4,512,512]{2,1,0:T(8,128)(2,1)}, u32[]{:S(2)}, u32[]{:S(2)}) collective-permute-start(bf16[4,512,512]{2,1,0:T(8,128)(2,1)S(1)} %arrange.5.refs_0_), channel_id=1, source_target_pairs={{0,4},{4,0},{1,5},{5,1},{2,6},{6,2},{3,7},{7,3},{8,12},{12,8},{9,1... | collective-permute-start | bytes 6291464 | tf_op jit(solution)/shard_map/ppermute | solution.py:928
  443.7 30.2 %collective-permute-start.16 = (bf16[256,512]{1,0:T(8,128)(2,1)}, bf16[256,512]{1,0:T(8,128)(2,1)}, u32[]{:S(2)}, u32[]{:S(2)}) collective-permute-start(bf16[256,512]{1,0:T(8,128)(2,1)} %bitcast.25), channel_id=1, source_target_pairs={{0,1},{1,2},{2,3},{3,0},{4,5},{5,6},{6,7},{7,4},{8,9},{9,10},{10,1... | collective-permute-start | bytes 786440 | tf_op jit(solution)/shard_map/ppermute | solution.py:701
  447.7 31.0 %collective-permute-start.17 = (bf16[256,512]{1,0:T(8,128)(2,1)}, bf16[256,512]{1,0:T(8,128)(2,1)}, u32[]{:S(2)}, u32[]{:S(2)}) collective-permute-start(bf16[256,512]{1,0:T(8,128)(2,1)} %bitcast.26), channel_id=1, source_target_pairs={{0,2},{1,3},{2,0},{3,1},{4,6},{5,7},{6,4},{7,5},{8,10},{9,11},{10,... | collective-permute-start | bytes 786440 | tf_op jit(solution)/shard_map/ppermute | solution.py:701
  450.1 31.6 %collective-permute-start.18 = (bf16[256,512]{1,0:T(8,128)(2,1)}, bf16[256,512]{1,0:T(8,128)(2,1)}, u32[]{:S(2)}, u32[]{:S(2)}) collective-permute-start(bf16[256,512]{1,0:T(8,128)(2,1)} %bitcast.170), channel_id=1, source_target_pairs={{0,3},{1,0},{2,1},{3,2},{4,7},{5,4},{6,5},{7,6},{8,11},{9,8},{10,9... | collective-permute-start | bytes 786440 | tf_op jit(solution)/shard_map/ppermute | solution.py:701
  488.2 35.9 %collective-permute-start.20 = (bf16[4,512,512]{2,1,0:T(8,128)(2,1)S(1)}, bf16[4,512,512]{2,1,0:T(8,128)(2,1)}, u32[]{:S(2)}, u32[]{:S(2)}) collective-permute-start(bf16[4,512,512]{2,1,0:T(8,128)(2,1)S(1)} %arrange.5.refs_0_), channel_id=1, source_target_pairs={{0,8},{8,0},{16,24},{24,16},{1,9},{9,1},{17,25},{25,17},{2,10},{10... | collective-permute-start | bytes 6291464 | tf_op jit(solution)/shard_map/ppermute | solution.py:937
  488.2 35.9 %collective-permute-start.21 = (bf16[4,512,512]{2,1,0:T(8,128)(2,1)}, bf16[4,512,512]{2,1,0:T(8,128)(2,1)}, u32[]{:S(2)}, u32[]{:S(2)}) collective-permute-start(bf16[4,512,512]{2,1,0:T(8,128)(2,1)} %collective-permute-done.19.refs_1_), channel_id=1, source_target_pairs={{0,8},{8,0},{16,24},{24,16},{1,9},{9,1},{17,25},{25,17},{2,10},{10... | collective-permute-start | bytes 6291464 | tf_op jit(solution)/shard_map/ppermute | solution.py:937
  539.7 109.4 %collective-permute-start.22 = (bf16[256,512]{1,0:T(8,128)(2,1)}, bf16[256,512]{1,0:T(8,128)(2,1)}, u32[]{:S(2)}, u32[]{:S(2)}) collective-permute-start(bf16[256,512]{1,0:T(8,128)(2,1)} %bitcast.166), channel_id=1, source_target_pairs={{0,4},{1,5},{2,6},{3,7},{4,0},{5,1},{6,2},{7,3},{8,12},{9,13},{10,... | collective-permute-start | bytes 786440 | tf_op jit(solution)/shard_map/ppermute | solution.py:691
  542.9 106.1 %collective-permute-start.23 = (bf16[256,512]{1,0:T(8,128)(2,1)}, bf16[256,512]{1,0:T(8,128)(2,1)}, u32[]{:S(2)}, u32[]{:S(2)}) collective-permute-start(bf16[256,512]{1,0:T(8,128)(2,1)} %bitcast.167), channel_id=1, source_target_pairs={{0,5},{1,6},{2,7},{3,4},{4,1},{5,2},{6,3},{7,0},{8,13},{9,14},{10,... | collective-permute-start | bytes 786440 | tf_op jit(solution)/shard_map/ppermute | solution.py:691
  554.9 94.1 %collective-permute-start.24 = (bf16[256,512]{1,0:T(8,128)(2,1)}, bf16[256,512]{1,0:T(8,128)(2,1)}, u32[]{:S(2)}, u32[]{:S(2)}) collective-permute-start(bf16[256,512]{1,0:T(8,128)(2,1)} %bitcast.168), channel_id=1, source_target_pairs={{0,6},{1,7},{2,4},{3,5},{4,2},{5,3},{6,0},{7,1},{8,14},{9,15},{10,... | collective-permute-start | bytes 786440 | tf_op jit(solution)/shard_map/ppermute | solution.py:691
  560.7 88.3 %collective-permute-start.25 = (bf16[256,512]{1,0:T(8,128)(2,1)}, bf16[256,512]{1,0:T(8,128)(2,1)S(1)}, u32[]{:S(2)}, u32[]{:S(2)}) collective-permute-start(bf16[256,512]{1,0:T(8,128)(2,1)} %bitcast.169), channel_id=1, source_target_pairs={{0,7},{1,4},{2,5},{3,6},{4,3},{5,0},{6,1},{7,2},{8,15},{9,12},{10,... | collective-permute-start | bytes 786440 | tf_op jit(solution)/shard_map/ppermute | solution.py:691
  651.1 49.3 %collective-permute-start.26 = (bf16[256,512]{1,0:T(8,128)(2,1)}, bf16[256,512]{1,0:T(8,128)(2,1)}, u32[]{:S(2)}, u32[]{:S(2)}) collective-permute-start(bf16[256,512]{1,0:T(8,128)(2,1)} %get-tuple-element.411), channel_id=1, source_target_pairs={{0,1},{1,2},{2,3},{3,0},{4,5},{5,6},{6,7},{7,4},{8,9},{9,10},{10,1... | collective-permute-start | bytes 786440 | tf_op jit(solution)/shard_map/ppermute | solution.py:701
  653.0 47.4 %collective-permute-start.27 = (bf16[256,512]{1,0:T(8,128)(2,1)}, bf16[256,512]{1,0:T(8,128)(2,1)}, u32[]{:S(2)}, u32[]{:S(2)}) collective-permute-start(bf16[256,512]{1,0:T(8,128)(2,1)} %get-tuple-element.410), channel_id=1, source_target_pairs={{0,2},{1,3},{2,0},{3,1},{4,6},{5,7},{6,4},{7,5},{8,10},{9,11},{10,... | collective-permute-start | bytes 786440 | tf_op jit(solution)/shard_map/ppermute | solution.py:701
  653.2 47.3 %collective-permute-start.28 = (bf16[256,512]{1,0:T(8,128)(2,1)S(1)}, bf16[256,512]{1,0:T(8,128)(2,1)}, u32[]{:S(2)}, u32[]{:S(2)}) collective-permute-start(bf16[256,512]{1,0:T(8,128)(2,1)S(1)} %get-tuple-element.409), channel_id=1, source_target_pairs={{0,3},{1,0},{2,1},{3,2},{4,7},{5,4},{6,5},{7,6},{8,11},{9,8},{10,9... | collective-permute-start | bytes 786440 | tf_op jit(solution)/shard_map/ppermute | solution.py:701
  703.0 52.5 %collective-permute-start.35 = (bf16[256,768]{1,0:T(8,128)(2,1)S(1)}, bf16[256,768]{1,0:T(8,128)(2,1)S(1)}, u32[]{:S(2)}, u32[]{:S(2)}) collective-permute-start(bf16[256,768]{1,0:T(8,128)(2,1)S(1)} %pad_maximum_fusion.17), channel_id=1, source_target_pairs={{0,7},{1,4},{2,5},{3,6},{4,3},{5,0},{6,1},{7,2},{8,15},{9,12},{10,... | collective-permute-start | bytes 1179656 | tf_op jit(solution)/shard_map/ppermute | solution.py:691
  708.2 47.3 %collective-permute-start.34 = (bf16[256,768]{1,0:T(8,128)(2,1)S(1)}, bf16[256,768]{1,0:T(8,128)(2,1)S(1)}, u32[]{:S(2)}, u32[]{:S(2)}) collective-permute-start(bf16[256,768]{1,0:T(8,128)(2,1)S(1)} %pad_maximum_fusion.16), channel_id=1, source_target_pairs={{0,6},{1,7},{2,4},{3,5},{4,2},{5,3},{6,0},{7,1},{8,14},{9,15},{10,... | collective-permute-start | bytes 1179656 | tf_op jit(solution)/shard_map/ppermute | solution.py:691
  708.3 47.2 %collective-permute-start.33 = (bf16[256,768]{1,0:T(8,128)(2,1)S(1)}, bf16[256,768]{1,0:T(8,128)(2,1)S(1)}, u32[]{:S(2)}, u32[]{:S(2)}) collective-permute-start(bf16[256,768]{1,0:T(8,128)(2,1)S(1)} %pad_maximum_fusion.15), channel_id=1, source_target_pairs={{0,5},{1,6},{2,7},{3,4},{4,1},{5,2},{6,3},{7,0},{8,13},{9,14},{10,... | collective-permute-start | bytes 1179656 | tf_op jit(solution)/shard_map/ppermute | solution.py:691
  710.0 23.8 %collective-permute-start.31 = (bf16[256,256]{1,0:T(8,128)(2,1)S(1)}, bf16[256,256]{1,0:T(8,128)(2,1)S(1)}, u32[]{:S(2)}, u32[]{:S(2)}) collective-permute-start(bf16[256,256]{1,0:T(8,128)(2,1)S(1)} %pad_maximum_fusion.21), channel_id=1, source_target_pairs={{0,3},{1,0},{2,1},{3,2},{4,7},{5,4},{6,5},{7,6},{8,11},{9,8},{10,9... | collective-permute-start | bytes 393224 | tf_op jit(solution)/shard_map/ppermute | solution.py:701
  712.7 33.3 %collective-permute-start.30 = (bf16[256,256]{1,0:T(8,128)(2,1)S(1)}, bf16[256,256]{1,0:T(8,128)(2,1)S(1)}, u32[]{:S(2)}, u32[]{:S(2)}) collective-permute-start(bf16[256,256]{1,0:T(8,128)(2,1)S(1)} %pad_maximum_fusion.20), channel_id=1, source_target_pairs={{0,2},{1,3},{2,0},{3,1},{4,6},{5,7},{6,4},{7,5},{8,10},{9,11},{10,... | collective-permute-start | bytes 393224 | tf_op jit(solution)/shard_map/ppermute | solution.py:701
  733.9 21.6 %collective-permute-start.32 = (bf16[256,768]{1,0:T(8,128)(2,1)S(1)}, bf16[256,768]{1,0:T(8,128)(2,1)S(1)}, u32[]{:S(2)}, u32[]{:S(2)}) collective-permute-start(bf16[256,768]{1,0:T(8,128)(2,1)S(1)} %pad_maximum_fusion.14), channel_id=1, source_target_pairs={{0,4},{1,5},{2,6},{3,7},{4,0},{5,1},{6,2},{7,3},{8,12},{9,13},{10,... | collective-permute-start | bytes 1179656 | tf_op jit(solution)/shard_map/ppermute | solution.py:691
  746.0 9.5 collective-permute-start.29
  770.0 303.1 %reduce-scatter.12.cloned.1.call-start = ((), (), s32[]{:S(2)}) async-start(), calls=%async_computation.8 | async-start | bytes 19464192 | tf_op jit(solution)/shard_map/reduce_scatter | solution.py:894
  772.2 95.7 %collective-permute-start.36 = (bf16[512,2048]{1,0:T(8,128)(2,1)}, bf16[512,2048]{1,0:T(8,128)(2,1)}, u32[]{:S(2)}, u32[]{:S(2)}) collective-permute-start(bf16[512,2048]{1,0:T(8,128)(2,1)} %fusion.6), channel_id=1, source_target_pairs={{0,1},{1,2},{2,3},{4,5},{5,6},{6,7},{8,9},{9,10},{10,11},{12,13},{... | collective-permute-start | bytes 6291464 | tf_op jit(solution)/shard_map/ppermute | solution.py:638
  775.4 92.5 %collective-permute-start.37 = (bf16[512,2048]{1,0:T(8,128)(2,1)}, bf16[512,2048]{1,0:T(8,128)(2,1)}, u32[]{:S(2)}, u32[]{:S(2)}) collective-permute-start(bf16[512,2048]{1,0:T(8,128)(2,1)} %fusion.6), channel_id=1, source_target_pairs={{1,0},{2,1},{3,2},{5,4},{6,5},{7,6},{9,8},{10,9},{11,10},{13,12},{... | collective-permute-start | bytes 6291464 | tf_op jit(solution)/shard_map/ppermute | solution.py:639
  777.0 15.0 %collective-permute-start.41 = (bf16[2048,128]{1,0:T(8,128)(2,1)S(1)}, bf16[2048,128]{1,0:T(8,128)(2,1)}, u32[]{:S(2)}, u32[]{:S(2)}) collective-permute-start(bf16[2048,128]{1,0:T(8,128)(2,1)S(1)} %copy-done.43), channel_id=1, source_target_pairs={{0,4},{4,0},{1,5},{5,1},{2,6},{6,2},{3,7},{7,3},{8,12},{12,8},{9,1... | collective-permute-start | bytes 1572872 | tf_op jit(solution)/shard_map/ppermute | solution.py:1032
  777.3 50.5 %collective-permute-start.40 = (bf16[1024,512]{1,0:T(8,128)(2,1)S(1)}, bf16[1024,512]{1,0:T(8,128)(2,1)}, u32[]{:S(2)}, u32[]{:S(2)}) collective-permute-start(bf16[1024,512]{1,0:T(8,128)(2,1)S(1)} %copy-done.40), channel_id=1, source_target_pairs={{0,4},{4,0},{1,5},{5,1},{2,6},{6,2},{3,7},{7,3},{8,12},{12,8},{9,1... | collective-permute-start | bytes 3145736 | tf_op jit(solution)/shard_map/ppermute | solution.py:1033
  788.2 39.6 %copy-start.48 = (bf16[512,512]{1,0:T(8,128)(2,1)S(1)}, bf16[512,512]{1,0:T(8,128)(2,1)}, u32[]{:S(2)}) copy-start(bf16[512,512]{1,0:T(8,128)(2,1)} %get-tuple-element.395) | copy-start | bytes 1572868
  847.9 170.8 %copy-start.25 = (bf16[512,2048]{1,0:T(8,128)(2,1)}, bf16[512,2048]{1,0:T(8,128)(2,1)S(1)}, u32[]{:S(2)}) copy-start(bf16[512,2048]{1,0:T(8,128)(2,1)S(1)} %get-tuple-element.376) | copy-start | bytes 6291460
  847.9 47.0 %collective-permute-start.38 = (bf16[512,2048]{1,0:T(8,128)(2,1)S(1)}, bf16[512,2048]{1,0:T(8,128)(2,1)}, u32[]{:S(2)}, u32[]{:S(2)}) collective-permute-start(bf16[512,2048]{1,0:T(8,128)(2,1)S(1)} %get-tuple-element.376), channel_id=1, source_target_pairs={{0,1},{1,2},{2,3},{4,5},{5,6},{6,7},{8,9},{9,10},{10,11},{12,13},{... | collective-permute-start | bytes 6291464 | tf_op jit(solution)/shard_map/ppermute | solution.py:638
  856.0 44.5 %collective-permute-start.39 = (bf16[512,2048]{1,0:T(8,128)(2,1)S(1)}, bf16[512,2048]{1,0:T(8,128)(2,1)}, u32[]{:S(2)}, u32[]{:S(2)}) collective-permute-start(bf16[512,2048]{1,0:T(8,128)(2,1)S(1)} %get-tuple-element.376), channel_id=1, source_target_pairs={{1,0},{2,1},{3,2},{5,4},{6,5},{7,6},{9,8},{10,9},{11,10},{13,12},{... | collective-permute-start | bytes 6291464 | tf_op jit(solution)/shard_map/ppermute | solution.py:639
  915.5 20.1 %collective-permute-start.42 = (bf16[512,2048]{1,0:T(8,128)(2,1)}, bf16[512,2048]{1,0:T(8,128)(2,1)}, u32[]{:S(2)}, u32[]{:S(2)}) collective-permute-start(bf16[512,2048]{1,0:T(8,128)(2,1)} %collective-permute-done.36), channel_id=1, source_target_pairs={{1,2},{2,3},{5,6},{6,7},{9,10},{10,11},{13,14},{14,15},{17,18},{18... | collective-permute-start | bytes 6291464 | tf_op jit(solution)/shard_map/ppermute | solution.py:638
  917.5 52.4 %collective-permute-start.43 = (bf16[512,2048]{1,0:T(8,128)(2,1)}, bf16[512,2048]{1,0:T(8,128)(2,1)}, u32[]{:S(2)}, u32[]{:S(2)}) collective-permute-start(bf16[512,2048]{1,0:T(8,128)(2,1)} %collective-permute-done.37), channel_id=1, source_target_pairs={{1,0},{2,1},{5,4},{6,5},{9,8},{10,9},{13,12},{14,13},{17,16},{18,1... | collective-permute-start | bytes 6291464 | tf_op jit(solution)/shard_map/ppermute | solution.py:639
  918.8 51.1 %collective-permute-start.44 = (bf16[512,2048]{1,0:T(8,128)(2,1)}, bf16[512,2048]{1,0:T(8,128)(2,1)}, u32[]{:S(2)}, u32[]{:S(2)}) collective-permute-start(bf16[512,2048]{1,0:T(8,128)(2,1)} %collective-permute-done.38), channel_id=1, source_target_pairs={{1,2},{2,3},{5,6},{6,7},{9,10},{10,11},{13,14},{14,15},{17,18},{18... | collective-permute-start | bytes 6291464 | tf_op jit(solution)/shard_map/ppermute | solution.py:638
  920.8 87.1 %collective-permute-start.45 = (bf16[512,2048]{1,0:T(8,128)(2,1)}, bf16[512,2048]{1,0:T(8,128)(2,1)}, u32[]{:S(2)}, u32[]{:S(2)}) collective-permute-start(bf16[512,2048]{1,0:T(8,128)(2,1)} %collective-permute-done.39), channel_id=1, source_target_pairs={{1,0},{2,1},{5,4},{6,5},{9,8},{10,9},{13,12},{14,13},{17,16},{18,1... | collective-permute-start | bytes 6291464 | tf_op jit(solution)/shard_map/ppermute | solution.py:639
  1007.9 18.3 %collective-permute-start.46 = (bf16[512,2048]{1,0:T(8,128)(2,1)}, bf16[512,2048]{1,0:T(8,128)(2,1)}, u32[]{:S(2)}, u32[]{:S(2)}) collective-permute-start(bf16[512,2048]{1,0:T(8,128)(2,1)} %collective-permute-done.42), channel_id=1, source_target_pairs={{2,3},{6,7},{10,11},{14,15},{18,19},{22,23},{26,27},{30,31}} | collective-permute-start | bytes 6291464 | tf_op jit(solution)/shard_map/ppermute | solution.py:638
  1009.8 59.2 %collective-permute-start.47 = (bf16[512,2048]{1,0:T(8,128)(2,1)}, bf16[512,2048]{1,0:T(8,128)(2,1)}, u32[]{:S(2)}, u32[]{:S(2)}) collective-permute-start(bf16[512,2048]{1,0:T(8,128)(2,1)} %collective-permute-done.43), channel_id=1, source_target_pairs={{1,0},{5,4},{9,8},{13,12},{17,16},{21,20},{25,24},{29,28}} | collective-permute-start | bytes 6291464 | tf_op jit(solution)/shard_map/ppermute | solution.py:639
  1011.1 69.3 %collective-permute-start.48 = (bf16[512,2048]{1,0:T(8,128)(2,1)}, bf16[512,2048]{1,0:T(8,128)(2,1)}, u32[]{:S(2)}, u32[]{:S(2)}) collective-permute-start(bf16[512,2048]{1,0:T(8,128)(2,1)} %collective-permute-done.44), channel_id=1, source_target_pairs={{2,3},{6,7},{10,11},{14,15},{18,19},{22,23},{26,27},{30,31}} | collective-permute-start | bytes 6291464 | tf_op jit(solution)/shard_map/ppermute | solution.py:638
  1013.1 105.7 %collective-permute-start.49 = (bf16[512,2048]{1,0:T(8,128)(2,1)}, bf16[512,2048]{1,0:T(8,128)(2,1)}, u32[]{:S(2)}, u32[]{:S(2)}) collective-permute-start(bf16[512,2048]{1,0:T(8,128)(2,1)} %collective-permute-done.45), channel_id=1, source_target_pairs={{1,0},{5,4},{9,8},{13,12},{17,16},{21,20},{25,24},{29,28}} | collective-permute-start | bytes 6291464 | tf_op jit(solution)/shard_map/ppermute | solution.py:639
  1074.5 44.3 %collective-permute-start.50 = (bf16[256,768]{1,0:T(8,128)(2,1)S(1)}, bf16[256,768]{1,0:T(8,128)(2,1)S(1)}, u32[]{:S(2)}, u32[]{:S(2)}) collective-permute-start(bf16[256,768]{1,0:T(8,128)(2,1)S(1)} %get-tuple-element.448), channel_id=1, source_target_pairs={{0,1},{1,2},{2,3},{3,0},{4,5},{5,6},{6,7},{7,4},{8,9},{9,10},{10,1... | collective-permute-start | bytes 1179656 | tf_op jit(solution)/shard_map/ppermute | solution.py:701
  1074.6 44.2 %collective-permute-start.51 = (bf16[256,768]{1,0:T(8,128)(2,1)S(1)}, bf16[256,768]{1,0:T(8,128)(2,1)S(1)}, u32[]{:S(2)}, u32[]{:S(2)}) collective-permute-start(bf16[256,768]{1,0:T(8,128)(2,1)S(1)} %get-tuple-element.449), channel_id=1, source_target_pairs={{0,2},{1,3},{2,0},{3,1},{4,6},{5,7},{6,4},{7,5},{8,10},{9,11},{10,... | collective-permute-start | bytes 1179656 | tf_op jit(solution)/shard_map/ppermute | solution.py:701
  1074.7 48.2 %collective-permute-start.52 = (bf16[256,768]{1,0:T(8,128)(2,1)S(1)}, bf16[256,768]{1,0:T(8,128)(2,1)S(1)}, u32[]{:S(2)}, u32[]{:S(2)}) collective-permute-start(bf16[256,768]{1,0:T(8,128)(2,1)S(1)} %get-tuple-element.447), channel_id=1, source_target_pairs={{0,3},{1,0},{2,1},{3,2},{4,7},{5,4},{6,5},{7,6},{8,11},{9,8},{10,9... | collective-permute-start | bytes 1179656 | tf_op jit(solution)/shard_map/ppermute | solution.py:701
  (55 other events, 314.2 us)
Sparse Core Ops, SparseCore 0:
  139.1 80.1 all-gather.4
  220.9 85.7 all-gather.6
  308.9 91.6 reduce-scatter.5
  402.9 93.5 reduce-scatter.7
  498.7 182.0 reduce-scatter.9
  770.1 101.9 reduce-scatter.13
  900.6 116.9 reduce-scatter.11

commit v6 on v5

--- a/solution.py
+++ b/solution.py
@@ -517,7 +517,6 @@
         jax.ShapeDtypeStruct((rows, width), BF16),
         jax.ShapeDtypeStruct((rows, units), BF16),
         jax.ShapeDtypeStruct((rows, 2 * units), BF16),
-        jax.ShapeDtypeStruct((rows, width), BF16),
     ]
     gain = gain.reshape(1, width)
     return pl.pallas_call(
@@ -533,8 +532,8 @@
         + [whole(weight) for weight in weights]
         + [pl.BlockSpec(memory_space=pl.ANY) for _ in earlier],
         out_specs=[natural(shape.shape[1]) for shape in shapes]
-        + [pl.BlockSpec((block, width), lambda i: (i, 0))],
-        out_shape=shapes + [jax.ShapeDtypeStruct((rows // 2, width), BF16)],
+        + [pl.BlockSpec((block, width), lambda i: (i, 0))] * 2,
+        out_shape=shapes + [jax.ShapeDtypeStruct((rows // 2, width), BF16)] * 2,
         input_output_aliases={8 + k: k for k in range(len(earlier))},
         compiler_params=pltpu.CompilerParams(vmem_limit_bytes=60 * 2**20),
         cost_estimate=LIGHT,
@@ -899,16 +898,18 @@
     hop = query_gather.step()
     weights = (w_gate, w_up, w_down)
     fixed = (tokens, cotangent, norm_mlp, output_whole, weights)
-    *fed, grad_first = feed_forward(0, first_whole, *fixed, ())
-    fed, grad_first, second_whole, hop = hold(fed, grad_first, second_whole, hop)
+    *fed, down_first, grad_first = feed_forward(0, first_whole, *fixed, ())
+    fed, down_first, grad_first, second_whole, hop = hold(
+        fed, down_first, grad_first, second_whole, hop
+    )
     query_gather.held(hop)
 
     share_first = line_sum(grad_first)
     hop = query_gather.step()
-    *fed, grad_second = feed_forward(1, second_whole, *fixed, fed)
-    fed, grad_second, hop = hold(fed, grad_second, hop)
+    *fed, down_second, grad_second = feed_forward(1, second_whole, *fixed, fed)
+    fed, down_second, grad_second, hop = hold(fed, down_second, grad_second, hop)
     query_gather.held(hop)
-    middle, normed_mlp, hidden, gates, mlp_part = fed
+    middle, normed_mlp, hidden, gates = fed
 
     share_second = line_sum(grad_second)
     hop = query_gather.step()
@@ -916,7 +917,7 @@
     w_gates, hop, share_first = hold(w_gates, hop, share_first)
     query_gather.held(hop)
 
-    mlp_share = line_sum(after(mlp_part, w_gates))
+    mixed_first = line_sum(after(down_first, w_gates))
 
     gain_first, middle_first, low_first, blocks = to_attention(0, middle, share_first)
     query_part = query_gather.whole()
@@ -927,8 +928,7 @@
     came_first = send_blocks(block_of(blocks))
     query_over = lax.ppermute(query_part, "ctx", over)
     w_downs = t_dot(cotangent, hidden).astype(BF16)
-    n_part = tok_rows // groups
-    middle_own = lax.dynamic_slice_in_dim(middle, member * n_part, n_part, 0)
+    middle_own = [own_rows(middle, c) for c in chunks]
     came_first, middle_own, query_part, query_over, w_downs = hold(
         came_first, middle_own, query_part, query_over, w_downs
     )
@@ -936,22 +936,15 @@
     query_near = (query_part, query_over)
     query_far = tuple(lax.ppermute(part, "dp", beside) for part in query_near)
     grads_first = stack_blocks(came_first).reshape(span, features)
-    attention_rows = jnp.concatenate(
-        [
-            lax.dynamic_slice_in_dim(whole, member * share, share, 1)
-            for whole in (first_whole, second_whole)
-        ],
-        axis=1,
-    )
-    attention_rows = jnp.swapaxes(attention_rows, 0, 1).reshape(2 * share, groups * features)
-    query_near, query_far, grads_first, attention_rows, share_second = hold(
-        query_near, query_far, grads_first, attention_rows, share_second
+    query_near, query_far, grads_first, share_second = hold(
+        query_near, query_far, grads_first, share_second
     )
 
     gain_second, middle_second, low_second, blocks = to_attention(1, middle, share_second)
     gain_second, middle_second, low_second, blocks = hold(
         gain_second, middle_second, low_second, blocks
     )
+    mixed_second = line_sum(after(down_second, blocks))
 
     def back_arguments(c, grads):
         return metas[c], offsets[c], queries[c], attention[c], grads, log_totals[c], forms, *tables[c]
@@ -965,7 +958,12 @@
     dq_second, kv_near, kv_far = attend_back_last(
         *back_arguments(1, grads_second), dk, dv, cos_pair, sin_pair
     )
-    dq_second, kv_near, kv_far, rows_first = hold(dq_second, kv_near, kv_far, rows_first)
+    mixed_gathers = [Gather((middle_own[0] + mixed_first.astype(F32)).astype(BF16)), None]
+    mixed_hop = mixed_gathers[0].step()
+    dq_second, kv_near, kv_far, rows_first, mixed_hop = hold(
+        dq_second, kv_near, kv_far, rows_first, mixed_hop
+    )
+    mixed_gathers[0].held(mixed_hop)
 
     def kv_share_of(array, j):
         return [lax.dynamic_slice_in_dim(array, row_of[c][j], share, 0) for c in chunks]
@@ -978,8 +976,17 @@
     )
     query_parts = query_near + query_far
     first_part = join(quarters, stack_blocks(rows_first), query_parts)
+    attention_rows = jnp.concatenate(
+        [
+            lax.dynamic_slice_in_dim(whole, member * share, share, 1)
+            for whole in after((first_whole, second_whole), dq_second)
+        ],
+        axis=1,
+    )
+    attention_rows = jnp.swapaxes(attention_rows, 0, 1).reshape(2 * share, groups * features)
     w_outs = t_dot(jnp.concatenate([low_first, low_second], axis=0), attention_rows).astype(BF16)
     near_blocks, far_blocks, first_part, w_outs = hold(near_blocks, far_blocks, first_part, w_outs)
+    mixed_hop = mixed_gathers[0].step()
     far_blocks = stack_blocks(far_blocks)
     kv_blocks = (
         stack_blocks(near_blocks).astype(F32) + far_blocks[:, :, features:].astype(F32)
@@ -1016,50 +1023,64 @@
         return target
 
     gains = jnp.stack([attn_gain, gain_first + gain_second], axis=1).astype(BF16)
-    grad_inputs, gains, dq_second, kv_far, kv_near, w_gates = hold(
-        grad_inputs, gains, dq_second, kv_far, kv_near, w_gates
-    )
+    grad_inputs, gains, dq_second, kv_far, kv_near, w_gates, mixed_hop = hold(
+        grad_inputs, gains, dq_second, kv_far, kv_near, w_gates, mixed_hop
+    )
+    mixed_gathers[0].held(mixed_hop)
     gate_up_grad = plane_sum(w_gates)
 
-    def put_share(target, piece, source):
-        return lax.dynamic_update_slice_in_dim(target, piece, source * n_part, 0)
-
-    mixed_share = (middle_own + mlp_share.astype(F32)).astype(BF16)
-    tokens_gather, mixed_gather = Gather(grad_inputs), Gather(mixed_share)
+    def put_chunk(c):
+        def put(target, piece, source):
+            return lax.dynamic_update_slice_in_dim(target, piece, row_of[c][source], 0)
+
+        return put
+
+    tokens_gather = Gather(grad_inputs)
     tokens_grad = jnp.zeros((tok_rows, width), BF16)
     mixed = jnp.zeros((tok_rows, width), BF16)
-    hop, mixed_hop = tokens_gather.step(), mixed_gather.step()
-    kv_sent = lax.ppermute(kv_far, "ctx", over)
-    dq_home = lax.ppermute(dq_second, "ctx", over)
+    hop, mixed_hop = tokens_gather.step(), mixed_gathers[0].step()
+    home = lax.ppermute(
+        jnp.concatenate([dq_second, kv_far[:span], kv_far[span:]], axis=1), "ctx", over
+    )
+    dq_home, kv_sent = home[:, :features], home[:, features:]
+    kv_sent = jnp.concatenate([kv_sent[:, : 2 * HD], kv_sent[:, 2 * HD :]], axis=0)
     grad_kv_raw = (kv_near + kv_sent.astype(F32)).astype(BF16)
     query_kv = t_dot(
         normed, jnp.concatenate([natural(dq_first, dq_home), grad_kv_raw], axis=1)
     ).astype(BF16)
     gains = jnp.pad(gains, ((0, 0), (0, 126)))
     rest = jnp.concatenate([w_downs, w_outs, query_kv, gains], axis=1)
+    for count in range(3):
+        mixed = mixed_gathers[0].place_hop(put_chunk(0), mixed, count)
+    hop, mixed_hop, rest, mixed = hold(hop, mixed_hop, rest, mixed)
+    tokens_gather.held(hop)
+    mixed_gathers[0].held(mixed_hop)
+    rest = plane_sum(rest)
+
+    mixed_gathers[1] = Gather((middle_own[1] + after(mixed_second, hop).astype(F32)).astype(BF16))
+    hop, mixed_hop = tokens_gather.step(), mixed_gathers[1].step()
+    for count in range(3, groups):
+        mixed = mixed_gathers[0].place_hop(put_chunk(0), mixed, count)
+        if count + 1 < groups:
+            mixed_gathers[0].step()
     tokens_grad = tokens_gather.place_hop(put_rows, tokens_grad, 0)
-    mixed = mixed_gather.place_hop(put_share, mixed, 0)
-    hop, mixed_hop, rest, tokens_grad, mixed = hold(hop, mixed_hop, rest, tokens_grad, mixed)
-    tokens_gather.held(hop)
-    mixed_gather.held(mixed_hop)
-    rest = plane_sum(rest)
-
-    hop, mixed_hop = tokens_gather.step(), mixed_gather.step()
     tokens_grad = tokens_gather.place_hop(put_rows, tokens_grad, 1)
-    mixed = mixed_gather.place_hop(put_share, mixed, 1)
+    mixed = mixed_gathers[1].place_hop(put_chunk(1), mixed, 0)
     hop, mixed_hop, tokens_grad, mixed = hold(hop, mixed_hop, tokens_grad, mixed)
     tokens_gather.held(hop)
-    mixed_gather.held(mixed_hop)
-
-    hop = tokens_gather.step()
+    mixed_gathers[1].held(mixed_hop)
+
+    hop, mixed_hop = tokens_gather.step(), mixed_gathers[1].step()
     tokens_grad = tokens_gather.place_hop(put_rows, tokens_grad, 2)
-    mixed = mixed_gather.place_hop(put_share, mixed, 2)
-    hop, tokens_grad, mixed = hold(hop, tokens_grad, mixed)
+    mixed = mixed_gathers[1].place_hop(put_chunk(1), mixed, 1)
+    hop, mixed_hop, tokens_grad, mixed = hold(hop, mixed_hop, tokens_grad, mixed)
     tokens_gather.held(hop)
-
-    mixed_hop = mixed_gather.step()
+    mixed_gathers[1].held(mixed_hop)
+
+    mixed_hop = mixed_gathers[1].step()
     if groups > 3:
         tokens_grad = tokens_gather.place_hop(put_rows, tokens_grad, 3)
+    mixed = mixed_gathers[1].place_hop(put_chunk(1), mixed, 2)
     hidden_units = w_down.shape[1]
     rest = after(rest, hop)
     down_grad = rest[:, :hidden_units]
@@ -1071,8 +1092,8 @@
             [lax.dynamic_slice_in_dim(output_plane, j * features, features, 1), small], axis=1
         )
     )
-    mixed_hop, tokens_grad, blocks = hold(mixed_hop, tokens_grad, blocks)
-    mixed_gather.held(mixed_hop)
+    mixed_hop, tokens_grad, mixed, blocks = hold(mixed_hop, tokens_grad, mixed, blocks)
+    mixed_gathers[1].held(mixed_hop)
     blocks = stack_blocks(blocks).astype(F32)
     output_grad = jnp.sum(blocks[:, :, :features], axis=0)
     kv_share = blocks.shape[1] // groups
@@ -1081,10 +1102,10 @@
     )
     gains = jnp.sum(blocks[:, :, features + 2 * HD : features + 2 * HD + 2], axis=0).T
     for count in range(3, groups):
-        mixed = mixed_gather.place_hop(put_share, mixed, count)
+        mixed = mixed_gathers[1].place_hop(put_chunk(1), mixed, count)
         if count + 1 < groups:
             tokens_gather.step()
-            mixed_gather.step()
+            mixed_gathers[1].step()
             tokens_grad = tokens_gather.place_hop(put_rows, tokens_grad, count + 1)
 
     key_heads, value_heads = [], []

time: 1140 us -> 1140 us (level); the launches traced: 1140 us -> 1130 us
  local copies, waits for them, and re-layouts: 107 us -> 86.6 us
    ppermute x12, waiting for transfers between devices: 40.6 us -> 67.2 us  [send_blocks(): lax.ppermute(block, 'tensor', [(i, (i + shift) % size) for i in range(siz...]
    pallas_call x1, Pallas kernels: 78.1 us -> 55.9 us  [attend_back_first(): pl.pallas_call(kernel, grid_spec=pltpu.PrefetchScalarGridSpec(num_scalar_...]
    pallas_call x1, Pallas kernels: 38.1 us -> 60 us  [attend_back_last(): pl.pallas_call(kernel, grid_spec=pltpu.PrefetchScalarGridSpec(num_scalar_...]
    ppermute x12 -> x15, waiting for transfers between devices: 173 us -> 153 us  [step(): self.lefts.append(lax.ppermute(self.lefts[-1], 'tensor', to_left))]
    pallas_call x1, Pallas kernels: 25.7 us -> 41.4 us  [attend(): pl.pallas_call(kernel, grid_spec=pltpu.PrefetchScalarGridSpec(num_scalar_...]
    pallas_call x1, Pallas kernels: 59.1 us -> 43.6 us  [attend_first(): pl.pallas_call(kernel, grid_spec=pltpu.PrefetchScalarGridSpec(num_scalar_...]
    ppermute x12 -> x15, waiting for transfers between devices: 27.1 us -> 12.4 us  [step(): self.rights.append(lax.ppermute(self.rights[-1], 'tensor', to_right))]
    ppermute x1, starting transfers between devices: 14.2 us -> 0.49 us  [body(): second_home = lax.ppermute(second, 'ctx', over)]
  transfers between devices with their start and end apart: 60 -> 66, of which waited for: 19 -> 22; matrix products, arithmetic and copies ran while one was open for 23% -> 20% of each run, Pallas kernels for 33% -> 33%
where the time goes in v6:
time: 1140 us; the launch traced here: 1130 us
  Pallas kernels  371 us (33%)
  waiting for transfers between devices  331 us (29%)
  starting transfers between devices  120 us (11%)
  local copies, waits for them, and re-layouts  86.6 us (8%)
  other arithmetic  86.3 us (8%)
  matrix products  81.8 us (7%)
  between operations  50.2 us (4%)
    ppermute x15, waiting for transfers between devices, step(): self.lefts.append(lax.ppermute(self.lefts[-1], 'tensor', to_left))  153 us
    pallas_call x2, Pallas kernels, feed_forward(): pl.pallas_call(feed_kernel, grid=(2 * quarter,), in_specs=[pl.BlockSpec((...  124 us
    dot_general x4, matrix products, t_dot(): return jnp.einsum('rd,rf->df', a, b, preferred_element_type=F32)  67.7 us
    ppermute x12, waiting for transfers between devices, send_blocks(): lax.ppermute(block, 'tensor', [(i, (i + shift) % size) for i in range(siz...  67.2 us
    pallas_call x1, Pallas kernels, attend_back_last(): pl.pallas_call(kernel, grid_spec=pltpu.PrefetchScalarGridSpec(num_scalar_...  60 us
    pallas_call x1, Pallas kernels, attend_back_first(): pl.pallas_call(kernel, grid_spec=pltpu.PrefetchScalarGridSpec(num_scalar_...  55.9 us
    pallas_call x1, Pallas kernels, attend_first(): pl.pallas_call(kernel, grid_spec=pltpu.PrefetchScalarGridSpec(num_scalar_...  43.6 us
    pallas_call x1, Pallas kernels, attend(): pl.pallas_call(kernel, grid_spec=pltpu.PrefetchScalarGridSpec(num_scalar_...  41.4 us
  transfers between devices with their start and end apart: 66, of which 22 were waited for; matrix products, arithmetic and copies ran while one was open for 20% of the time, Pallas kernels for 33%

profile of v6, /device:TPU:0, one launch (start us, length us, event | category | flops | bytes accessed | tf_op | source)
XLA Modules:
  0.0 1127.0 jit_solution(10729364230103741507)
XLA Ops:
  9.8 6.0 collective-permute-start
  18.2 5.4 multiply_sine_fusion.1
  27.1 17.5 %project.1 = (bf16[2048,128]{1,0:T(8,128)(2,1)S(1)}, bf16[2048,512]{1,0:T(8,128)(2,1)}, bf16[2048,2048]{1,0:T(8,128)(2,1)}, f32[2048,128]{1,0:T(8,128)S(1)}, f32[2048,128]{1,0:T(8,128)S(1)}) custom-call(s32[1]{0:T(128)} %bitcast.1.head, bf16[2048,2048]{1,0:T(8,128)(2,1)} %tokens_ref.5, f32[1,2048]{1,0:T(1,128)S(1)} %bitcast.150, ...), custom_call_target="tpu_custom_call" | custom-call | flops 1 | bytes 1 | tf_op jit(solution)/shard_map/project/pallas_call | solution.py:68
  54.2 8.0 collective-permute-done.2.other
  62.2 13.9 %collective-permute-done.4.refs_2_ = bf16[1024,512]{1,0:T(8,128)(2,1)S(1)} collective-permute-done((bf16[1024,512]{1,0:T(8,128)(2,1)}, bf16[1024,512]{1,0:T(8,128)(2,1)S(1)}, u32[]{:S(2)}, u32[]{:S(2)}) %collective-permute-start.4) | collective-permute-done | bytes 1048608 | tf_op jit(solution)/shard_map/ppermute | solution.py:638
  79.7 43.6 %attend_first.1 = (bf16[1024,512]{1,0:T(8,128)(2,1)}, f32[4,8,1024]{2,1,0:T(8,128)}, bf16[4096,128]{1,0:T(8,128)(2,1)}, bf16[4096,128]{1,0:T(8,128)(2,1)}, bf16[...) custom-call(s32[6]{0:T(128)} %get-tuple-element.520.meta.refs_0_, ...), custom_call_target="tpu_custom_call" | custom-call | flops 17179869184 | bytes 8388608 | tf_op jit(solution)/shard_map/attend_first/pallas_call | solution.py:208
  128.1 6.9 arrange.3.refs_0_
  136.9 41.4 %attend.1 = (bf16[1024,512]{1,0:T(8,128)(2,1)}, f32[4,8,1024]{2,1,0:T(8,128)}) custom-call(s32[6]{0:T(128)} %get-tuple-element.519.refs_0_, bf16[1024,512]{1,0:T(8,128)(2,1)} %collective-permute-done.5.refs_1_, bf16[4096,128]{1,0:T(8,128)(2,1)} %get-tuple-element.224.refs_2_.refs_5_, bf16[4096,128]{1,0:T(8,128)(2,1)} %get-tuple-element.225.refs_3_.refs_6_, ...), custom_call_target="tpu_custom_call" | custom-call | flops 17179869184 | bytes 8388608 | tf_op jit(solution)/shard_map/attend/pallas_call | solution.py:245
  180.9 6.5 arrange.4.output_weight
  187.4 3.7 multiply_sine_fusion
  193.1 3.7 maximum_maximum_fusion
  196.9 7.3 collective-permute-done.9
  204.2 9.3 all-gather.5.cloned.1.call-done
  217.3 62.6 %feed_forward.2 = (f32[2048,2048]{1,0:T(8,128)}, bf16[2048,2048]{1,0:T(8,128)(2,1)}, bf16[2048,1408]{1,0:T(8,128)(2,1)}, bf16[2048,2816]{1,0:T(8,128)(2,1)}, bf1...) custom-call(bf16[4,1024,512]{2,1,0:T(8,128)(2,1)} %bitcast.157, bf16[2048,2048]{1,0:T(8,128)(2,1)} %tokens_ref.5, ...), custom_call_target="tpu_custom_call" | custom-call | flops 1 | bytes 1 | tf_op jit(solution)/shard_map/feed_forward/pallas_call | solution.py:522
  279.9 21.0 %all-gather.7.cloned.1.call-done = bf16[4096,512]{1,0:T(8,128)(2,1)} async-done(((bf16[1024,512]{1,0:T(8,128)(2,1)}), bf16[4096,512]{1,0:T(8,128)(2,1)}) %all-gather.7.cloned.1.call-update) | async-done | bytes 4194320 | tf_op jit(solution)/shard_map/all_gather | solution.py:853
  311.6 61.3 %feed_forward.3 = (f32[2048,2048]{1,0:T(8,128)}, bf16[2048,2048]{1,0:T(8,128)(2,1)}, bf16[2048,1408]{1,0:T(8,128)(2,1)}, bf16[2048,2816]{1,0:T(8,128)(2,1)}, bf1...) custom-call(bf16[4,1024,512]{2,1,0:T(8,128)(2,1)} %bitcast.159, ...), custom_call_target="tpu_custom_call", output_to_operand_aliasing={{0}: (8, {}), {1}: (9, {}), {2}: (10, {}), {3}: (11, {})} | custom-call | flops 1 | bytes 1 | tf_op jit(solution)/shard_map/feed_forward/pallas_call | solution.py:522
  375.1 31.8 %convolution_convert_fusion = bf16[2048,2816]{1,0:T(8,128)(2,1)} fusion(bf16[2048,2048]{1,0:T(8,128)(2,1)} %get-tuple-element.261, bf16[2048,2816]{1,0:T(8,128)(2,1)} %get-tuple-element.262), kind=kOutput, calls=%fused_computation.3 | convolution fusion | flops 23628087296 | bytes 31457280 | tf_op jit(solution)/shard_map/rd,rf->df/dot_general | solution.py:732
  406.8 4.5 multiply_reduce_fusion.1
  411.4 2.8 fusion.26
  415.4 4.0 fusion.54
  421.6 5.8 fusion.41
  430.6 3.3 collective-permute-start.16
  437.7 2.9 collective-permute-start.18
  440.6 19.4 %fusion.2 = bf16[2048,1408]{1,0:T(8,128)(2,1)} fusion(bf16[2048,1408]{1,0:T(8,128)(2,1)} %get-tuple-element.274, bf16[2048,2048]{1,0:T(8,128)(2,1)} %cotangent_ref.3), kind=kOutput, calls=%fused_computation.10 | convolution fusion | flops 11814043648 | bytes 19922944 | tf_op jit(solution)/shard_map/rd,rf->df/dot_general | solution.py:732
  461.8 6.6 collective-permute-done.17
  468.7 6.5 collective-permute-done.19.refs_1_
  482.4 10.7 reduce-scatter.9.cloned.1.call-done
  495.9 3.3 fusion.52
  499.2 6.2 fusion.42
  508.6 7.8 collective-permute-start.23
  518.2 3.8 collective-permute-start.25
  537.3 55.9 %attend_back_first.1 = (bf16[1024,512]{1,0:T(8,128)(2,1)}, f32[4096,128]{1,0:T(8,128)}, f32[4096,128]{1,0:T(8,128)}) custom-call(s32[6]{0:T(128)} %get-tuple-element.520.meta.refs_0_, bf16[1024,512]{1,0:T(8,128)(2,1)} %pad_maximum_fusion.2.q_ref.refs_1_, bf16[1024,512]{1,0:T(8,128)(2,1)} %get-tuple-element.222.refs_2_, bf16[1024,512]{1,0:T(8,128)(2,1)} %bitcast.163, ...), custom_call_target="tpu_custom_call" | custom-call | flops 1 | bytes 1 | tf_op jit(solution)/shard_map/attend_back_first/pallas_call | solution.py:381
  594.2 4.5 broadcast.124.clone
  600.0 9.5 collective-permute-start.29
  620.7 60.0 %attend_back_last.1 = (bf16[1024,512]{1,0:T(8,128)(2,1)}, f32[2048,128]{1,0:T(8,128)}, bf16[2048,128]{1,0:T(8,128)(2,1)}) custom-call(s32[6]{0:T(128)} %get-tuple-element.519.refs_0_, bf16[1024,512]{1,0:T(8,128)(2,1)} %collective-permute-done.5.refs_1_, bf16[1024,512]{1,0:T(8,128)(2,1)} %get-tuple-element.231.refs_2_, bf16[1024,512]{1,0:T(8,128)(2,1)} %bitcast.45.refs_3_, ...), custom_call_target="tpu_custom_call" | custom-call | flops 1 | bytes 1 | tf_op jit(solution)/shard_map/attend_back_last/pallas_call | solution.py:436
  680.7 28.9 %collective-permute-done.27 = bf16[256,512]{1,0:T(8,128)(2,1)} collective-permute-done((bf16[256,512]{1,0:T(8,128)(2,1)S(1)}, bf16[256,512]{1,0:T(8,128)(2,1)}, u32[]{:S(2)}, u32[]{:S(2)}) %collective-permute-start.27) | collective-permute-done | bytes 262176 | tf_op jit(solution)/shard_map/ppermute | solution.py:700
  714.3 4.2 copy.89
  721.0 14.1 %collective-permute-start.37 = (bf16[256,768]{1,0:T(8,128)(2,1)S(1)}, bf16[256,768]{1,0:T(8,128)(2,1)S(1)}, u32[]{:S(2)}, u32[]{:S(2)}) collective-permute-start(bf16[256,768]{1,0:T(8,128)(2,1)S(1)} %pad_maximum_fusion.18), channel_id=1, source_target_pairs={{0,7},{1,4},{2,5},{3,6},{4,3},{5,0},{6,1},{7,2},{8,15},{9,12},{10,... | collective-permute-start | bytes 1179656 | tf_op jit(solution)/shard_map/ppermute | solution.py:690
  736.8 4.4 collective-permute-start.33
  743.0 6.9 convolution_convert_fusion.1
  750.9 13.6 %collective-permute-done.33 = bf16[256,256]{1,0:T(8,128)(2,1)S(1)} collective-permute-done((bf16[256,256]{1,0:T(8,128)(2,1)S(1)}, bf16[256,256]{1,0:T(8,128)(2,1)S(1)}, u32[]{:S(2)}, u32[]{:S(2)}) %collective-permute-start.33) | collective-permute-done | bytes 131104 | tf_op jit(solution)/shard_map/ppermute | solution.py:700
  764.9 13.3 %collective-permute-done.32 = bf16[256,256]{1,0:T(8,128)(2,1)S(1)} collective-permute-done((bf16[256,256]{1,0:T(8,128)(2,1)S(1)}, bf16[256,256]{1,0:T(8,128)(2,1)S(1)}, u32[]{:S(2)}, u32[]{:S(2)}) %collective-permute-start.32) | collective-permute-done | bytes 131104 | tf_op jit(solution)/shard_map/ppermute | solution.py:700
  779.2 6.6 join.2
  789.2 6.6 join.3
  802.6 14.2 %collective-permute-done.39 = bf16[256,2048]{1,0:T(8,128)(2,1)} collective-permute-done((bf16[256,2048]{1,0:T(8,128)(2,1)}, bf16[256,2048]{1,0:T(8,128)(2,1)}, u32[]{:S(2)}, u32[]{:S(2)}) %collective-permute-start.39) | collective-permute-done | bytes 1048608 | tf_op jit(solution)/shard_map/ppermute | solution.py:638
  830.1 2.8 select_dynamic-update-slice_fusion.6
  832.9 6.6 collective-permute-start.40
  844.7 2.8 select_dynamic-update-slice_fusion.5
  847.5 34.6 %collective-permute-done.44 = bf16[1024,768]{1,0:T(8,128)(2,1)} collective-permute-done((bf16[1024,768]{1,0:T(8,128)(2,1)}, bf16[1024,768]{1,0:T(8,128)(2,1)}, u32[]{:S(2)}, u32[]{:S(2)}) %collective-permute-start.44) | collective-permute-done | bytes 1572896 | tf_op jit(solution)/shard_map/ppermute | solution.py:1042
  884.9 9.7 convolution_convert_fusion.3
  894.6 6.9 fusion.1
  901.5 7.4 collective-permute-done.43
  918.3 4.5 broadcast.124
  928.2 2.8 select_dynamic-update-slice_fusion.4
  936.0 4.3 collective-permute-start.47
  945.7 12.4 %collective-permute-done.47 = bf16[256,2048]{1,0:T(8,128)(2,1)S(1)} collective-permute-done((bf16[256,2048]{1,0:T(8,128)(2,1)S(1)}, bf16[256,2048]{1,0:T(8,128)(2,1)S(1)}, u32[]{:S(2)}, u32[]{:S(2)}) %collective-permute-start.47) | collective-permute-done | bytes 1048608 | tf_op jit(solution)/shard_map/ppermute | solution.py:637
  958.1 37.4 %collective-permute-done.48 = bf16[256,2048]{1,0:T(8,128)(2,1)S(1)} collective-permute-done((bf16[256,2048]{1,0:T(8,128)(2,1)S(1)}, bf16[256,2048]{1,0:T(8,128)(2,1)S(1)}, u32[]{:S(2)}, u32[]{:S(2)}) %collective-permute-start.48) | collective-permute-done | bytes 1048608 | tf_op jit(solution)/shard_map/ppermute | solution.py:638
  1007.3 56.9 %collective-permute-done.52 = bf16[256,2048]{1,0:T(8,128)(2,1)} collective-permute-done((bf16[256,2048]{1,0:T(8,128)(2,1)S(1)}, bf16[256,2048]{1,0:T(8,128)(2,1)}, u32[]{:S(2)}, u32[]{:S(2)}) %collective-permute-start.52) | collective-permute-done | bytes 1048608 | tf_op jit(solution)/shard_map/ppermute | solution.py:638
  1070.0 2.7 select_dynamic-update-slice_fusion.1
  1072.8 3.1 slice_convert_fusion
  1077.3 3.7 collective-permute-start.55
  1085.5 23.4 %collective-permute-done.54 = bf16[256,2048]{1,0:T(8,128)(2,1)} collective-permute-done((bf16[256,2048]{1,0:T(8,128)(2,1)}, bf16[256,2048]{1,0:T(8,128)(2,1)}, u32[]{:S(2)}, u32[]{:S(2)}) %collective-permute-start.54) | collective-permute-done | bytes 1048608 | tf_op jit(solution)/shard_map/ppermute | solution.py:638
  1108.9 4.1 collective-permute-done.57
  1115.7 2.7 select_dynamic-update-slice_fusion
  (421 shorter events, 167.9 us)
Async XLA Ops:
  7.2 206.4 %all-gather.5.cloned.1.call-start = ((), (), s32[]{:S(2)}) async-start(), calls=%async_computation.12 | async-start | bytes 5242880 | tf_op jit(solution)/shard_map/all_gather | solution.py:828
  9.8 36.5 %collective-permute-start = (bf16[1024,512]{1,0:T(8,128)(2,1)}, bf16[1024,512]{1,0:T(8,128)(2,1)}, u32[]{:S(2)}, u32[]{:S(2)}) collective-permute-start(bf16[1024,512]{1,0:T(8,128)(2,1)} %constant_dynamic-slice_fusion.43.refs_6_), channel_id=1, source_target_pairs={{0,1},{1,2},{2,3},{4,5},{5,6},{6,7},{8,9},{9,10},{10,11},{12,13},{... | collective-permute-start | bytes 3145736 | tf_op jit(solution)/shard_map/ppermute | solution.py:637
  15.9 30.5 %collective-permute-start.1 = (bf16[1024,512]{1,0:T(8,128)(2,1)}, bf16[1024,512]{1,0:T(8,128)(2,1)}, u32[]{:S(2)}, u32[]{:S(2)}) collective-permute-start(bf16[1024,512]{1,0:T(8,128)(2,1)} %constant_dynamic-slice_fusion.43.refs_6_), channel_id=1, source_target_pairs={{1,0},{2,1},{3,2},{5,4},{6,5},{7,6},{9,8},{10,9},{11,10},{13,12},{... | collective-permute-start | bytes 3145736 | tf_op jit(solution)/shard_map/ppermute | solution.py:638
  46.3 15.8 %collective-permute-start.3 = (bf16[1024,512]{1,0:T(8,128)(2,1)}, bf16[1024,512]{1,0:T(8,128)(2,1)S(1)}, u32[]{:S(2)}, u32[]{:S(2)}) collective-permute-start(bf16[1024,512]{1,0:T(8,128)(2,1)} %collective-permute-done.refs_5_), channel_id=1, source_target_pairs={{1,2},{2,3},{5,6},{6,7},{9,10},{10,11},{13,14},{14,15},{17,18},{18... | collective-permute-start | bytes 3145736 | tf_op jit(solution)/shard_map/ppermute | solution.py:637
  47.2 28.9 %collective-permute-start.4 = (bf16[1024,512]{1,0:T(8,128)(2,1)}, bf16[1024,512]{1,0:T(8,128)(2,1)S(1)}, u32[]{:S(2)}, u32[]{:S(2)}) collective-permute-start(bf16[1024,512]{1,0:T(8,128)(2,1)} %collective-permute-done.1.refs_4_), channel_id=1, source_target_pairs={{1,0},{2,1},{5,4},{6,5},{9,8},{10,9},{13,12},{14,13},{17,16},{18,1... | collective-permute-start | bytes 3145736 | tf_op jit(solution)/shard_map/ppermute | solution.py:638
  48.6 13.6 %collective-permute-start.2 = (bf16[2048,128]{1,0:T(8,128)(2,1)}, bf16[2048,128]{1,0:T(8,128)(2,1)S(1)}, u32[]{:S(2)}, u32[]{:S(2)}) collective-permute-start(bf16[2048,128]{1,0:T(8,128)(2,1)} %copy-done.24), channel_id=1, source_target_pairs={{0,4},{4,0},{1,5},{5,1},{2,6},{6,2},{3,7},{7,3},{8,12},{12,8},{9,1... | collective-permute-start | bytes 1572872 | tf_op jit(solution)/shard_map/ppermute | solution.py:814
  76.1 47.1 %collective-permute-start.5 = (bf16[1024,512]{1,0:T(8,128)(2,1)}, bf16[1024,512]{1,0:T(8,128)(2,1)}, u32[]{:S(2)}, u32[]{:S(2)}) collective-permute-start(bf16[1024,512]{1,0:T(8,128)(2,1)} %slice.207), channel_id=1, source_target_pairs={{0,4},{4,0},{1,5},{5,1},{2,6},{6,2},{3,7},{7,3},{8,12},{12,8},{9,1... | collective-permute-start | bytes 3145736 | tf_op jit(solution)/shard_map/ppermute | solution.py:822
  77.6 45.6 %collective-permute-start.6 = (bf16[1024,512]{1,0:T(8,128)(2,1)S(1)}, bf16[1024,512]{1,0:T(8,128)(2,1)S(1)}, u32[]{:S(2)}, u32[]{:S(2)}) collective-permute-start(bf16[1024,512]{1,0:T(8,128)(2,1)S(1)} %collective-permute-done.3.refs_3_), channel_id=1, source_target_pairs={{2,3},{6,7},{10,11},{14,15},{18,19},{22,23},{26,27},{30,31}} | collective-permute-start | bytes 3145736 | tf_op jit(solution)/shard_map/ppermute | solution.py:637
  78.3 45.9 %collective-permute-start.7 = (bf16[1024,512]{1,0:T(8,128)(2,1)S(1)}, bf16[1024,512]{1,0:T(8,128)(2,1)}, u32[]{:S(2)}, u32[]{:S(2)}) collective-permute-start(bf16[1024,512]{1,0:T(8,128)(2,1)S(1)} %collective-permute-done.4.refs_2_), channel_id=1, source_target_pairs={{1,0},{5,4},{9,8},{13,12},{17,16},{21,20},{25,24},{29,28}} | collective-permute-start | bytes 3145736 | tf_op jit(solution)/shard_map/ppermute | solution.py:638
  124.3 176.6 %all-gather.7.cloned.1.call-start = ((), (), s32[]{:S(2)}) async-start(), calls=%async_computation.13 | async-start | bytes 5242880 | tf_op jit(solution)/shard_map/all_gather | solution.py:853
  135.1 43.2 %collective-permute-start.8 = (bf16[4,1024,512]{2,1,0:T(8,128)(2,1)}, bf16[4,1024,512]{2,1,0:T(8,128)(2,1)}, u32[]{:S(2)}, u32[]{:S(2)}) collective-permute-start(bf16[4,1024,512]{2,1,0:T(8,128)(2,1)} %arrange.3.refs_0_), channel_id=1, source_target_pairs={{0,8},{8,0},{16,24},{24,16},{1,9},{9,1},{17,25},{25,17},{2,10},{10... | collective-permute-start | bytes 12582920 | tf_op jit(solution)/shard_map/ppermute | solution.py:831
  178.3 25.9 %collective-permute-start.9 = (bf16[1024,512]{1,0:T(8,128)(2,1)}, bf16[1024,512]{1,0:T(8,128)(2,1)}, u32[]{:S(2)}, u32[]{:S(2)}) collective-permute-start(bf16[1024,512]{1,0:T(8,128)(2,1)} %get-tuple-element.231.refs_2_), channel_id=1, source_target_pairs={{0,4},{4,0},{1,5},{5,1},{2,6},{6,2},{3,7},{7,3},{8,12},{12,8},{9,1... | collective-permute-start | bytes 3145736 | tf_op jit(solution)/shard_map/ppermute | solution.py:841
  204.2 207.2 %reduce-scatter.7.cloned.1.call-start = ((), (), s32[]{:S(2)}) async-start(), calls=%async_computation.6 | async-start | bytes 5242880 | tf_op jit(solution)/shard_map/reduce_scatter | solution.py:890
  214.6 65.2 %collective-permute-start.10 = (bf16[512,512]{1,0:T(8,128)(2,1)S(1)}, bf16[512,512]{1,0:T(8,128)(2,1)S(1)}, u32[]{:S(2)}, u32[]{:S(2)}) collective-permute-start(bf16[512,512]{1,0:T(8,128)(2,1)S(1)} %constant_dynamic-slice_fusion.42.refs_6_), channel_id=1, source_target_pairs={{0,1},{1,2},{2,3},{4,5},{5,6},{6,7},{8,9},{9,10},{10,11},{12,13},{... | collective-permute-start | bytes 1572872 | tf_op jit(solution)/shard_map/ppermute | solution.py:637
  216.0 63.9 %collective-permute-start.11 = (bf16[512,512]{1,0:T(8,128)(2,1)S(1)}, bf16[512,512]{1,0:T(8,128)(2,1)S(1)}, u32[]{:S(2)}, u32[]{:S(2)}) collective-permute-start(bf16[512,512]{1,0:T(8,128)(2,1)S(1)} %constant_dynamic-slice_fusion.42.refs_6_), channel_id=1, source_target_pairs={{1,0},{2,1},{3,2},{5,4},{6,5},{7,6},{9,8},{10,9},{11,10},{13,12},{... | collective-permute-start | bytes 1572872 | tf_op jit(solution)/shard_map/ppermute | solution.py:638
  300.9 192.2 %reduce-scatter.9.cloned.1.call-start = ((), (), s32[]{:S(2)}) async-start(), calls=%async_computation.7 | async-start | bytes 5242880 | tf_op jit(solution)/shard_map/reduce_scatter | solution.py:890
  307.4 65.6 %collective-permute-start.12 = (bf16[512,512]{1,0:T(8,128)(2,1)S(1)}, bf16[512,512]{1,0:T(8,128)(2,1)S(1)}, u32[]{:S(2)}, u32[]{:S(2)}) collective-permute-start(bf16[512,512]{1,0:T(8,128)(2,1)S(1)} %collective-permute-done.10.refs_5_), channel_id=1, source_target_pairs={{1,2},{2,3},{5,6},{6,7},{9,10},{10,11},{13,14},{14,15},{17,18},{18... | collective-permute-start | bytes 1572872 | tf_op jit(solution)/shard_map/ppermute | solution.py:637
  308.1 64.9 %collective-permute-start.13 = (bf16[512,512]{1,0:T(8,128)(2,1)S(1)}, bf16[512,512]{1,0:T(8,128)(2,1)}, u32[]{:S(2)}, u32[]{:S(2)}) collective-permute-start(bf16[512,512]{1,0:T(8,128)(2,1)S(1)} %collective-permute-done.11.refs_4_), channel_id=1, source_target_pairs={{1,0},{2,1},{5,4},{6,5},{9,8},{10,9},{13,12},{14,13},{17,16},{18,1... | collective-permute-start | bytes 1572872 | tf_op jit(solution)/shard_map/ppermute | solution.py:638
  373.0 38.3 %collective-permute-start.14 = (bf16[512,512]{1,0:T(8,128)(2,1)S(1)}, bf16[512,512]{1,0:T(8,128)(2,1)S(1)}, u32[]{:S(2)}, u32[]{:S(2)}) collective-permute-start(bf16[512,512]{1,0:T(8,128)(2,1)S(1)} %collective-permute-done.12.refs_3_), channel_id=1, source_target_pairs={{2,3},{6,7},{10,11},{14,15},{18,19},{22,23},{26,27},{30,31}} | collective-permute-start | bytes 1572872 | tf_op jit(solution)/shard_map/ppermute | solution.py:637
  373.7 37.6 %collective-permute-start.15 = (bf16[512,512]{1,0:T(8,128)(2,1)}, bf16[512,512]{1,0:T(8,128)(2,1)S(1)}, u32[]{:S(2)}, u32[]{:S(2)}) collective-permute-start(bf16[512,512]{1,0:T(8,128)(2,1)} %collective-permute-done.13.refs_2_), channel_id=1, source_target_pairs={{1,0},{5,4},{9,8},{13,12},{17,16},{21,20},{25,24},{29,28}} | collective-permute-start | bytes 1572872 | tf_op jit(solution)/shard_map/ppermute | solution.py:638
  375.0 218.6 %reduce-scatter.11.cloned.1.call-start = ((), (), s32[]{:S(2)}) async-start(), calls=%async_computation.8 | async-start | bytes 5242880 | tf_op jit(solution)/shard_map/reduce_scatter | solution.py:890
  414.2 514.0 %reduce-scatter.13.cloned.1.call-start = ((), (), s32[]{:S(2)}) async-start(), calls=%async_computation.9 | async-start | bytes 5242880 | tf_op jit(solution)/shard_map/reduce_scatter | solution.py:890
  427.4 47.7 %collective-permute-start.19 = (bf16[4,512,512]{2,1,0:T(8,128)(2,1)S(1)}, bf16[4,512,512]{2,1,0:T(8,128)(2,1)}, u32[]{:S(2)}, u32[]{:S(2)}) collective-permute-start(bf16[4,512,512]{2,1,0:T(8,128)(2,1)S(1)} %arrange.5.refs_0_), channel_id=1, source_target_pairs={{0,4},{4,0},{1,5},{5,1},{2,6},{6,2},{3,7},{7,3},{8,12},{12,8},{9,1... | collective-permute-start | bytes 6291464 | tf_op jit(solution)/shard_map/ppermute | solution.py:929
  430.6 31.2 %collective-permute-start.16 = (bf16[256,512]{1,0:T(8,128)(2,1)}, bf16[256,512]{1,0:T(8,128)(2,1)}, u32[]{:S(2)}, u32[]{:S(2)}) collective-permute-start(bf16[256,512]{1,0:T(8,128)(2,1)} %bitcast.25), channel_id=1, source_target_pairs={{0,1},{1,2},{2,3},{3,0},{4,5},{5,6},{6,7},{7,4},{8,9},{9,10},{10,1... | collective-permute-start | bytes 786440 | tf_op jit(solution)/shard_map/ppermute | solution.py:700
  434.7 33.7 %collective-permute-start.17 = (bf16[256,512]{1,0:T(8,128)(2,1)}, bf16[256,512]{1,0:T(8,128)(2,1)}, u32[]{:S(2)}, u32[]{:S(2)}) collective-permute-start(bf16[256,512]{1,0:T(8,128)(2,1)} %bitcast.26), channel_id=1, source_target_pairs={{0,2},{1,3},{2,0},{3,1},{4,6},{5,7},{6,4},{7,5},{8,10},{9,11},{10,... | collective-permute-start | bytes 786440 | tf_op jit(solution)/shard_map/ppermute | solution.py:700
  437.7 31.0 %collective-permute-start.18 = (bf16[256,512]{1,0:T(8,128)(2,1)}, bf16[256,512]{1,0:T(8,128)(2,1)}, u32[]{:S(2)}, u32[]{:S(2)}) collective-permute-start(bf16[256,512]{1,0:T(8,128)(2,1)} %bitcast.173), channel_id=1, source_target_pairs={{0,3},{1,0},{2,1},{3,2},{4,7},{5,4},{6,5},{7,6},{8,11},{9,8},{10,9... | collective-permute-start | bytes 786440 | tf_op jit(solution)/shard_map/ppermute | solution.py:700
  475.2 17.9 %collective-permute-start.20 = (bf16[4,512,512]{2,1,0:T(8,128)(2,1)S(1)}, bf16[4,512,512]{2,1,0:T(8,128)(2,1)}, u32[]{:S(2)}, u32[]{:S(2)}) collective-permute-start(bf16[4,512,512]{2,1,0:T(8,128)(2,1)S(1)} %arrange.5.refs_0_), channel_id=1, source_target_pairs={{0,8},{8,0},{16,24},{24,16},{1,9},{9,1},{17,25},{25,17},{2,10},{10... | collective-permute-start | bytes 6291464 | tf_op jit(solution)/shard_map/ppermute | solution.py:937
  475.2 17.9 %collective-permute-start.21 = (bf16[4,512,512]{2,1,0:T(8,128)(2,1)}, bf16[4,512,512]{2,1,0:T(8,128)(2,1)}, u32[]{:S(2)}, u32[]{:S(2)}) collective-permute-start(bf16[4,512,512]{2,1,0:T(8,128)(2,1)} %collective-permute-done.19.refs_1_), channel_id=1, source_target_pairs={{0,8},{8,0},{16,24},{24,16},{1,9},{9,1},{17,25},{25,17},{2,10},{10... | collective-permute-start | bytes 6291464 | tf_op jit(solution)/shard_map/ppermute | solution.py:937
  506.3 86.9 %collective-permute-start.22 = (bf16[256,512]{1,0:T(8,128)(2,1)}, bf16[256,512]{1,0:T(8,128)(2,1)S(1)}, u32[]{:S(2)}, u32[]{:S(2)}) collective-permute-start(bf16[256,512]{1,0:T(8,128)(2,1)} %bitcast.169), channel_id=1, source_target_pairs={{0,4},{1,5},{2,6},{3,7},{4,0},{5,1},{6,2},{7,3},{8,12},{9,13},{10,... | collective-permute-start | bytes 786440 | tf_op jit(solution)/shard_map/ppermute | solution.py:690
  508.6 84.6 %collective-permute-start.23 = (bf16[256,512]{1,0:T(8,128)(2,1)}, bf16[256,512]{1,0:T(8,128)(2,1)S(1)}, u32[]{:S(2)}, u32[]{:S(2)}) collective-permute-start(bf16[256,512]{1,0:T(8,128)(2,1)} %bitcast.170), channel_id=1, source_target_pairs={{0,5},{1,6},{2,7},{3,4},{4,1},{5,2},{6,3},{7,0},{8,13},{9,14},{10,... | collective-permute-start | bytes 786440 | tf_op jit(solution)/shard_map/ppermute | solution.py:690
  517.3 75.9 %collective-permute-start.24 = (bf16[256,512]{1,0:T(8,128)(2,1)}, bf16[256,512]{1,0:T(8,128)(2,1)S(1)}, u32[]{:S(2)}, u32[]{:S(2)}) collective-permute-start(bf16[256,512]{1,0:T(8,128)(2,1)} %bitcast.171), channel_id=1, source_target_pairs={{0,6},{1,7},{2,4},{3,5},{4,2},{5,3},{6,0},{7,1},{8,14},{9,15},{10,... | collective-permute-start | bytes 786440 | tf_op jit(solution)/shard_map/ppermute | solution.py:690
  518.2 75.1 %collective-permute-start.25 = (bf16[256,512]{1,0:T(8,128)(2,1)}, bf16[256,512]{1,0:T(8,128)(2,1)S(1)}, u32[]{:S(2)}, u32[]{:S(2)}) collective-permute-start(bf16[256,512]{1,0:T(8,128)(2,1)} %bitcast.172), channel_id=1, source_target_pairs={{0,7},{1,4},{2,5},{3,6},{4,3},{5,0},{6,1},{7,2},{8,15},{9,12},{10,... | collective-permute-start | bytes 786440 | tf_op jit(solution)/shard_map/ppermute | solution.py:690
  537.2 535.5 %reduce-scatter.17.cloned.1.call-start = ((), (), s32[]{:S(2)}) async-start(), calls=%async_computation.11 | async-start | bytes 12976128 | tf_op jit(solution)/shard_map/reduce_scatter | solution.py:893
  600.0 110.1 %collective-permute-start.29 = (bf16[256,2048]{1,0:T(8,128)(2,1)S(1)}, bf16[256,2048]{1,0:T(8,128)(2,1)}, u32[]{:S(2)}, u32[]{:S(2)}) collective-permute-start(bf16[256,2048]{1,0:T(8,128)(2,1)S(1)} %get-tuple-element.396), channel_id=1, source_target_pairs={{0,1},{1,2},{2,3},{4,5},{5,6},{6,7},{8,9},{9,10},{10,11},{12,13},{... | collective-permute-start | bytes 3145736 | tf_op jit(solution)/shard_map/ppermute | solution.py:637
  609.6 100.6 %collective-permute-start.30 = (bf16[256,2048]{1,0:T(8,128)(2,1)S(1)}, bf16[256,2048]{1,0:T(8,128)(2,1)}, u32[]{:S(2)}, u32[]{:S(2)}) collective-permute-start(bf16[256,2048]{1,0:T(8,128)(2,1)S(1)} %get-tuple-element.396), channel_id=1, source_target_pairs={{1,0},{2,1},{3,2},{5,4},{6,5},{7,6},{9,8},{10,9},{11,10},{13,12},{... | collective-permute-start | bytes 3145736 | tf_op jit(solution)/shard_map/ppermute | solution.py:638
  611.8 69.0 %collective-permute-start.26 = (bf16[256,512]{1,0:T(8,128)(2,1)}, bf16[256,512]{1,0:T(8,128)(2,1)}, u32[]{:S(2)}, u32[]{:S(2)}) collective-permute-start(bf16[256,512]{1,0:T(8,128)(2,1)} %get-tuple-element.439), channel_id=1, source_target_pairs={{0,1},{1,2},{2,3},{3,0},{4,5},{5,6},{6,7},{7,4},{8,9},{9,10},{10,1... | collective-permute-start | bytes 786440 | tf_op jit(solution)/shard_map/ppermute | solution.py:700
  614.4 95.2 %collective-permute-start.27 = (bf16[256,512]{1,0:T(8,128)(2,1)S(1)}, bf16[256,512]{1,0:T(8,128)(2,1)}, u32[]{:S(2)}, u32[]{:S(2)}) collective-permute-start(bf16[256,512]{1,0:T(8,128)(2,1)S(1)} %get-tuple-element.438), channel_id=1, source_target_pairs={{0,2},{1,3},{2,0},{3,1},{4,6},{5,7},{6,4},{7,5},{8,10},{9,11},{10,... | collective-permute-start | bytes 786440 | tf_op jit(solution)/shard_map/ppermute | solution.py:700
  614.4 95.7 %collective-permute-start.28 = (bf16[256,512]{1,0:T(8,128)(2,1)S(1)}, bf16[256,512]{1,0:T(8,128)(2,1)}, u32[]{:S(2)}, u32[]{:S(2)}) collective-permute-start(bf16[256,512]{1,0:T(8,128)(2,1)S(1)} %get-tuple-element.437), channel_id=1, source_target_pairs={{0,3},{1,0},{2,1},{3,2},{4,7},{5,4},{6,5},{7,6},{8,11},{9,8},{10,9... | collective-permute-start | bytes 786440 | tf_op jit(solution)/shard_map/ppermute | solution.py:700
  721.0 66.5 %collective-permute-start.37 = (bf16[256,768]{1,0:T(8,128)(2,1)S(1)}, bf16[256,768]{1,0:T(8,128)(2,1)S(1)}, u32[]{:S(2)}, u32[]{:S(2)}) collective-permute-start(bf16[256,768]{1,0:T(8,128)(2,1)S(1)} %pad_maximum_fusion.18), channel_id=1, source_target_pairs={{0,7},{1,4},{2,5},{3,6},{4,3},{5,0},{6,1},{7,2},{8,15},{9,12},{10,... | collective-permute-start | bytes 1179656 | tf_op jit(solution)/shard_map/ppermute | solution.py:690
  735.1 52.4 %collective-permute-start.36 = (bf16[256,768]{1,0:T(8,128)(2,1)S(1)}, bf16[256,768]{1,0:T(8,128)(2,1)S(1)}, u32[]{:S(2)}, u32[]{:S(2)}) collective-permute-start(bf16[256,768]{1,0:T(8,128)(2,1)S(1)} %pad_maximum_fusion.17), channel_id=1, source_target_pairs={{0,6},{1,7},{2,4},{3,5},{4,2},{5,3},{6,0},{7,1},{8,14},{9,15},{10,... | collective-permute-start | bytes 1179656 | tf_op jit(solution)/shard_map/ppermute | solution.py:690
  735.8 51.7 %collective-permute-start.35 = (bf16[256,768]{1,0:T(8,128)(2,1)S(1)}, bf16[256,768]{1,0:T(8,128)(2,1)S(1)}, u32[]{:S(2)}, u32[]{:S(2)}) collective-permute-start(bf16[256,768]{1,0:T(8,128)(2,1)S(1)} %pad_maximum_fusion.16), channel_id=1, source_target_pairs={{0,5},{1,6},{2,7},{3,4},{4,1},{5,2},{6,3},{7,0},{8,13},{9,14},{10,... | collective-permute-start | bytes 1179656 | tf_op jit(solution)/shard_map/ppermute | solution.py:690
  736.8 27.7 %collective-permute-start.33 = (bf16[256,256]{1,0:T(8,128)(2,1)S(1)}, bf16[256,256]{1,0:T(8,128)(2,1)S(1)}, u32[]{:S(2)}, u32[]{:S(2)}) collective-permute-start(bf16[256,256]{1,0:T(8,128)(2,1)S(1)} %pad_maximum_fusion.22), channel_id=1, source_target_pairs={{0,3},{1,0},{2,1},{3,2},{4,7},{5,4},{6,5},{7,6},{8,11},{9,8},{10,9... | collective-permute-start | bytes 393224 | tf_op jit(solution)/shard_map/ppermute | solution.py:700
  741.2 37.0 %collective-permute-start.32 = (bf16[256,256]{1,0:T(8,128)(2,1)S(1)}, bf16[256,256]{1,0:T(8,128)(2,1)S(1)}, u32[]{:S(2)}, u32[]{:S(2)}) collective-permute-start(bf16[256,256]{1,0:T(8,128)(2,1)S(1)} %pad_maximum_fusion.21), channel_id=1, source_target_pairs={{0,2},{1,3},{2,0},{3,1},{4,6},{5,7},{6,4},{7,5},{8,10},{9,11},{10,... | collective-permute-start | bytes 393224 | tf_op jit(solution)/shard_map/ppermute | solution.py:700
  764.5 23.1 %collective-permute-start.34 = (bf16[256,768]{1,0:T(8,128)(2,1)S(1)}, bf16[256,768]{1,0:T(8,128)(2,1)S(1)}, u32[]{:S(2)}, u32[]{:S(2)}) collective-permute-start(bf16[256,768]{1,0:T(8,128)(2,1)S(1)} %pad_maximum_fusion.15), channel_id=1, source_target_pairs={{0,4},{1,5},{2,6},{3,7},{4,0},{5,1},{6,2},{7,3},{8,12},{9,13},{10,... | collective-permute-start | bytes 1179656 | tf_op jit(solution)/shard_map/ppermute | solution.py:690
  785.9 16.8 %collective-permute-start.38 = (bf16[256,2048]{1,0:T(8,128)(2,1)}, bf16[256,2048]{1,0:T(8,128)(2,1)}, u32[]{:S(2)}, u32[]{:S(2)}) collective-permute-start(bf16[256,2048]{1,0:T(8,128)(2,1)} %collective-permute-done.29), channel_id=1, source_target_pairs={{1,2},{2,3},{5,6},{6,7},{9,10},{10,11},{13,14},{14,15},{17,18},{18... | collective-permute-start | bytes 3145736 | tf_op jit(solution)/shard_map/ppermute | solution.py:637
  787.9 28.9 %collective-permute-start.39 = (bf16[256,2048]{1,0:T(8,128)(2,1)}, bf16[256,2048]{1,0:T(8,128)(2,1)}, u32[]{:S(2)}, u32[]{:S(2)}) collective-permute-start(bf16[256,2048]{1,0:T(8,128)(2,1)} %collective-permute-done.30), channel_id=1, source_target_pairs={{1,0},{2,1},{5,4},{6,5},{9,8},{10,9},{13,12},{14,13},{17,16},{18,1... | collective-permute-start | bytes 3145736 | tf_op jit(solution)/shard_map/ppermute | solution.py:638
  816.8 259.0 %reduce-scatter.15.cloned.1.call-start = ((), (), s32[]{:S(2)}) async-start(), calls=%async_computation.10 | async-start | bytes 19464192 | tf_op jit(solution)/shard_map/reduce_scatter | solution.py:893
  827.8 54.3 %collective-permute-start.44 = (bf16[1024,768]{1,0:T(8,128)(2,1)}, bf16[1024,768]{1,0:T(8,128)(2,1)}, u32[]{:S(2)}, u32[]{:S(2)}) collective-permute-start(bf16[1024,768]{1,0:T(8,128)(2,1)} %pad_maximum_fusion.1), channel_id=1, source_target_pairs={{0,4},{4,0},{1,5},{5,1},{2,6},{6,2},{3,7},{7,3},{8,12},{12,8},{9,1... | collective-permute-start | bytes 4718600 | tf_op jit(solution)/shard_map/ppermute | solution.py:1042
  832.9 76.0 %collective-permute-start.40 = (bf16[512,2048]{1,0:T(8,128)(2,1)S(1)}, bf16[512,2048]{1,0:T(8,128)(2,1)}, u32[]{:S(2)}, u32[]{:S(2)}) collective-permute-start(bf16[512,2048]{1,0:T(8,128)(2,1)S(1)} %fusion.6), channel_id=1, source_target_pairs={{0,1},{1,2},{2,3},{4,5},{5,6},{6,7},{8,9},{9,10},{10,11},{12,13},{... | collective-permute-start | bytes 6291464 | tf_op jit(solution)/shard_map/ppermute | solution.py:637
  839.5 69.4 %collective-permute-start.41 = (bf16[512,2048]{1,0:T(8,128)(2,1)S(1)}, bf16[512,2048]{1,0:T(8,128)(2,1)}, u32[]{:S(2)}, u32[]{:S(2)}) collective-permute-start(bf16[512,2048]{1,0:T(8,128)(2,1)S(1)} %fusion.6), channel_id=1, source_target_pairs={{1,0},{2,1},{3,2},{5,4},{6,5},{7,6},{9,8},{10,9},{11,10},{13,12},{... | collective-permute-start | bytes 6291464 | tf_op jit(solution)/shard_map/ppermute | solution.py:638
  841.8 59.7 %collective-permute-start.42 = (bf16[256,2048]{1,0:T(8,128)(2,1)}, bf16[256,2048]{1,0:T(8,128)(2,1)}, u32[]{:S(2)}, u32[]{:S(2)}) collective-permute-start(bf16[256,2048]{1,0:T(8,128)(2,1)} %collective-permute-done.38), channel_id=1, source_target_pairs={{2,3},{6,7},{10,11},{14,15},{18,19},{22,23},{26,27},{30,31}} | collective-permute-start | bytes 3145736 | tf_op jit(solution)/shard_map/ppermute | solution.py:637
  843.4 65.5 %collective-permute-start.43 = (bf16[256,2048]{1,0:T(8,128)(2,1)}, bf16[256,2048]{1,0:T(8,128)(2,1)}, u32[]{:S(2)}, u32[]{:S(2)}) collective-permute-start(bf16[256,2048]{1,0:T(8,128)(2,1)} %collective-permute-done.39), channel_id=1, source_target_pairs={{1,0},{5,4},{9,8},{13,12},{17,16},{21,20},{25,24},{29,28}} | collective-permute-start | bytes 3145736 | tf_op jit(solution)/shard_map/ppermute | solution.py:638
  924.9 70.6 %collective-permute-start.45 = (bf16[512,2048]{1,0:T(8,128)(2,1)}, bf16[512,2048]{1,0:T(8,128)(2,1)}, u32[]{:S(2)}, u32[]{:S(2)}) collective-permute-start(bf16[512,2048]{1,0:T(8,128)(2,1)} %collective-permute-done.40), channel_id=1, source_target_pairs={{1,2},{2,3},{5,6},{6,7},{9,10},{10,11},{13,14},{14,15},{17,18},{18... | collective-permute-start | bytes 6291464 | tf_op jit(solution)/shard_map/ppermute | solution.py:637
  926.9 68.6 %collective-permute-start.46 = (bf16[512,2048]{1,0:T(8,128)(2,1)}, bf16[512,2048]{1,0:T(8,128)(2,1)}, u32[]{:S(2)}, u32[]{:S(2)}) collective-permute-start(bf16[512,2048]{1,0:T(8,128)(2,1)} %collective-permute-done.41), channel_id=1, source_target_pairs={{1,0},{2,1},{5,4},{6,5},{9,8},{10,9},{13,12},{14,13},{17,16},{18,1... | collective-permute-start | bytes 6291464 | tf_op jit(solution)/shard_map/ppermute | solution.py:638
  936.0 22.2 %collective-permute-start.47 = (bf16[256,2048]{1,0:T(8,128)(2,1)S(1)}, bf16[256,2048]{1,0:T(8,128)(2,1)S(1)}, u32[]{:S(2)}, u32[]{:S(2)}) collective-permute-start(bf16[256,2048]{1,0:T(8,128)(2,1)S(1)} %get-tuple-element.394), channel_id=1, source_target_pairs={{0,1},{1,2},{2,3},{4,5},{5,6},{6,7},{8,9},{9,10},{10,11},{12,13},{... | collective-permute-start | bytes 3145736 | tf_op jit(solution)/shard_map/ppermute | solution.py:637
  940.3 55.2 %collective-permute-start.48 = (bf16[256,2048]{1,0:T(8,128)(2,1)S(1)}, bf16[256,2048]{1,0:T(8,128)(2,1)S(1)}, u32[]{:S(2)}, u32[]{:S(2)}) collective-permute-start(bf16[256,2048]{1,0:T(8,128)(2,1)S(1)} %get-tuple-element.394), channel_id=1, source_target_pairs={{1,0},{2,1},{3,2},{5,4},{6,5},{7,6},{9,8},{10,9},{11,10},{13,12},{... | collective-permute-start | bytes 3145736 | tf_op jit(solution)/shard_map/ppermute | solution.py:638
  995.5 68.7 %collective-permute-start.49 = (bf16[512,2048]{1,0:T(8,128)(2,1)}, bf16[512,2048]{1,0:T(8,128)(2,1)S(1)}, u32[]{:S(2)}, u32[]{:S(2)}) collective-permute-start(bf16[512,2048]{1,0:T(8,128)(2,1)} %collective-permute-done.45), channel_id=1, source_target_pairs={{2,3},{6,7},{10,11},{14,15},{18,19},{22,23},{26,27},{30,31}} | collective-permute-start | bytes 6291464 | tf_op jit(solution)/shard_map/ppermute | solution.py:637
  996.3 67.9 %collective-permute-start.50 = (bf16[512,2048]{1,0:T(8,128)(2,1)}, bf16[512,2048]{1,0:T(8,128)(2,1)S(1)}, u32[]{:S(2)}, u32[]{:S(2)}) collective-permute-start(bf16[512,2048]{1,0:T(8,128)(2,1)} %collective-permute-done.46), channel_id=1, source_target_pairs={{1,0},{5,4},{9,8},{13,12},{17,16},{21,20},{25,24},{29,28}} | collective-permute-start | bytes 6291464 | tf_op jit(solution)/shard_map/ppermute | solution.py:638
  1001.1 63.1 %collective-permute-start.52 = (bf16[256,2048]{1,0:T(8,128)(2,1)S(1)}, bf16[256,2048]{1,0:T(8,128)(2,1)}, u32[]{:S(2)}, u32[]{:S(2)}) collective-permute-start(bf16[256,2048]{1,0:T(8,128)(2,1)S(1)} %collective-permute-done.48), channel_id=1, source_target_pairs={{1,0},{2,1},{5,4},{6,5},{9,8},{10,9},{13,12},{14,13},{17,16},{18,1... | collective-permute-start | bytes 3145736 | tf_op jit(solution)/shard_map/ppermute | solution.py:638
  1064.2 21.3 %collective-permute-start.53 = (bf16[256,2048]{1,0:T(8,128)(2,1)}, bf16[256,2048]{1,0:T(8,128)(2,1)}, u32[]{:S(2)}, u32[]{:S(2)}) collective-permute-start(bf16[256,2048]{1,0:T(8,128)(2,1)} %collective-permute-done.51), channel_id=1, source_target_pairs={{2,3},{6,7},{10,11},{14,15},{18,19},{22,23},{26,27},{30,31}} | collective-permute-start | bytes 3145736 | tf_op jit(solution)/shard_map/ppermute | solution.py:637
  1065.8 43.1 %collective-permute-start.54 = (bf16[256,2048]{1,0:T(8,128)(2,1)}, bf16[256,2048]{1,0:T(8,128)(2,1)}, u32[]{:S(2)}, u32[]{:S(2)}) collective-permute-start(bf16[256,2048]{1,0:T(8,128)(2,1)} %collective-permute-done.52), channel_id=1, source_target_pairs={{1,0},{5,4},{9,8},{13,12},{17,16},{21,20},{25,24},{29,28}} | collective-permute-start | bytes 3145736 | tf_op jit(solution)/shard_map/ppermute | solution.py:638
  1077.3 31.6 %collective-permute-start.55 = (bf16[256,768]{1,0:T(8,128)(2,1)S(1)}, bf16[256,768]{1,0:T(8,128)(2,1)S(1)}, u32[]{:S(2)}, u32[]{:S(2)}) collective-permute-start(bf16[256,768]{1,0:T(8,128)(2,1)S(1)} %get-tuple-element.478), channel_id=1, source_target_pairs={{0,1},{1,2},{2,3},{3,0},{4,5},{5,6},{6,7},{7,4},{8,9},{9,10},{10,1... | collective-permute-start | bytes 1179656 | tf_op jit(solution)/shard_map/ppermute | solution.py:700
  1081.0 27.9 %collective-permute-start.56 = (bf16[256,768]{1,0:T(8,128)(2,1)S(1)}, bf16[256,768]{1,0:T(8,128)(2,1)S(1)}, u32[]{:S(2)}, u32[]{:S(2)}) collective-permute-start(bf16[256,768]{1,0:T(8,128)(2,1)S(1)} %get-tuple-element.479), channel_id=1, source_target_pairs={{0,2},{1,3},{2,0},{3,1},{4,6},{5,7},{6,4},{7,5},{8,10},{9,11},{10,... | collective-permute-start | bytes 1179656 | tf_op jit(solution)/shard_map/ppermute | solution.py:700
  1081.0 32.0 %collective-permute-start.57 = (bf16[256,768]{1,0:T(8,128)(2,1)S(1)}, bf16[256,768]{1,0:T(8,128)(2,1)S(1)}, u32[]{:S(2)}, u32[]{:S(2)}) collective-permute-start(bf16[256,768]{1,0:T(8,128)(2,1)S(1)} %get-tuple-element.477), channel_id=1, source_target_pairs={{0,3},{1,0},{2,1},{3,2},{4,7},{5,4},{6,5},{7,6},{8,11},{9,8},{10,9... | collective-permute-start | bytes 1179656 | tf_op jit(solution)/shard_map/ppermute | solution.py:700
  (83 other events, 801.9 us)
Sparse Core Ops, SparseCore 0:
  124.4 89.1 all-gather.4
  215.1 85.7 all-gather.6
  303.2 94.0 reduce-scatter.6
  399.5 93.5 reduce-scatter.8
  495.2 98.2 reduce-scatter.10
  595.8 120.7 reduce-scatter.12
  817.0 100.8 reduce-scatter.16
  921.4 118.5 reduce-scatter.14

commit v7 on v6

--- a/solution.py
+++ b/solution.py
@@ -917,7 +917,7 @@
     w_gates, hop, share_first = hold(w_gates, hop, share_first)
     query_gather.held(hop)
 
-    mixed_first = line_sum(after(down_first, w_gates))
+    mixed_shares = [line_sum(after(down, w_gates)) for down in (down_first, down_second)]
 
     gain_first, middle_first, low_first, blocks = to_attention(0, middle, share_first)
     query_part = query_gather.whole()
@@ -944,7 +944,6 @@
     gain_second, middle_second, low_second, blocks = hold(
         gain_second, middle_second, low_second, blocks
     )
-    mixed_second = line_sum(after(down_second, blocks))
 
     def back_arguments(c, grads):
         return metas[c], offsets[c], queries[c], attention[c], grads, log_totals[c], forms, *tables[c]
@@ -958,12 +957,7 @@
     dq_second, kv_near, kv_far = attend_back_last(
         *back_arguments(1, grads_second), dk, dv, cos_pair, sin_pair
     )
-    mixed_gathers = [Gather((middle_own[0] + mixed_first.astype(F32)).astype(BF16)), None]
-    mixed_hop = mixed_gathers[0].step()
-    dq_second, kv_near, kv_far, rows_first, mixed_hop = hold(
-        dq_second, kv_near, kv_far, rows_first, mixed_hop
-    )
-    mixed_gathers[0].held(mixed_hop)
+    dq_second, kv_near, kv_far, rows_first = hold(dq_second, kv_near, kv_far, rows_first)
 
     def kv_share_of(array, j):
         return [lax.dynamic_slice_in_dim(array, row_of[c][j], share, 0) for c in chunks]
@@ -986,7 +980,6 @@
     attention_rows = jnp.swapaxes(attention_rows, 0, 1).reshape(2 * share, groups * features)
     w_outs = t_dot(jnp.concatenate([low_first, low_second], axis=0), attention_rows).astype(BF16)
     near_blocks, far_blocks, first_part, w_outs = hold(near_blocks, far_blocks, first_part, w_outs)
-    mixed_hop = mixed_gathers[0].step()
     far_blocks = stack_blocks(far_blocks)
     kv_blocks = (
         stack_blocks(near_blocks).astype(F32) + far_blocks[:, :, features:].astype(F32)
@@ -1023,22 +1016,18 @@
         return target
 
     gains = jnp.stack([attn_gain, gain_first + gain_second], axis=1).astype(BF16)
-    grad_inputs, gains, dq_second, kv_far, kv_near, w_gates, mixed_hop = hold(
-        grad_inputs, gains, dq_second, kv_far, kv_near, w_gates, mixed_hop
-    )
-    mixed_gathers[0].held(mixed_hop)
+    grad_inputs, gains, dq_second, kv_far, kv_near, w_gates = hold(
+        grad_inputs, gains, dq_second, kv_far, kv_near, w_gates
+    )
     gate_up_grad = plane_sum(w_gates)
 
-    def put_chunk(c):
-        def put(target, piece, source):
-            return lax.dynamic_update_slice_in_dim(target, piece, row_of[c][source], 0)
-
-        return put
-
-    tokens_gather = Gather(grad_inputs)
+    mixed_share = jnp.concatenate(
+        [(middle_own[c] + mixed_shares[c].astype(F32)).astype(BF16) for c in chunks], axis=0
+    )
+    tokens_gather, mixed_gather = Gather(grad_inputs), Gather(mixed_share)
     tokens_grad = jnp.zeros((tok_rows, width), BF16)
     mixed = jnp.zeros((tok_rows, width), BF16)
-    hop, mixed_hop = tokens_gather.step(), mixed_gathers[0].step()
+    hop, mixed_hop = tokens_gather.step(), mixed_gather.step()
     home = lax.ppermute(
         jnp.concatenate([dq_second, kv_far[:span], kv_far[span:]], axis=1), "ctx", over
     )
@@ -1050,37 +1039,28 @@
     ).astype(BF16)
     gains = jnp.pad(gains, ((0, 0), (0, 126)))
     rest = jnp.concatenate([w_downs, w_outs, query_kv, gains], axis=1)
-    for count in range(3):
-        mixed = mixed_gathers[0].place_hop(put_chunk(0), mixed, count)
-    hop, mixed_hop, rest, mixed = hold(hop, mixed_hop, rest, mixed)
+    hop, mixed_hop, rest = hold(hop, mixed_hop, rest)
     tokens_gather.held(hop)
-    mixed_gathers[0].held(mixed_hop)
+    mixed_gather.held(mixed_hop)
     rest = plane_sum(rest)
 
-    mixed_gathers[1] = Gather((middle_own[1] + after(mixed_second, hop).astype(F32)).astype(BF16))
-    hop, mixed_hop = tokens_gather.step(), mixed_gathers[1].step()
-    for count in range(3, groups):
-        mixed = mixed_gathers[0].place_hop(put_chunk(0), mixed, count)
-        if count + 1 < groups:
-            mixed_gathers[0].step()
-    tokens_grad = tokens_gather.place_hop(put_rows, tokens_grad, 0)
-    tokens_grad = tokens_gather.place_hop(put_rows, tokens_grad, 1)
-    mixed = mixed_gathers[1].place_hop(put_chunk(1), mixed, 0)
+    hop, mixed_hop = tokens_gather.step(), mixed_gather.step()
+    for count in range(2):
+        tokens_grad = tokens_gather.place_hop(put_rows, tokens_grad, count)
+        mixed = mixed_gather.place_hop(put_rows, mixed, count)
     hop, mixed_hop, tokens_grad, mixed = hold(hop, mixed_hop, tokens_grad, mixed)
     tokens_gather.held(hop)
-    mixed_gathers[1].held(mixed_hop)
-
-    hop, mixed_hop = tokens_gather.step(), mixed_gathers[1].step()
+    mixed_gather.held(mixed_hop)
+
+    hop = tokens_gather.step()
     tokens_grad = tokens_gather.place_hop(put_rows, tokens_grad, 2)
-    mixed = mixed_gathers[1].place_hop(put_chunk(1), mixed, 1)
-    hop, mixed_hop, tokens_grad, mixed = hold(hop, mixed_hop, tokens_grad, mixed)
+    mixed = mixed_gather.place_hop(put_rows, mixed, 2)
+    hop, tokens_grad, mixed = hold(hop, tokens_grad, mixed)
     tokens_gather.held(hop)
-    mixed_gathers[1].held(mixed_hop)
-
-    mixed_hop = mixed_gathers[1].step()
+
+    mixed_hop = mixed_gather.step()
     if groups > 3:
         tokens_grad = tokens_gather.place_hop(put_rows, tokens_grad, 3)
-    mixed = mixed_gathers[1].place_hop(put_chunk(1), mixed, 2)
     hidden_units = w_down.shape[1]
     rest = after(rest, hop)
     down_grad = rest[:, :hidden_units]
@@ -1092,8 +1072,8 @@
             [lax.dynamic_slice_in_dim(output_plane, j * features, features, 1), small], axis=1
         )
     )
-    mixed_hop, tokens_grad, mixed, blocks = hold(mixed_hop, tokens_grad, mixed, blocks)
-    mixed_gathers[1].held(mixed_hop)
+    mixed_hop, tokens_grad, blocks = hold(mixed_hop, tokens_grad, blocks)
+    mixed_gather.held(mixed_hop)
     blocks = stack_blocks(blocks).astype(F32)
     output_grad = jnp.sum(blocks[:, :, :features], axis=0)
     kv_share = blocks.shape[1] // groups
@@ -1102,10 +1082,10 @@
     )
     gains = jnp.sum(blocks[:, :, features + 2 * HD : features + 2 * HD + 2], axis=0).T
     for count in range(3, groups):
-        mixed = mixed_gathers[1].place_hop(put_chunk(1), mixed, count)
+        mixed = mixed_gather.place_hop(put_rows, mixed, count)
         if count + 1 < groups:
             tokens_gather.step()
-            mixed_gathers[1].step()
+            mixed_gather.step()
             tokens_grad = tokens_gather.place_hop(put_rows, tokens_grad, count + 1)
 
     key_heads, value_heads = [], []

time: 1140 us -> 1150 us (level)
  local copies, waits for them, and re-layouts: 86.6 us -> 98.5 us
    ppermute x15 -> x12, waiting for transfers between devices: 153 us -> 177 us  [step(): self.lefts.append(lax.ppermute(self.lefts[-1], 'tensor', to_left))]
    pallas_call x1, Pallas kernels: 60 us -> 81.9 us  [attend_back_last(): pl.pallas_call(kernel, grid_spec=pltpu.PrefetchScalarGridSpec(num_scalar_...]
    pallas_call x1, Pallas kernels: 55.9 us -> 34.1 us  [attend_back_first(): pl.pallas_call(kernel, grid_spec=pltpu.PrefetchScalarGridSpec(num_scalar_...]
    ppermute x1, starting transfers between devices: 0.01 us -> 21.6 us  [body(): output_far = lax.ppermute(output_near, 'dp', beside)]
    ppermute x12, waiting for transfers between devices: 67.2 us -> 50.5 us  [send_blocks(): lax.ppermute(block, 'tensor', [(i, (i + shift) % size) for i in range(siz...]
    dynamic_update_slice x10 -> x2, other arithmetic: 20.7 us -> 4.55 us  [put_rows(): lax.dynamic_update_slice_in_dim(target, piece[c * share:(c + 1) * share],...]
    pallas_call x1, Pallas kernels: 43.6 us -> 28 us  [attend_first(): pl.pallas_call(kernel, grid_spec=pltpu.PrefetchScalarGridSpec(num_scalar_...]
    pallas_call x1, Pallas kernels: 41.4 us -> 56.9 us  [attend(): pl.pallas_call(kernel, grid_spec=pltpu.PrefetchScalarGridSpec(num_scalar_...]
  transfers between devices with their start and end apart: 66 -> 60, of which waited for: 22 -> 18; matrix products, arithmetic and copies ran while one was open for 20% -> 20% of each run, Pallas kernels for 33% -> 32%
where the time goes in v7:
time: 1150 us; the launch traced here: 1140 us
  Pallas kernels  370 us (32%)
  waiting for transfers between devices  339 us (29%)
  starting transfers between devices  123 us (11%)
  local copies, waits for them, and re-layouts  98.5 us (9%)
  matrix products  83 us (7%)
  other arithmetic  81.8 us (7%)
  between operations  49.6 us (4%)
    ppermute x12, waiting for transfers between devices, step(): self.lefts.append(lax.ppermute(self.lefts[-1], 'tensor', to_left))  177 us
    pallas_call x2, Pallas kernels, feed_forward(): pl.pallas_call(feed_kernel, grid=(2 * quarter,), in_specs=[pl.BlockSpec((...  123 us
    pallas_call x1, Pallas kernels, attend_back_last(): pl.pallas_call(kernel, grid_spec=pltpu.PrefetchScalarGridSpec(num_scalar_...  81.9 us
    dot_general x4, matrix products, t_dot(): return jnp.einsum('rd,rf->df', a, b, preferred_element_type=F32)  68.5 us
    pallas_call x1, Pallas kernels, attend(): pl.pallas_call(kernel, grid_spec=pltpu.PrefetchScalarGridSpec(num_scalar_...  56.9 us
    ppermute x12, waiting for transfers between devices, send_blocks(): lax.ppermute(block, 'tensor', [(i, (i + shift) % size) for i in range(siz...  50.5 us
    ppermute x1, waiting for transfers between devices, body(): lax.ppermute(jnp.concatenate([dq_second, kv_far[:span], kv_far[span:]], a...  37 us
    pallas_call x1, Pallas kernels, attend_back_first(): pl.pallas_call(kernel, grid_spec=pltpu.PrefetchScalarGridSpec(num_scalar_...  34.1 us
  transfers between devices with their start and end apart: 60, of which 18 were waited for; matrix products, arithmetic and copies ran while one was open for 20% of the time, Pallas kernels for 32%

profile of v7, /device:TPU:0, one launch (start us, length us, event | category | flops | bytes accessed | tf_op | source)
XLA Modules:
  0.0 1144.5 jit_solution(16123967824152209394)
XLA Ops:
  9.8 5.9 collective-permute-start
  17.4 5.4 multiply_sine_fusion.1
  26.2 17.5 %project.1 = (bf16[2048,128]{1,0:T(8,128)(2,1)S(1)}, bf16[2048,512]{1,0:T(8,128)(2,1)}, bf16[2048,2048]{1,0:T(8,128)(2,1)}, f32[2048,128]{1,0:T(8,128)S(1)}, f32[2048,128]{1,0:T(8,128)S(1)}) custom-call(s32[1]{0:T(128)} %bitcast.1.head, bf16[2048,2048]{1,0:T(8,128)(2,1)} %tokens_ref.5, f32[1,2048]{1,0:T(1,128)S(1)} %bitcast.150, ...), custom_call_target="tpu_custom_call" | custom-call | flops 1 | bytes 1 | tf_op jit(solution)/shard_map/project/pallas_call | solution.py:68
  53.4 7.9 collective-permute-done.2.other
  61.4 13.9 %collective-permute-done.4.refs_2_ = bf16[1024,512]{1,0:T(8,128)(2,1)S(1)} collective-permute-done((bf16[1024,512]{1,0:T(8,128)(2,1)}, bf16[1024,512]{1,0:T(8,128)(2,1)S(1)}, u32[]{:S(2)}, u32[]{:S(2)}) %collective-permute-start.4) | collective-permute-done | bytes 1048608 | tf_op jit(solution)/shard_map/ppermute | solution.py:638
  78.8 28.0 %attend_first.1 = (bf16[1024,512]{1,0:T(8,128)(2,1)}, f32[4,8,1024]{2,1,0:T(8,128)}, bf16[4096,128]{1,0:T(8,128)(2,1)}, bf16[4096,128]{1,0:T(8,128)(2,1)}, bf16[...) custom-call(s32[6]{0:T(128)} %get-tuple-element.504.meta.refs_0_, ...), custom_call_target="tpu_custom_call" | custom-call | flops 17179869184 | bytes 8388608 | tf_op jit(solution)/shard_map/attend_first/pallas_call | solution.py:208
  111.7 6.9 arrange.3.refs_0_
  118.7 21.6 %collective-permute-start.8 = (bf16[4,1024,512]{2,1,0:T(8,128)(2,1)}, bf16[4,1024,512]{2,1,0:T(8,128)(2,1)}, u32[]{:S(2)}, u32[]{:S(2)}) collective-permute-start(bf16[4,1024,512]{2,1,0:T(8,128)(2,1)} %arrange.3.refs_0_), channel_id=1, source_target_pairs={{0,8},{8,0},{16,24},{24,16},{1,9},{9,1},{17,25},{25,17},{2,10},{10... | collective-permute-start | bytes 12582920 | tf_op jit(solution)/shard_map/ppermute | solution.py:831
  142.2 56.9 %attend.1 = (bf16[1024,512]{1,0:T(8,128)(2,1)}, f32[4,8,1024]{2,1,0:T(8,128)}) custom-call(s32[6]{0:T(128)} %get-tuple-element.503.refs_0_, bf16[1024,512]{1,0:T(8,128)(2,1)} %collective-permute-done.5.refs_1_, bf16[4096,128]{1,0:T(8,128)(2,1)} %get-tuple-element.215.refs_2_.refs_5_, bf16[4096,128]{1,0:T(8,128)(2,1)} %get-tuple-element.216.refs_3_.refs_6_, ...), custom_call_target="tpu_custom_call" | custom-call | flops 17179869184 | bytes 8388608 | tf_op jit(solution)/shard_map/attend/pallas_call | solution.py:245
  201.3 6.4 arrange.4.output_weight
  207.7 3.7 multiply_sine_fusion
  213.4 3.7 maximum_maximum_fusion
  217.1 8.0 collective-permute-done.9
  226.4 4.4 collective-permute-start.10
  232.1 61.8 %feed_forward.2 = (f32[2048,2048]{1,0:T(8,128)}, bf16[2048,2048]{1,0:T(8,128)(2,1)}, bf16[2048,1408]{1,0:T(8,128)(2,1)}, bf16[2048,2816]{1,0:T(8,128)(2,1)}, bf1...) custom-call(bf16[4,1024,512]{2,1,0:T(8,128)(2,1)} %bitcast.155, bf16[2048,2048]{1,0:T(8,128)(2,1)} %tokens_ref.5, ...), custom_call_target="tpu_custom_call" | custom-call | flops 1 | bytes 1 | tf_op jit(solution)/shard_map/feed_forward/pallas_call | solution.py:522
  293.9 20.7 %all-gather.7.cloned.1.call-done = bf16[4096,512]{1,0:T(8,128)(2,1)} async-done(((bf16[1024,512]{1,0:T(8,128)(2,1)}), bf16[4096,512]{1,0:T(8,128)(2,1)}) %all-gather.7.cloned.1.call-update) | async-done | bytes 4194320 | tf_op jit(solution)/shard_map/all_gather | solution.py:853
  325.9 61.3 %feed_forward.3 = (f32[2048,2048]{1,0:T(8,128)}, bf16[2048,2048]{1,0:T(8,128)(2,1)}, bf16[2048,1408]{1,0:T(8,128)(2,1)}, bf16[2048,2816]{1,0:T(8,128)(2,1)}, bf1...) custom-call(bf16[4,1024,512]{2,1,0:T(8,128)(2,1)} %bitcast.157, ...), custom_call_target="tpu_custom_call", output_to_operand_aliasing={{0}: (8, {}), {1}: (9, {}), {2}: (10, {}), {3}: (11, {})} | custom-call | flops 1 | bytes 1 | tf_op jit(solution)/shard_map/feed_forward/pallas_call | solution.py:522
  389.3 31.8 %convolution_convert_fusion = bf16[2048,2816]{1,0:T(8,128)(2,1)} fusion(bf16[2048,2048]{1,0:T(8,128)(2,1)} %get-tuple-element.252, bf16[2048,2816]{1,0:T(8,128)(2,1)} %get-tuple-element.253), kind=kOutput, calls=%fused_computation.3 | convolution fusion | flops 23628087296 | bytes 31457280 | tf_op jit(solution)/shard_map/rd,rf->df/dot_general | solution.py:732
  421.1 4.4 multiply_reduce_fusion.1
  431.4 2.4 arrange.5.refs_0_
  435.7 4.0 fusion.54
  439.7 6.1 fusion.41
  448.0 2.7 collective-permute-start.16
  454.3 2.9 collective-permute-start.18
  457.2 19.4 %fusion.2 = bf16[2048,1408]{1,0:T(8,128)(2,1)} fusion(bf16[2048,1408]{1,0:T(8,128)(2,1)} %get-tuple-element.265, bf16[2048,2048]{1,0:T(8,128)(2,1)} %cotangent_ref.3), kind=kOutput, calls=%fused_computation.10 | convolution fusion | flops 11814043648 | bytes 19922944 | tf_op jit(solution)/shard_map/rd,rf->df/dot_general | solution.py:732
  478.4 6.6 collective-permute-done.17
  485.5 8.1 collective-permute-done.19.refs_1_
  501.0 2.8 reduce-scatter.9.cloned.1.call-done
  503.8 2.6 fusion.23
  506.6 3.3 fusion.52
  509.9 6.2 fusion.42
  519.3 9.2 collective-permute-start.23
  529.3 4.4 collective-permute-start.24
  549.3 34.1 %attend_back_first.1 = (bf16[1024,512]{1,0:T(8,128)(2,1)}, f32[4096,128]{1,0:T(8,128)}, f32[4096,128]{1,0:T(8,128)}) custom-call(s32[6]{0:T(128)} %get-tuple-element.504.meta.refs_0_, bf16[1024,512]{1,0:T(8,128)(2,1)} %pad_maximum_fusion.3.q_ref.refs_1_, bf16[1024,512]{1,0:T(8,128)(2,1)} %get-tuple-element.213.refs_2_, bf16[1024,512]{1,0:T(8,128)(2,1)} %bitcast.159, ...), custom_call_target="tpu_custom_call" | custom-call | flops 1 | bytes 1 | tf_op jit(solution)/shard_map/attend_back_first/pallas_call | solution.py:381
  592.7 81.9 %attend_back_last.1 = (bf16[1024,512]{1,0:T(8,128)(2,1)}, f32[2048,128]{1,0:T(8,128)}, bf16[2048,128]{1,0:T(8,128)(2,1)}) custom-call(s32[6]{0:T(128)} %get-tuple-element.503.refs_0_, bf16[1024,512]{1,0:T(8,128)(2,1)} %collective-permute-done.5.refs_1_, bf16[1024,512]{1,0:T(8,128)(2,1)} %get-tuple-element.222.refs_2_, bf16[1024,512]{1,0:T(8,128)(2,1)} %bitcast.160, ...), custom_call_target="tpu_custom_call" | custom-call | flops 1 | bytes 1 | tf_op jit(solution)/shard_map/attend_back_last/pallas_call | solution.py:436
  678.7 4.2 copy.89
  684.2 3.8 collective-permute-start.35
  695.9 6.9 convolution_convert_fusion.1
  703.8 30.1 %collective-permute-done.31 = bf16[256,256]{1,0:T(8,128)(2,1)S(1)} collective-permute-done((bf16[256,256]{1,0:T(8,128)(2,1)S(1)}, bf16[256,256]{1,0:T(8,128)(2,1)S(1)}, u32[]{:S(2)}, u32[]{:S(2)}) %collective-permute-start.31) | collective-permute-done | bytes 131104 | tf_op jit(solution)/shard_map/ppermute | solution.py:700
  733.9 6.2 collective-permute-start.32
  740.2 9.2 collective-permute-done.30
  749.4 6.1 collective-permute-start.29
  756.4 6.6 join.2
  763.5 6.6 join.3
  782.2 4.1 collective-permute-start.36
  788.8 37.0 %collective-permute-done.40 = bf16[1024,768]{1,0:T(8,128)(2,1)} collective-permute-done((bf16[1024,768]{1,0:T(8,128)(2,1)}, bf16[1024,768]{1,0:T(8,128)(2,1)}, u32[]{:S(2)}, u32[]{:S(2)}) %collective-permute-start.40) | collective-permute-done | bytes 1572896 | tf_op jit(solution)/shard_map/ppermute | solution.py:1031
  828.5 10.5 convolution_convert_fusion.3
  839.0 4.5 broadcast.124.clone
  844.9 3.2 constant_dynamic-update-slice_fusion
  849.8 2.7 collective-permute-start.38
  853.8 13.1 %fusion.1 = bf16[2048,4224]{1,0:T(8,128)(2,1)} fusion(bf16[2048,2]{1,0:T(8,128)(2,1)S(1)} %copy-done.48, bf16[2048,640]{1,0:T(8,128)(2,1)S(1)} %copy-done.47, bf16[2048,2048]{1,0:T(8,128)(2,1)} %convolution_convert_fusion.1, bf16[2048,1408]{1,0:T(8,128)(2,1)} %fusion.2), kind=kLoop, calls=%fused_computation.2 | loop fusion | flops 86507520 | bytes 34086912 | tf_op jit(solution)/shard_map/concatenate | solution.py:1041
  866.9 26.2 %collective-permute-done.38 = bf16[512,2048]{1,0:T(8,128)(2,1)} collective-permute-done((bf16[512,2048]{1,0:T(8,128)(2,1)}, bf16[512,2048]{1,0:T(8,128)(2,1)}, u32[]{:S(2)}, u32[]{:S(2)}) %collective-permute-start.38) | collective-permute-done | bytes 2097184 | tf_op jit(solution)/shard_map/ppermute | solution.py:637
  893.1 5.4 collective-permute-done.39
  913.5 5.7 broadcast.124.clone.1
  926.7 3.2 broadcast_select_fusion
  940.2 34.8 %collective-permute-done.42 = bf16[512,2048]{1,0:T(8,128)(2,1)S(1)} collective-permute-done((bf16[512,2048]{1,0:T(8,128)(2,1)}, bf16[512,2048]{1,0:T(8,128)(2,1)S(1)}, u32[]{:S(2)}, u32[]{:S(2)}) %collective-permute-start.42) | collective-permute-done | bytes 2097184 | tf_op jit(solution)/shard_map/ppermute | solution.py:638
  974.9 39.5 %collective-permute-done.44 = bf16[512,2048]{1,0:T(8,128)(2,1)} collective-permute-done((bf16[512,2048]{1,0:T(8,128)(2,1)}, bf16[512,2048]{1,0:T(8,128)(2,1)}, u32[]{:S(2)}, u32[]{:S(2)}) %collective-permute-start.44) | collective-permute-done | bytes 2097184 | tf_op jit(solution)/shard_map/ppermute | solution.py:638
  1020.0 2.9 select_select_fusion.2
  1027.7 46.4 %collective-permute-done.46 = bf16[512,2048]{1,0:T(8,128)(2,1)S(1)} collective-permute-done((bf16[512,2048]{1,0:T(8,128)(2,1)S(1)}, bf16[512,2048]{1,0:T(8,128)(2,1)S(1)}, u32[]{:S(2)}, u32[]{:S(2)}) %collective-permute-start.46) | collective-permute-done | bytes 2097184 | tf_op jit(solution)/shard_map/ppermute | solution.py:638
  1076.6 3.1 slice_convert_fusion
  1081.3 3.7 collective-permute-start.51
  1087.0 37.0 %collective-permute-done.48 = bf16[512,2048]{1,0:T(8,128)(2,1)} collective-permute-done((bf16[512,2048]{1,0:T(8,128)(2,1)}, bf16[512,2048]{1,0:T(8,128)(2,1)}, u32[]{:S(2)}, u32[]{:S(2)}) %collective-permute-start.48) | collective-permute-done | bytes 2097184 | tf_op jit(solution)/shard_map/ppermute | solution.py:638
  1124.1 4.1 collective-permute-done.51
  1130.9 3.0 select_select_fusion
  (415 shorter events, 158.1 us)
Async XLA Ops:
  7.2 218.1 %all-gather.5.cloned.1.call-start = ((), (), s32[]{:S(2)}) async-start(), calls=%async_computation.12 | async-start | bytes 5242880 | tf_op jit(solution)/shard_map/all_gather | solution.py:828
  9.8 35.7 %collective-permute-start = (bf16[1024,512]{1,0:T(8,128)(2,1)}, bf16[1024,512]{1,0:T(8,128)(2,1)}, u32[]{:S(2)}, u32[]{:S(2)}) collective-permute-start(bf16[1024,512]{1,0:T(8,128)(2,1)} %constant_dynamic-slice_fusion.43.refs_6_), channel_id=1, source_target_pairs={{0,1},{1,2},{2,3},{4,5},{5,6},{6,7},{8,9},{9,10},{10,11},{12,13},{... | collective-permute-start | bytes 3145736 | tf_op jit(solution)/shard_map/ppermute | solution.py:637
  15.7 29.8 %collective-permute-start.1 = (bf16[1024,512]{1,0:T(8,128)(2,1)}, bf16[1024,512]{1,0:T(8,128)(2,1)}, u32[]{:S(2)}, u32[]{:S(2)}) collective-permute-start(bf16[1024,512]{1,0:T(8,128)(2,1)} %constant_dynamic-slice_fusion.43.refs_6_), channel_id=1, source_target_pairs={{1,0},{2,1},{3,2},{5,4},{6,5},{7,6},{9,8},{10,9},{11,10},{13,12},{... | collective-permute-start | bytes 3145736 | tf_op jit(solution)/shard_map/ppermute | solution.py:638
  45.5 15.8 %collective-permute-start.3 = (bf16[1024,512]{1,0:T(8,128)(2,1)}, bf16[1024,512]{1,0:T(8,128)(2,1)S(1)}, u32[]{:S(2)}, u32[]{:S(2)}) collective-permute-start(bf16[1024,512]{1,0:T(8,128)(2,1)} %collective-permute-done.refs_5_), channel_id=1, source_target_pairs={{1,2},{2,3},{5,6},{6,7},{9,10},{10,11},{13,14},{14,15},{17,18},{18... | collective-permute-start | bytes 3145736 | tf_op jit(solution)/shard_map/ppermute | solution.py:637
  46.4 28.9 %collective-permute-start.4 = (bf16[1024,512]{1,0:T(8,128)(2,1)}, bf16[1024,512]{1,0:T(8,128)(2,1)S(1)}, u32[]{:S(2)}, u32[]{:S(2)}) collective-permute-start(bf16[1024,512]{1,0:T(8,128)(2,1)} %collective-permute-done.1.refs_4_), channel_id=1, source_target_pairs={{1,0},{2,1},{5,4},{6,5},{9,8},{10,9},{13,12},{14,13},{17,16},{18,1... | collective-permute-start | bytes 3145736 | tf_op jit(solution)/shard_map/ppermute | solution.py:638
  47.7 13.6 %collective-permute-start.2 = (bf16[2048,128]{1,0:T(8,128)(2,1)}, bf16[2048,128]{1,0:T(8,128)(2,1)S(1)}, u32[]{:S(2)}, u32[]{:S(2)}) collective-permute-start(bf16[2048,128]{1,0:T(8,128)(2,1)} %copy-done.24), channel_id=1, source_target_pairs={{0,4},{4,0},{1,5},{5,1},{2,6},{6,2},{3,7},{7,3},{8,12},{12,8},{9,1... | collective-permute-start | bytes 1572872 | tf_op jit(solution)/shard_map/ppermute | solution.py:814
  61.4 45.4 %copy-start.8 = (bf16[1024,512]{1,0:T(8,128)(2,1)}, bf16[1024,512]{1,0:T(8,128)(2,1)S(1)}, u32[]{:S(2)}) copy-start(bf16[1024,512]{1,0:T(8,128)(2,1)S(1)} %collective-permute-done.3.refs_3_) | copy-start | bytes 3145732
  75.3 31.5 %copy-start.10 = (bf16[1024,512]{1,0:T(8,128)(2,1)}, bf16[1024,512]{1,0:T(8,128)(2,1)S(1)}, u32[]{:S(2)}) copy-start(bf16[1024,512]{1,0:T(8,128)(2,1)S(1)} %collective-permute-done.4.refs_2_) | copy-start | bytes 3145732
  75.3 31.5 %collective-permute-start.5 = (bf16[1024,512]{1,0:T(8,128)(2,1)}, bf16[1024,512]{1,0:T(8,128)(2,1)}, u32[]{:S(2)}, u32[]{:S(2)}) collective-permute-start(bf16[1024,512]{1,0:T(8,128)(2,1)} %slice.231), channel_id=1, source_target_pairs={{0,4},{4,0},{1,5},{5,1},{2,6},{6,2},{3,7},{7,3},{8,12},{12,8},{9,1... | collective-permute-start | bytes 3145736 | tf_op jit(solution)/shard_map/ppermute | solution.py:822
  76.8 30.0 %collective-permute-start.6 = (bf16[1024,512]{1,0:T(8,128)(2,1)S(1)}, bf16[1024,512]{1,0:T(8,128)(2,1)S(1)}, u32[]{:S(2)}, u32[]{:S(2)}) collective-permute-start(bf16[1024,512]{1,0:T(8,128)(2,1)S(1)} %collective-permute-done.3.refs_3_), channel_id=1, source_target_pairs={{2,3},{6,7},{10,11},{14,15},{18,19},{22,23},{26,27},{30,31}} | collective-permute-start | bytes 3145736 | tf_op jit(solution)/shard_map/ppermute | solution.py:637
  77.5 30.3 %collective-permute-start.7 = (bf16[1024,512]{1,0:T(8,128)(2,1)S(1)}, bf16[1024,512]{1,0:T(8,128)(2,1)}, u32[]{:S(2)}, u32[]{:S(2)}) collective-permute-start(bf16[1024,512]{1,0:T(8,128)(2,1)S(1)} %collective-permute-done.4.refs_2_), channel_id=1, source_target_pairs={{1,0},{5,4},{9,8},{13,12},{17,16},{21,20},{25,24},{29,28}} | collective-permute-start | bytes 3145736 | tf_op jit(solution)/shard_map/ppermute | solution.py:638
  107.8 206.8 %all-gather.7.cloned.1.call-start = ((), (), s32[]{:S(2)}) async-start(), calls=%async_computation.13 | async-start | bytes 5242880 | tf_op jit(solution)/shard_map/all_gather | solution.py:853
  118.7 80.4 %collective-permute-start.8 = (bf16[4,1024,512]{2,1,0:T(8,128)(2,1)}, bf16[4,1024,512]{2,1,0:T(8,128)(2,1)}, u32[]{:S(2)}, u32[]{:S(2)}) collective-permute-start(bf16[4,1024,512]{2,1,0:T(8,128)(2,1)} %arrange.3.refs_0_), channel_id=1, source_target_pairs={{0,8},{8,0},{16,24},{24,16},{1,9},{9,1},{17,25},{25,17},{2,10},{10... | collective-permute-start | bytes 12582920 | tf_op jit(solution)/shard_map/ppermute | solution.py:831
  199.0 26.1 %collective-permute-start.9 = (bf16[1024,512]{1,0:T(8,128)(2,1)}, bf16[1024,512]{1,0:T(8,128)(2,1)}, u32[]{:S(2)}, u32[]{:S(2)}) collective-permute-start(bf16[1024,512]{1,0:T(8,128)(2,1)} %get-tuple-element.222.refs_2_), channel_id=1, source_target_pairs={{0,4},{4,0},{1,5},{5,1},{2,6},{6,2},{3,7},{7,3},{8,12},{12,8},{9,1... | collective-permute-start | bytes 3145736 | tf_op jit(solution)/shard_map/ppermute | solution.py:841
  225.2 202.0 %reduce-scatter.7.cloned.1.call-start = ((), (), s32[]{:S(2)}) async-start(), calls=%async_computation.6 | async-start | bytes 5242880 | tf_op jit(solution)/shard_map/reduce_scatter | solution.py:890
  226.4 67.5 %collective-permute-start.10 = (bf16[512,512]{1,0:T(8,128)(2,1)S(1)}, bf16[512,512]{1,0:T(8,128)(2,1)S(1)}, u32[]{:S(2)}, u32[]{:S(2)}) collective-permute-start(bf16[512,512]{1,0:T(8,128)(2,1)S(1)} %constant_dynamic-slice_fusion.42.refs_6_), channel_id=1, source_target_pairs={{0,1},{1,2},{2,3},{4,5},{5,6},{6,7},{8,9},{9,10},{10,11},{12,13},{... | collective-permute-start | bytes 1572872 | tf_op jit(solution)/shard_map/ppermute | solution.py:637
  230.8 63.1 %collective-permute-start.11 = (bf16[512,512]{1,0:T(8,128)(2,1)S(1)}, bf16[512,512]{1,0:T(8,128)(2,1)S(1)}, u32[]{:S(2)}, u32[]{:S(2)}) collective-permute-start(bf16[512,512]{1,0:T(8,128)(2,1)S(1)} %constant_dynamic-slice_fusion.42.refs_6_), channel_id=1, source_target_pairs={{1,0},{2,1},{3,2},{5,4},{6,5},{7,6},{9,8},{10,9},{11,10},{13,12},{... | collective-permute-start | bytes 1572872 | tf_op jit(solution)/shard_map/ppermute | solution.py:638
  314.6 189.2 %reduce-scatter.9.cloned.1.call-start = ((), (), s32[]{:S(2)}) async-start(), calls=%async_computation.7 | async-start | bytes 5242880 | tf_op jit(solution)/shard_map/reduce_scatter | solution.py:890
  321.6 65.6 %collective-permute-start.12 = (bf16[512,512]{1,0:T(8,128)(2,1)S(1)}, bf16[512,512]{1,0:T(8,128)(2,1)S(1)}, u32[]{:S(2)}, u32[]{:S(2)}) collective-permute-start(bf16[512,512]{1,0:T(8,128)(2,1)S(1)} %collective-permute-done.10.refs_5_), channel_id=1, source_target_pairs={{1,2},{2,3},{5,6},{6,7},{9,10},{10,11},{13,14},{14,15},{17,18},{18... | collective-permute-start | bytes 1572872 | tf_op jit(solution)/shard_map/ppermute | solution.py:637
  322.3 64.9 %collective-permute-start.13 = (bf16[512,512]{1,0:T(8,128)(2,1)S(1)}, bf16[512,512]{1,0:T(8,128)(2,1)}, u32[]{:S(2)}, u32[]{:S(2)}) collective-permute-start(bf16[512,512]{1,0:T(8,128)(2,1)S(1)} %collective-permute-done.11.refs_4_), channel_id=1, source_target_pairs={{1,0},{2,1},{5,4},{6,5},{9,8},{10,9},{13,12},{14,13},{17,16},{18,1... | collective-permute-start | bytes 1572872 | tf_op jit(solution)/shard_map/ppermute | solution.py:638
  387.3 38.3 %collective-permute-start.14 = (bf16[512,512]{1,0:T(8,128)(2,1)S(1)}, bf16[512,512]{1,0:T(8,128)(2,1)S(1)}, u32[]{:S(2)}, u32[]{:S(2)}) collective-permute-start(bf16[512,512]{1,0:T(8,128)(2,1)S(1)} %collective-permute-done.12.refs_3_), channel_id=1, source_target_pairs={{2,3},{6,7},{10,11},{14,15},{18,19},{22,23},{26,27},{30,31}} | collective-permute-start | bytes 1572872 | tf_op jit(solution)/shard_map/ppermute | solution.py:637
  388.0 38.4 %collective-permute-start.15 = (bf16[512,512]{1,0:T(8,128)(2,1)}, bf16[512,512]{1,0:T(8,128)(2,1)S(1)}, u32[]{:S(2)}, u32[]{:S(2)}) collective-permute-start(bf16[512,512]{1,0:T(8,128)(2,1)} %collective-permute-done.13.refs_2_), channel_id=1, source_target_pairs={{1,0},{5,4},{9,8},{13,12},{17,16},{21,20},{25,24},{29,28}} | collective-permute-start | bytes 1572872 | tf_op jit(solution)/shard_map/ppermute | solution.py:638
  389.3 449.7 %reduce-scatter.11.cloned.1.call-start = ((), (), s32[]{:S(2)}) async-start(), calls=%async_computation.8 | async-start | bytes 5242880 | tf_op jit(solution)/shard_map/reduce_scatter | solution.py:890
  434.5 410.4 %reduce-scatter.13.cloned.1.call-start = ((), (), s32[]{:S(2)}) async-start(), calls=%async_computation.9 | async-start | bytes 5242880 | tf_op jit(solution)/shard_map/reduce_scatter | solution.py:890
  445.8 47.7 %collective-permute-start.19 = (bf16[4,512,512]{2,1,0:T(8,128)(2,1)S(1)}, bf16[4,512,512]{2,1,0:T(8,128)(2,1)}, u32[]{:S(2)}, u32[]{:S(2)}) collective-permute-start(bf16[4,512,512]{2,1,0:T(8,128)(2,1)S(1)} %arrange.5.refs_0_), channel_id=1, source_target_pairs={{0,4},{4,0},{1,5},{5,1},{2,6},{6,2},{3,7},{7,3},{8,12},{12,8},{9,1... | collective-permute-start | bytes 6291464 | tf_op jit(solution)/shard_map/ppermute | solution.py:929
  448.0 30.4 %collective-permute-start.16 = (bf16[256,512]{1,0:T(8,128)(2,1)}, bf16[256,512]{1,0:T(8,128)(2,1)}, u32[]{:S(2)}, u32[]{:S(2)}) collective-permute-start(bf16[256,512]{1,0:T(8,128)(2,1)} %bitcast.25), channel_id=1, source_target_pairs={{0,1},{1,2},{2,3},{3,0},{4,5},{5,6},{6,7},{7,4},{8,9},{9,10},{10,1... | collective-permute-start | bytes 786440 | tf_op jit(solution)/shard_map/ppermute | solution.py:700
  451.6 33.4 %collective-permute-start.17 = (bf16[256,512]{1,0:T(8,128)(2,1)}, bf16[256,512]{1,0:T(8,128)(2,1)}, u32[]{:S(2)}, u32[]{:S(2)}) collective-permute-start(bf16[256,512]{1,0:T(8,128)(2,1)} %bitcast.26), channel_id=1, source_target_pairs={{0,2},{1,3},{2,0},{3,1},{4,6},{5,7},{6,4},{7,5},{8,10},{9,11},{10,... | collective-permute-start | bytes 786440 | tf_op jit(solution)/shard_map/ppermute | solution.py:700
  454.3 39.7 %copy-start.5 = (bf16[2048,256]{1,0:T(8,128)(2,1)S(1)}, bf16[2048,256]{1,0:T(8,128)(2,1)}, u32[]{:S(2)}) copy-start(bf16[2048,256]{1,0:T(8,128)(2,1)} %v_weight.1) | copy-start | bytes 3145732
  454.3 31.2 %collective-permute-start.18 = (bf16[256,512]{1,0:T(8,128)(2,1)}, bf16[256,512]{1,0:T(8,128)(2,1)}, u32[]{:S(2)}, u32[]{:S(2)}) collective-permute-start(bf16[256,512]{1,0:T(8,128)(2,1)} %bitcast.170), channel_id=1, source_target_pairs={{0,3},{1,0},{2,1},{3,2},{4,7},{5,4},{6,5},{7,6},{8,11},{9,8},{10,9... | collective-permute-start | bytes 786440 | tf_op jit(solution)/shard_map/ppermute | solution.py:700
  493.5 10.3 collective-permute-start.20
  493.5 10.3 collective-permute-start.21
  517.0 66.3 %collective-permute-start.22 = (bf16[256,512]{1,0:T(8,128)(2,1)}, bf16[256,512]{1,0:T(8,128)(2,1)S(1)}, u32[]{:S(2)}, u32[]{:S(2)}) collective-permute-start(bf16[256,512]{1,0:T(8,128)(2,1)} %bitcast.166), channel_id=1, source_target_pairs={{0,4},{1,5},{2,6},{3,7},{4,0},{5,1},{6,2},{7,3},{8,12},{9,13},{10,... | collective-permute-start | bytes 786440 | tf_op jit(solution)/shard_map/ppermute | solution.py:690
  519.3 64.0 %collective-permute-start.23 = (bf16[256,512]{1,0:T(8,128)(2,1)}, bf16[256,512]{1,0:T(8,128)(2,1)S(1)}, u32[]{:S(2)}, u32[]{:S(2)}) collective-permute-start(bf16[256,512]{1,0:T(8,128)(2,1)} %bitcast.167), channel_id=1, source_target_pairs={{0,5},{1,6},{2,7},{3,4},{4,1},{5,2},{6,3},{7,0},{8,13},{9,14},{10,... | collective-permute-start | bytes 786440 | tf_op jit(solution)/shard_map/ppermute | solution.py:690
  529.3 54.0 %collective-permute-start.24 = (bf16[256,512]{1,0:T(8,128)(2,1)}, bf16[256,512]{1,0:T(8,128)(2,1)S(1)}, u32[]{:S(2)}, u32[]{:S(2)}) collective-permute-start(bf16[256,512]{1,0:T(8,128)(2,1)} %bitcast.168), channel_id=1, source_target_pairs={{0,6},{1,7},{2,4},{3,5},{4,2},{5,3},{6,0},{7,1},{8,14},{9,15},{10,... | collective-permute-start | bytes 786440 | tf_op jit(solution)/shard_map/ppermute | solution.py:690
  534.6 48.8 %collective-permute-start.25 = (bf16[256,512]{1,0:T(8,128)(2,1)}, bf16[256,512]{1,0:T(8,128)(2,1)S(1)}, u32[]{:S(2)}, u32[]{:S(2)}) collective-permute-start(bf16[256,512]{1,0:T(8,128)(2,1)} %bitcast.169), channel_id=1, source_target_pairs={{0,7},{1,4},{2,5},{3,6},{4,3},{5,0},{6,1},{7,2},{8,15},{9,12},{10,... | collective-permute-start | bytes 786440 | tf_op jit(solution)/shard_map/ppermute | solution.py:690
  549.2 527.3 %reduce-scatter.17.cloned.1.call-start = ((), (), s32[]{:S(2)}) async-start(), calls=%async_computation.11 | async-start | bytes 12976128 | tf_op jit(solution)/shard_map/reduce_scatter | solution.py:893
  586.4 88.2 %collective-permute-start.26 = (bf16[256,512]{1,0:T(8,128)(2,1)}, bf16[256,512]{1,0:T(8,128)(2,1)}, u32[]{:S(2)}, u32[]{:S(2)}) collective-permute-start(bf16[256,512]{1,0:T(8,128)(2,1)} %get-tuple-element.423), channel_id=1, source_target_pairs={{0,1},{1,2},{2,3},{3,0},{4,5},{5,6},{6,7},{7,4},{8,9},{9,10},{10,1... | collective-permute-start | bytes 786440 | tf_op jit(solution)/shard_map/ppermute | solution.py:700
  588.0 86.6 %collective-permute-start.27 = (bf16[256,512]{1,0:T(8,128)(2,1)S(1)}, bf16[256,512]{1,0:T(8,128)(2,1)}, u32[]{:S(2)}, u32[]{:S(2)}) collective-permute-start(bf16[256,512]{1,0:T(8,128)(2,1)S(1)} %get-tuple-element.422), channel_id=1, source_target_pairs={{0,2},{1,3},{2,0},{3,1},{4,6},{5,7},{6,4},{7,5},{8,10},{9,11},{10,... | collective-permute-start | bytes 786440 | tf_op jit(solution)/shard_map/ppermute | solution.py:700
  588.4 86.2 %collective-permute-start.28 = (bf16[256,512]{1,0:T(8,128)(2,1)S(1)}, bf16[256,512]{1,0:T(8,128)(2,1)}, u32[]{:S(2)}, u32[]{:S(2)}) collective-permute-start(bf16[256,512]{1,0:T(8,128)(2,1)S(1)} %get-tuple-element.421), channel_id=1, source_target_pairs={{0,3},{1,0},{2,1},{3,2},{4,7},{5,4},{6,5},{7,6},{8,11},{9,8},{10,9... | collective-permute-start | bytes 786440 | tf_op jit(solution)/shard_map/ppermute | solution.py:700
  684.2 78.9 %collective-permute-start.35 = (bf16[256,768]{1,0:T(8,128)(2,1)S(1)}, bf16[256,768]{1,0:T(8,128)(2,1)S(1)}, u32[]{:S(2)}, u32[]{:S(2)}) collective-permute-start(bf16[256,768]{1,0:T(8,128)(2,1)S(1)} %pad_maximum_fusion.19), channel_id=1, source_target_pairs={{0,7},{1,4},{2,5},{3,6},{4,3},{5,0},{6,1},{7,2},{8,15},{9,12},{10,... | collective-permute-start | bytes 1179656 | tf_op jit(solution)/shard_map/ppermute | solution.py:690
  688.1 75.1 %collective-permute-start.34 = (bf16[256,768]{1,0:T(8,128)(2,1)S(1)}, bf16[256,768]{1,0:T(8,128)(2,1)S(1)}, u32[]{:S(2)}, u32[]{:S(2)}) collective-permute-start(bf16[256,768]{1,0:T(8,128)(2,1)S(1)} %pad_maximum_fusion.18), channel_id=1, source_target_pairs={{0,6},{1,7},{2,4},{3,5},{4,2},{5,3},{6,0},{7,1},{8,14},{9,15},{10,... | collective-permute-start | bytes 1179656 | tf_op jit(solution)/shard_map/ppermute | solution.py:690
  688.2 75.0 %collective-permute-start.33 = (bf16[256,768]{1,0:T(8,128)(2,1)S(1)}, bf16[256,768]{1,0:T(8,128)(2,1)S(1)}, u32[]{:S(2)}, u32[]{:S(2)}) collective-permute-start(bf16[256,768]{1,0:T(8,128)(2,1)S(1)} %pad_maximum_fusion.17), channel_id=1, source_target_pairs={{0,5},{1,6},{2,7},{3,4},{4,1},{5,2},{6,3},{7,0},{8,13},{9,14},{10,... | collective-permute-start | bytes 1179656 | tf_op jit(solution)/shard_map/ppermute | solution.py:690
  690.3 43.6 %collective-permute-start.31 = (bf16[256,256]{1,0:T(8,128)(2,1)S(1)}, bf16[256,256]{1,0:T(8,128)(2,1)S(1)}, u32[]{:S(2)}, u32[]{:S(2)}) collective-permute-start(bf16[256,256]{1,0:T(8,128)(2,1)S(1)} %pad_maximum_fusion.23), channel_id=1, source_target_pairs={{0,3},{1,0},{2,1},{3,2},{4,7},{5,4},{6,5},{7,6},{8,11},{9,8},{10,9... | collective-permute-start | bytes 393224 | tf_op jit(solution)/shard_map/ppermute | solution.py:700
  692.7 56.7 %collective-permute-start.30 = (bf16[256,256]{1,0:T(8,128)(2,1)S(1)}, bf16[256,256]{1,0:T(8,128)(2,1)S(1)}, u32[]{:S(2)}, u32[]{:S(2)}) collective-permute-start(bf16[256,256]{1,0:T(8,128)(2,1)S(1)} %pad_maximum_fusion.22), channel_id=1, source_target_pairs={{0,2},{1,3},{2,0},{3,1},{4,6},{5,7},{6,4},{7,5},{8,10},{9,11},{10,... | collective-permute-start | bytes 393224 | tf_op jit(solution)/shard_map/ppermute | solution.py:700
  733.9 29.2 %collective-permute-start.32 = (bf16[256,768]{1,0:T(8,128)(2,1)S(1)}, bf16[256,768]{1,0:T(8,128)(2,1)S(1)}, u32[]{:S(2)}, u32[]{:S(2)}) collective-permute-start(bf16[256,768]{1,0:T(8,128)(2,1)S(1)} %pad_maximum_fusion.16), channel_id=1, source_target_pairs={{0,4},{1,5},{2,6},{3,7},{4,0},{5,1},{6,2},{7,3},{8,12},{9,13},{10,... | collective-permute-start | bytes 1179656 | tf_op jit(solution)/shard_map/ppermute | solution.py:690
  749.4 13.8 %collective-permute-start.29 = (bf16[256,256]{1,0:T(8,128)(2,1)S(1)}, bf16[256,256]{1,0:T(8,128)(2,1)S(1)}, u32[]{:S(2)}, u32[]{:S(2)}) collective-permute-start(bf16[256,256]{1,0:T(8,128)(2,1)S(1)} %pad_maximum_fusion.21), channel_id=1, source_target_pairs={{0,1},{1,2},{2,3},{3,0},{4,5},{5,6},{6,7},{7,4},{8,9},{9,10},{10,1... | collective-permute-start | bytes 393224 | tf_op jit(solution)/shard_map/ppermute | solution.py:700
  777.0 302.7 %reduce-scatter.15.cloned.1.call-start = ((), (), s32[]{:S(2)}) async-start(), calls=%async_computation.10 | async-start | bytes 19464192 | tf_op jit(solution)/shard_map/reduce_scatter | solution.py:893
  779.5 46.4 %collective-permute-start.40 = (bf16[1024,768]{1,0:T(8,128)(2,1)}, bf16[1024,768]{1,0:T(8,128)(2,1)}, u32[]{:S(2)}, u32[]{:S(2)}) collective-permute-start(bf16[1024,768]{1,0:T(8,128)(2,1)} %pad_maximum_fusion.2), channel_id=1, source_target_pairs={{0,4},{4,0},{1,5},{5,1},{2,6},{6,2},{3,7},{7,3},{8,12},{12,8},{9,1... | collective-permute-start | bytes 4718600 | tf_op jit(solution)/shard_map/ppermute | solution.py:1031
  782.2 46.1 %copy-start.43 = (f32[2048,128]{1,0:T(8,128)S(1)}, f32[2048,128]{1,0:T(8,128)}, u32[]{:S(2)}) copy-start(f32[2048,128]{1,0:T(8,128)} %get-tuple-element.341) | copy-start | bytes 3145732
  782.2 84.6 %collective-permute-start.36 = (bf16[512,2048]{1,0:T(8,128)(2,1)S(1)}, bf16[512,2048]{1,0:T(8,128)(2,1)}, u32[]{:S(2)}, u32[]{:S(2)}) collective-permute-start(bf16[512,2048]{1,0:T(8,128)(2,1)S(1)} %fusion.6), channel_id=1, source_target_pairs={{0,1},{1,2},{2,3},{4,5},{5,6},{6,7},{8,9},{9,10},{10,11},{12,13},{... | collective-permute-start | bytes 6291464 | tf_op jit(solution)/shard_map/ppermute | solution.py:637
  786.3 80.6 %collective-permute-start.37 = (bf16[512,2048]{1,0:T(8,128)(2,1)S(1)}, bf16[512,2048]{1,0:T(8,128)(2,1)}, u32[]{:S(2)}, u32[]{:S(2)}) collective-permute-start(bf16[512,2048]{1,0:T(8,128)(2,1)S(1)} %fusion.6), channel_id=1, source_target_pairs={{1,0},{2,1},{3,2},{5,4},{6,5},{7,6},{9,8},{10,9},{11,10},{13,12},{... | collective-permute-start | bytes 6291464 | tf_op jit(solution)/shard_map/ppermute | solution.py:638
  849.8 43.3 %collective-permute-start.38 = (bf16[512,2048]{1,0:T(8,128)(2,1)}, bf16[512,2048]{1,0:T(8,128)(2,1)}, u32[]{:S(2)}, u32[]{:S(2)}) collective-permute-start(bf16[512,2048]{1,0:T(8,128)(2,1)} %pad_maximum_fusion.1), channel_id=1, source_target_pairs={{0,1},{1,2},{2,3},{4,5},{5,6},{6,7},{8,9},{9,10},{10,11},{12,13},{... | collective-permute-start | bytes 6291464 | tf_op jit(solution)/shard_map/ppermute | solution.py:637
  852.5 46.0 %collective-permute-start.39 = (bf16[512,2048]{1,0:T(8,128)(2,1)}, bf16[512,2048]{1,0:T(8,128)(2,1)}, u32[]{:S(2)}, u32[]{:S(2)}) collective-permute-start(bf16[512,2048]{1,0:T(8,128)(2,1)} %pad_maximum_fusion.1), channel_id=1, source_target_pairs={{1,0},{2,1},{3,2},{5,4},{6,5},{7,6},{9,8},{10,9},{11,10},{13,12},{... | collective-permute-start | bytes 6291464 | tf_op jit(solution)/shard_map/ppermute | solution.py:638
  921.3 18.8 %collective-permute-start.41 = (bf16[512,2048]{1,0:T(8,128)(2,1)}, bf16[512,2048]{1,0:T(8,128)(2,1)S(1)}, u32[]{:S(2)}, u32[]{:S(2)}) collective-permute-start(bf16[512,2048]{1,0:T(8,128)(2,1)} %collective-permute-done.36), channel_id=1, source_target_pairs={{1,2},{2,3},{5,6},{6,7},{9,10},{10,11},{13,14},{14,15},{17,18},{18... | collective-permute-start | bytes 6291464 | tf_op jit(solution)/shard_map/ppermute | solution.py:637
  922.1 52.8 %collective-permute-start.42 = (bf16[512,2048]{1,0:T(8,128)(2,1)}, bf16[512,2048]{1,0:T(8,128)(2,1)S(1)}, u32[]{:S(2)}, u32[]{:S(2)}) collective-permute-start(bf16[512,2048]{1,0:T(8,128)(2,1)} %collective-permute-done.37), channel_id=1, source_target_pairs={{1,0},{2,1},{5,4},{6,5},{9,8},{10,9},{13,12},{14,13},{17,16},{18,1... | collective-permute-start | bytes 6291464 | tf_op jit(solution)/shard_map/ppermute | solution.py:638
  923.4 51.5 %collective-permute-start.43 = (bf16[512,2048]{1,0:T(8,128)(2,1)}, bf16[512,2048]{1,0:T(8,128)(2,1)}, u32[]{:S(2)}, u32[]{:S(2)}) collective-permute-start(bf16[512,2048]{1,0:T(8,128)(2,1)} %collective-permute-done.38), channel_id=1, source_target_pairs={{1,2},{2,3},{5,6},{6,7},{9,10},{10,11},{13,14},{14,15},{17,18},{18... | collective-permute-start | bytes 6291464 | tf_op jit(solution)/shard_map/ppermute | solution.py:637
  925.4 89.0 %collective-permute-start.44 = (bf16[512,2048]{1,0:T(8,128)(2,1)}, bf16[512,2048]{1,0:T(8,128)(2,1)}, u32[]{:S(2)}, u32[]{:S(2)}) collective-permute-start(bf16[512,2048]{1,0:T(8,128)(2,1)} %collective-permute-done.39), channel_id=1, source_target_pairs={{1,0},{2,1},{5,4},{6,5},{9,8},{10,9},{13,12},{14,13},{17,16},{18,1... | collective-permute-start | bytes 6291464 | tf_op jit(solution)/shard_map/ppermute | solution.py:638
  1014.4 13.2 %collective-permute-start.45 = (bf16[512,2048]{1,0:T(8,128)(2,1)S(1)}, bf16[512,2048]{1,0:T(8,128)(2,1)S(1)}, u32[]{:S(2)}, u32[]{:S(2)}) collective-permute-start(bf16[512,2048]{1,0:T(8,128)(2,1)S(1)} %collective-permute-done.41), channel_id=1, source_target_pairs={{2,3},{6,7},{10,11},{14,15},{18,19},{22,23},{26,27},{30,31}} | collective-permute-start | bytes 6291464 | tf_op jit(solution)/shard_map/ppermute | solution.py:637
  1015.2 58.9 %collective-permute-start.46 = (bf16[512,2048]{1,0:T(8,128)(2,1)S(1)}, bf16[512,2048]{1,0:T(8,128)(2,1)S(1)}, u32[]{:S(2)}, u32[]{:S(2)}) collective-permute-start(bf16[512,2048]{1,0:T(8,128)(2,1)S(1)} %collective-permute-done.42), channel_id=1, source_target_pairs={{1,0},{5,4},{9,8},{13,12},{17,16},{21,20},{25,24},{29,28}} | collective-permute-start | bytes 6291464 | tf_op jit(solution)/shard_map/ppermute | solution.py:638
  1016.5 70.5 %collective-permute-start.47 = (bf16[512,2048]{1,0:T(8,128)(2,1)}, bf16[512,2048]{1,0:T(8,128)(2,1)}, u32[]{:S(2)}, u32[]{:S(2)}) collective-permute-start(bf16[512,2048]{1,0:T(8,128)(2,1)} %collective-permute-done.43), channel_id=1, source_target_pairs={{2,3},{6,7},{10,11},{14,15},{18,19},{22,23},{26,27},{30,31}} | collective-permute-start | bytes 6291464 | tf_op jit(solution)/shard_map/ppermute | solution.py:637
  1018.5 105.6 %collective-permute-start.48 = (bf16[512,2048]{1,0:T(8,128)(2,1)}, bf16[512,2048]{1,0:T(8,128)(2,1)}, u32[]{:S(2)}, u32[]{:S(2)}) collective-permute-start(bf16[512,2048]{1,0:T(8,128)(2,1)} %collective-permute-done.44), channel_id=1, source_target_pairs={{1,0},{5,4},{9,8},{13,12},{17,16},{21,20},{25,24},{29,28}} | collective-permute-start | bytes 6291464 | tf_op jit(solution)/shard_map/ppermute | solution.py:638
  1081.1 43.0 %collective-permute-start.49 = (bf16[256,768]{1,0:T(8,128)(2,1)S(1)}, bf16[256,768]{1,0:T(8,128)(2,1)S(1)}, u32[]{:S(2)}, u32[]{:S(2)}) collective-permute-start(bf16[256,768]{1,0:T(8,128)(2,1)S(1)} %get-tuple-element.462), channel_id=1, source_target_pairs={{0,1},{1,2},{2,3},{3,0},{4,5},{5,6},{6,7},{7,4},{8,9},{9,10},{10,1... | collective-permute-start | bytes 1179656 | tf_op jit(solution)/shard_map/ppermute | solution.py:700
  1081.2 42.9 %collective-permute-start.50 = (bf16[256,768]{1,0:T(8,128)(2,1)S(1)}, bf16[256,768]{1,0:T(8,128)(2,1)S(1)}, u32[]{:S(2)}, u32[]{:S(2)}) collective-permute-start(bf16[256,768]{1,0:T(8,128)(2,1)S(1)} %get-tuple-element.463), channel_id=1, source_target_pairs={{0,2},{1,3},{2,0},{3,1},{4,6},{5,7},{6,4},{7,5},{8,10},{9,11},{10,... | collective-permute-start | bytes 1179656 | tf_op jit(solution)/shard_map/ppermute | solution.py:700
  1081.3 46.9 %collective-permute-start.51 = (bf16[256,768]{1,0:T(8,128)(2,1)S(1)}, bf16[256,768]{1,0:T(8,128)(2,1)S(1)}, u32[]{:S(2)}, u32[]{:S(2)}) collective-permute-start(bf16[256,768]{1,0:T(8,128)(2,1)S(1)} %get-tuple-element.461), channel_id=1, source_target_pairs={{0,3},{1,0},{2,1},{3,2},{4,7},{5,4},{6,5},{7,6},{8,11},{9,8},{10,9... | collective-permute-start | bytes 1179656 | tf_op jit(solution)/shard_map/ppermute | solution.py:700
  (79 other events, 313.2 us)
Sparse Core Ops, SparseCore 0:
  108.0 111.5 all-gather.4
  225.3 89.2 all-gather.6
  316.9 90.7 reduce-scatter.6
  410.0 93.8 reduce-scatter.8
  505.9 105.9 reduce-scatter.10
  614.1 111.4 reduce-scatter.12
  777.1 96.1 reduce-scatter.16
  898.6 118.5 reduce-scatter.14

commit v8 on v7

--- a/solution.py
+++ b/solution.py
@@ -517,6 +517,7 @@
         jax.ShapeDtypeStruct((rows, width), BF16),
         jax.ShapeDtypeStruct((rows, units), BF16),
         jax.ShapeDtypeStruct((rows, 2 * units), BF16),
+        jax.ShapeDtypeStruct((rows, width), BF16),
     ]
     gain = gain.reshape(1, width)
     return pl.pallas_call(
@@ -532,8 +533,8 @@
         + [whole(weight) for weight in weights]
         + [pl.BlockSpec(memory_space=pl.ANY) for _ in earlier],
         out_specs=[natural(shape.shape[1]) for shape in shapes]
-        + [pl.BlockSpec((block, width), lambda i: (i, 0))] * 2,
-        out_shape=shapes + [jax.ShapeDtypeStruct((rows // 2, width), BF16)] * 2,
+        + [pl.BlockSpec((block, width), lambda i: (i, 0))],
+        out_shape=shapes + [jax.ShapeDtypeStruct((rows // 2, width), BF16)],
         input_output_aliases={8 + k: k for k in range(len(earlier))},
         compiler_params=pltpu.CompilerParams(vmem_limit_bytes=60 * 2**20),
         cost_estimate=LIGHT,
@@ -898,18 +899,16 @@
     hop = query_gather.step()
     weights = (w_gate, w_up, w_down)
     fixed = (tokens, cotangent, norm_mlp, output_whole, weights)
-    *fed, down_first, grad_first = feed_forward(0, first_whole, *fixed, ())
-    fed, down_first, grad_first, second_whole, hop = hold(
-        fed, down_first, grad_first, second_whole, hop
-    )
+    *fed, grad_first = feed_forward(0, first_whole, *fixed, ())
+    fed, grad_first, second_whole, hop = hold(fed, grad_first, second_whole, hop)
     query_gather.held(hop)
 
     share_first = line_sum(grad_first)
     hop = query_gather.step()
-    *fed, down_second, grad_second = feed_forward(1, second_whole, *fixed, fed)
-    fed, down_second, grad_second, hop = hold(fed, down_second, grad_second, hop)
+    *fed, grad_second = feed_forward(1, second_whole, *fixed, fed)
+    fed, grad_second, hop = hold(fed, grad_second, hop)
     query_gather.held(hop)
-    middle, normed_mlp, hidden, gates = fed
+    middle, normed_mlp, hidden, gates, mlp_part = fed
 
     share_second = line_sum(grad_second)
     hop = query_gather.step()
@@ -917,7 +916,7 @@
     w_gates, hop, share_first = hold(w_gates, hop, share_first)
     query_gather.held(hop)
 
-    mixed_shares = [line_sum(after(down, w_gates)) for down in (down_first, down_second)]
+    mlp_share = line_sum(after(mlp_part, w_gates))
 
     gain_first, middle_first, low_first, blocks = to_attention(0, middle, share_first)
     query_part = query_gather.whole()
@@ -928,7 +927,8 @@
     came_first = send_blocks(block_of(blocks))
     query_over = lax.ppermute(query_part, "ctx", over)
     w_downs = t_dot(cotangent, hidden).astype(BF16)
-    middle_own = [own_rows(middle, c) for c in chunks]
+    n_part = tok_rows // groups
+    middle_own = lax.dynamic_slice_in_dim(middle, member * n_part, n_part, 0)
     came_first, middle_own, query_part, query_over, w_downs = hold(
         came_first, middle_own, query_part, query_over, w_downs
     )
@@ -1016,14 +1016,15 @@
         return target
 
     gains = jnp.stack([attn_gain, gain_first + gain_second], axis=1).astype(BF16)
-    grad_inputs, gains, dq_second, kv_far, kv_near, w_gates = hold(
-        grad_inputs, gains, dq_second, kv_far, kv_near, w_gates
+    mixed_share = (middle_own + mlp_share.astype(F32)).astype(BF16)
+    grad_inputs, gains, dq_second, kv_far, kv_near, w_gates, mixed_share = hold(
+        grad_inputs, gains, dq_second, kv_far, kv_near, w_gates, mixed_share
     )
     gate_up_grad = plane_sum(w_gates)
 
-    mixed_share = jnp.concatenate(
-        [(middle_own[c] + mixed_shares[c].astype(F32)).astype(BF16) for c in chunks], axis=0
-    )
+    def put_share(target, piece, source):
+        return lax.dynamic_update_slice_in_dim(target, piece, source * n_part, 0)
+
     tokens_gather, mixed_gather = Gather(grad_inputs), Gather(mixed_share)
     tokens_grad = jnp.zeros((tok_rows, width), BF16)
     mixed = jnp.zeros((tok_rows, width), BF16)
@@ -1047,14 +1048,14 @@
     hop, mixed_hop = tokens_gather.step(), mixed_gather.step()
     for count in range(2):
         tokens_grad = tokens_gather.place_hop(put_rows, tokens_grad, count)
-        mixed = mixed_gather.place_hop(put_rows, mixed, count)
+        mixed = mixed_gather.place_hop(put_share, mixed, count)
     hop, mixed_hop, tokens_grad, mixed = hold(hop, mixed_hop, tokens_grad, mixed)
     tokens_gather.held(hop)
     mixed_gather.held(mixed_hop)
 
     hop = tokens_gather.step()
     tokens_grad = tokens_gather.place_hop(put_rows, tokens_grad, 2)
-    mixed = mixed_gather.place_hop(put_rows, mixed, 2)
+    mixed = mixed_gather.place_hop(put_share, mixed, 2)
     hop, tokens_grad, mixed = hold(hop, tokens_grad, mixed)
     tokens_gather.held(hop)
 
@@ -1082,7 +1083,7 @@
     )
     gains = jnp.sum(blocks[:, :, features + 2 * HD : features + 2 * HD + 2], axis=0).T
     for count in range(3, groups):
-        mixed = mixed_gather.place_hop(put_rows, mixed, count)
+        mixed = mixed_gather.place_hop(put_share, mixed, count)
         if count + 1 < groups:
             tokens_gather.step()
             mixed_gather.step()

time: 1150 us -> 1140 us (level)
  starting transfers between devices: 123 us -> 101 us
  waiting for transfers between devices: 339 us -> 352 us
    pallas_call x1, Pallas kernels: 34.1 us -> 67 us  [attend_back_first(): pl.pallas_call(kernel, grid_spec=pltpu.PrefetchScalarGridSpec(num_scalar_...]
    pallas_call x1, Pallas kernels: 81.9 us -> 49 us  [attend_back_last(): pl.pallas_call(kernel, grid_spec=pltpu.PrefetchScalarGridSpec(num_scalar_...]
    pallas_call x1, Pallas kernels: 28 us -> 51.6 us  [attend_first(): pl.pallas_call(kernel, grid_spec=pltpu.PrefetchScalarGridSpec(num_scalar_...]
    pallas_call x1, Pallas kernels: 56.9 us -> 33.5 us  [attend(): pl.pallas_call(kernel, grid_spec=pltpu.PrefetchScalarGridSpec(num_scalar_...]
    ppermute x1, starting transfers between devices: 21.6 us -> 0.01 us  [body(): output_far = lax.ppermute(output_near, 'dp', beside)]
    ppermute x1, starting transfers between devices: 0.07 us -> 14.3 us  [body(): second_home = lax.ppermute(second, 'ctx', over)]
    unnamed x164 -> x160, local copies, waits for them, and re-layouts: 23.5 us -> 21.8 us
  transfers between devices with their start and end apart: 60 -> 59, of which waited for: 18 -> 18; matrix products, arithmetic and copies ran while one was open for 20% -> 19% of each run, Pallas kernels for 32% -> 33%
where the time goes in v8:
time: 1140 us; the launch traced here: 1130 us
  Pallas kernels  371 us (33%)
  waiting for transfers between devices  352 us (31%)
  starting transfers between devices  101 us (9%)
  local copies, waits for them, and re-layouts  93.5 us (8%)
  matrix products  82.3 us (7%)
  other arithmetic  77.7 us (7%)
  between operations  49.7 us (4%)
    ppermute x12, waiting for transfers between devices, step(): self.lefts.append(lax.ppermute(self.lefts[-1], 'tensor', to_left))  185 us
    pallas_call x2, Pallas kernels, feed_forward(): pl.pallas_call(feed_kernel, grid=(2 * quarter,), in_specs=[pl.BlockSpec((...  124 us
    dot_general x4, matrix products, t_dot(): return jnp.einsum('rd,rf->df', a, b, preferred_element_type=F32)  68.1 us
    pallas_call x1, Pallas kernels, attend_back_first(): pl.pallas_call(kernel, grid_spec=pltpu.PrefetchScalarGridSpec(num_scalar_...  67 us
    pallas_call x1, Pallas kernels, attend_first(): pl.pallas_call(kernel, grid_spec=pltpu.PrefetchScalarGridSpec(num_scalar_...  51.6 us
    ppermute x12, waiting for transfers between devices, send_blocks(): lax.ppermute(block, 'tensor', [(i, (i + shift) % size) for i in range(siz...  51.3 us
    pallas_call x1, Pallas kernels, attend_back_last(): pl.pallas_call(kernel, grid_spec=pltpu.PrefetchScalarGridSpec(num_scalar_...  49 us
    pallas_call x1, Pallas kernels, attend(): pl.pallas_call(kernel, grid_spec=pltpu.PrefetchScalarGridSpec(num_scalar_...  33.5 us
  transfers between devices with their start and end apart: 59, of which 18 were waited for; matrix products, arithmetic and copies ran while one was open for 19% of the time, Pallas kernels for 33%

profile of v8, /device:TPU:0, one launch (start us, length us, event | category | flops | bytes accessed | tf_op | source)
XLA Modules:
  0.0 1127.2 jit_solution(15711382106586728973)
XLA Ops:
  9.8 5.9 collective-permute-start
  17.3 5.4 multiply_sine_fusion.1
  26.2 17.5 %project.1 = (bf16[2048,128]{1,0:T(8,128)(2,1)S(1)}, bf16[2048,512]{1,0:T(8,128)(2,1)}, bf16[2048,2048]{1,0:T(8,128)(2,1)}, f32[2048,128]{1,0:T(8,128)S(1)}, f32[2048,128]{1,0:T(8,128)S(1)}) custom-call(s32[1]{0:T(128)} %bitcast.1.head, bf16[2048,2048]{1,0:T(8,128)(2,1)} %tokens_ref.5, f32[1,2048]{1,0:T(1,128)S(1)} %bitcast.150, ...), custom_call_target="tpu_custom_call" | custom-call | flops 1 | bytes 1 | tf_op jit(solution)/shard_map/project/pallas_call | solution.py:68
  53.3 8.0 collective-permute-done.2.other
  61.4 14.0 %collective-permute-done.4.refs_2_ = bf16[1024,512]{1,0:T(8,128)(2,1)S(1)} collective-permute-done((bf16[1024,512]{1,0:T(8,128)(2,1)}, bf16[1024,512]{1,0:T(8,128)(2,1)S(1)}, u32[]{:S(2)}, u32[]{:S(2)}) %collective-permute-start.4) | collective-permute-done | bytes 1048608 | tf_op jit(solution)/shard_map/ppermute | solution.py:639
  78.9 51.6 %attend_first.1 = (bf16[1024,512]{1,0:T(8,128)(2,1)}, f32[4,8,1024]{2,1,0:T(8,128)}, bf16[4096,128]{1,0:T(8,128)(2,1)}, bf16[4096,128]{1,0:T(8,128)(2,1)}, bf16[...) custom-call(s32[6]{0:T(128)} %get-tuple-element.492.meta.refs_0_, ...), custom_call_target="tpu_custom_call" | custom-call | flops 17179869184 | bytes 8388608 | tf_op jit(solution)/shard_map/attend_first/pallas_call | solution.py:208
  135.3 6.9 arrange.3.refs_0_
  144.2 33.5 %attend.1 = (bf16[1024,512]{1,0:T(8,128)(2,1)}, f32[4,8,1024]{2,1,0:T(8,128)}) custom-call(s32[6]{0:T(128)} %get-tuple-element.491.refs_0_, bf16[1024,512]{1,0:T(8,128)(2,1)} %collective-permute-done.5.refs_1_, bf16[4096,128]{1,0:T(8,128)(2,1)} %get-tuple-element.214.refs_2_.refs_5_, bf16[4096,128]{1,0:T(8,128)(2,1)} %get-tuple-element.215.refs_3_.refs_6_, ...), custom_call_target="tpu_custom_call" | custom-call | flops 17179869184 | bytes 8388608 | tf_op jit(solution)/shard_map/attend/pallas_call | solution.py:245
  177.7 14.3 %collective-permute-start.9 = (bf16[1024,512]{1,0:T(8,128)(2,1)}, bf16[1024,512]{1,0:T(8,128)(2,1)}, u32[]{:S(2)}, u32[]{:S(2)}) collective-permute-start(bf16[1024,512]{1,0:T(8,128)(2,1)} %get-tuple-element.221.refs_2_), channel_id=1, source_target_pairs={{0,4},{4,0},{1,5},{5,1},{2,6},{6,2},{3,7},{7,3},{8,12},{12,8},{9,1... | collective-permute-start | bytes 3145736 | tf_op jit(solution)/shard_map/ppermute | solution.py:842
  194.2 6.4 arrange.4.output_weight
  200.6 3.7 multiply_sine_fusion
  206.3 3.7 maximum_maximum_fusion
  210.0 4.4 collective-permute-done.9
  214.5 6.1 all-gather.5.cloned.1.call-done
  224.3 62.4 %feed_forward.2 = (f32[2048,2048]{1,0:T(8,128)}, bf16[2048,2048]{1,0:T(8,128)(2,1)}, bf16[2048,1408]{1,0:T(8,128)(2,1)}, bf16[2048,2816]{1,0:T(8,128)(2,1)}, bf1...) custom-call(bf16[4,1024,512]{2,1,0:T(8,128)(2,1)} %bitcast.157, bf16[2048,2048]{1,0:T(8,128)(2,1)} %tokens_ref.5, ...), custom_call_target="tpu_custom_call" | custom-call | flops 1 | bytes 1 | tf_op jit(solution)/shard_map/feed_forward/pallas_call | solution.py:523
  286.7 21.3 %all-gather.7.cloned.1.call-done = bf16[4096,512]{1,0:T(8,128)(2,1)} async-done(((bf16[1024,512]{1,0:T(8,128)(2,1)}), bf16[4096,512]{1,0:T(8,128)(2,1)}) %all-gather.7.cloned.1.call-update) | async-done | bytes 4194320 | tf_op jit(solution)/shard_map/all_gather | solution.py:854
  319.3 61.8 %feed_forward.3 = (f32[2048,2048]{1,0:T(8,128)}, bf16[2048,2048]{1,0:T(8,128)(2,1)}, bf16[2048,1408]{1,0:T(8,128)(2,1)}, bf16[2048,2816]{1,0:T(8,128)(2,1)}, bf1...) custom-call(bf16[4,1024,512]{2,1,0:T(8,128)(2,1)} %bitcast.159, ...), custom_call_target="tpu_custom_call", output_to_operand_aliasing={{0}: (8, {}), {1}: (9, {}), {2}: (10, {}), {3}: (11, {}), {... | custom-call | flops 1 | bytes 1 | tf_op jit(solution)/shard_map/feed_forward/pallas_call | solution.py:523
  383.1 2.6 multiply_reduce_fusion
  385.8 31.7 %convolution_convert_fusion = bf16[2048,2816]{1,0:T(8,128)(2,1)} fusion(bf16[2048,2048]{1,0:T(8,128)(2,1)} %get-tuple-element.252, bf16[2048,2816]{1,0:T(8,128)(2,1)} %get-tuple-element.253), kind=kOutput, calls=%fused_computation.3 | convolution fusion | flops 23628087296 | bytes 31457280 | tf_op jit(solution)/shard_map/rd,rf->df/dot_general | solution.py:733
  417.5 4.9 constant_dynamic-slice_fusion.36
  422.4 2.8 fusion.26
  426.5 3.9 fusion.54
  431.4 6.0 fusion.41
  449.1 2.9 collective-permute-start.18
  452.0 19.6 %fusion.2 = bf16[2048,1408]{1,0:T(8,128)(2,1)} fusion(bf16[2048,1408]{1,0:T(8,128)(2,1)} %get-tuple-element.265, bf16[2048,2048]{1,0:T(8,128)(2,1)} %cotangent_ref.3), kind=kOutput, calls=%fused_computation.10 | convolution fusion | flops 11814043648 | bytes 19922944 | tf_op jit(solution)/shard_map/rd,rf->df/dot_general | solution.py:733
  473.4 6.9 collective-permute-done.17
  480.3 7.2 collective-permute-done.19.refs_1_
  495.0 10.0 reduce-scatter.8.cloned.1.call-done
  505.0 2.6 fusion.23
  507.6 3.9 fusion.52
  511.5 6.1 fusion.42
  520.9 7.7 collective-permute-start.23
  530.5 3.8 collective-permute-start.25
  548.9 67.0 %attend_back_first.1 = (bf16[1024,512]{1,0:T(8,128)(2,1)}, f32[4096,128]{1,0:T(8,128)}, f32[4096,128]{1,0:T(8,128)}) custom-call(s32[6]{0:T(128)} %get-tuple-element.492.meta.refs_0_, bf16[1024,512]{1,0:T(8,128)(2,1)} %pad_maximum_fusion.2.q_ref.refs_1_, bf16[1024,512]{1,0:T(8,128)(2,1)} %get-tuple-element.212.refs_2_, bf16[1024,512]{1,0:T(8,128)(2,1)} %bitcast.163, ...), custom_call_target="tpu_custom_call" | custom-call | flops 1 | bytes 1 | tf_op jit(solution)/shard_map/attend_back_first/pallas_call | solution.py:381
  624.7 49.0 %attend_back_last.1 = (bf16[1024,512]{1,0:T(8,128)(2,1)}, f32[2048,128]{1,0:T(8,128)}, bf16[2048,128]{1,0:T(8,128)(2,1)}) custom-call(s32[6]{0:T(128)} %get-tuple-element.491.refs_0_, bf16[1024,512]{1,0:T(8,128)(2,1)} %collective-permute-done.5.refs_1_, bf16[1024,512]{1,0:T(8,128)(2,1)} %get-tuple-element.221.refs_2_, bf16[1024,512]{1,0:T(8,128)(2,1)} %bitcast.164, ...), custom_call_target="tpu_custom_call" | custom-call | flops 1 | bytes 1 | tf_op jit(solution)/shard_map/attend_back_last/pallas_call | solution.py:436
  677.8 4.3 copy.90
  686.8 3.4 collective-permute-start.33
  693.3 6.8 convolution_convert_fusion.1
  701.1 17.1 %collective-permute-done.31 = bf16[256,256]{1,0:T(8,128)(2,1)S(1)} collective-permute-done((bf16[256,256]{1,0:T(8,128)(2,1)S(1)}, bf16[256,256]{1,0:T(8,128)(2,1)S(1)}, u32[]{:S(2)}, u32[]{:S(2)}) %collective-permute-start.31) | collective-permute-done | bytes 131104 | tf_op jit(solution)/shard_map/ppermute | solution.py:701
  719.6 23.1 %collective-permute-done.30 = bf16[256,256]{1,0:T(8,128)(2,1)S(1)} collective-permute-done((bf16[256,256]{1,0:T(8,128)(2,1)S(1)}, bf16[256,256]{1,0:T(8,128)(2,1)S(1)}, u32[]{:S(2)}, u32[]{:S(2)}) %collective-permute-start.30) | collective-permute-done | bytes 131104 | tf_op jit(solution)/shard_map/ppermute | solution.py:701
  743.7 6.6 join.2
  750.8 6.6 join.3
  761.8 3.3 fusion.6
  765.1 3.6 add_convert_fusion
  774.1 4.1 collective-permute-start.36
  779.5 6.1 collective-permute-start.38
  787.9 29.2 %collective-permute-done.40 = bf16[1024,768]{1,0:T(8,128)(2,1)} collective-permute-done((bf16[1024,768]{1,0:T(8,128)(2,1)}, bf16[1024,768]{1,0:T(8,128)(2,1)}, u32[]{:S(2)}, u32[]{:S(2)}) %collective-permute-start.40) | collective-permute-done | bytes 1572896 | tf_op jit(solution)/shard_map/ppermute | solution.py:1032
  820.0 10.0 convolution_convert_fusion.3
  830.0 6.9 fusion.1
  836.9 28.6 %collective-permute-done.38 = bf16[512,2048]{1,0:T(8,128)(2,1)} collective-permute-done((bf16[512,2048]{1,0:T(8,128)(2,1)S(1)}, bf16[512,2048]{1,0:T(8,128)(2,1)}, u32[]{:S(2)}, u32[]{:S(2)}) %collective-permute-start.38) | collective-permute-done | bytes 2097184 | tf_op jit(solution)/shard_map/ppermute | solution.py:638
  865.6 5.5 collective-permute-done.39
  887.5 5.6 broadcast.124.clone
  893.1 2.5 slice_dynamic-update-slice_fusion.9
  903.5 2.6 broadcast_select_fusion
  913.6 38.8 %collective-permute-done.42 = bf16[512,2048]{1,0:T(8,128)(2,1)S(1)} collective-permute-done((bf16[512,2048]{1,0:T(8,128)(2,1)}, bf16[512,2048]{1,0:T(8,128)(2,1)S(1)}, u32[]{:S(2)}, u32[]{:S(2)}) %collective-permute-start.42) | collective-permute-done | bytes 2097184 | tf_op jit(solution)/shard_map/ppermute | solution.py:639
  952.4 41.9 %collective-permute-done.44 = bf16[512,2048]{1,0:T(8,128)(2,1)} collective-permute-done((bf16[512,2048]{1,0:T(8,128)(2,1)}, bf16[512,2048]{1,0:T(8,128)(2,1)}, u32[]{:S(2)}, u32[]{:S(2)}) %collective-permute-start.44) | collective-permute-done | bytes 2097184 | tf_op jit(solution)/shard_map/ppermute | solution.py:639
  1002.3 3.4 select_dynamic-update-slice_fusion.1
  1005.7 3.4 copy-done.31
  1009.1 36.4 %collective-permute-done.46 = bf16[512,2048]{1,0:T(8,128)(2,1)S(1)} collective-permute-done((bf16[512,2048]{1,0:T(8,128)(2,1)S(1)}, bf16[512,2048]{1,0:T(8,128)(2,1)S(1)}, u32[]{:S(2)}, u32[]{:S(2)}) %collective-permute-start.46) | collective-permute-done | bytes 2097184 | tf_op jit(solution)/shard_map/ppermute | solution.py:639
  1048.2 3.1 slice_convert_fusion
  1054.0 2.7 collective-permute-start.51
  1058.7 48.7 %collective-permute-done.48 = bf16[512,2048]{1,0:T(8,128)(2,1)} collective-permute-done((bf16[512,2048]{1,0:T(8,128)(2,1)}, bf16[512,2048]{1,0:T(8,128)(2,1)}, u32[]{:S(2)}, u32[]{:S(2)}) %collective-permute-start.48) | collective-permute-done | bytes 2097184 | tf_op jit(solution)/shard_map/ppermute | solution.py:639
  1107.4 4.2 collective-permute-done.51
  1115.8 4.3 select_dynamic-update-slice_fusion
  (403 shorter events, 149.2 us)
Async XLA Ops:
  7.2 213.4 %all-gather.5.cloned.1.call-start = ((), (), s32[]{:S(2)}) async-start(), calls=%async_computation.10 | async-start | bytes 5242880 | tf_op jit(solution)/shard_map/all_gather | solution.py:829
  9.8 35.7 %collective-permute-start = (bf16[1024,512]{1,0:T(8,128)(2,1)}, bf16[1024,512]{1,0:T(8,128)(2,1)}, u32[]{:S(2)}, u32[]{:S(2)}) collective-permute-start(bf16[1024,512]{1,0:T(8,128)(2,1)} %constant_dynamic-slice_fusion.42.refs_6_), channel_id=1, source_target_pairs={{0,1},{1,2},{2,3},{4,5},{5,6},{6,7},{8,9},{9,10},{10,11},{12,13},{... | collective-permute-start | bytes 3145736 | tf_op jit(solution)/shard_map/ppermute | solution.py:638
  15.7 29.8 %collective-permute-start.1 = (bf16[1024,512]{1,0:T(8,128)(2,1)}, bf16[1024,512]{1,0:T(8,128)(2,1)}, u32[]{:S(2)}, u32[]{:S(2)}) collective-permute-start(bf16[1024,512]{1,0:T(8,128)(2,1)} %constant_dynamic-slice_fusion.42.refs_6_), channel_id=1, source_target_pairs={{1,0},{2,1},{3,2},{5,4},{6,5},{7,6},{9,8},{10,9},{11,10},{13,12},{... | collective-permute-start | bytes 3145736 | tf_op jit(solution)/shard_map/ppermute | solution.py:639
  45.5 15.8 %collective-permute-start.3 = (bf16[1024,512]{1,0:T(8,128)(2,1)}, bf16[1024,512]{1,0:T(8,128)(2,1)S(1)}, u32[]{:S(2)}, u32[]{:S(2)}) collective-permute-start(bf16[1024,512]{1,0:T(8,128)(2,1)} %collective-permute-done.refs_5_), channel_id=1, source_target_pairs={{1,2},{2,3},{5,6},{6,7},{9,10},{10,11},{13,14},{14,15},{17,18},{18... | collective-permute-start | bytes 3145736 | tf_op jit(solution)/shard_map/ppermute | solution.py:638
  46.4 29.0 %collective-permute-start.4 = (bf16[1024,512]{1,0:T(8,128)(2,1)}, bf16[1024,512]{1,0:T(8,128)(2,1)S(1)}, u32[]{:S(2)}, u32[]{:S(2)}) collective-permute-start(bf16[1024,512]{1,0:T(8,128)(2,1)} %collective-permute-done.1.refs_4_), channel_id=1, source_target_pairs={{1,0},{2,1},{5,4},{6,5},{9,8},{10,9},{13,12},{14,13},{17,16},{18,1... | collective-permute-start | bytes 3145736 | tf_op jit(solution)/shard_map/ppermute | solution.py:639
  47.7 13.6 %collective-permute-start.2 = (bf16[2048,128]{1,0:T(8,128)(2,1)}, bf16[2048,128]{1,0:T(8,128)(2,1)S(1)}, u32[]{:S(2)}, u32[]{:S(2)}) collective-permute-start(bf16[2048,128]{1,0:T(8,128)(2,1)} %copy-done.24), channel_id=1, source_target_pairs={{0,4},{4,0},{1,5},{5,1},{2,6},{6,2},{3,7},{7,3},{8,12},{12,8},{9,1... | collective-permute-start | bytes 1572872 | tf_op jit(solution)/shard_map/ppermute | solution.py:815
  61.3 69.1 %copy-start.8 = (bf16[1024,512]{1,0:T(8,128)(2,1)}, bf16[1024,512]{1,0:T(8,128)(2,1)S(1)}, u32[]{:S(2)}) copy-start(bf16[1024,512]{1,0:T(8,128)(2,1)S(1)} %collective-permute-done.3.refs_3_) | copy-start | bytes 3145732
  75.3 55.1 %copy-start.10 = (bf16[1024,512]{1,0:T(8,128)(2,1)}, bf16[1024,512]{1,0:T(8,128)(2,1)S(1)}, u32[]{:S(2)}) copy-start(bf16[1024,512]{1,0:T(8,128)(2,1)S(1)} %collective-permute-done.4.refs_2_) | copy-start | bytes 3145732
  75.3 55.1 %collective-permute-start.5 = (bf16[1024,512]{1,0:T(8,128)(2,1)}, bf16[1024,512]{1,0:T(8,128)(2,1)}, u32[]{:S(2)}, u32[]{:S(2)}) collective-permute-start(bf16[1024,512]{1,0:T(8,128)(2,1)} %slice.207), channel_id=1, source_target_pairs={{0,4},{4,0},{1,5},{5,1},{2,6},{6,2},{3,7},{7,3},{8,12},{12,8},{9,1... | collective-permute-start | bytes 3145736 | tf_op jit(solution)/shard_map/ppermute | solution.py:823
  76.8 53.6 %collective-permute-start.6 = (bf16[1024,512]{1,0:T(8,128)(2,1)S(1)}, bf16[1024,512]{1,0:T(8,128)(2,1)S(1)}, u32[]{:S(2)}, u32[]{:S(2)}) collective-permute-start(bf16[1024,512]{1,0:T(8,128)(2,1)S(1)} %collective-permute-done.3.refs_3_), channel_id=1, source_target_pairs={{2,3},{6,7},{10,11},{14,15},{18,19},{22,23},{26,27},{30,31}} | collective-permute-start | bytes 3145736 | tf_op jit(solution)/shard_map/ppermute | solution.py:638
  77.5 53.9 %collective-permute-start.7 = (bf16[1024,512]{1,0:T(8,128)(2,1)S(1)}, bf16[1024,512]{1,0:T(8,128)(2,1)}, u32[]{:S(2)}, u32[]{:S(2)}) collective-permute-start(bf16[1024,512]{1,0:T(8,128)(2,1)S(1)} %collective-permute-done.4.refs_2_), channel_id=1, source_target_pairs={{1,0},{5,4},{9,8},{13,12},{17,16},{21,20},{25,24},{29,28}} | collective-permute-start | bytes 3145736 | tf_op jit(solution)/shard_map/ppermute | solution.py:639
  131.5 176.5 %all-gather.7.cloned.1.call-start = ((), (), s32[]{:S(2)}) async-start(), calls=%async_computation.11 | async-start | bytes 5242880 | tf_op jit(solution)/shard_map/all_gather | solution.py:854
  142.3 35.4 %collective-permute-start.8 = (bf16[4,1024,512]{2,1,0:T(8,128)(2,1)}, bf16[4,1024,512]{2,1,0:T(8,128)(2,1)}, u32[]{:S(2)}, u32[]{:S(2)}) collective-permute-start(bf16[4,1024,512]{2,1,0:T(8,128)(2,1)} %arrange.3.refs_0_), channel_id=1, source_target_pairs={{0,8},{8,0},{16,24},{24,16},{1,9},{9,1},{17,25},{25,17},{2,10},{10... | collective-permute-start | bytes 12582920 | tf_op jit(solution)/shard_map/ppermute | solution.py:832
  177.7 36.7 %collective-permute-start.9 = (bf16[1024,512]{1,0:T(8,128)(2,1)}, bf16[1024,512]{1,0:T(8,128)(2,1)}, u32[]{:S(2)}, u32[]{:S(2)}) collective-permute-start(bf16[1024,512]{1,0:T(8,128)(2,1)} %get-tuple-element.221.refs_2_), channel_id=1, source_target_pairs={{0,4},{4,0},{1,5},{5,1},{2,6},{6,2},{3,7},{7,3},{8,12},{12,8},{9,1... | collective-permute-start | bytes 3145736 | tf_op jit(solution)/shard_map/ppermute | solution.py:842
  214.4 208.0 %reduce-scatter.6.cloned.1.call-start = ((), (), s32[]{:S(2)}) async-start(), calls=%async_computation.5 | async-start | bytes 5242880 | tf_op jit(solution)/shard_map/reduce_scatter | solution.py:891
  221.7 65.0 %collective-permute-start.10 = (bf16[512,512]{1,0:T(8,128)(2,1)S(1)}, bf16[512,512]{1,0:T(8,128)(2,1)S(1)}, u32[]{:S(2)}, u32[]{:S(2)}) collective-permute-start(bf16[512,512]{1,0:T(8,128)(2,1)S(1)} %constant_dynamic-slice_fusion.41.refs_6_), channel_id=1, source_target_pairs={{0,1},{1,2},{2,3},{4,5},{5,6},{6,7},{8,9},{9,10},{10,11},{12,13},{... | collective-permute-start | bytes 1572872 | tf_op jit(solution)/shard_map/ppermute | solution.py:638
  223.0 63.7 %collective-permute-start.11 = (bf16[512,512]{1,0:T(8,128)(2,1)S(1)}, bf16[512,512]{1,0:T(8,128)(2,1)S(1)}, u32[]{:S(2)}, u32[]{:S(2)}) collective-permute-start(bf16[512,512]{1,0:T(8,128)(2,1)S(1)} %constant_dynamic-slice_fusion.41.refs_6_), channel_id=1, source_target_pairs={{1,0},{2,1},{3,2},{5,4},{6,5},{7,6},{9,8},{10,9},{11,10},{13,12},{... | collective-permute-start | bytes 1572872 | tf_op jit(solution)/shard_map/ppermute | solution.py:639
  308.0 197.0 %reduce-scatter.8.cloned.1.call-start = ((), (), s32[]{:S(2)}) async-start(), calls=%async_computation.6 | async-start | bytes 5242880 | tf_op jit(solution)/shard_map/reduce_scatter | solution.py:891
  315.0 66.1 %collective-permute-start.12 = (bf16[512,512]{1,0:T(8,128)(2,1)S(1)}, bf16[512,512]{1,0:T(8,128)(2,1)S(1)}, u32[]{:S(2)}, u32[]{:S(2)}) collective-permute-start(bf16[512,512]{1,0:T(8,128)(2,1)S(1)} %collective-permute-done.10.refs_5_), channel_id=1, source_target_pairs={{1,2},{2,3},{5,6},{6,7},{9,10},{10,11},{13,14},{14,15},{17,18},{18... | collective-permute-start | bytes 1572872 | tf_op jit(solution)/shard_map/ppermute | solution.py:638
  315.7 65.4 %collective-permute-start.13 = (bf16[512,512]{1,0:T(8,128)(2,1)S(1)}, bf16[512,512]{1,0:T(8,128)(2,1)}, u32[]{:S(2)}, u32[]{:S(2)}) collective-permute-start(bf16[512,512]{1,0:T(8,128)(2,1)S(1)} %collective-permute-done.11.refs_4_), channel_id=1, source_target_pairs={{1,0},{2,1},{5,4},{6,5},{9,8},{10,9},{13,12},{14,13},{17,16},{18,1... | collective-permute-start | bytes 1572872 | tf_op jit(solution)/shard_map/ppermute | solution.py:639
  381.1 41.2 %collective-permute-start.14 = (bf16[512,512]{1,0:T(8,128)(2,1)S(1)}, bf16[512,512]{1,0:T(8,128)(2,1)S(1)}, u32[]{:S(2)}, u32[]{:S(2)}) collective-permute-start(bf16[512,512]{1,0:T(8,128)(2,1)S(1)} %collective-permute-done.12.refs_3_), channel_id=1, source_target_pairs={{2,3},{6,7},{10,11},{14,15},{18,19},{22,23},{26,27},{30,31}} | collective-permute-start | bytes 1572872 | tf_op jit(solution)/shard_map/ppermute | solution.py:638
  381.8 40.5 %collective-permute-start.15 = (bf16[512,512]{1,0:T(8,128)(2,1)}, bf16[512,512]{1,0:T(8,128)(2,1)S(1)}, u32[]{:S(2)}, u32[]{:S(2)}) collective-permute-start(bf16[512,512]{1,0:T(8,128)(2,1)} %collective-permute-done.13.refs_2_), channel_id=1, source_target_pairs={{1,0},{5,4},{9,8},{13,12},{17,16},{21,20},{25,24},{29,28}} | collective-permute-start | bytes 1572872 | tf_op jit(solution)/shard_map/ppermute | solution.py:639
  385.7 379.4 %reduce-scatter.10.cloned.1.call-start = ((), (), s32[]{:S(2)}) async-start(), calls=%async_computation.7 | async-start | bytes 10485760 | tf_op jit(solution)/shard_map/reduce_scatter | solution.py:891
  425.3 622.9 %reduce-scatter.14.cloned.1.call-start = ((), (), s32[]{:S(2)}) async-start(), calls=%async_computation.9 | async-start | bytes 12976128 | tf_op jit(solution)/shard_map/reduce_scatter | solution.py:894
  439.6 47.9 %collective-permute-start.19 = (bf16[4,512,512]{2,1,0:T(8,128)(2,1)S(1)}, bf16[4,512,512]{2,1,0:T(8,128)(2,1)}, u32[]{:S(2)}, u32[]{:S(2)}) collective-permute-start(bf16[4,512,512]{2,1,0:T(8,128)(2,1)S(1)} %arrange.5.refs_0_), channel_id=1, source_target_pairs={{0,4},{4,0},{1,5},{5,1},{2,6},{6,2},{3,7},{7,3},{8,12},{12,8},{9,1... | collective-permute-start | bytes 6291464 | tf_op jit(solution)/shard_map/ppermute | solution.py:928
  443.0 30.5 %collective-permute-start.16 = (bf16[256,512]{1,0:T(8,128)(2,1)}, bf16[256,512]{1,0:T(8,128)(2,1)}, u32[]{:S(2)}, u32[]{:S(2)}) collective-permute-start(bf16[256,512]{1,0:T(8,128)(2,1)} %bitcast.25), channel_id=1, source_target_pairs={{0,1},{1,2},{2,3},{3,0},{4,5},{5,6},{6,7},{7,4},{8,9},{9,10},{10,1... | collective-permute-start | bytes 786440 | tf_op jit(solution)/shard_map/ppermute | solution.py:701
  446.1 34.2 %collective-permute-start.17 = (bf16[256,512]{1,0:T(8,128)(2,1)}, bf16[256,512]{1,0:T(8,128)(2,1)}, u32[]{:S(2)}, u32[]{:S(2)}) collective-permute-start(bf16[256,512]{1,0:T(8,128)(2,1)} %bitcast.26), channel_id=1, source_target_pairs={{0,2},{1,3},{2,0},{3,1},{4,6},{5,7},{6,4},{7,5},{8,10},{9,11},{10,... | collective-permute-start | bytes 786440 | tf_op jit(solution)/shard_map/ppermute | solution.py:701
  449.1 38.9 %copy-start.5 = (bf16[2048,256]{1,0:T(8,128)(2,1)S(1)}, bf16[2048,256]{1,0:T(8,128)(2,1)}, u32[]{:S(2)}) copy-start(bf16[2048,256]{1,0:T(8,128)(2,1)} %v_weight.1) | copy-start | bytes 3145732
  449.1 31.2 %collective-permute-start.18 = (bf16[256,512]{1,0:T(8,128)(2,1)}, bf16[256,512]{1,0:T(8,128)(2,1)}, u32[]{:S(2)}, u32[]{:S(2)}) collective-permute-start(bf16[256,512]{1,0:T(8,128)(2,1)} %bitcast.174), channel_id=1, source_target_pairs={{0,3},{1,0},{2,1},{3,2},{4,7},{5,4},{6,5},{7,6},{8,11},{9,8},{10,9... | collective-permute-start | bytes 786440 | tf_op jit(solution)/shard_map/ppermute | solution.py:701
  487.5 17.5 %collective-permute-start.20 = (bf16[4,512,512]{2,1,0:T(8,128)(2,1)S(1)}, bf16[4,512,512]{2,1,0:T(8,128)(2,1)}, u32[]{:S(2)}, u32[]{:S(2)}) collective-permute-start(bf16[4,512,512]{2,1,0:T(8,128)(2,1)S(1)} %arrange.5.refs_0_), channel_id=1, source_target_pairs={{0,8},{8,0},{16,24},{24,16},{1,9},{9,1},{17,25},{25,17},{2,10},{10... | collective-permute-start | bytes 6291464 | tf_op jit(solution)/shard_map/ppermute | solution.py:937
  487.5 17.5 %collective-permute-start.21 = (bf16[4,512,512]{2,1,0:T(8,128)(2,1)}, bf16[4,512,512]{2,1,0:T(8,128)(2,1)}, u32[]{:S(2)}, u32[]{:S(2)}) collective-permute-start(bf16[4,512,512]{2,1,0:T(8,128)(2,1)} %collective-permute-done.19.refs_1_), channel_id=1, source_target_pairs={{0,8},{8,0},{16,24},{24,16},{1,9},{9,1},{17,25},{25,17},{2,10},{10... | collective-permute-start | bytes 6291464 | tf_op jit(solution)/shard_map/ppermute | solution.py:937
  518.6 97.3 %collective-permute-start.22 = (bf16[256,512]{1,0:T(8,128)(2,1)}, bf16[256,512]{1,0:T(8,128)(2,1)S(1)}, u32[]{:S(2)}, u32[]{:S(2)}) collective-permute-start(bf16[256,512]{1,0:T(8,128)(2,1)} %bitcast.170), channel_id=1, source_target_pairs={{0,4},{1,5},{2,6},{3,7},{4,0},{5,1},{6,2},{7,3},{8,12},{9,13},{10,... | collective-permute-start | bytes 786440 | tf_op jit(solution)/shard_map/ppermute | solution.py:691
  520.9 95.0 %collective-permute-start.23 = (bf16[256,512]{1,0:T(8,128)(2,1)}, bf16[256,512]{1,0:T(8,128)(2,1)S(1)}, u32[]{:S(2)}, u32[]{:S(2)}) collective-permute-start(bf16[256,512]{1,0:T(8,128)(2,1)} %bitcast.171), channel_id=1, source_target_pairs={{0,5},{1,6},{2,7},{3,4},{4,1},{5,2},{6,3},{7,0},{8,13},{9,14},{10,... | collective-permute-start | bytes 786440 | tf_op jit(solution)/shard_map/ppermute | solution.py:691
  529.5 86.5 %collective-permute-start.24 = (bf16[256,512]{1,0:T(8,128)(2,1)}, bf16[256,512]{1,0:T(8,128)(2,1)S(1)}, u32[]{:S(2)}, u32[]{:S(2)}) collective-permute-start(bf16[256,512]{1,0:T(8,128)(2,1)} %bitcast.172), channel_id=1, source_target_pairs={{0,6},{1,7},{2,4},{3,5},{4,2},{5,3},{6,0},{7,1},{8,14},{9,15},{10,... | collective-permute-start | bytes 786440 | tf_op jit(solution)/shard_map/ppermute | solution.py:691
  530.5 85.5 %collective-permute-start.25 = (bf16[256,512]{1,0:T(8,128)(2,1)}, bf16[256,512]{1,0:T(8,128)(2,1)S(1)}, u32[]{:S(2)}, u32[]{:S(2)}) collective-permute-start(bf16[256,512]{1,0:T(8,128)(2,1)} %bitcast.173), channel_id=1, source_target_pairs={{0,7},{1,4},{2,5},{3,6},{4,3},{5,0},{6,1},{7,2},{8,15},{9,12},{10,... | collective-permute-start | bytes 786440 | tf_op jit(solution)/shard_map/ppermute | solution.py:691
  618.9 54.8 %collective-permute-start.26 = (bf16[256,512]{1,0:T(8,128)(2,1)}, bf16[256,512]{1,0:T(8,128)(2,1)}, u32[]{:S(2)}, u32[]{:S(2)}) collective-permute-start(bf16[256,512]{1,0:T(8,128)(2,1)} %get-tuple-element.411), channel_id=1, source_target_pairs={{0,1},{1,2},{2,3},{3,0},{4,5},{5,6},{6,7},{7,4},{8,9},{9,10},{10,1... | collective-permute-start | bytes 786440 | tf_op jit(solution)/shard_map/ppermute | solution.py:701
  618.9 54.8 %collective-permute-start.27 = (bf16[256,512]{1,0:T(8,128)(2,1)S(1)}, bf16[256,512]{1,0:T(8,128)(2,1)}, u32[]{:S(2)}, u32[]{:S(2)}) collective-permute-start(bf16[256,512]{1,0:T(8,128)(2,1)S(1)} %get-tuple-element.410), channel_id=1, source_target_pairs={{0,2},{1,3},{2,0},{3,1},{4,6},{5,7},{6,4},{7,5},{8,10},{9,11},{10,... | collective-permute-start | bytes 786440 | tf_op jit(solution)/shard_map/ppermute | solution.py:701
  620.7 53.0 %collective-permute-start.28 = (bf16[256,512]{1,0:T(8,128)(2,1)S(1)}, bf16[256,512]{1,0:T(8,128)(2,1)}, u32[]{:S(2)}, u32[]{:S(2)}) collective-permute-start(bf16[256,512]{1,0:T(8,128)(2,1)S(1)} %get-tuple-element.409), channel_id=1, source_target_pairs={{0,3},{1,0},{2,1},{3,2},{4,7},{5,4},{6,5},{7,6},{8,11},{9,8},{10,9... | collective-permute-start | bytes 786440 | tf_op jit(solution)/shard_map/ppermute | solution.py:701
  683.3 67.0 %collective-permute-start.35 = (bf16[256,768]{1,0:T(8,128)(2,1)S(1)}, bf16[256,768]{1,0:T(8,128)(2,1)S(1)}, u32[]{:S(2)}, u32[]{:S(2)}) collective-permute-start(bf16[256,768]{1,0:T(8,128)(2,1)S(1)} %pad_maximum_fusion.18), channel_id=1, source_target_pairs={{0,7},{1,4},{2,5},{3,6},{4,3},{5,0},{6,1},{7,2},{8,15},{9,12},{10,... | collective-permute-start | bytes 1179656 | tf_op jit(solution)/shard_map/ppermute | solution.py:691
  685.0 65.4 %collective-permute-start.34 = (bf16[256,768]{1,0:T(8,128)(2,1)S(1)}, bf16[256,768]{1,0:T(8,128)(2,1)S(1)}, u32[]{:S(2)}, u32[]{:S(2)}) collective-permute-start(bf16[256,768]{1,0:T(8,128)(2,1)S(1)} %pad_maximum_fusion.17), channel_id=1, source_target_pairs={{0,6},{1,7},{2,4},{3,5},{4,2},{5,3},{6,0},{7,1},{8,14},{9,15},{10,... | collective-permute-start | bytes 1179656 | tf_op jit(solution)/shard_map/ppermute | solution.py:691
  686.8 63.5 %collective-permute-start.33 = (bf16[256,768]{1,0:T(8,128)(2,1)S(1)}, bf16[256,768]{1,0:T(8,128)(2,1)S(1)}, u32[]{:S(2)}, u32[]{:S(2)}) collective-permute-start(bf16[256,768]{1,0:T(8,128)(2,1)S(1)} %pad_maximum_fusion.16), channel_id=1, source_target_pairs={{0,5},{1,6},{2,7},{3,4},{4,1},{5,2},{6,3},{7,0},{8,13},{9,14},{10,... | collective-permute-start | bytes 1179656 | tf_op jit(solution)/shard_map/ppermute | solution.py:691
  690.4 27.8 %collective-permute-start.31 = (bf16[256,256]{1,0:T(8,128)(2,1)S(1)}, bf16[256,256]{1,0:T(8,128)(2,1)S(1)}, u32[]{:S(2)}, u32[]{:S(2)}) collective-permute-start(bf16[256,256]{1,0:T(8,128)(2,1)S(1)} %pad_maximum_fusion.22), channel_id=1, source_target_pairs={{0,3},{1,0},{2,1},{3,2},{4,7},{5,4},{6,5},{7,6},{8,11},{9,8},{10,9... | collective-permute-start | bytes 393224 | tf_op jit(solution)/shard_map/ppermute | solution.py:701
  692.0 50.7 %collective-permute-start.30 = (bf16[256,256]{1,0:T(8,128)(2,1)S(1)}, bf16[256,256]{1,0:T(8,128)(2,1)S(1)}, u32[]{:S(2)}, u32[]{:S(2)}) collective-permute-start(bf16[256,256]{1,0:T(8,128)(2,1)S(1)} %pad_maximum_fusion.21), channel_id=1, source_target_pairs={{0,2},{1,3},{2,0},{3,1},{4,6},{5,7},{6,4},{7,5},{8,10},{9,11},{10,... | collective-permute-start | bytes 393224 | tf_op jit(solution)/shard_map/ppermute | solution.py:701
  718.2 32.2 %collective-permute-start.32 = (bf16[256,768]{1,0:T(8,128)(2,1)S(1)}, bf16[256,768]{1,0:T(8,128)(2,1)S(1)}, u32[]{:S(2)}, u32[]{:S(2)}) collective-permute-start(bf16[256,768]{1,0:T(8,128)(2,1)S(1)} %pad_maximum_fusion.15), channel_id=1, source_target_pairs={{0,4},{1,5},{2,6},{3,7},{4,0},{5,1},{6,2},{7,3},{8,12},{9,13},{10,... | collective-permute-start | bytes 1179656 | tf_op jit(solution)/shard_map/ppermute | solution.py:691
  742.7 7.6 collective-permute-start.29
  768.7 233.6 %copy-start.25 = (bf16[512,2048]{1,0:T(8,128)(2,1)}, bf16[512,2048]{1,0:T(8,128)(2,1)S(1)}, u32[]{:S(2)}) copy-start(bf16[512,2048]{1,0:T(8,128)(2,1)S(1)} %add_convert_fusion) | copy-start | bytes 6291460
  768.7 282.6 %reduce-scatter.12.cloned.1.call-start = ((), (), s32[]{:S(2)}) async-start(), calls=%async_computation.8 | async-start | bytes 19464192 | tf_op jit(solution)/shard_map/reduce_scatter | solution.py:894
  771.6 45.5 %collective-permute-start.40 = (bf16[1024,768]{1,0:T(8,128)(2,1)}, bf16[1024,768]{1,0:T(8,128)(2,1)}, u32[]{:S(2)}, u32[]{:S(2)}) collective-permute-start(bf16[1024,768]{1,0:T(8,128)(2,1)} %pad_maximum_fusion.1), channel_id=1, source_target_pairs={{0,4},{4,0},{1,5},{5,1},{2,6},{6,2},{3,7},{7,3},{8,12},{12,8},{9,1... | collective-permute-start | bytes 4718600 | tf_op jit(solution)/shard_map/ppermute | solution.py:1032
  774.1 45.6 %copy-start.40 = (f32[2048,128]{1,0:T(8,128)S(1)}, f32[2048,128]{1,0:T(8,128)}, u32[]{:S(2)}) copy-start(f32[2048,128]{1,0:T(8,128)} %get-tuple-element.339) | copy-start | bytes 3145732
  774.1 62.8 %collective-permute-start.36 = (bf16[512,2048]{1,0:T(8,128)(2,1)}, bf16[512,2048]{1,0:T(8,128)(2,1)}, u32[]{:S(2)}, u32[]{:S(2)}) collective-permute-start(bf16[512,2048]{1,0:T(8,128)(2,1)} %fusion.6), channel_id=1, source_target_pairs={{0,1},{1,2},{2,3},{4,5},{5,6},{6,7},{8,9},{9,10},{10,11},{12,13},{... | collective-permute-start | bytes 6291464 | tf_op jit(solution)/shard_map/ppermute | solution.py:638
  778.2 58.7 %collective-permute-start.37 = (bf16[512,2048]{1,0:T(8,128)(2,1)}, bf16[512,2048]{1,0:T(8,128)(2,1)}, u32[]{:S(2)}, u32[]{:S(2)}) collective-permute-start(bf16[512,2048]{1,0:T(8,128)(2,1)} %fusion.6), channel_id=1, source_target_pairs={{1,0},{2,1},{3,2},{5,4},{6,5},{7,6},{9,8},{10,9},{11,10},{13,12},{... | collective-permute-start | bytes 6291464 | tf_op jit(solution)/shard_map/ppermute | solution.py:639
  779.5 86.1 %collective-permute-start.38 = (bf16[512,2048]{1,0:T(8,128)(2,1)S(1)}, bf16[512,2048]{1,0:T(8,128)(2,1)}, u32[]{:S(2)}, u32[]{:S(2)}) collective-permute-start(bf16[512,2048]{1,0:T(8,128)(2,1)S(1)} %add_convert_fusion), channel_id=1, source_target_pairs={{0,1},{1,2},{2,3},{4,5},{5,6},{6,7},{8,9},{9,10},{10,11},{12,13},{... | collective-permute-start | bytes 6291464 | tf_op jit(solution)/shard_map/ppermute | solution.py:638
  785.6 85.5 %collective-permute-start.39 = (bf16[512,2048]{1,0:T(8,128)(2,1)S(1)}, bf16[512,2048]{1,0:T(8,128)(2,1)}, u32[]{:S(2)}, u32[]{:S(2)}) collective-permute-start(bf16[512,2048]{1,0:T(8,128)(2,1)S(1)} %add_convert_fusion), channel_id=1, source_target_pairs={{1,0},{2,1},{3,2},{5,4},{6,5},{7,6},{9,8},{10,9},{11,10},{13,12},{... | collective-permute-start | bytes 6291464 | tf_op jit(solution)/shard_map/ppermute | solution.py:639
  898.1 15.5 %collective-permute-start.41 = (bf16[512,2048]{1,0:T(8,128)(2,1)}, bf16[512,2048]{1,0:T(8,128)(2,1)S(1)}, u32[]{:S(2)}, u32[]{:S(2)}) collective-permute-start(bf16[512,2048]{1,0:T(8,128)(2,1)} %collective-permute-done.36), channel_id=1, source_target_pairs={{1,2},{2,3},{5,6},{6,7},{9,10},{10,11},{13,14},{14,15},{17,18},{18... | collective-permute-start | bytes 6291464 | tf_op jit(solution)/shard_map/ppermute | solution.py:638
  898.9 53.5 %collective-permute-start.42 = (bf16[512,2048]{1,0:T(8,128)(2,1)}, bf16[512,2048]{1,0:T(8,128)(2,1)S(1)}, u32[]{:S(2)}, u32[]{:S(2)}) collective-permute-start(bf16[512,2048]{1,0:T(8,128)(2,1)} %collective-permute-done.37), channel_id=1, source_target_pairs={{1,0},{2,1},{5,4},{6,5},{9,8},{10,9},{13,12},{14,13},{17,16},{18,1... | collective-permute-start | bytes 6291464 | tf_op jit(solution)/shard_map/ppermute | solution.py:639
  900.2 52.2 %collective-permute-start.43 = (bf16[512,2048]{1,0:T(8,128)(2,1)}, bf16[512,2048]{1,0:T(8,128)(2,1)}, u32[]{:S(2)}, u32[]{:S(2)}) collective-permute-start(bf16[512,2048]{1,0:T(8,128)(2,1)} %collective-permute-done.38), channel_id=1, source_target_pairs={{1,2},{2,3},{5,6},{6,7},{9,10},{10,11},{13,14},{14,15},{17,18},{18... | collective-permute-start | bytes 6291464 | tf_op jit(solution)/shard_map/ppermute | solution.py:638
  902.2 92.1 %collective-permute-start.44 = (bf16[512,2048]{1,0:T(8,128)(2,1)}, bf16[512,2048]{1,0:T(8,128)(2,1)}, u32[]{:S(2)}, u32[]{:S(2)}) collective-permute-start(bf16[512,2048]{1,0:T(8,128)(2,1)} %collective-permute-done.39), channel_id=1, source_target_pairs={{1,0},{2,1},{5,4},{6,5},{9,8},{10,9},{13,12},{14,13},{17,16},{18,1... | collective-permute-start | bytes 6291464 | tf_op jit(solution)/shard_map/ppermute | solution.py:639
  994.2 11.4 %collective-permute-start.45 = (bf16[512,2048]{1,0:T(8,128)(2,1)S(1)}, bf16[512,2048]{1,0:T(8,128)(2,1)S(1)}, u32[]{:S(2)}, u32[]{:S(2)}) collective-permute-start(bf16[512,2048]{1,0:T(8,128)(2,1)S(1)} %collective-permute-done.41), channel_id=1, source_target_pairs={{2,3},{6,7},{10,11},{14,15},{18,19},{22,23},{26,27},{30,31}} | collective-permute-start | bytes 6291464 | tf_op jit(solution)/shard_map/ppermute | solution.py:638
  995.0 50.5 %collective-permute-start.46 = (bf16[512,2048]{1,0:T(8,128)(2,1)S(1)}, bf16[512,2048]{1,0:T(8,128)(2,1)S(1)}, u32[]{:S(2)}, u32[]{:S(2)}) collective-permute-start(bf16[512,2048]{1,0:T(8,128)(2,1)S(1)} %collective-permute-done.42), channel_id=1, source_target_pairs={{1,0},{5,4},{9,8},{13,12},{17,16},{21,20},{25,24},{29,28}} | collective-permute-start | bytes 6291464 | tf_op jit(solution)/shard_map/ppermute | solution.py:639
  996.3 62.4 %collective-permute-start.47 = (bf16[512,2048]{1,0:T(8,128)(2,1)}, bf16[512,2048]{1,0:T(8,128)(2,1)}, u32[]{:S(2)}, u32[]{:S(2)}) collective-permute-start(bf16[512,2048]{1,0:T(8,128)(2,1)} %collective-permute-done.43), channel_id=1, source_target_pairs={{2,3},{6,7},{10,11},{14,15},{18,19},{22,23},{26,27},{30,31}} | collective-permute-start | bytes 6291464 | tf_op jit(solution)/shard_map/ppermute | solution.py:638
  998.3 109.1 %collective-permute-start.48 = (bf16[512,2048]{1,0:T(8,128)(2,1)}, bf16[512,2048]{1,0:T(8,128)(2,1)}, u32[]{:S(2)}, u32[]{:S(2)}) collective-permute-start(bf16[512,2048]{1,0:T(8,128)(2,1)} %collective-permute-done.44), channel_id=1, source_target_pairs={{1,0},{5,4},{9,8},{13,12},{17,16},{21,20},{25,24},{29,28}} | collective-permute-start | bytes 6291464 | tf_op jit(solution)/shard_map/ppermute | solution.py:639
  1052.8 54.6 %collective-permute-start.49 = (bf16[256,768]{1,0:T(8,128)(2,1)S(1)}, bf16[256,768]{1,0:T(8,128)(2,1)S(1)}, u32[]{:S(2)}, u32[]{:S(2)}) collective-permute-start(bf16[256,768]{1,0:T(8,128)(2,1)S(1)} %get-tuple-element.450), channel_id=1, source_target_pairs={{0,1},{1,2},{2,3},{3,0},{4,5},{5,6},{6,7},{7,4},{8,9},{9,10},{10,1... | collective-permute-start | bytes 1179656 | tf_op jit(solution)/shard_map/ppermute | solution.py:701
  1053.9 53.5 %collective-permute-start.50 = (bf16[256,768]{1,0:T(8,128)(2,1)S(1)}, bf16[256,768]{1,0:T(8,128)(2,1)S(1)}, u32[]{:S(2)}, u32[]{:S(2)}) collective-permute-start(bf16[256,768]{1,0:T(8,128)(2,1)S(1)} %get-tuple-element.451), channel_id=1, source_target_pairs={{0,2},{1,3},{2,0},{3,1},{4,6},{5,7},{6,4},{7,5},{8,10},{9,11},{10,... | collective-permute-start | bytes 1179656 | tf_op jit(solution)/shard_map/ppermute | solution.py:701
  1054.0 57.7 %collective-permute-start.51 = (bf16[256,768]{1,0:T(8,128)(2,1)S(1)}, bf16[256,768]{1,0:T(8,128)(2,1)S(1)}, u32[]{:S(2)}, u32[]{:S(2)}) collective-permute-start(bf16[256,768]{1,0:T(8,128)(2,1)S(1)} %get-tuple-element.449), channel_id=1, source_target_pairs={{0,3},{1,0},{2,1},{3,2},{4,7},{5,4},{6,5},{7,6},{8,11},{9,8},{10,9... | collective-permute-start | bytes 1179656 | tf_op jit(solution)/shard_map/ppermute | solution.py:701
  (76 other events, 333.3 us)
Sparse Core Ops, SparseCore 0:
  131.6 88.9 all-gather.4
  222.2 85.7 all-gather.6
  310.3 100.0 reduce-scatter.5
  412.6 92.3 reduce-scatter.7
  507.2 193.3 reduce-scatter.9
  768.9 97.6 reduce-scatter.13
  871.2 118.8 reduce-scatter.11

commit v9 on v8

--- a/solution.py
+++ b/solution.py
@@ -1040,22 +1040,22 @@
     ).astype(BF16)
     gains = jnp.pad(gains, ((0, 0), (0, 126)))
     rest = jnp.concatenate([w_downs, w_outs, query_kv, gains], axis=1)
-    hop, mixed_hop, rest = hold(hop, mixed_hop, rest)
+    tokens_grad = tokens_gather.place_hop(put_rows, tokens_grad, 0)
+    mixed = mixed_gather.place_hop(put_share, mixed, 0)
+    hop, mixed_hop, rest, tokens_grad, mixed = hold(hop, mixed_hop, rest, tokens_grad, mixed)
     tokens_gather.held(hop)
     mixed_gather.held(mixed_hop)
     rest = plane_sum(rest)
 
     hop, mixed_hop = tokens_gather.step(), mixed_gather.step()
-    for count in range(2):
+    hop, mixed_hop = hold(hop, mixed_hop)
+    tokens_gather.held(hop)
+    mixed_gather.held(mixed_hop)
+
+    hop = tokens_gather.step()
+    for count in (1, 2):
         tokens_grad = tokens_gather.place_hop(put_rows, tokens_grad, count)
         mixed = mixed_gather.place_hop(put_share, mixed, count)
-    hop, mixed_hop, tokens_grad, mixed = hold(hop, mixed_hop, tokens_grad, mixed)
-    tokens_gather.held(hop)
-    mixed_gather.held(mixed_hop)
-
-    hop = tokens_gather.step()
-    tokens_grad = tokens_gather.place_hop(put_rows, tokens_grad, 2)
-    mixed = mixed_gather.place_hop(put_share, mixed, 2)
     hop, tokens_grad, mixed = hold(hop, tokens_grad, mixed)
     tokens_gather.held(hop)
 

time: 1140 us -> 1100 us (0.965)
  waiting for transfers between devices: 352 us -> 318 us
    ppermute x12, waiting for transfers between devices: 185 us -> 167 us  [step(): self.lefts.append(lax.ppermute(self.lefts[-1], 'tensor', to_left))]
  transfers between devices with their start and end apart: 59 -> 59, of which waited for: 18 -> 19; matrix products, arithmetic and copies ran while one was open for 19% -> 20% of each run, Pallas kernels for 33% -> 34%
where the time goes in v9:
time: 1100 us
  Pallas kernels  371 us (34%)
  waiting for transfers between devices  318 us (29%)
  starting transfers between devices  107 us (10%)
  local copies, waits for them, and re-layouts  88.7 us (8%)
  other arithmetic  82 us (7%)
  matrix products  79.5 us (7%)
  between operations  50.8 us (5%)
    ppermute x12, waiting for transfers between devices, step(): self.lefts.append(lax.ppermute(self.lefts[-1], 'tensor', to_left))  167 us
    pallas_call x2, Pallas kernels, feed_forward(): pl.pallas_call(feed_kernel, grid=(2 * quarter,), in_specs=[pl.BlockSpec((...  124 us
    pallas_call x1, Pallas kernels, attend_back_first(): pl.pallas_call(kernel, grid_spec=pltpu.PrefetchScalarGridSpec(num_scalar_...  78.2 us
    dot_general x4, matrix products, t_dot(): return jnp.einsum('rd,rf->df', a, b, preferred_element_type=F32)  65.3 us
    pallas_call x1, Pallas kernels, attend_first(): pl.pallas_call(kernel, grid_spec=pltpu.PrefetchScalarGridSpec(num_scalar_...  59.5 us
    ppermute x12, waiting for transfers between devices, send_blocks(): lax.ppermute(block, 'tensor', [(i, (i + shift) % size) for i in range(siz...  49.2 us
    pallas_call x1, Pallas kernels, attend_back_last(): pl.pallas_call(kernel, grid_spec=pltpu.PrefetchScalarGridSpec(num_scalar_...  38.1 us
    ppermute x12, waiting for transfers between devices, step(): self.rights.append(lax.ppermute(self.rights[-1], 'tensor', to_right))  30.2 us
  transfers between devices with their start and end apart: 59, of which 19 were waited for; matrix products, arithmetic and copies ran while one was open for 20% of the time, Pallas kernels for 34%

profile of v9, /device:TPU:0, one launch (start us, length us, event | category | flops | bytes accessed | tf_op | source)
XLA Modules:
  0.0 1097.3 jit_solution(7988733021797456887)
XLA Ops:
  9.8 5.9 collective-permute-start
  17.3 5.4 multiply_sine_fusion.1
  26.2 17.5 %project.1 = (bf16[2048,128]{1,0:T(8,128)(2,1)S(1)}, bf16[2048,512]{1,0:T(8,128)(2,1)}, bf16[2048,2048]{1,0:T(8,128)(2,1)}, f32[2048,128]{1,0:T(8,128)S(1)}, f32[2048,128]{1,0:T(8,128)S(1)}) custom-call(s32[1]{0:T(128)} %bitcast.1.head, bf16[2048,2048]{1,0:T(8,128)(2,1)} %tokens_ref.5, f32[1,2048]{1,0:T(1,128)S(1)} %bitcast.150, ...), custom_call_target="tpu_custom_call" | custom-call | flops 1 | bytes 1 | tf_op jit(solution)/shard_map/project/pallas_call | solution.py:68
  53.3 8.0 collective-permute-done.2.other
  61.3 14.0 %collective-permute-done.4.refs_2_ = bf16[1024,512]{1,0:T(8,128)(2,1)S(1)} collective-permute-done((bf16[1024,512]{1,0:T(8,128)(2,1)}, bf16[1024,512]{1,0:T(8,128)(2,1)S(1)}, u32[]{:S(2)}, u32[]{:S(2)}) %collective-permute-start.4) | collective-permute-done | bytes 1048608 | tf_op jit(solution)/shard_map/ppermute | solution.py:639
  78.8 59.5 %attend_first.1 = (bf16[1024,512]{1,0:T(8,128)(2,1)}, f32[4,8,1024]{2,1,0:T(8,128)}, bf16[4096,128]{1,0:T(8,128)(2,1)}, bf16[4096,128]{1,0:T(8,128)(2,1)}, bf16[...) custom-call(s32[6]{0:T(128)} %get-tuple-element.493.meta.refs_0_, ...), custom_call_target="tpu_custom_call" | custom-call | flops 17179869184 | bytes 8388608 | tf_op jit(solution)/shard_map/attend_first/pallas_call | solution.py:208
  143.2 6.9 arrange.3.refs_0_
  152.0 25.4 %attend.1 = (bf16[1024,512]{1,0:T(8,128)(2,1)}, f32[4,8,1024]{2,1,0:T(8,128)}) custom-call(s32[6]{0:T(128)} %get-tuple-element.492.refs_0_, bf16[1024,512]{1,0:T(8,128)(2,1)} %collective-permute-done.5.refs_1_, bf16[4096,128]{1,0:T(8,128)(2,1)} %get-tuple-element.214.refs_2_.refs_5_, bf16[4096,128]{1,0:T(8,128)(2,1)} %get-tuple-element.215.refs_3_.refs_6_, ...), custom_call_target="tpu_custom_call" | custom-call | flops 17179869184 | bytes 8388608 | tf_op jit(solution)/shard_map/attend/pallas_call | solution.py:245
  177.4 14.4 %collective-permute-start.9 = (bf16[1024,512]{1,0:T(8,128)(2,1)}, bf16[1024,512]{1,0:T(8,128)(2,1)}, u32[]{:S(2)}, u32[]{:S(2)}) collective-permute-start(bf16[1024,512]{1,0:T(8,128)(2,1)} %get-tuple-element.221.refs_2_), channel_id=1, source_target_pairs={{0,4},{4,0},{1,5},{5,1},{2,6},{6,2},{3,7},{7,3},{8,12},{12,8},{9,1... | collective-permute-start | bytes 3145736 | tf_op jit(solution)/shard_map/ppermute | solution.py:842
  194.1 6.4 arrange.4.output_weight
  200.5 3.7 multiply_sine_fusion
  206.1 3.7 maximum_maximum_fusion
  209.8 4.6 collective-permute-done.9
  214.6 6.1 all-gather.5.cloned.1.call-done
  224.4 62.4 %feed_forward.2 = (f32[2048,2048]{1,0:T(8,128)}, bf16[2048,2048]{1,0:T(8,128)(2,1)}, bf16[2048,1408]{1,0:T(8,128)(2,1)}, bf16[2048,2816]{1,0:T(8,128)(2,1)}, bf1...) custom-call(bf16[4,1024,512]{2,1,0:T(8,128)(2,1)} %bitcast.157, bf16[2048,2048]{1,0:T(8,128)(2,1)} %tokens_ref.5, ...), custom_call_target="tpu_custom_call" | custom-call | flops 1 | bytes 1 | tf_op jit(solution)/shard_map/feed_forward/pallas_call | solution.py:523
  286.8 21.2 %all-gather.7.cloned.1.call-done = bf16[4096,512]{1,0:T(8,128)(2,1)} async-done(((bf16[1024,512]{1,0:T(8,128)(2,1)}), bf16[4096,512]{1,0:T(8,128)(2,1)}) %all-gather.7.cloned.1.call-update) | async-done | bytes 4194320 | tf_op jit(solution)/shard_map/all_gather | solution.py:854
  319.5 61.5 %feed_forward.3 = (f32[2048,2048]{1,0:T(8,128)}, bf16[2048,2048]{1,0:T(8,128)(2,1)}, bf16[2048,1408]{1,0:T(8,128)(2,1)}, bf16[2048,2816]{1,0:T(8,128)(2,1)}, bf1...) custom-call(bf16[4,1024,512]{2,1,0:T(8,128)(2,1)} %bitcast.159, ...), custom_call_target="tpu_custom_call", output_to_operand_aliasing={{0}: (8, {}), {1}: (9, {}), {2}: (10, {}), {3}: (11, {}), {... | custom-call | flops 1 | bytes 1 | tf_op jit(solution)/shard_map/feed_forward/pallas_call | solution.py:523
  385.8 31.7 %convolution_convert_fusion = bf16[2048,2816]{1,0:T(8,128)(2,1)} fusion(bf16[2048,2048]{1,0:T(8,128)(2,1)} %get-tuple-element.252, bf16[2048,2816]{1,0:T(8,128)(2,1)} %get-tuple-element.253), kind=kOutput, calls=%fused_computation.3 | convolution fusion | flops 23628087296 | bytes 31457280 | tf_op jit(solution)/shard_map/rd,rf->df/dot_general | solution.py:733
  417.5 4.7 constant_dynamic-slice_fusion.36
  422.3 2.8 fusion.26
  426.4 3.9 fusion.54
  431.3 6.0 fusion.41
  442.4 3.1 collective-permute-start.16
  449.6 2.9 collective-permute-start.18
  452.5 19.4 %fusion.2 = bf16[2048,1408]{1,0:T(8,128)(2,1)} fusion(bf16[2048,1408]{1,0:T(8,128)(2,1)} %get-tuple-element.265, bf16[2048,2048]{1,0:T(8,128)(2,1)} %cotangent_ref.3), kind=kOutput, calls=%fused_computation.10 | convolution fusion | flops 11814043648 | bytes 19922944 | tf_op jit(solution)/shard_map/rd,rf->df/dot_general | solution.py:733
  473.7 5.9 collective-permute-done.17
  480.4 6.6 collective-permute-done.19.refs_1_
  494.3 5.4 reduce-scatter.8.cloned.1.call-done
  502.4 4.0 fusion.52
  506.4 6.1 fusion.42
  515.7 8.4 collective-permute-start.23
  525.0 3.3 collective-permute-start.24
  544.3 78.2 %attend_back_first.1 = (bf16[1024,512]{1,0:T(8,128)(2,1)}, f32[4096,128]{1,0:T(8,128)}, f32[4096,128]{1,0:T(8,128)}) custom-call(s32[6]{0:T(128)} %get-tuple-element.493.meta.refs_0_, bf16[1024,512]{1,0:T(8,128)(2,1)} %pad_maximum_fusion.2.q_ref.refs_1_, bf16[1024,512]{1,0:T(8,128)(2,1)} %get-tuple-element.212.refs_2_, bf16[1024,512]{1,0:T(8,128)(2,1)} %bitcast.163, ...), custom_call_target="tpu_custom_call" | custom-call | flops 1 | bytes 1 | tf_op jit(solution)/shard_map/attend_back_first/pallas_call | solution.py:381
  632.7 38.1 %attend_back_last.1 = (bf16[1024,512]{1,0:T(8,128)(2,1)}, f32[2048,128]{1,0:T(8,128)}, bf16[2048,128]{1,0:T(8,128)(2,1)}) custom-call(s32[6]{0:T(128)} %get-tuple-element.492.refs_0_, bf16[1024,512]{1,0:T(8,128)(2,1)} %collective-permute-done.5.refs_1_, bf16[1024,512]{1,0:T(8,128)(2,1)} %get-tuple-element.221.refs_2_, bf16[1024,512]{1,0:T(8,128)(2,1)} %bitcast.164, ...), custom_call_target="tpu_custom_call" | custom-call | flops 1 | bytes 1 | tf_op jit(solution)/shard_map/attend_back_last/pallas_call | solution.py:436
  674.9 4.3 copy.90
  682.7 3.4 collective-permute-start.34
  686.7 3.3 collective-permute-start.31
  691.3 6.9 convolution_convert_fusion.1
  699.1 14.7 %collective-permute-done.31 = bf16[256,256]{1,0:T(8,128)(2,1)S(1)} collective-permute-done((bf16[256,256]{1,0:T(8,128)(2,1)S(1)}, bf16[256,256]{1,0:T(8,128)(2,1)S(1)}, u32[]{:S(2)}, u32[]{:S(2)}) %collective-permute-start.31) | collective-permute-done | bytes 131104 | tf_op jit(solution)/shard_map/ppermute | solution.py:701
  714.3 23.8 %collective-permute-done.30 = bf16[256,256]{1,0:T(8,128)(2,1)S(1)} collective-permute-done((bf16[256,256]{1,0:T(8,128)(2,1)S(1)}, bf16[256,256]{1,0:T(8,128)(2,1)S(1)}, u32[]{:S(2)}, u32[]{:S(2)}) %collective-permute-start.30) | collective-permute-done | bytes 131104 | tf_op jit(solution)/shard_map/ppermute | solution.py:701
  738.1 3.4 collective-permute-start.29
  742.5 6.6 join.2
  749.6 6.6 join.3
  760.6 3.3 fusion.6
  763.9 3.6 add_convert_fusion
  772.2 3.3 collective-permute-start.36
  776.9 6.3 collective-permute-start.38
  786.1 4.8 broadcast.124.clone
  790.9 3.1 slice_dynamic-update-slice_fusion.9
  796.3 19.2 %collective-permute-done.40 = bf16[1024,768]{1,0:T(8,128)(2,1)} collective-permute-done((bf16[1024,768]{1,0:T(8,128)(2,1)}, bf16[1024,768]{1,0:T(8,128)(2,1)}, u32[]{:S(2)}, u32[]{:S(2)}) %collective-permute-start.40) | collective-permute-done | bytes 1572896 | tf_op jit(solution)/shard_map/ppermute | solution.py:1032
  818.3 7.3 convolution_convert_fusion.3
  825.7 7.0 fusion.1
  832.6 30.1 %collective-permute-done.38 = bf16[512,2048]{1,0:T(8,128)(2,1)} collective-permute-done((bf16[512,2048]{1,0:T(8,128)(2,1)S(1)}, bf16[512,2048]{1,0:T(8,128)(2,1)}, u32[]{:S(2)}, u32[]{:S(2)}) %collective-permute-start.38) | collective-permute-done | bytes 2097184 | tf_op jit(solution)/shard_map/ppermute | solution.py:638
  862.8 5.5 collective-permute-done.39
  892.8 4.1 select_dynamic-update-slice_fusion.2
  896.9 27.0 %collective-permute-done.42 = bf16[512,2048]{1,0:T(8,128)(2,1)} collective-permute-done((bf16[512,2048]{1,0:T(8,128)(2,1)}, bf16[512,2048]{1,0:T(8,128)(2,1)}, u32[]{:S(2)}, u32[]{:S(2)}) %collective-permute-start.42) | collective-permute-done | bytes 2097184 | tf_op jit(solution)/shard_map/ppermute | solution.py:639
  923.9 41.0 %collective-permute-done.44 = bf16[512,2048]{1,0:T(8,128)(2,1)} collective-permute-done((bf16[512,2048]{1,0:T(8,128)(2,1)}, bf16[512,2048]{1,0:T(8,128)(2,1)}, u32[]{:S(2)}, u32[]{:S(2)}) %collective-permute-start.44) | collective-permute-done | bytes 2097184 | tf_op jit(solution)/shard_map/ppermute | solution.py:639
  970.3 3.7 select_select_fusion.1
  980.2 4.3 select_dynamic-update-slice_fusion.1
  984.6 31.8 %collective-permute-done.46 = bf16[512,2048]{1,0:T(8,128)(2,1)S(1)} collective-permute-done((bf16[512,2048]{1,0:T(8,128)(2,1)}, bf16[512,2048]{1,0:T(8,128)(2,1)S(1)}, u32[]{:S(2)}, u32[]{:S(2)}) %collective-permute-start.46) | collective-permute-done | bytes 2097184 | tf_op jit(solution)/shard_map/ppermute | solution.py:639
  1018.8 3.1 slice_convert_fusion
  1029.5 48.2 %collective-permute-done.48 = bf16[512,2048]{1,0:T(8,128)(2,1)} collective-permute-done((bf16[512,2048]{1,0:T(8,128)(2,1)}, bf16[512,2048]{1,0:T(8,128)(2,1)}, u32[]{:S(2)}, u32[]{:S(2)}) %collective-permute-start.48) | collective-permute-done | bytes 2097184 | tf_op jit(solution)/shard_map/ppermute | solution.py:639
  1077.7 4.1 collective-permute-done.51
  1085.9 4.3 select_dynamic-update-slice_fusion
  (403 shorter events, 151.1 us)
Async XLA Ops:
  7.2 213.5 %all-gather.5.cloned.1.call-start = ((), (), s32[]{:S(2)}) async-start(), calls=%async_computation.10 | async-start | bytes 5242880 | tf_op jit(solution)/shard_map/all_gather | solution.py:829
  9.8 35.7 %collective-permute-start = (bf16[1024,512]{1,0:T(8,128)(2,1)}, bf16[1024,512]{1,0:T(8,128)(2,1)}, u32[]{:S(2)}, u32[]{:S(2)}) collective-permute-start(bf16[1024,512]{1,0:T(8,128)(2,1)} %constant_dynamic-slice_fusion.42.refs_6_), channel_id=1, source_target_pairs={{0,1},{1,2},{2,3},{4,5},{5,6},{6,7},{8,9},{9,10},{10,11},{12,13},{... | collective-permute-start | bytes 3145736 | tf_op jit(solution)/shard_map/ppermute | solution.py:638
  15.7 29.8 %collective-permute-start.1 = (bf16[1024,512]{1,0:T(8,128)(2,1)}, bf16[1024,512]{1,0:T(8,128)(2,1)}, u32[]{:S(2)}, u32[]{:S(2)}) collective-permute-start(bf16[1024,512]{1,0:T(8,128)(2,1)} %constant_dynamic-slice_fusion.42.refs_6_), channel_id=1, source_target_pairs={{1,0},{2,1},{3,2},{5,4},{6,5},{7,6},{9,8},{10,9},{11,10},{13,12},{... | collective-permute-start | bytes 3145736 | tf_op jit(solution)/shard_map/ppermute | solution.py:639
  45.5 15.8 %collective-permute-start.3 = (bf16[1024,512]{1,0:T(8,128)(2,1)}, bf16[1024,512]{1,0:T(8,128)(2,1)S(1)}, u32[]{:S(2)}, u32[]{:S(2)}) collective-permute-start(bf16[1024,512]{1,0:T(8,128)(2,1)} %collective-permute-done.refs_5_), channel_id=1, source_target_pairs={{1,2},{2,3},{5,6},{6,7},{9,10},{10,11},{13,14},{14,15},{17,18},{18... | collective-permute-start | bytes 3145736 | tf_op jit(solution)/shard_map/ppermute | solution.py:638
  46.4 28.9 %collective-permute-start.4 = (bf16[1024,512]{1,0:T(8,128)(2,1)}, bf16[1024,512]{1,0:T(8,128)(2,1)S(1)}, u32[]{:S(2)}, u32[]{:S(2)}) collective-permute-start(bf16[1024,512]{1,0:T(8,128)(2,1)} %collective-permute-done.1.refs_4_), channel_id=1, source_target_pairs={{1,0},{2,1},{5,4},{6,5},{9,8},{10,9},{13,12},{14,13},{17,16},{18,1... | collective-permute-start | bytes 3145736 | tf_op jit(solution)/shard_map/ppermute | solution.py:639
  47.7 13.6 %collective-permute-start.2 = (bf16[2048,128]{1,0:T(8,128)(2,1)}, bf16[2048,128]{1,0:T(8,128)(2,1)S(1)}, u32[]{:S(2)}, u32[]{:S(2)}) collective-permute-start(bf16[2048,128]{1,0:T(8,128)(2,1)} %copy-done.24), channel_id=1, source_target_pairs={{0,4},{4,0},{1,5},{5,1},{2,6},{6,2},{3,7},{7,3},{8,12},{12,8},{9,1... | collective-permute-start | bytes 1572872 | tf_op jit(solution)/shard_map/ppermute | solution.py:815
  61.3 77.0 %copy-start.8 = (bf16[1024,512]{1,0:T(8,128)(2,1)}, bf16[1024,512]{1,0:T(8,128)(2,1)S(1)}, u32[]{:S(2)}) copy-start(bf16[1024,512]{1,0:T(8,128)(2,1)S(1)} %collective-permute-done.3.refs_3_) | copy-start | bytes 3145732
  75.3 63.0 %copy-start.10 = (bf16[1024,512]{1,0:T(8,128)(2,1)}, bf16[1024,512]{1,0:T(8,128)(2,1)S(1)}, u32[]{:S(2)}) copy-start(bf16[1024,512]{1,0:T(8,128)(2,1)S(1)} %collective-permute-done.4.refs_2_) | copy-start | bytes 3145732
  75.3 63.0 %collective-permute-start.5 = (bf16[1024,512]{1,0:T(8,128)(2,1)}, bf16[1024,512]{1,0:T(8,128)(2,1)}, u32[]{:S(2)}, u32[]{:S(2)}) collective-permute-start(bf16[1024,512]{1,0:T(8,128)(2,1)} %slice.207), channel_id=1, source_target_pairs={{0,4},{4,0},{1,5},{5,1},{2,6},{6,2},{3,7},{7,3},{8,12},{12,8},{9,1... | collective-permute-start | bytes 3145736 | tf_op jit(solution)/shard_map/ppermute | solution.py:823
  76.8 61.6 %collective-permute-start.6 = (bf16[1024,512]{1,0:T(8,128)(2,1)S(1)}, bf16[1024,512]{1,0:T(8,128)(2,1)S(1)}, u32[]{:S(2)}, u32[]{:S(2)}) collective-permute-start(bf16[1024,512]{1,0:T(8,128)(2,1)S(1)} %collective-permute-done.3.refs_3_), channel_id=1, source_target_pairs={{2,3},{6,7},{10,11},{14,15},{18,19},{22,23},{26,27},{30,31}} | collective-permute-start | bytes 3145736 | tf_op jit(solution)/shard_map/ppermute | solution.py:638
  77.5 61.8 %collective-permute-start.7 = (bf16[1024,512]{1,0:T(8,128)(2,1)S(1)}, bf16[1024,512]{1,0:T(8,128)(2,1)}, u32[]{:S(2)}, u32[]{:S(2)}) collective-permute-start(bf16[1024,512]{1,0:T(8,128)(2,1)S(1)} %collective-permute-done.4.refs_2_), channel_id=1, source_target_pairs={{1,0},{5,4},{9,8},{13,12},{17,16},{21,20},{25,24},{29,28}} | collective-permute-start | bytes 3145736 | tf_op jit(solution)/shard_map/ppermute | solution.py:639
  139.4 168.6 %all-gather.7.cloned.1.call-start = ((), (), s32[]{:S(2)}) async-start(), calls=%async_computation.11 | async-start | bytes 5242880 | tf_op jit(solution)/shard_map/all_gather | solution.py:854
  150.2 27.2 %collective-permute-start.8 = (bf16[4,1024,512]{2,1,0:T(8,128)(2,1)}, bf16[4,1024,512]{2,1,0:T(8,128)(2,1)}, u32[]{:S(2)}, u32[]{:S(2)}) collective-permute-start(bf16[4,1024,512]{2,1,0:T(8,128)(2,1)} %arrange.3.refs_0_), channel_id=1, source_target_pairs={{0,8},{8,0},{16,24},{24,16},{1,9},{9,1},{17,25},{25,17},{2,10},{10... | collective-permute-start | bytes 12582920 | tf_op jit(solution)/shard_map/ppermute | solution.py:832
  177.4 37.0 %collective-permute-start.9 = (bf16[1024,512]{1,0:T(8,128)(2,1)}, bf16[1024,512]{1,0:T(8,128)(2,1)}, u32[]{:S(2)}, u32[]{:S(2)}) collective-permute-start(bf16[1024,512]{1,0:T(8,128)(2,1)} %get-tuple-element.221.refs_2_), channel_id=1, source_target_pairs={{0,4},{4,0},{1,5},{5,1},{2,6},{6,2},{3,7},{7,3},{8,12},{12,8},{9,1... | collective-permute-start | bytes 3145736 | tf_op jit(solution)/shard_map/ppermute | solution.py:842
  214.5 207.8 %reduce-scatter.6.cloned.1.call-start = ((), (), s32[]{:S(2)}) async-start(), calls=%async_computation.5 | async-start | bytes 5242880 | tf_op jit(solution)/shard_map/reduce_scatter | solution.py:891
  221.8 65.0 %collective-permute-start.10 = (bf16[512,512]{1,0:T(8,128)(2,1)S(1)}, bf16[512,512]{1,0:T(8,128)(2,1)S(1)}, u32[]{:S(2)}, u32[]{:S(2)}) collective-permute-start(bf16[512,512]{1,0:T(8,128)(2,1)S(1)} %constant_dynamic-slice_fusion.41.refs_6_), channel_id=1, source_target_pairs={{0,1},{1,2},{2,3},{4,5},{5,6},{6,7},{8,9},{9,10},{10,11},{12,13},{... | collective-permute-start | bytes 1572872 | tf_op jit(solution)/shard_map/ppermute | solution.py:638
  223.1 63.7 %collective-permute-start.11 = (bf16[512,512]{1,0:T(8,128)(2,1)S(1)}, bf16[512,512]{1,0:T(8,128)(2,1)S(1)}, u32[]{:S(2)}, u32[]{:S(2)}) collective-permute-start(bf16[512,512]{1,0:T(8,128)(2,1)S(1)} %constant_dynamic-slice_fusion.41.refs_6_), channel_id=1, source_target_pairs={{1,0},{2,1},{3,2},{5,4},{6,5},{7,6},{9,8},{10,9},{11,10},{13,12},{... | collective-permute-start | bytes 1572872 | tf_op jit(solution)/shard_map/ppermute | solution.py:639
  308.0 191.7 %reduce-scatter.8.cloned.1.call-start = ((), (), s32[]{:S(2)}) async-start(), calls=%async_computation.6 | async-start | bytes 5242880 | tf_op jit(solution)/shard_map/reduce_scatter | solution.py:891
  315.3 65.8 %collective-permute-start.12 = (bf16[512,512]{1,0:T(8,128)(2,1)S(1)}, bf16[512,512]{1,0:T(8,128)(2,1)S(1)}, u32[]{:S(2)}, u32[]{:S(2)}) collective-permute-start(bf16[512,512]{1,0:T(8,128)(2,1)S(1)} %collective-permute-done.10.refs_5_), channel_id=1, source_target_pairs={{1,2},{2,3},{5,6},{6,7},{9,10},{10,11},{13,14},{14,15},{17,18},{18... | collective-permute-start | bytes 1572872 | tf_op jit(solution)/shard_map/ppermute | solution.py:638
  316.0 65.1 %collective-permute-start.13 = (bf16[512,512]{1,0:T(8,128)(2,1)S(1)}, bf16[512,512]{1,0:T(8,128)(2,1)}, u32[]{:S(2)}, u32[]{:S(2)}) collective-permute-start(bf16[512,512]{1,0:T(8,128)(2,1)S(1)} %collective-permute-done.11.refs_4_), channel_id=1, source_target_pairs={{1,0},{2,1},{5,4},{6,5},{9,8},{10,9},{13,12},{14,13},{17,16},{18,1... | collective-permute-start | bytes 1572872 | tf_op jit(solution)/shard_map/ppermute | solution.py:639
  381.1 41.1 %collective-permute-start.14 = (bf16[512,512]{1,0:T(8,128)(2,1)S(1)}, bf16[512,512]{1,0:T(8,128)(2,1)S(1)}, u32[]{:S(2)}, u32[]{:S(2)}) collective-permute-start(bf16[512,512]{1,0:T(8,128)(2,1)S(1)} %collective-permute-done.12.refs_3_), channel_id=1, source_target_pairs={{2,3},{6,7},{10,11},{14,15},{18,19},{22,23},{26,27},{30,31}} | collective-permute-start | bytes 1572872 | tf_op jit(solution)/shard_map/ppermute | solution.py:638
  381.8 40.4 %collective-permute-start.15 = (bf16[512,512]{1,0:T(8,128)(2,1)}, bf16[512,512]{1,0:T(8,128)(2,1)S(1)}, u32[]{:S(2)}, u32[]{:S(2)}) collective-permute-start(bf16[512,512]{1,0:T(8,128)(2,1)} %collective-permute-done.13.refs_2_), channel_id=1, source_target_pairs={{1,0},{5,4},{9,8},{13,12},{17,16},{21,20},{25,24},{29,28}} | collective-permute-start | bytes 1572872 | tf_op jit(solution)/shard_map/ppermute | solution.py:639
  385.7 378.2 %reduce-scatter.10.cloned.1.call-start = ((), (), s32[]{:S(2)}) async-start(), calls=%async_computation.7 | async-start | bytes 10485760 | tf_op jit(solution)/shard_map/reduce_scatter | solution.py:891
  425.2 593.6 %reduce-scatter.14.cloned.1.call-start = ((), (), s32[]{:S(2)}) async-start(), calls=%async_computation.9 | async-start | bytes 12976128 | tf_op jit(solution)/shard_map/reduce_scatter | solution.py:894
  439.5 47.4 %collective-permute-start.19 = (bf16[4,512,512]{2,1,0:T(8,128)(2,1)S(1)}, bf16[4,512,512]{2,1,0:T(8,128)(2,1)}, u32[]{:S(2)}, u32[]{:S(2)}) collective-permute-start(bf16[4,512,512]{2,1,0:T(8,128)(2,1)S(1)} %arrange.5.refs_0_), channel_id=1, source_target_pairs={{0,4},{4,0},{1,5},{5,1},{2,6},{6,2},{3,7},{7,3},{8,12},{12,8},{9,1... | collective-permute-start | bytes 6291464 | tf_op jit(solution)/shard_map/ppermute | solution.py:928
  442.4 31.3 %collective-permute-start.16 = (bf16[256,512]{1,0:T(8,128)(2,1)}, bf16[256,512]{1,0:T(8,128)(2,1)}, u32[]{:S(2)}, u32[]{:S(2)}) collective-permute-start(bf16[256,512]{1,0:T(8,128)(2,1)} %bitcast.25), channel_id=1, source_target_pairs={{0,1},{1,2},{2,3},{3,0},{4,5},{5,6},{6,7},{7,4},{8,9},{9,10},{10,1... | collective-permute-start | bytes 786440 | tf_op jit(solution)/shard_map/ppermute | solution.py:701
  446.4 33.2 %collective-permute-start.17 = (bf16[256,512]{1,0:T(8,128)(2,1)}, bf16[256,512]{1,0:T(8,128)(2,1)}, u32[]{:S(2)}, u32[]{:S(2)}) collective-permute-start(bf16[256,512]{1,0:T(8,128)(2,1)} %bitcast.26), channel_id=1, source_target_pairs={{0,2},{1,3},{2,0},{3,1},{4,6},{5,7},{6,4},{7,5},{8,10},{9,11},{10,... | collective-permute-start | bytes 786440 | tf_op jit(solution)/shard_map/ppermute | solution.py:701
  449.6 37.8 %copy-start.5 = (bf16[2048,256]{1,0:T(8,128)(2,1)S(1)}, bf16[2048,256]{1,0:T(8,128)(2,1)}, u32[]{:S(2)}) copy-start(bf16[2048,256]{1,0:T(8,128)(2,1)} %v_weight.1) | copy-start | bytes 3145732
  449.6 30.8 %collective-permute-start.18 = (bf16[256,512]{1,0:T(8,128)(2,1)}, bf16[256,512]{1,0:T(8,128)(2,1)}, u32[]{:S(2)}, u32[]{:S(2)}) collective-permute-start(bf16[256,512]{1,0:T(8,128)(2,1)} %bitcast.174), channel_id=1, source_target_pairs={{0,3},{1,0},{2,1},{3,2},{4,7},{5,4},{6,5},{7,6},{8,11},{9,8},{10,9... | collective-permute-start | bytes 786440 | tf_op jit(solution)/shard_map/ppermute | solution.py:701
  486.9 12.8 %collective-permute-start.20 = (bf16[4,512,512]{2,1,0:T(8,128)(2,1)S(1)}, bf16[4,512,512]{2,1,0:T(8,128)(2,1)}, u32[]{:S(2)}, u32[]{:S(2)}) collective-permute-start(bf16[4,512,512]{2,1,0:T(8,128)(2,1)S(1)} %arrange.5.refs_0_), channel_id=1, source_target_pairs={{0,8},{8,0},{16,24},{24,16},{1,9},{9,1},{17,25},{25,17},{2,10},{10... | collective-permute-start | bytes 6291464 | tf_op jit(solution)/shard_map/ppermute | solution.py:937
  486.9 12.8 %collective-permute-start.21 = (bf16[4,512,512]{2,1,0:T(8,128)(2,1)}, bf16[4,512,512]{2,1,0:T(8,128)(2,1)}, u32[]{:S(2)}, u32[]{:S(2)}) collective-permute-start(bf16[4,512,512]{2,1,0:T(8,128)(2,1)} %collective-permute-done.19.refs_1_), channel_id=1, source_target_pairs={{0,8},{8,0},{16,24},{24,16},{1,9},{9,1},{17,25},{25,17},{2,10},{10... | collective-permute-start | bytes 6291464 | tf_op jit(solution)/shard_map/ppermute | solution.py:937
  513.4 109.1 %collective-permute-start.22 = (bf16[256,512]{1,0:T(8,128)(2,1)}, bf16[256,512]{1,0:T(8,128)(2,1)S(1)}, u32[]{:S(2)}, u32[]{:S(2)}) collective-permute-start(bf16[256,512]{1,0:T(8,128)(2,1)} %bitcast.170), channel_id=1, source_target_pairs={{0,4},{1,5},{2,6},{3,7},{4,0},{5,1},{6,2},{7,3},{8,12},{9,13},{10,... | collective-permute-start | bytes 786440 | tf_op jit(solution)/shard_map/ppermute | solution.py:691
  515.7 106.8 %collective-permute-start.23 = (bf16[256,512]{1,0:T(8,128)(2,1)}, bf16[256,512]{1,0:T(8,128)(2,1)S(1)}, u32[]{:S(2)}, u32[]{:S(2)}) collective-permute-start(bf16[256,512]{1,0:T(8,128)(2,1)} %bitcast.171), channel_id=1, source_target_pairs={{0,5},{1,6},{2,7},{3,4},{4,1},{5,2},{6,3},{7,0},{8,13},{9,14},{10,... | collective-permute-start | bytes 786440 | tf_op jit(solution)/shard_map/ppermute | solution.py:691
  525.0 97.6 %collective-permute-start.24 = (bf16[256,512]{1,0:T(8,128)(2,1)}, bf16[256,512]{1,0:T(8,128)(2,1)S(1)}, u32[]{:S(2)}, u32[]{:S(2)}) collective-permute-start(bf16[256,512]{1,0:T(8,128)(2,1)} %bitcast.172), channel_id=1, source_target_pairs={{0,6},{1,7},{2,4},{3,5},{4,2},{5,3},{6,0},{7,1},{8,14},{9,15},{10,... | collective-permute-start | bytes 786440 | tf_op jit(solution)/shard_map/ppermute | solution.py:691
  529.1 93.5 %collective-permute-start.25 = (bf16[256,512]{1,0:T(8,128)(2,1)}, bf16[256,512]{1,0:T(8,128)(2,1)S(1)}, u32[]{:S(2)}, u32[]{:S(2)}) collective-permute-start(bf16[256,512]{1,0:T(8,128)(2,1)} %bitcast.173), channel_id=1, source_target_pairs={{0,7},{1,4},{2,5},{3,6},{4,3},{5,0},{6,1},{7,2},{8,15},{9,12},{10,... | collective-permute-start | bytes 786440 | tf_op jit(solution)/shard_map/ppermute | solution.py:691
  625.5 45.2 %collective-permute-start.26 = (bf16[256,512]{1,0:T(8,128)(2,1)}, bf16[256,512]{1,0:T(8,128)(2,1)}, u32[]{:S(2)}, u32[]{:S(2)}) collective-permute-start(bf16[256,512]{1,0:T(8,128)(2,1)} %get-tuple-element.412), channel_id=1, source_target_pairs={{0,1},{1,2},{2,3},{3,0},{4,5},{5,6},{6,7},{7,4},{8,9},{9,10},{10,1... | collective-permute-start | bytes 786440 | tf_op jit(solution)/shard_map/ppermute | solution.py:701
  628.4 42.4 %collective-permute-start.27 = (bf16[256,512]{1,0:T(8,128)(2,1)S(1)}, bf16[256,512]{1,0:T(8,128)(2,1)}, u32[]{:S(2)}, u32[]{:S(2)}) collective-permute-start(bf16[256,512]{1,0:T(8,128)(2,1)S(1)} %get-tuple-element.411), channel_id=1, source_target_pairs={{0,2},{1,3},{2,0},{3,1},{4,6},{5,7},{6,4},{7,5},{8,10},{9,11},{10,... | collective-permute-start | bytes 786440 | tf_op jit(solution)/shard_map/ppermute | solution.py:701
  628.4 42.4 %collective-permute-start.28 = (bf16[256,512]{1,0:T(8,128)(2,1)S(1)}, bf16[256,512]{1,0:T(8,128)(2,1)}, u32[]{:S(2)}, u32[]{:S(2)}) collective-permute-start(bf16[256,512]{1,0:T(8,128)(2,1)S(1)} %get-tuple-element.410), channel_id=1, source_target_pairs={{0,3},{1,0},{2,1},{3,2},{4,7},{5,4},{6,5},{7,6},{8,11},{9,8},{10,9... | collective-permute-start | bytes 786440 | tf_op jit(solution)/shard_map/ppermute | solution.py:701
  680.4 68.8 %collective-permute-start.35 = (bf16[256,768]{1,0:T(8,128)(2,1)S(1)}, bf16[256,768]{1,0:T(8,128)(2,1)S(1)}, u32[]{:S(2)}, u32[]{:S(2)}) collective-permute-start(bf16[256,768]{1,0:T(8,128)(2,1)S(1)} %pad_maximum_fusion.18), channel_id=1, source_target_pairs={{0,7},{1,4},{2,5},{3,6},{4,3},{5,0},{6,1},{7,2},{8,15},{9,12},{10,... | collective-permute-start | bytes 1179656 | tf_op jit(solution)/shard_map/ppermute | solution.py:691
  682.7 66.5 %collective-permute-start.34 = (bf16[256,768]{1,0:T(8,128)(2,1)S(1)}, bf16[256,768]{1,0:T(8,128)(2,1)S(1)}, u32[]{:S(2)}, u32[]{:S(2)}) collective-permute-start(bf16[256,768]{1,0:T(8,128)(2,1)S(1)} %pad_maximum_fusion.17), channel_id=1, source_target_pairs={{0,6},{1,7},{2,4},{3,5},{4,2},{5,3},{6,0},{7,1},{8,14},{9,15},{10,... | collective-permute-start | bytes 1179656 | tf_op jit(solution)/shard_map/ppermute | solution.py:691
  686.1 63.1 %collective-permute-start.33 = (bf16[256,768]{1,0:T(8,128)(2,1)S(1)}, bf16[256,768]{1,0:T(8,128)(2,1)S(1)}, u32[]{:S(2)}, u32[]{:S(2)}) collective-permute-start(bf16[256,768]{1,0:T(8,128)(2,1)S(1)} %pad_maximum_fusion.16), channel_id=1, source_target_pairs={{0,5},{1,6},{2,7},{3,4},{4,1},{5,2},{6,3},{7,0},{8,13},{9,14},{10,... | collective-permute-start | bytes 1179656 | tf_op jit(solution)/shard_map/ppermute | solution.py:691
  686.7 27.1 %collective-permute-start.31 = (bf16[256,256]{1,0:T(8,128)(2,1)S(1)}, bf16[256,256]{1,0:T(8,128)(2,1)S(1)}, u32[]{:S(2)}, u32[]{:S(2)}) collective-permute-start(bf16[256,256]{1,0:T(8,128)(2,1)S(1)} %pad_maximum_fusion.22), channel_id=1, source_target_pairs={{0,3},{1,0},{2,1},{3,2},{4,7},{5,4},{6,5},{7,6},{8,11},{9,8},{10,9... | collective-permute-start | bytes 393224 | tf_op jit(solution)/shard_map/ppermute | solution.py:701
  690.0 48.1 %collective-permute-start.30 = (bf16[256,256]{1,0:T(8,128)(2,1)S(1)}, bf16[256,256]{1,0:T(8,128)(2,1)S(1)}, u32[]{:S(2)}, u32[]{:S(2)}) collective-permute-start(bf16[256,256]{1,0:T(8,128)(2,1)S(1)} %pad_maximum_fusion.21), channel_id=1, source_target_pairs={{0,2},{1,3},{2,0},{3,1},{4,6},{5,7},{6,4},{7,5},{8,10},{9,11},{10,... | collective-permute-start | bytes 393224 | tf_op jit(solution)/shard_map/ppermute | solution.py:701
  713.8 35.4 %collective-permute-start.32 = (bf16[256,768]{1,0:T(8,128)(2,1)S(1)}, bf16[256,768]{1,0:T(8,128)(2,1)S(1)}, u32[]{:S(2)}, u32[]{:S(2)}) collective-permute-start(bf16[256,768]{1,0:T(8,128)(2,1)S(1)} %pad_maximum_fusion.15), channel_id=1, source_target_pairs={{0,4},{1,5},{2,6},{3,7},{4,0},{5,1},{6,2},{7,3},{8,12},{9,13},{10,... | collective-permute-start | bytes 1179656 | tf_op jit(solution)/shard_map/ppermute | solution.py:691
  738.1 11.1 %collective-permute-start.29 = (bf16[256,256]{1,0:T(8,128)(2,1)S(1)}, bf16[256,256]{1,0:T(8,128)(2,1)S(1)}, u32[]{:S(2)}, u32[]{:S(2)}) collective-permute-start(bf16[256,256]{1,0:T(8,128)(2,1)S(1)} %pad_maximum_fusion.20), channel_id=1, source_target_pairs={{0,1},{1,2},{2,3},{3,0},{4,5},{5,6},{6,7},{7,4},{8,9},{9,10},{10,1... | collective-permute-start | bytes 393224 | tf_op jit(solution)/shard_map/ppermute | solution.py:701
  767.5 212.7 %copy-start.25 = (bf16[512,2048]{1,0:T(8,128)(2,1)}, bf16[512,2048]{1,0:T(8,128)(2,1)S(1)}, u32[]{:S(2)}) copy-start(bf16[512,2048]{1,0:T(8,128)(2,1)S(1)} %add_convert_fusion) | copy-start | bytes 6291460
  767.6 254.4 %reduce-scatter.12.cloned.1.call-start = ((), (), s32[]{:S(2)}) async-start(), calls=%async_computation.8 | async-start | bytes 19464192 | tf_op jit(solution)/shard_map/reduce_scatter | solution.py:894
  770.4 45.1 %collective-permute-start.40 = (bf16[1024,768]{1,0:T(8,128)(2,1)}, bf16[1024,768]{1,0:T(8,128)(2,1)}, u32[]{:S(2)}, u32[]{:S(2)}) collective-permute-start(bf16[1024,768]{1,0:T(8,128)(2,1)} %pad_maximum_fusion.1), channel_id=1, source_target_pairs={{0,4},{4,0},{1,5},{5,1},{2,6},{6,2},{3,7},{7,3},{8,12},{12,8},{9,1... | collective-permute-start | bytes 4718600 | tf_op jit(solution)/shard_map/ppermute | solution.py:1032
  772.2 60.4 %collective-permute-start.36 = (bf16[512,2048]{1,0:T(8,128)(2,1)}, bf16[512,2048]{1,0:T(8,128)(2,1)}, u32[]{:S(2)}, u32[]{:S(2)}) collective-permute-start(bf16[512,2048]{1,0:T(8,128)(2,1)} %fusion.6), channel_id=1, source_target_pairs={{0,1},{1,2},{2,3},{4,5},{5,6},{6,7},{8,9},{9,10},{10,11},{12,13},{... | collective-permute-start | bytes 6291464 | tf_op jit(solution)/shard_map/ppermute | solution.py:638
  775.6 57.1 %collective-permute-start.37 = (bf16[512,2048]{1,0:T(8,128)(2,1)}, bf16[512,2048]{1,0:T(8,128)(2,1)}, u32[]{:S(2)}, u32[]{:S(2)}) collective-permute-start(bf16[512,2048]{1,0:T(8,128)(2,1)} %fusion.6), channel_id=1, source_target_pairs={{1,0},{2,1},{3,2},{5,4},{6,5},{7,6},{9,8},{10,9},{11,10},{13,12},{... | collective-permute-start | bytes 6291464 | tf_op jit(solution)/shard_map/ppermute | solution.py:639
  776.9 85.9 %collective-permute-start.38 = (bf16[512,2048]{1,0:T(8,128)(2,1)S(1)}, bf16[512,2048]{1,0:T(8,128)(2,1)}, u32[]{:S(2)}, u32[]{:S(2)}) collective-permute-start(bf16[512,2048]{1,0:T(8,128)(2,1)S(1)} %add_convert_fusion), channel_id=1, source_target_pairs={{0,1},{1,2},{2,3},{4,5},{5,6},{6,7},{8,9},{9,10},{10,11},{12,13},{... | collective-permute-start | bytes 6291464 | tf_op jit(solution)/shard_map/ppermute | solution.py:638
  783.1 85.2 %collective-permute-start.39 = (bf16[512,2048]{1,0:T(8,128)(2,1)S(1)}, bf16[512,2048]{1,0:T(8,128)(2,1)}, u32[]{:S(2)}, u32[]{:S(2)}) collective-permute-start(bf16[512,2048]{1,0:T(8,128)(2,1)S(1)} %add_convert_fusion), channel_id=1, source_target_pairs={{1,0},{2,1},{3,2},{5,4},{6,5},{7,6},{9,8},{10,9},{11,10},{13,12},{... | collective-permute-start | bytes 6291464 | tf_op jit(solution)/shard_map/ppermute | solution.py:639
  784.7 33.5 %slice-start.6 = ((s8[8388608]{0:T(1024)(128)(4,1)}), s8[4194304]{0:T(1024)(128)(4,1)S(1)}, s32[]{:S(2)}) async-start(s8[8388608]{0:T(1024)(128)(4,1)} %bitcast.177), calls=%async_computation.18 | async-start | bytes 8388608
  868.3 28.6 %collective-permute-start.41 = (bf16[512,2048]{1,0:T(8,128)(2,1)}, bf16[512,2048]{1,0:T(8,128)(2,1)}, u32[]{:S(2)}, u32[]{:S(2)}) collective-permute-start(bf16[512,2048]{1,0:T(8,128)(2,1)} %collective-permute-done.36), channel_id=1, source_target_pairs={{1,2},{2,3},{5,6},{6,7},{9,10},{10,11},{13,14},{14,15},{17,18},{18... | collective-permute-start | bytes 6291464 | tf_op jit(solution)/shard_map/ppermute | solution.py:638
  870.3 53.5 %collective-permute-start.42 = (bf16[512,2048]{1,0:T(8,128)(2,1)}, bf16[512,2048]{1,0:T(8,128)(2,1)}, u32[]{:S(2)}, u32[]{:S(2)}) collective-permute-start(bf16[512,2048]{1,0:T(8,128)(2,1)} %collective-permute-done.37), channel_id=1, source_target_pairs={{1,0},{2,1},{5,4},{6,5},{9,8},{10,9},{13,12},{14,13},{17,16},{18,1... | collective-permute-start | bytes 6291464 | tf_op jit(solution)/shard_map/ppermute | solution.py:639
  871.6 52.2 %collective-permute-start.43 = (bf16[512,2048]{1,0:T(8,128)(2,1)}, bf16[512,2048]{1,0:T(8,128)(2,1)}, u32[]{:S(2)}, u32[]{:S(2)}) collective-permute-start(bf16[512,2048]{1,0:T(8,128)(2,1)} %collective-permute-done.38), channel_id=1, source_target_pairs={{1,2},{2,3},{5,6},{6,7},{9,10},{10,11},{13,14},{14,15},{17,18},{18... | collective-permute-start | bytes 6291464 | tf_op jit(solution)/shard_map/ppermute | solution.py:638
  873.6 91.3 %collective-permute-start.44 = (bf16[512,2048]{1,0:T(8,128)(2,1)}, bf16[512,2048]{1,0:T(8,128)(2,1)}, u32[]{:S(2)}, u32[]{:S(2)}) collective-permute-start(bf16[512,2048]{1,0:T(8,128)(2,1)} %collective-permute-done.39), channel_id=1, source_target_pairs={{1,0},{2,1},{5,4},{6,5},{9,8},{10,9},{13,12},{14,13},{17,16},{18,1... | collective-permute-start | bytes 6291464 | tf_op jit(solution)/shard_map/ppermute | solution.py:639
  964.9 19.6 %collective-permute-start.45 = (bf16[512,2048]{1,0:T(8,128)(2,1)}, bf16[512,2048]{1,0:T(8,128)(2,1)S(1)}, u32[]{:S(2)}, u32[]{:S(2)}) collective-permute-start(bf16[512,2048]{1,0:T(8,128)(2,1)} %collective-permute-done.41), channel_id=1, source_target_pairs={{2,3},{6,7},{10,11},{14,15},{18,19},{22,23},{26,27},{30,31}} | collective-permute-start | bytes 6291464 | tf_op jit(solution)/shard_map/ppermute | solution.py:638
  965.7 50.7 %collective-permute-start.46 = (bf16[512,2048]{1,0:T(8,128)(2,1)}, bf16[512,2048]{1,0:T(8,128)(2,1)S(1)}, u32[]{:S(2)}, u32[]{:S(2)}) collective-permute-start(bf16[512,2048]{1,0:T(8,128)(2,1)} %collective-permute-done.42), channel_id=1, source_target_pairs={{1,0},{5,4},{9,8},{13,12},{17,16},{21,20},{25,24},{29,28}} | collective-permute-start | bytes 6291464 | tf_op jit(solution)/shard_map/ppermute | solution.py:639
  967.0 62.5 %collective-permute-start.47 = (bf16[512,2048]{1,0:T(8,128)(2,1)}, bf16[512,2048]{1,0:T(8,128)(2,1)}, u32[]{:S(2)}, u32[]{:S(2)}) collective-permute-start(bf16[512,2048]{1,0:T(8,128)(2,1)} %collective-permute-done.43), channel_id=1, source_target_pairs={{2,3},{6,7},{10,11},{14,15},{18,19},{22,23},{26,27},{30,31}} | collective-permute-start | bytes 6291464 | tf_op jit(solution)/shard_map/ppermute | solution.py:638
  969.0 108.7 %collective-permute-start.48 = (bf16[512,2048]{1,0:T(8,128)(2,1)}, bf16[512,2048]{1,0:T(8,128)(2,1)}, u32[]{:S(2)}, u32[]{:S(2)}) collective-permute-start(bf16[512,2048]{1,0:T(8,128)(2,1)} %collective-permute-done.44), channel_id=1, source_target_pairs={{1,0},{5,4},{9,8},{13,12},{17,16},{21,20},{25,24},{29,28}} | collective-permute-start | bytes 6291464 | tf_op jit(solution)/shard_map/ppermute | solution.py:639
  1023.4 54.3 %collective-permute-start.49 = (bf16[256,768]{1,0:T(8,128)(2,1)S(1)}, bf16[256,768]{1,0:T(8,128)(2,1)S(1)}, u32[]{:S(2)}, u32[]{:S(2)}) collective-permute-start(bf16[256,768]{1,0:T(8,128)(2,1)S(1)} %get-tuple-element.451), channel_id=1, source_target_pairs={{0,1},{1,2},{2,3},{3,0},{4,5},{5,6},{6,7},{7,4},{8,9},{9,10},{10,1... | collective-permute-start | bytes 1179656 | tf_op jit(solution)/shard_map/ppermute | solution.py:701
  1024.8 52.8 %collective-permute-start.50 = (bf16[256,768]{1,0:T(8,128)(2,1)S(1)}, bf16[256,768]{1,0:T(8,128)(2,1)S(1)}, u32[]{:S(2)}, u32[]{:S(2)}) collective-permute-start(bf16[256,768]{1,0:T(8,128)(2,1)S(1)} %get-tuple-element.452), channel_id=1, source_target_pairs={{0,2},{1,3},{2,0},{3,1},{4,6},{5,7},{6,4},{7,5},{8,10},{9,11},{10,... | collective-permute-start | bytes 1179656 | tf_op jit(solution)/shard_map/ppermute | solution.py:701
  1024.8 56.9 %collective-permute-start.51 = (bf16[256,768]{1,0:T(8,128)(2,1)S(1)}, bf16[256,768]{1,0:T(8,128)(2,1)S(1)}, u32[]{:S(2)}, u32[]{:S(2)}) collective-permute-start(bf16[256,768]{1,0:T(8,128)(2,1)S(1)} %get-tuple-element.450), channel_id=1, source_target_pairs={{0,3},{1,0},{2,1},{3,2},{4,7},{5,4},{6,5},{7,6},{8,11},{9,8},{10,9... | collective-permute-start | bytes 1179656 | tf_op jit(solution)/shard_map/ppermute | solution.py:701
  (76 other events, 373.8 us)
Sparse Core Ops, SparseCore 0:
  139.5 81.1 all-gather.4
  222.3 85.7 all-gather.6
  310.3 94.5 reduce-scatter.5
  407.1 92.5 reduce-scatter.7
  502.0 192.5 reduce-scatter.9
  767.7 94.9 reduce-scatter.13
  868.4 117.3 reduce-scatter.11
